TPU v7x, 32 devices: a whole 2x2x4 slice. The times are simulated.
32 devices in a mesh: dp: 8 (over y, x, core), tensor: 4 (over z).
Axes of the slice: x: 2, y: 2, z: 4, core: 2. Of those that a mesh axis runs over, the one named last changes fastest.
Arguments:
- latents: bfloat16 [8, 512, 1536], P('dp', 'tensor'), may hold values from -6 to 6
- features: bfloat16 [8, 2048, 1536], P('dp', 'tensor'), may hold values from -6 to 6
- lengths: int32 [8, 8], P('dp'), may hold values from 1 to 512, 2048 in all within a row
- valid_media: int32 [8, 8], P('dp'), may hold values from 0 to 1, as said below
- media_gain: float32 [1536], replicated, may hold values from 0.5 to 1.5
- media_shift: float32 [1536], replicated, may hold values from -2 to 2
- latent_gain: float32 [1536], replicated, may hold values from 0.5 to 1.5
- latent_shift: float32 [1536], replicated, may hold values from -2 to 2
- feed_gain: float32 [1536], replicated, may hold values from 0.5 to 1.5
- feed_shift: float32 [1536], replicated, may hold values from -2 to 2
- query_weight: bfloat16 [1536, 1536], P(None, 'tensor'), may hold values from -0.15625 to 0.15625
- key_value_weight: bfloat16 [1536, 2, 1536], P(None, None, 'tensor'), may hold values from -0.15625 to 0.15625
- output_weight: bfloat16 [1536, 1536], P('tensor'), may hold values from -1.5 to 1.5
- up_weight: bfloat16 [1536, 6144], P(None, 'tensor'), may hold values from -0.15625 to 0.15625
- down_weight: bfloat16 [6144, 1536], P('tensor'), may hold values from -0.078125 to 0.078125
- cotangent: bfloat16 [8, 512, 1536], P('dp', 'tensor'), may hold values from -0.00059890747 to 0.00059890747
Outputs:
- result: bfloat16 [8, 512, 1536], P('dp', 'tensor')
- penalty: float32 [], replicated
- latents_grad: float32 [8, 512, 1536], P('dp', 'tensor')
- features_grad: float32 [8, 2048, 1536], P('dp', 'tensor')
- media_gain_grad: float32 [1536], P(('dp', 'tensor'))
- media_shift_grad: float32 [1536], P(('dp', 'tensor'))
- latent_gain_grad: float32 [1536], P(('dp', 'tensor'))
- latent_shift_grad: float32 [1536], P(('dp', 'tensor'))
- feed_gain_grad: float32 [1536], P(('dp', 'tensor'))
- feed_shift_grad: float32 [1536], P(('dp', 'tensor'))
- query_grad: float32 [1536, 1536], P('dp', 'tensor')
- keyval_grad: float32 [1536, 2, 1536], P('dp', None, 'tensor')
- output_grad: float32 [1536, 1536], P('tensor', 'dp')
- up_grad: float32 [1536, 6144], P('dp', 'tensor')
- down_grad: float32 [6144, 1536], P('tensor', 'dp')
Inputs may be any that keep to these rules, and one draw needn't show every extreme that they name: `lengths`: each row holds the patch counts of 8 image slots that sum to 2048; the largest of each row is exactly 512. `valid_media`: 0 or 1; the first slot of every sequence holds 1.
All inputs are finite; a program needn't handle non-finite values.
Results may differ from a plain program's by a relative error of at most 0.012.
Values may be sent and summed in bfloat16 or wider, within the bound.
No kernel may reach another device: no remote copies, remote signals or barrier semaphores. Data moves between devices by JAX's collectives and lax.ppermute only.
A program may use at most 192 MiB of HBM per device.

v0:
```python
from functools import partial

import jax
import jax.numpy as jnp
from jax import lax
from jax.sharding import PartitionSpec as P

HD = 96
LAT = 64
IMGS = 8
P_SEQ = 2048


EPSILON = 1e-05
NEGATIVE = -1e30


def norm_forward(values, gain_row, offset):
    center = values - jnp.mean(values, axis=-1, keepdims=True)
    inv_root = lax.rsqrt(jnp.mean(center * center, axis=-1, keepdims=True) + EPSILON)
    normal = center * inv_root
    return (normal * gain_row + offset, normal, inv_root)


def norm_backward(grad_rows, normal, inv_root, gain_row):
    scaled = grad_rows * gain_row
    reduced = (
        scaled
        - jnp.mean(scaled, axis=-1, keepdims=True)
        - normal * jnp.mean(scaled * normal, axis=-1, keepdims=True)
    )
    return (
        reduced * inv_root,
        jnp.sum(grad_rows * normal, axis=(0, 1)),
        jnp.sum(grad_rows, axis=(0, 1)),
    )


def key_tables(lengths, valid_media):
    ends_at = jnp.cumsum(lengths, axis=1)
    positions = jnp.arange(P_SEQ, dtype=jnp.int32)
    patch_segment = jnp.sum(
        (positions[None, :, None] >= ends_at[:, None, :]).astype(jnp.int32), axis=2
    )
    image_index = jnp.arange(IMGS, dtype=jnp.int32)
    patch_valid = jnp.sum(
        jnp.where(
            patch_segment[:, :, None] == image_index[None, None, :], valid_media[:, None, :], 0
        ),
        axis=2,
    )
    latent_segment = jnp.arange(LAT * IMGS, dtype=jnp.int32) // LAT
    seq_total = lengths.shape[0]
    key_segment = jnp.concatenate(
        [patch_segment, jnp.broadcast_to(latent_segment, (seq_total, LAT * IMGS))], axis=1
    )
    key_valid = jnp.concatenate([patch_valid, jnp.ones((seq_total, LAT * IMGS), jnp.int32)], axis=1)
    row_weight = jnp.repeat(valid_media, LAT, axis=1).astype(jnp.float32)
    return (key_segment, key_valid, row_weight)


def allowed_table(key_segment, key_valid):
    latent_segment = jnp.arange(LAT * IMGS, dtype=jnp.int32) // LAT
    return (latent_segment[:, None] == key_segment[None, :]) & (key_valid[None, :] > 0)


def softmax_parts(head_query, head_key, allowed):
    scores = jnp.einsum(
        "qhe,khe->hqk", head_query, head_key, preferred_element_type=jnp.float32
    ) * HD ** (-0.5)
    masked = jnp.where(allowed[None], scores, NEGATIVE)
    top_score = jnp.max(masked, axis=-1, keepdims=True)
    unnormed = jnp.where(allowed[None], jnp.exp(masked - top_score), 0.0)
    denominator = jnp.sum(unnormed, axis=-1, keepdims=True)
    return (scores, top_score, denominator, unnormed / denominator)


def split_heads(query_low, keyval_low):
    rows_all = query_low.shape[0]
    heads_here = query_low.shape[1] // HD
    head_query = query_low.reshape(rows_all, heads_here, HD)
    head_key = keyval_low[0].reshape(-1, heads_here, HD)
    head_value = keyval_low[1].reshape(-1, heads_here, HD)
    return (head_query, head_key, head_value)


def attend_forward(pieces):
    query_low, keyval_low, key_segment, key_valid = pieces
    head_query, head_key, head_value = split_heads(query_low, keyval_low)
    allowed = allowed_table(key_segment, key_valid)
    scores, top_score, denominator, probability = softmax_parts(head_query, head_key, allowed)
    entropy = (
        top_score[..., 0]
        + jnp.log(denominator[..., 0])
        - jnp.sum(jnp.where(allowed[None], probability * scores, 0.0), axis=-1)
    )
    attended = jnp.einsum(
        "hqk,khe->qhe",
        probability.astype(jnp.bfloat16),
        head_value,
        preferred_element_type=jnp.float32,
    )
    return (attended.reshape(query_low.shape[0], query_low.shape[1]).astype(jnp.bfloat16), entropy)


def attend_backward(pieces):
    query_low, keyval_low, key_segment, key_valid, back_attended, coefficient = pieces
    head_query, head_key, head_value = split_heads(query_low, keyval_low)
    allowed = allowed_table(key_segment, key_valid)
    scores, top_score, denominator, probability = softmax_parts(head_query, head_key, allowed)
    back_heads = back_attended.reshape(head_query.shape)
    back_prob = jnp.einsum(
        "qhe,khe->hqk", back_heads, head_value, preferred_element_type=jnp.float32
    )
    adjusted = back_prob - coefficient[None, :, None] * scores
    back_scores = (
        probability * (adjusted - jnp.sum(probability * adjusted, axis=-1, keepdims=True))
    ).astype(jnp.bfloat16)
    back_queries = (
        jnp.einsum("hqk,khe->qhe", back_scores, head_key, preferred_element_type=jnp.float32)
        * HD ** (-0.5)
    ).astype(jnp.bfloat16)
    back_keys = (
        jnp.einsum("hqk,qhe->khe", back_scores, head_query, preferred_element_type=jnp.float32)
        * HD ** (-0.5)
    ).astype(jnp.bfloat16)
    back_values = jnp.einsum(
        "hqk,qhe->khe",
        probability.astype(jnp.bfloat16),
        back_heads,
        preferred_element_type=jnp.float32,
    ).astype(jnp.bfloat16)
    width_here = query_low.shape[1]
    return (
        back_queries.reshape(-1, width_here),
        jnp.stack([back_keys.reshape(-1, width_here), back_values.reshape(-1, width_here)]),
    )


def local(
    latents,
    features,
    lengths,
    valid_media,
    media_gain,
    media_shift,
    latent_gain,
    latent_shift,
    feed_gain,
    feed_shift,
    query_weight,
    key_value_weight,
    output_weight,
    up_weight,
    down_weight,
    cotangent,
):
    tensor_count = lax.axis_size("tensor")
    latent_in = latents.astype(jnp.float32)
    media_in = features.astype(jnp.float32)
    media_normed, media_hat, media_root = norm_forward(media_in, media_gain, media_shift)
    latent_normed, latent_hat, latent_root = norm_forward(latent_in, latent_gain, latent_shift)
    media_all, latent_all = (
        lax.all_gather(media_normed.astype(jnp.bfloat16), "tensor", axis=1, tiled=True),
        lax.all_gather(latent_normed.astype(jnp.bfloat16), "tensor", axis=1, tiled=True),
    )
    key_segment, key_valid, row_weight = key_tables(lengths, valid_media)
    query_low = jnp.einsum(
        "sqd,di->sqi", latent_all, query_weight, preferred_element_type=jnp.float32
    ).astype(jnp.bfloat16)
    media_key_input = jnp.concatenate([media_all, latent_all], axis=1)
    keyval_low = jnp.einsum(
        "equ,uyf->eyqf", media_key_input, key_value_weight, preferred_element_type=jnp.float32
    ).astype(jnp.bfloat16)
    attended_low, entropy = lax.map(attend_forward, (query_low, keyval_low, key_segment, key_valid))
    attend_terms = jnp.einsum(
        "sqi,id->sqd", attended_low, output_weight, preferred_element_type=jnp.float32
    )
    middle = latent_in + lax.psum_scatter(attend_terms, "tensor", scatter_dimension=1, tiled=True)
    feed_normed, feed_hat, feed_root = norm_forward(middle, feed_gain, feed_shift)
    feed_all = lax.all_gather(feed_normed.astype(jnp.bfloat16), "tensor", axis=1, tiled=True)
    hidden = jnp.einsum("sqd,df->sqf", feed_all, up_weight, preferred_element_type=jnp.float32)
    activation = jax.nn.gelu(hidden, approximate=False).astype(jnp.bfloat16)
    feed_terms = jnp.einsum(
        "sqf,fd->sqd", activation, down_weight, preferred_element_type=jnp.float32
    )
    result = middle + lax.psum_scatter(
        feed_terms.astype(jnp.bfloat16), "tensor", scatter_dimension=1, tiled=True
    ).astype(jnp.float32)
    entropy_part = jnp.sum(entropy * row_weight[:, None, :])
    count_part = jnp.sum(valid_media).astype(jnp.float32) / tensor_count
    penalty_total, count_total = lax.psum((entropy_part, count_part), ("dp", "tensor"))
    penalty = penalty_total / count_total
    grad_rows = lax.all_gather(cotangent, "tensor", axis=1, tiled=True)
    grad_down = jnp.einsum("sqf,sqd->fd", activation, grad_rows, preferred_element_type=jnp.float32)
    back_activation = jnp.einsum(
        "sqd,fd->sqf", grad_rows, down_weight, preferred_element_type=jnp.float32
    )
    gelu_pull = jax.vjp(partial(jax.nn.gelu, approximate=False), hidden)[1]
    back_hidden = gelu_pull(back_activation)[0].astype(jnp.bfloat16)
    grad_up = jnp.einsum("sqd,sqf->df", feed_all, back_hidden, preferred_element_type=jnp.float32)
    back_terms = jnp.einsum(
        "sqf,df->sqd", back_hidden, up_weight, preferred_element_type=jnp.float32
    )
    back_feed = lax.psum_scatter(back_terms, "tensor", scatter_dimension=1, tiled=True)
    feed_part, feed_gain_grad, feed_shift_grad = norm_backward(
        back_feed, feed_hat, feed_root, feed_gain
    )
    back_middle = cotangent.astype(jnp.float32) + feed_part
    back_branch = lax.all_gather(back_middle.astype(jnp.bfloat16), "tensor", axis=1, tiled=True)
    grad_output = jnp.einsum(
        "sqi,sqd->id", attended_low, back_branch, preferred_element_type=jnp.float32
    )
    back_attended = jnp.einsum(
        "sqd,id->sqi", back_branch, output_weight, preferred_element_type=jnp.float32
    ).astype(jnp.bfloat16)
    coefficient = row_weight / count_total
    back_queries, backward_key_value_rows = lax.map(
        attend_backward, (query_low, keyval_low, key_segment, key_valid, back_attended, coefficient)
    )
    grad_query = jnp.einsum(
        "sqd,sqi->di", latent_all, back_queries, preferred_element_type=jnp.float32
    )
    grad_keyval = jnp.einsum(
        "raj,ryah->jyh",
        media_key_input,
        backward_key_value_rows,
        preferred_element_type=jnp.float32,
    )
    back_inputs = jnp.einsum(
        "xypa,eya->xpe",
        backward_key_value_rows,
        key_value_weight,
        preferred_element_type=jnp.float32,
    )
    latent_terms = (
        jnp.einsum("sqi,di->sqd", back_queries, query_weight, preferred_element_type=jnp.float32)
        + back_inputs[:, P_SEQ:]
    )
    back_media, back_latent = (
        lax.psum_scatter(back_inputs[:, :P_SEQ], "tensor", scatter_dimension=1, tiled=True),
        lax.psum_scatter(latent_terms, "tensor", scatter_dimension=1, tiled=True),
    )
    features_grad, media_gain_grad, media_shift_grad = norm_backward(
        back_media, media_hat, media_root, media_gain
    )
    latent_part, latent_gain_grad, latent_shift_grad = norm_backward(
        back_latent, latent_hat, latent_root, latent_gain
    )
    latents_grad = back_middle + latent_part
    norm_rows = jnp.stack(
        [
            media_gain_grad,
            media_shift_grad,
            latent_gain_grad,
            latent_shift_grad,
            feed_gain_grad,
            feed_shift_grad,
        ]
    )
    norm_shares = lax.psum_scatter(norm_rows, ("dp", "tensor"), scatter_dimension=1, tiled=True)
    query_share, keyval_share, output_share, up_share, down_share = (
        lax.psum_scatter(grad_query, "dp", scatter_dimension=0, tiled=True),
        lax.psum_scatter(grad_keyval, "dp", scatter_dimension=0, tiled=True),
        lax.psum_scatter(grad_output, "dp", scatter_dimension=1, tiled=True),
        lax.psum_scatter(grad_up, "dp", scatter_dimension=0, tiled=True),
        lax.psum_scatter(grad_down, "dp", scatter_dimension=1, tiled=True),
    )
    return (
        result.astype(jnp.bfloat16),
        penalty,
        latents_grad,
        features_grad,
        norm_shares[0],
        norm_shares[1],
        norm_shares[2],
        norm_shares[3],
        norm_shares[4],
        norm_shares[5],
        query_share,
        keyval_share,
        output_share,
        up_share,
        down_share,
    )


def solution(mesh):
    return jax.shard_map(
        local,
        mesh=mesh,
        in_specs=(
            P("dp", "tensor", None),
            P("dp", "tensor", None),
            P("dp", None),
            P("dp", None),
            P(),
            P(),
            P(),
            P(),
            P(),
            P(),
            P(None, "tensor"),
            P(None, None, "tensor"),
            P("tensor", None),
            P(None, "tensor"),
            P("tensor", None),
            P("dp", "tensor", None),
        ),
        out_specs=(
            P("dp", "tensor", None),
            P(),
            P("dp", "tensor", None),
            P("dp", "tensor", None),
            P(("dp", "tensor")),
            P(("dp", "tensor")),
            P(("dp", "tensor")),
            P(("dp", "tensor")),
            P(("dp", "tensor")),
            P(("dp", "tensor")),
            P("dp", "tensor"),
            P("dp", None, "tensor"),
            P("tensor", "dp"),
            P("dp", "tensor"),
            P("tensor", "dp"),
        ),
        check_vma=False,
    )
```

profile of v0, /device:TPU:0, one launch (start us, length us, event | category | flops | bytes accessed | tf_op | source)
XLA Modules:
  0.0 1291.0 jit_solution(63317459219674474)
XLA Ops:
  7.3 1.3 convert_reduce_fusion.1
  8.6 1.3 fusion.76
  10.3 2.1 fusion.70
  12.5 1.8 convert_reduce_fusion
  14.3 2.0 fusion.25
  16.9 1.8 fusion.20
  19.3 2.0 compare_and_fusion
  21.2 31.2 %all-gather.8.cloned.1.call-done = bf16[1,512,1536]{2,1,0:T(8,128)(2,1)} async-done(((bf16[1,128,1536]{2,1,0:T(8,128)(2,1)}), bf16[1,512,1536]{2,1,0:T(8,128)(2,1)}) %all-gather.8.cloned.1.call-update) | async-done | bytes 1572880 | tf_op jit(solution)/shard_map/all_gather | solution.py:165
  52.4 2.6 fusion.54
  55.0 113.8 %all-gather.6.cloned.1.call-done = bf16[1,2048,1536]{2,1,0:T(8,128)(2,1)} async-done(((bf16[1,512,1536]{2,1,0:T(8,128)(2,1)}), bf16[1,2048,1536]{2,1,0:T(8,128)(2,1)}) %all-gather.6.cloned.1.call-update) | async-done | bytes 6291472 | tf_op jit(solution)/shard_map/all_gather | solution.py:164
  168.8 9.3 fusion.7
  178.1 2.3 fusion.88
  180.4 6.2 select_reduce_fusion.1
  186.6 9.3 fusion.1
  195.9 11.8 fusion.60
  208.4 2.7 convolution_bitcast_fusion.3
  211.1 58.6 %reduce-scatter.14.cloned.1.call-done = f32[1,128,1536]{2,1,0:T(8,128)} async-done(((f32[1,512,1536]{2,1,0:T(8,128)}), f32[1,128,1536]{2,1,0:T(8,128)}) %reduce-scatter.14.cloned.1.call-update) | async-done | bytes 786448 | tf_op jit(solution)/shard_map/reduce_scatter | solution.py:179
  269.7 1.3 fusion.87
  271.3 1.6 add_convert_fusion.2
  273.6 36.6 %all-gather.10.cloned.1.call-done = bf16[1,512,1536]{2,1,0:T(8,128)(2,1)} async-done(((bf16[1,128,1536]{2,1,0:T(8,128)(2,1)}), bf16[1,512,1536]{2,1,0:T(8,128)(2,1)}) %all-gather.10.cloned.1.call-update) | async-done | bytes 1572880 | tf_op jit(solution)/shard_map/all_gather | solution.py:181
  310.2 12.8 multiply_convert_fusion.1
  323.1 24.6 %all-gather.12.cloned.1.call-done = bf16[1,512,1536]{2,1,0:T(8,128)(2,1)} async-done(((bf16[1,128,1536]{2,1,0:T(8,128)(2,1)}), bf16[1,512,1536]{2,1,0:T(8,128)(2,1)}) %all-gather.12.cloned.1.call-update) | async-done | bytes 1572880 | tf_op jit(solution)/shard_map/all_gather | solution.py:194
  347.7 8.0 add_convert_fusion
  356.8 6.6 convolution_bitcast_fusion.2
  363.5 6.6 fusion.32
  370.2 52.5 %reduce-scatter.18.cloned.1.call-done = f32[1,128,1536]{2,1,0:T(8,128)} async-done(((f32[1,512,1536]{2,1,0:T(8,128)}), f32[1,128,1536]{2,1,0:T(8,128)}) %reduce-scatter.18.cloned.1.call-update) | async-done | bytes 786448 | tf_op jit(solution)/shard_map/reduce_scatter | solution.py:205
  422.7 2.1 multiply_reduce_fusion.2
  425.3 35.0 %reduce-scatter.16.cloned.1.call-done = bf16[1,128,1536]{2,1,0:T(8,128)(2,1)} async-done(((bf16[1,512,1536]{2,1,0:T(8,128)(2,1)}), bf16[1,128,1536]{2,1,0:T(8,128)(2,1)}) %reduce-scatter.16.cloned.1.call-update) | async-done | bytes 393232 | tf_op jit(solution)/shard_map/reduce_scatter | solution.py:187
  460.4 2.9 fusion.85
  463.3 1.3 fusion.90
  465.3 41.6 %psum.15 = f32[]{:T(128)} all-reduce(f32[]{:T(128)S(6)} %div.104), channel_id=1, replica_groups=mesh['dp'=8,'tensor'=4] {'dp','tensor'}, use_global_device_ids=true, to_apply=%region_17.18 | all-reduce | flops 1 | bytes 8 | tf_op jit(solution)/shard_map/psum | solution.py:192
  507.8 2.7 fusion.57
  510.5 13.1 %fusion.9 = bf16[4,96,2560]{2,1,0:T(8,128)(2,1)} fusion(bf16[512,4,96]{0,2,1:T(8,128)(2,1)S(1)} %bitcast.137, f32[4,512,2560]{2,1,0:T(8,128)} %copy-done.1, f32[4,512]{1,0:T(4,128)S(1)} %copy-done.23, f32[4,512]{1,0:T(4,128)S(1)} %get-tuple-element.139, pred[512,2560]{1,0:T(8,128)(4,1)S(1)} %copy-done.4), kind=kOutput, calls=%fused_computation.21 | convolution fusion | flops 1039073280 | bytes 24657920 | tf_op jit(solution)/shard_map/while/body/eval_jaxpr/hqk,qhe->khe/dot_general | solution.py:127
  523.6 20.4 %multiply_reduce_fusion = (f32[4,512]{1,0:T(4,128)S(1)}, f32[4,512]{1,0:T(4,128)}, f32[4,512,2560]{2,1,0:T(8,128)}) fusion(f32[4,512]{1,0:T(4,128)S(1)} %copy-done.23, f32[4,512]{1,0:T(4,128)S(1)} %get-tuple-element.139, f32[4,512,2560]{2,1,0:T(8,128)} %copy-done.1, pred[512,2560]{1,0:T(8,128)(4,1)S(1)} %copy-done.4, f32[512]{0:T(512)S(1)} %divide_multiply_fusion, ...), kind=kOutput, calls=%fused_computation.1 | convolution fusion | flops 1069543424 | bytes 45647872 | tf_op jit(solution)/shard_map/while/body/eval_jaxpr/qhe,khe->hqk/dot_general | solution.py:112
  544.0 16.0 %multiply_convert_fusion = bf16[4,512,2560]{2,1,0:T(8,128)(2,1)} fusion(f32[4,512,2560]{2,1,0:T(8,128)} %get-tuple-element.142, f32[4,512]{1,0:T(4,128)S(1)} %get-tuple-element.108, f32[4,512]{1,0:T(4,128)S(1)} %copy-done.23, f32[4,512]{1,0:T(4,128)S(1)} %get-tuple-element.139, f32[4,512,2560]{2,1,0:T(8,128)S(1)} %bitcast.112, pred[512,2560]{1,0:T(8,128)(4,1)S(1)} %copy-done.4), kind=kLoop, calls=%fused_computation | loop fusion | flops 41943040 | bytes 53764096 | tf_op jit(solution)/shard_map/while/body/eval_jaxpr/convert_element_type | solution.py:118
  560.1 7.4 fusion.53
  567.5 3.1 fusion.8
  570.6 4.0 copy.45
  574.6 4.0 copy.44
  578.6 8.7 convolution_bitcast_fusion
  587.3 5.5 copy-done.6
  592.8 2.7 fusion.18
  595.6 10.5 slice.51
  606.2 11.8 fusion.6
  619.9 35.4 %reduce-scatter.20.cloned.1.call-done = f32[1,128,1536]{2,1,0:T(8,128)} async-done(((f32[1,512,1536]{2,1,0:T(8,128)}), f32[1,128,1536]{2,1,0:T(8,128)}) %reduce-scatter.20.cloned.1.call-update) | async-done | bytes 786448 | tf_op jit(solution)/shard_map/reduce_scatter | solution.py:242
  655.4 2.0 fusion.75
  658.6 210.9 %reduce-scatter.22.cloned.1.call-done = f32[1,512,1536]{2,1,0:T(8,128)} async-done(((f32[1,2048,1536]{2,1,0:T(8,128)}), f32[1,512,1536]{2,1,0:T(8,128)}) %reduce-scatter.22.cloned.1.call-update) | async-done | bytes 3145744 | tf_op jit(solution)/shard_map/reduce_scatter | solution.py:241
  869.5 4.3 fusion.24
  874.9 1.4 stack.32
  876.4 2.0 copy.51
  878.4 4.2 fusion.35
  882.7 4.1 fusion.49
  886.9 8.3 fusion.45
  895.4 8.8 fusion.39
  904.2 1.4 multiply_reduce_fusion.7
  905.6 41.5 %psum.14 = f32[]{:T(128)} all-reduce(f32[]{:T(128)} %multiply_reduce_fusion.7), channel_id=1, replica_groups=mesh['dp'=8,'tensor'=4] {'dp','tensor'}, use_global_device_ids=true, to_apply=%region_15.16 | all-reduce | flops 1 | bytes 8 | tf_op jit(solution)/shard_map/psum | solution.py:192
  949.8 2.4 fusion.74
  952.2 2.3 copy.48
  955.9 5.0 fusion.23
  960.9 68.4 %reduce-scatter.34.cloned.1.call-done = f32[48,6]{1,0:T(8,128)} async-done(((f32[1536,6]{1,0:T(8,128)}), f32[48,6]{1,0:T(8,128)}) %reduce-scatter.34.cloned.1.call-update) | async-done | bytes 1168
  1033.9 41.3 %reduce-scatter.28.cloned.1.call-done = f32[384,192]{0,1:T(8,128)} async-done(((f32[384,1536]{0,1:T(8,128)}), f32[384,192]{0,1:T(8,128)}) %reduce-scatter.28.cloned.1.call-update) | async-done | bytes 294928 | tf_op jit(solution)/shard_map/reduce_scatter | solution.py:265
  1075.2 46.3 %reduce-scatter.24.cloned.1.call-done = f32[192,384]{1,0:T(8,128)} async-done(((f32[1536,384]{1,0:T(8,128)}), f32[192,384]{1,0:T(8,128)}) %reduce-scatter.24.cloned.1.call-update) | async-done | bytes 294928 | tf_op jit(solution)/shard_map/reduce_scatter | solution.py:263
  1121.5 80.8 %reduce-scatter.30.cloned.1.call-done = f32[192,1536]{1,0:T(8,128)} async-done(((f32[1536,1536]{1,0:T(8,128)}), f32[192,1536]{1,0:T(8,128)}) %reduce-scatter.30.cloned.1.call-update) | async-done | bytes 1179664 | tf_op jit(solution)/shard_map/reduce_scatter | solution.py:266
  1202.3 80.8 %reduce-scatter.32.cloned.1.call-done = f32[1536,192]{0,1:T(8,128)} async-done(((f32[1536,1536]{0,1:T(8,128)}), f32[1536,192]{0,1:T(8,128)}) %reduce-scatter.32.cloned.1.call-update) | async-done | bytes 1179664 | tf_op jit(solution)/shard_map/reduce_scatter | solution.py:267
  (157 shorter events, 18.2 us)
Async XLA Ops:
  7.2 161.6 %copy-start = (bf16[1536,2,384]{2,1,0:T(2,128)(2,1)S(1)}, bf16[1536,2,384]{2,1,0:T(2,128)(2,1)}, u32[]{:S(2)}) copy-start(bf16[1536,2,384]{2,1,0:T(2,128)(2,1)} %param.27) | copy-start | bytes 7077892
  7.2 9.7 copy-start.20
  7.2 9.7 copy-start.29
  7.2 45.2 %all-gather.8.cloned.1.call-start = ((), (), s32[]{:S(2)}) async-start(), calls=%async_computation.12 | async-start | bytes 1966080 | tf_op jit(solution)/shard_map/all_gather | solution.py:165
  8.6 1.3 copy-start.30
  9.8 0.5 copy-start.33
  12.4 156.3 %all-gather.6.cloned.1.call-start = ((), (), s32[]{:S(2)}) async-start(), calls=%async_computation.11 | async-start | bytes 7864320 | tf_op jit(solution)/shard_map/all_gather | solution.py:164
  12.5 4.4 copy-start.3
  14.3 2.0 copy-start.24
  14.3 4.5 copy-start.37
  14.3 4.7 copy-start.36
  16.3 0.6 copy-start.27
  18.7 251.0 %reduce-scatter.14.cloned.1.call-start = ((), (), s32[]{:S(2)}) async-start(), calls=%async_computation.13 | async-start | bytes 3932160 | tf_op jit(solution)/shard_map/reduce_scatter | solution.py:179
  54.9 125.4 %copy-start.12 = (bf16[512,384]{0,1:T(8,128)(2,1)}, bf16[512,384]{0,1:T(8,128)(2,1)S(1)}, u32[]{:S(2)}) copy-start(bf16[512,384]{0,1:T(8,128)(2,1)S(1)} %fusion.54) | copy-start | bytes 1179652
  186.5 9.3 copy-start.1
  195.8 11.8 copy-start.22
  195.8 12.5 copy-start.16
  207.6 0.7 copy-start.10
  208.4 61.3 %copy-start.7 = (bf16[1,128,1536]{2,1,0:T(8,128)(2,1)S(1)}, bf16[1,128,1536]{2,1,0:T(8,128)(2,1)}, u32[]{:S(2)}) copy-start(bf16[1,128,1536]{2,1,0:T(8,128)(2,1)} %param.16) | copy-start | bytes 1179652
  211.1 60.2 %copy-start.18 = (f32[1536]{0:T(1024)S(1)}, f32[1536]{0:T(1024)}, u32[]{:S(2)}) copy-start(f32[1536]{0:T(1024)} %param.24) | copy-start | bytes 18436
  211.1 99.2 %all-gather.10.cloned.1.call-start = ((), (), s32[]{:S(2)}) async-start(), calls=%async_computation.14 | async-start | bytes 1966080 | tf_op jit(solution)/shard_map/all_gather | solution.py:181
  271.0 52.1 %copy-start.32 = (f32[128]{0:T(128)}, f32[128]{0:T(128)S(1)}, u32[]{:S(2)}) copy-start(f32[128]{0:T(128)S(1)} %broadcast_multiply_fusion.7) | copy-start | bytes 1540
  271.3 51.8 %copy-start.35 = (f32[128]{0:T(128)}, f32[128]{0:T(128)S(1)}, u32[]{:S(2)}) copy-start(f32[128]{0:T(128)S(1)} %add_rsqrt_fusion.1) | copy-start | bytes 1540
  273.0 74.7 %all-gather.12.cloned.1.call-start = ((), (), s32[]{:S(2)}) async-start(), calls=%async_computation.16 | async-start | bytes 1966080 | tf_op jit(solution)/shard_map/all_gather | solution.py:194
  273.6 149.2 %reduce-scatter.18.cloned.1.call-start = ((), (), s32[]{:S(2)}) async-start(), calls=%async_computation.17 | async-start | bytes 3932160 | tf_op jit(solution)/shard_map/reduce_scatter | solution.py:205
  355.6 1.2 copy-start.38
  363.5 96.9 %reduce-scatter.16.cloned.1.call-start = ((), (), s32[]{:S(2)}) async-start(), calls=%async_computation.15 | async-start | bytes 1966080 | tf_op jit(solution)/shard_map/reduce_scatter | solution.py:187
  370.1 90.3 %copy-start.15 = (bf16[1,128,1536]{2,1,0:T(8,128)(2,1)S(1)}, bf16[1,128,1536]{2,1,0:T(8,128)(2,1)}, u32[]{:S(2)}) copy-start(bf16[1,128,1536]{2,1,0:T(8,128)(2,1)} %param.31) | copy-start | bytes 1179652
  370.2 137.6 %all-gather.14.cloned.1.call-start = ((), (), s32[]{:S(2)}) async-start(), calls=%async_computation.18 | async-start | bytes 1966080 | tf_op jit(solution)/shard_map/all_gather | solution.py:210
  463.3 47.1 %copy-start.23 = (f32[4,512]{1,0:T(4,128)S(1)}, f32[4,512]{1,0:T(4,128)}, u32[]{:S(2)}) copy-start(f32[4,512]{1,0:T(4,128)} %copy-done.22) | copy-start | bytes 24580
  463.3 192.1 %reduce-scatter.20.cloned.1.call-start = ((), (), s32[]{:S(2)}) async-start(), calls=%async_computation.19 | async-start | bytes 3932160 | tf_op jit(solution)/shard_map/reduce_scatter | solution.py:242
  507.1 16.5 %copy-start.28 = (f32[512]{0:T(512)}, f32[512]{0:T(512)S(1)}, u32[]{:S(2)}) copy-start(f32[512]{0:T(512)S(1)} %convert_element_type.160) | copy-start | bytes 6148
  507.7 2.7 copy-start.4
  510.4 13.1 %copy-start.14 = (bf16[1,1,2560,384]{2,3,1,0:T(8,128)(2,1)S(1)}, bf16[1,1,2560,384]{2,3,1,0:T(8,128)(2,1)}, u32[]{:S(2)}) copy-start(bf16[1,1,2560,384]{2,3,1,0:T(8,128)(2,1)} %get-tuple-element.129) | copy-start | bytes 5898244
  510.4 33.5 %slice-start = ((s8[20971520]{0:T(1024)(128)(4,1)}), s8[4194304]{0:T(1024)(128)(4,1)S(1)}, s32[]{:S(2)}) async-start(s8[20971520]{0:T(1024)(128)(4,1)} %bitcast.111), calls=%async_computation.27 | async-start | bytes 8388608
  510.5 33.5 %slice-start.1 = ((s8[20971520]{0:T(1024)(128)(4,1)}), s8[4194304]{0:T(1024)(128)(4,1)S(1)}, s32[]{:S(2)}) async-start(s8[20971520]{0:T(1024)(128)(4,1)} %bitcast.111), calls=%async_computation.28 | async-start | bytes 8388608
  510.5 33.5 %slice-start.2 = ((s8[20971520]{0:T(1024)(128)(4,1)}), s8[4194304]{0:T(1024)(128)(4,1)S(1)}, s32[]{:S(2)}) async-start(s8[20971520]{0:T(1024)(128)(4,1)} %bitcast.111), calls=%async_computation.29 | async-start | bytes 8388608
  523.5 20.4 %slice-start.3 = ((s8[20971520]{0:T(1024)(128)(4,1)}), s8[4194304]{0:T(1024)(128)(4,1)S(1)}, s32[]{:S(2)}) async-start(s8[20971520]{0:T(1024)(128)(4,1)} %bitcast.111), calls=%async_computation.30 | async-start | bytes 8388608
  523.6 20.4 %slice-start.4 = ((s8[20971520]{0:T(1024)(128)(4,1)}), s8[4194304]{0:T(1024)(128)(4,1)S(1)}, s32[]{:S(2)}) async-start(s8[20971520]{0:T(1024)(128)(4,1)} %bitcast.111), calls=%async_computation.31 | async-start | bytes 8388608
  544.0 16.1 %copy-start.5 = (bf16[1,1,2560,384]{2,3,1,0:T(8,128)(2,1)S(1)}, bf16[1,1,2560,384]{2,3,1,0:T(8,128)(2,1)}, u32[]{:S(2)}) copy-start(bf16[1,1,2560,384]{2,3,1,0:T(8,128)(2,1)} %get-tuple-element.128) | copy-start | bytes 5898244
  560.0 7.4 copy-start.2
  560.0 7.4 copy-start.13
  578.6 14.2 %copy-start.17 = (bf16[1536,384]{1,0:T(8,128)(2,1)S(1)}, bf16[1536,384]{1,0:T(8,128)(2,1)}, u32[]{:S(2)}) copy-start(bf16[1536,384]{1,0:T(8,128)(2,1)} %param.26) | copy-start | bytes 3538948
  587.3 5.5 copy-start.6
  595.6 273.9 %reduce-scatter.22.cloned.1.call-start = ((), (), s32[]{:S(2)}) async-start(), calls=%async_computation.20 | async-start | bytes 15728640 | tf_op jit(solution)/shard_map/reduce_scatter | solution.py:241
  606.1 346.0 %reduce-scatter.26.cloned.1.call-start = ((), (), s32[]{:S(2)}) async-start(), calls=%async_computation.22 | async-start | bytes 5308416 | tf_op jit(solution)/shard_map/reduce_scatter | solution.py:264
  618.0 0.7 copy-start.26
  618.0 1.3 copy-start.25
  618.0 37.3 %copy-start.8 = (bf16[1,128,1536]{2,1,0:T(8,128)(2,1)S(1)}, bf16[1,128,1536]{2,1,0:T(8,128)(2,1)}, u32[]{:S(2)}) copy-start(bf16[1,128,1536]{2,1,0:T(8,128)(2,1)} %param.16) | copy-start | bytes 1179652
  618.0 37.3 %copy-start.19 = (f32[1536]{0:T(1024)S(1)}, f32[1536]{0:T(1024)}, u32[]{:S(2)}) copy-start(f32[1536]{0:T(1024)} %param.22) | copy-start | bytes 18436
  618.0 37.3 %copy-start.31 = (f32[128]{0:T(128)S(1)}, f32[128]{0:T(128)}, u32[]{:S(2)}) copy-start(f32[128]{0:T(128)} %copy-done.30) | copy-start | bytes 1540
  618.1 37.3 %copy-start.34 = (f32[128]{0:T(128)S(1)}, f32[128]{0:T(128)}, u32[]{:S(2)}) copy-start(f32[128]{0:T(128)} %copy-done.33) | copy-start | bytes 1540
  618.1 411.2 %reduce-scatter.34.cloned.1.call-start = ((), (), s32[]{:S(2)}) async-start(), calls=%async_computation.26 | async-start | bytes 811008
  658.6 219.8 %copy-start.11 = (bf16[4,96,512]{2,1,0:T(8,128)(2,1)S(1)}, bf16[4,96,512]{2,1,0:T(8,128)(2,1)}, u32[]{:S(2)}) copy-start(bf16[4,96,512]{2,1,0:T(8,128)(2,1)} %copy-done.10) | copy-start | bytes 1179652
  878.4 196.8 %reduce-scatter.28.cloned.1.call-start = ((), (), s32[]{:S(2)}) async-start(), calls=%async_computation.23 | async-start | bytes 2654208 | tf_op jit(solution)/shard_map/reduce_scatter | solution.py:265
  882.7 238.8 %reduce-scatter.24.cloned.1.call-start = ((), (), s32[]{:S(2)}) async-start(), calls=%async_computation.21 | async-start | bytes 2654208 | tf_op jit(solution)/shard_map/reduce_scatter | solution.py:263
  886.8 315.5 %reduce-scatter.30.cloned.1.call-start = ((), (), s32[]{:S(2)}) async-start(), calls=%async_computation.24 | async-start | bytes 10616832 | tf_op jit(solution)/shard_map/reduce_scatter | solution.py:266
  895.2 388.0 %reduce-scatter.32.cloned.1.call-start = ((), (), s32[]{:S(2)}) async-start(), calls=%async_computation.25 | async-start | bytes 10616832 | tf_op jit(solution)/shard_map/reduce_scatter | solution.py:267
  904.2 45.6 %copy-start.9 = (f32[1,128,1536]{2,1,0:T(8,128)S(1)}, f32[1,128,1536]{2,1,0:T(8,128)}, u32[]{:S(2)}) copy-start(f32[1,128,1536]{2,1,0:T(8,128)} %get-tuple-element.123) | copy-start | bytes 2359300
  905.6 50.2 %copy-start.21 = (f32[1536]{0:T(1024)S(1)}, f32[1536]{0:T(1024)}, u32[]{:S(2)}) copy-start(f32[1536]{0:T(1024)} %param.20) | copy-start | bytes 18436
Sparse Core Ops, SparseCore 0:
  12.6 39.7 all-gather.7
  54.5 114.2 all-gather.5
  211.2 58.4 reduce-scatter.13
  273.1 37.1 all-gather.9
  311.7 35.9 all-gather.11
  363.6 59.0 reduce-scatter.17
  425.0 35.3 reduce-scatter.15
  463.4 37.1 all-gather.13
  595.7 59.6 reduce-scatter.19
  657.6 211.8 reduce-scatter.21
  872.9 55.2 reduce-scatter.25
  933.9 95.3 reduce-scatter.33
  1033.6 41.5 reduce-scatter.27
  1079.0 42.4 reduce-scatter.23
  1125.8 76.4 reduce-scatter.29
  1206.6 76.4 reduce-scatter.31
where the time goes:
time: 1300 us; the launch traced here: 1290 us
  waiting for transfers between devices  917 us (71%)
  matrix products  162 us (12%)
  blocking collectives  83.1 us (6%)
  other arithmetic  66.3 us (5%)
  local copies, waits for them, and re-layouts  44 us (3%)
  between operations  17.8 us (1%)
    reduce_scatter x1, waiting for transfers between devices, local(): lax.psum_scatter(back_inputs[:, :P_SEQ], 'tensor', scatter_dimension=1, t...  211 us
    all_gather x1, waiting for transfers between devices, local(): lax.all_gather(media_normed.astype(jnp.bfloat16), 'tensor', axis=1, tiled...  114 us
    psum x2, blocking collectives, local(): lax.psum((entropy_part, count_part), ('dp', 'tensor'))  83.1 us
    reduce_scatter x1, waiting for transfers between devices, local(): lax.psum_scatter(grad_down, 'dp', scatter_dimension=1, tiled=True)  80.8 us
    reduce_scatter x1, waiting for transfers between devices, local(): lax.psum_scatter(grad_up, 'dp', scatter_dimension=0, tiled=True)  80.8 us
    unnamed x17, waiting for transfers between devices  69.2 us
    reduce_scatter x1, waiting for transfers between devices, local(): lax.psum_scatter(attend_terms, 'tensor', scatter_dimension=1, tiled=True)  58.6 us
    reduce_scatter x1, waiting for transfers between devices, local(): lax.psum_scatter(back_terms, 'tensor', scatter_dimension=1, tiled=True)  52.5 us
  transfers between devices with their start and end apart: 16, of which 14 were waited for; matrix products, arithmetic and copies ran while one was open for 9% of the time, Pallas kernels for 0%

commit v1 on v0

v1 whole, which is shorter than its diff:
```python
from functools import partial

import jax
import jax.numpy as jnp
from jax import lax
from jax.experimental import pallas as pl
from jax.experimental.pallas import tpu as pltpu
from jax.sharding import PartitionSpec as P

HD = 96
LAT = 64
EPSILON = 1e-05
NEGATIVE = -1e30
SCALE = HD ** (-0.5)
BF = jnp.bfloat16
F32 = jnp.float32
VMEM_LIMIT = 48 * 1024 * 1024


def rotate(x, count, shift):
    return lax.ppermute(x, "tensor", [(i, (i + shift) % count) for i in range(count)])


def gather_blocks(x, count):
    return [x] + [rotate(x, count, k) for k in range(1, count)]


def scatter_blocks(blocks, count):
    arrived = [rotate(blocks[k], count, -k) for k in range(1, count)]
    total = blocks[0].astype(F32)
    for part in arrived:
        total = total + part.astype(F32)
    return total


def swap(x, axis, count, bit):
    return lax.ppermute(x, axis, [(i, i ^ (1 << bit)) for i in range(count)])


def bits_of(count):
    return count.bit_length() - 1


def halve(parts, left, bit, count):
    place = left.index(bit)
    rest = parts.shape[1:]
    split = parts.reshape((1 << place, 2, 1 << (len(left) - place - 1)) + rest)
    mine = (lax.axis_index("dp") >> bit) & 1
    send = lax.dynamic_index_in_dim(split, 1 - mine, 1, keepdims=False)
    keep = lax.dynamic_index_in_dim(split, mine, 1, keepdims=False)
    got = swap(send, "dp", count, bit)
    total = keep.astype(F32) + got.astype(F32)
    left = [b for b in left if b != bit]
    return total.reshape((1 << len(left),) + rest), left


def bit_orders(count):
    outer = list(range(1, bits_of(count)))
    half = (len(outer) + 1) // 2
    return outer, outer[half:] + outer[:half]


def reduce_pair(one, two, count):
    left = list(range(bits_of(count) - 1, -1, -1))
    both, left = halve(jnp.stack([one, two], axis=1), left, 0, count)
    both = both.astype(BF)
    out = []
    for which, order in enumerate(bit_orders(count)):
        part, still = both[:, which], left
        for bit in order:
            part, still = halve(part.astype(BF), still, bit, count)
        out.append(part[0])
    return out


def all_sum(x, axes):
    for axis, count in axes:
        for bit in range(bits_of(count)):
            x = x + swap(x, axis, count, bit)
    return x


def place_kernel(n_dp, n_t, offsets, at_ref, own_ref, even_ref, odd_ref, out_ref, sem):
    z, p = at_ref[0], at_ref[1]
    copies = [pltpu.make_async_copy(own_ref, out_ref.at[z], sem)]
    for k in range(1, n_t):
        shard = lax.rem(z - k + n_t, n_t)
        for i, off in enumerate(offsets):
            copies.append(
                pltpu.make_async_copy(even_ref.at[i, k - 1], out_ref.at[shard, p ^ off], sem)
            )
            copies.append(
                pltpu.make_async_copy(
                    odd_ref.at[i, k - 1], out_ref.at[shard, p ^ (off ^ 1)], sem
                )
            )
    for copy in copies:
        copy.start()
    for copy in copies:
        copy.wait()


def place(own, even, odd, offsets, at, n_dp, n_t):
    unit = own.shape[0] // n_dp
    width = own.shape[1]
    out = pl.pallas_call(
        partial(place_kernel, n_dp, n_t, offsets),
        out_shape=jax.ShapeDtypeStruct((n_t, n_dp, unit, width), own.dtype),
        in_specs=[pl.BlockSpec(memory_space=pltpu.SMEM)] + [pl.BlockSpec(memory_space=pl.ANY)] * 3,
        out_specs=pl.BlockSpec(memory_space=pl.ANY),
        scratch_shapes=[pltpu.SemaphoreType.DMA],
    )(at, own.reshape(n_dp, unit, width), even, odd)
    return out.reshape(n_t * own.shape[0], width)


def gather_pair(one, two, at, n_dp, n_t):
    unit = one.shape[0] // n_dp
    width = one.shape[1]
    slices = jnp.stack([one, two]).reshape(2, n_dp, unit, width)
    mine = lax.dynamic_index_in_dim(slices, lax.axis_index("dp"), 1, keepdims=False)
    arrived = jnp.stack([rotate(mine, n_t, k) for k in range(1, n_t)], axis=1)
    out = []
    for which, (own, order) in enumerate(zip((one, two), bit_orders(n_dp))):
        held, offsets = arrived[which][None], [0]
        for bit in order:
            held = jnp.concatenate([held, swap(held, "dp", n_dp, bit)], axis=0)
            offsets = offsets + [o ^ (1 << bit) for o in offsets]
        other = swap(held, "dp", n_dp, 0)
        out.append(place(own, held, other, offsets, at, n_dp, n_t))
    return out


def three(x):
    high = x.astype(BF)
    left = x - high.astype(F32)
    middle = left.astype(BF)
    low = (left - middle.astype(F32)).astype(BF)
    return jnp.concatenate([high, middle, low], axis=0)


def join(x, count):
    x = x.astype(F32)
    return x[:count] + x[count : 2 * count] + x[2 * count :]


def forward_kernel(heads, n_t, q_ref, k_ref, v_ref, seg_ref, img_ref, *rest):
    msgs, stat = rest[:n_t], rest[n_t]
    h = pl.program_id(0)
    rows = q_ref.shape[1] // n_t
    scores = (
        lax.dot_general(
            k_ref[...], q_ref[...], (((0,), (0,)), ((), ())), preferred_element_type=F32
        )
        * SCALE
    )
    allowed = seg_ref[...] == img_ref[...]
    masked = jnp.where(allowed, scores, NEGATIVE)
    top = jnp.max(masked, axis=0, keepdims=True)
    weight = jnp.where(allowed, jnp.exp(masked - top), 0.0)
    total = jnp.sum(weight, axis=0, keepdims=True)
    mean = jnp.sum(weight * scores, axis=0, keepdims=True)
    some = total > 0.0
    inverse = jnp.where(some, 1.0 / jnp.where(some, total, 1.0), 0.0)
    out = jnp.dot(v_ref[...], weight.astype(BF), preferred_element_type=F32) * inverse
    stat[pl.ds(h, 1)] = jnp.where(some, top + jnp.log(jnp.where(some, total, 1.0)), NEGATIVE)
    stat[pl.ds(heads + h, 1)] = mean * inverse
    at = pl.ds(pl.multiple_of(h * HD, HD), HD)
    for k in range(n_t):
        msgs[k][at, :] = out[:, k * rows : (k + 1) * rows].astype(BF)

    @pl.when(h == heads - 1)
    def _():
        for k in range(n_t):
            cols = slice(k * rows, (k + 1) * rows)
            msgs[k][heads * HD : heads * (HD + 3), :] = three(stat[:heads, cols])
            msgs[k][heads * (HD + 3) :, :] = three(stat[heads:, cols])


def attend_forward(q, k, v, seg, img, n_t):
    heads = q.shape[0] // HD
    rows, keys = q.shape[1], k.shape[1]
    one = rows // n_t
    tall = heads * (HD + 6)
    return pl.pallas_call(
        partial(forward_kernel, heads, n_t),
        grid=(heads,),
        out_shape=[jax.ShapeDtypeStruct((tall, one), BF)] * n_t,
        in_specs=[
            pl.BlockSpec((HD, rows), lambda h: (h, 0)),
            pl.BlockSpec((HD, keys), lambda h: (h, 0)),
            pl.BlockSpec((HD, keys), lambda h: (h, 0)),
            pl.BlockSpec((keys, 1), lambda h: (0, 0)),
            pl.BlockSpec((1, rows), lambda h: (0, 0)),
        ],
        out_specs=[pl.BlockSpec((tall, one), lambda h: (0, 0))] * n_t,
        scratch_shapes=[pltpu.VMEM((2 * heads, rows), F32)],
        compiler_params=pltpu.CompilerParams(vmem_limit_bytes=VMEM_LIMIT),
    )(q, k, v, seg, img)


def combine_kernel(heads, n_t, *refs):
    msgs, (out_ref, stat_ref) = refs[:n_t], refs[n_t:]
    base = heads * HD
    logs = [join(m[base : base + 3 * heads, :], heads) for m in msgs]
    means = [join(m[base + 3 * heads :, :], heads) for m in msgs]
    top = logs[0]
    for x in logs[1:]:
        top = jnp.maximum(top, x)
    shares = [jnp.exp(x - top) for x in logs]
    total = shares[0]
    for x in shares[1:]:
        total = total + x
    shares = [x / total for x in shares]
    mean = shares[0] * means[0]
    for s, x in zip(shares[1:], means[1:]):
        mean = mean + s * x
    stat_ref[:heads, :] = top + jnp.log(total)
    stat_ref[heads:, :] = mean
    for h in range(heads):
        at = slice(h * HD, (h + 1) * HD)
        acc = msgs[0][at, :].astype(F32) * shares[0][h : h + 1, :]
        for s, m in zip(shares[1:], msgs[1:]):
            acc = acc + m[at, :].astype(F32) * s[h : h + 1, :]
        out_ref[at, :] = acc.astype(BF)


def combine(msgs, heads):
    one = msgs[0].shape[1]
    return pl.pallas_call(
        partial(combine_kernel, heads, len(msgs)),
        out_shape=[
            jax.ShapeDtypeStruct((heads * HD, one), BF),
            jax.ShapeDtypeStruct((2 * heads, one), F32),
        ],
        compiler_params=pltpu.CompilerParams(vmem_limit_bytes=VMEM_LIMIT),
    )(*msgs)


def message_kernel(heads, do_ref, out_ref, stat_ref, coef_ref, msg_ref):
    base = heads * HD
    deltas = []
    for h in range(heads):
        at = slice(h * HD, (h + 1) * HD)
        grad = do_ref[at, :].astype(F32)
        deltas.append(jnp.sum(grad * out_ref[at, :].astype(F32), axis=0, keepdims=True))
    msg_ref[:base, :] = do_ref[...]
    delta = jnp.concatenate(deltas, axis=0) - coef_ref[...] * stat_ref[heads:, :]
    msg_ref[base : base + 3 * heads, :] = three(stat_ref[:heads, :])
    msg_ref[base + 3 * heads :, :] = three(delta)


def make_message(do, out, stat, coef, heads):
    return pl.pallas_call(
        partial(message_kernel, heads),
        out_shape=jax.ShapeDtypeStruct((heads * (HD + 6), do.shape[1]), BF),
        compiler_params=pltpu.CompilerParams(vmem_limit_bytes=VMEM_LIMIT),
    )(do, out, stat, coef)


def backward_kernel(heads, n_t, q_ref, k_ref, v_ref, seg_ref, img_ref, coef_ref, *rest):
    grads, stats = rest[:n_t], rest[n_t : 2 * n_t]
    dq_ref, dk_ref, dv_ref, stat = rest[2 * n_t :]
    h = pl.program_id(0)

    @pl.when(h == 0)
    def _():
        rows = q_ref.shape[1] // n_t
        for i in range(n_t):
            cols = slice(i * rows, (i + 1) * rows)
            stat[:heads, cols] = join(stats[i][: 3 * heads, :], heads)
            stat[heads:, cols] = join(stats[i][3 * heads :, :], heads)

    q, k, v = q_ref[...], k_ref[...], v_ref[...]
    grad = jnp.concatenate([g[...] for g in grads], axis=1)
    scores = (
        lax.dot_general(k, q, (((0,), (0,)), ((), ())), preferred_element_type=F32) * SCALE
    )
    allowed = seg_ref[...] == img_ref[...]
    log_total = stat[pl.ds(h, 1)]
    delta = stat[pl.ds(heads + h, 1)]
    prob = jnp.where(allowed, jnp.exp(jnp.where(allowed, scores - log_total, 0.0)), 0.0)
    back_prob = lax.dot_general(v, grad, (((0,), (0,)), ((), ())), preferred_element_type=F32)
    back = (prob * (back_prob - coef_ref[...] * scores - delta)).astype(BF)
    dq_ref[...] = (jnp.dot(k, back, preferred_element_type=F32) * SCALE).astype(BF)
    nt = (((1,), (1,)), ((), ()))
    dk_ref[...] = (lax.dot_general(q, back, nt, preferred_element_type=F32) * SCALE).astype(BF)
    dv_ref[...] = lax.dot_general(
        grad, prob.astype(BF), nt, preferred_element_type=F32
    ).astype(BF)


def attend_backward(q, k, v, seg, img, coef, msgs):
    n_t = len(msgs)
    heads = q.shape[0] // HD
    rows, keys = q.shape[1], k.shape[1]
    one = rows // n_t
    return pl.pallas_call(
        partial(backward_kernel, heads, n_t),
        grid=(heads,),
        out_shape=[
            jax.ShapeDtypeStruct(q.shape, BF),
            jax.ShapeDtypeStruct(k.shape, BF),
            jax.ShapeDtypeStruct(v.shape, BF),
        ],
        in_specs=[
            pl.BlockSpec((HD, rows), lambda h: (h, 0)),
            pl.BlockSpec((HD, keys), lambda h: (h, 0)),
            pl.BlockSpec((HD, keys), lambda h: (h, 0)),
            pl.BlockSpec((keys, 1), lambda h: (0, 0)),
            pl.BlockSpec((1, rows), lambda h: (0, 0)),
            pl.BlockSpec((1, rows), lambda h: (0, 0)),
        ]
        + [pl.BlockSpec((HD, one), lambda h: (h, 0))] * n_t
        + [pl.BlockSpec((6 * heads, one), lambda h: (HD // 6, 0))] * n_t,
        out_specs=[
            pl.BlockSpec((HD, rows), lambda h: (h, 0)),
            pl.BlockSpec((HD, keys), lambda h: (h, 0)),
            pl.BlockSpec((HD, keys), lambda h: (h, 0)),
        ],
        scratch_shapes=[pltpu.VMEM((2 * heads, rows), F32)],
        compiler_params=pltpu.CompilerParams(vmem_limit_bytes=VMEM_LIMIT),
    )(q, k, v, seg, img, coef, *msgs, *msgs)


def norm_parts(values):
    values = values.astype(F32)
    center = values - jnp.mean(values, axis=-1, keepdims=True)
    inv_root = lax.rsqrt(jnp.mean(center * center, axis=-1, keepdims=True) + EPSILON)
    return center * inv_root, inv_root


def norm_backward(grad_rows, normal, inv_root, gain_row):
    scaled = grad_rows * gain_row
    reduced = (
        scaled
        - jnp.mean(scaled, axis=-1, keepdims=True)
        - normal * jnp.mean(scaled * normal, axis=-1, keepdims=True)
    )
    return reduced * inv_root


def gain_shift(grad_rows, normal):
    return [jnp.sum(grad_rows * normal, axis=0), jnp.sum(grad_rows, axis=0)]


def dot(equation, a, b):
    return jnp.einsum(equation, a, b, preferred_element_type=F32)


def local(
    latents,
    features,
    lengths,
    valid_media,
    media_gain,
    media_shift,
    latent_gain,
    latent_shift,
    feed_gain,
    feed_shift,
    query_weight,
    key_value_weight,
    output_weight,
    up_weight,
    down_weight,
    cotangent,
):
    n_t = lax.axis_size("tensor")
    n_dp = lax.axis_size("dp")
    z, p = lax.axis_index("tensor"), lax.axis_index("dp")
    at = jnp.stack([z, p]).astype(jnp.int32)
    latents, features, cotangent = latents[0], features[0], cotangent[0]
    lengths, valid = lengths[0], valid_media[0]
    width = latents.shape[1]
    own_rows, own_patches = latents.shape[0], features.shape[0]
    inner = query_weight.shape[1] * n_t
    heads = inner // HD
    images = lengths.shape[0]

    latent_blocks = gather_blocks(latents, n_t)
    wq, wk = gather_pair(query_weight.T, key_value_weight[:, 0].T, at, n_dp, n_t)
    wv, wo = gather_pair(key_value_weight[:, 1].T, output_weight, at, n_dp, n_t)
    cot_all = jnp.concatenate(gather_blocks(cotangent, n_t), axis=0)

    count_part = jnp.full((8, 128), jnp.sum(valid).astype(F32))
    count_total = all_sum(count_part, [("dp", n_dp)])[0, 0]

    ends = jnp.sum(
        jnp.where(jnp.arange(images)[:, None] <= jnp.arange(images)[None, :], lengths[:, None], 0),
        axis=0,
    )
    positions = z * own_patches + jnp.arange(own_patches, dtype=jnp.int32)
    segment = jnp.sum((positions[:, None] >= ends[None, :]).astype(jnp.int32), axis=1)
    hit = segment[:, None] == jnp.arange(images, dtype=jnp.int32)[None, :]
    patch_valid = jnp.sum(jnp.where(hit, valid[None, :], 0), axis=1)
    patch_segment = jnp.where(patch_valid > 0, segment, -1)
    own_images = (z * own_rows + jnp.arange(own_rows, dtype=jnp.int32)) // LAT
    key_image = jnp.concatenate([patch_segment, own_images])[:, None]
    block_of = (z - jnp.arange(n_t, dtype=jnp.int32) + n_t) % n_t
    row_index = block_of[:, None] * own_rows + jnp.arange(own_rows, dtype=jnp.int32)[None, :]
    row_image = (row_index // LAT).reshape(1, -1)
    row_valid = jnp.sum(
        jnp.where(row_image.T == jnp.arange(images, dtype=jnp.int32)[None, :], valid[None, :], 0),
        axis=1,
    ).astype(F32)[None, :]

    media_hat, media_root = norm_parts(features)
    media_normed = (media_hat * media_gain + media_shift).astype(BF)
    latent_all = jnp.concatenate(latent_blocks, axis=0)
    latent_hat, latent_root = norm_parts(latent_all)
    latent_normed = (latent_hat * latent_gain + latent_shift).astype(BF)
    key_input = jnp.concatenate([media_normed, latent_normed[:own_rows]], axis=0)
    queries = dot("hd,rd->hr", wq, latent_normed).astype(BF)
    keys = dot("hd,rd->hr", wk, key_input).astype(BF)
    values = dot("hd,rd->hr", wv, key_input).astype(BF)
    sent = attend_forward(queries, keys, values, key_image, row_image, n_t)
    got = [sent[0]] + [rotate(sent[k], n_t, -k) for k in range(1, n_t)]
    attended, stat = combine(got, heads)
    entropy = stat[:heads] - stat[heads:]
    own_valid = row_valid[:, :own_rows]
    penalty_part = jnp.sum(entropy * own_valid)

    latent_own = latents.astype(F32)
    middle = latent_own + dot("hr,hd->rd", attended, wo)
    feed_hat, feed_root = norm_parts(middle)
    feed_normed = (feed_hat * feed_gain + feed_shift).astype(BF)
    feed_all = jnp.concatenate(gather_blocks(feed_normed, n_t), axis=0)
    hidden = dot("rd,df->rf", feed_all, up_weight)
    cdf = 0.5 * (1.0 + lax.erf(hidden * (0.5**0.5)))
    slope = cdf + hidden * jnp.exp(-0.5 * hidden * hidden) * (0.5 / jnp.pi) ** 0.5
    activation = (hidden * cdf).astype(BF)
    back_activation = dot("rd,fd->rf", cot_all, down_weight)
    back_hidden = (back_activation * slope).astype(BF)
    back_terms = dot("rf,df->rd", back_hidden, up_weight).astype(BF)
    back_feed = scatter_blocks(
        [back_terms[k * own_rows : (k + 1) * own_rows] for k in range(n_t)], n_t
    )
    feed_terms = dot("rf,fd->rd", activation, down_weight).astype(BF)
    result = middle + scatter_blocks(
        [feed_terms[k * own_rows : (k + 1) * own_rows] for k in range(n_t)], n_t
    )
    grad_down = dot("rd,rf->df", cot_all, activation).astype(BF)
    grad_up = dot("rd,rf->df", feed_all, back_hidden).astype(BF)
    down_share, up_share = reduce_pair(
        grad_down.reshape(n_dp, width // n_dp, -1), grad_up.reshape(n_dp, width // n_dp, -1), n_dp
    )

    back_middle = cotangent.astype(F32) + norm_backward(back_feed, feed_hat, feed_root, feed_gain)
    back_branch = back_middle.astype(BF)
    back_attended = dot("hd,rd->hr", wo, back_branch).astype(BF)
    own_coef = own_valid / count_total
    message = make_message(back_attended, attended, stat, own_coef, heads)
    messages = gather_blocks(message, n_t)
    back_q, back_k, back_v = attend_backward(
        queries, keys, values, key_image, row_image, row_valid / count_total, messages
    )

    def shares(a, b):
        return dot("rd,hr->dh", a, b).astype(BF).reshape(n_dp, width // n_dp, inner)

    key_share, value_share = reduce_pair(shares(key_input, back_k), shares(key_input, back_v), n_dp)
    query_share, output_share = reduce_pair(
        shares(latent_normed, back_q), shares(back_branch, attended), n_dp
    )
    back_inputs = dot("hr,hd->rd", back_k, wk) + dot("hr,hd->rd", back_v, wv)
    back_media = back_inputs[:own_patches]
    latent_terms = dot("hr,hd->rd", back_q, wq)
    latent_terms = jnp.concatenate(
        [latent_terms[:own_rows] + back_inputs[own_patches:], latent_terms[own_rows:]], axis=0
    )
    terms_low = latent_terms.astype(BF)
    back_latent = scatter_blocks(
        [terms_low[k * own_rows : (k + 1) * own_rows] for k in range(n_t)], n_t
    )
    features_grad = norm_backward(back_media, media_hat, media_root, media_gain)
    latents_grad = back_middle + norm_backward(
        back_latent, latent_hat[:own_rows], latent_root[:own_rows], latent_gain
    )

    part = inner // n_t
    four = jnp.stack([query_share, key_share, value_share, output_share]).astype(BF)
    four = four.reshape(4, width // n_dp, n_t, part).transpose(2, 0, 1, 3)
    blocks = [
        lax.dynamic_index_in_dim(four, (z - k + n_t) % n_t, 0, keepdims=False) for k in range(n_t)
    ]
    four = scatter_blocks(blocks, n_t)

    sums = (
        gain_shift(back_media, media_hat)
        + gain_shift(latent_terms, latent_hat)
        + gain_shift(back_feed, feed_hat)
    )
    sums = jnp.stack(sums + [jnp.full((width,), penalty_part)] * 2)
    sums = all_sum(sums, [("dp", n_dp), ("tensor", n_t)])
    penalty = sums[6, 0] / count_total
    share = width // (n_dp * n_t)
    mine = lax.dynamic_index_in_dim(
        sums.reshape(8, n_dp * n_t, share), p * n_t + z, 1, keepdims=False
    )
    return (
        result.astype(BF)[None],
        penalty,
        latents_grad[None],
        features_grad[None],
        mine[0],
        mine[1],
        mine[2],
        mine[3],
        mine[4],
        mine[5],
        four[0],
        jnp.stack([four[1], four[2]], axis=1),
        four[3].T,
        up_share,
        down_share.T,
    )


def solution(mesh):
    return jax.shard_map(
        local,
        mesh=mesh,
        in_specs=(
            P("dp", "tensor", None),
            P("dp", "tensor", None),
            P("dp", None),
            P("dp", None),
            P(),
            P(),
            P(),
            P(),
            P(),
            P(),
            P(None, "tensor"),
            P(None, None, "tensor"),
            P("tensor", None),
            P(None, "tensor"),
            P("tensor", None),
            P("dp", "tensor", None),
        ),
        out_specs=(
            P("dp", "tensor", None),
            P(),
            P("dp", "tensor", None),
            P("dp", "tensor", None),
            P(("dp", "tensor")),
            P(("dp", "tensor")),
            P(("dp", "tensor")),
            P(("dp", "tensor")),
            P(("dp", "tensor")),
            P(("dp", "tensor")),
            P("dp", "tensor"),
            P("dp", None, "tensor"),
            P("tensor", "dp"),
            P("dp", "tensor"),
            P("tensor", "dp"),
        ),
        check_vma=False,
    )
```

time: 1300 us -> 1270 us (0.977)
  waiting for transfers between devices: 917 us -> 255 us
  Pallas kernels: 0 us -> 625 us
  starting transfers between devices: 0.83 us -> 148 us
  matrix products: 162 us -> 75.1 us
  blocking collectives: 83.1 us -> 0 us
  other arithmetic: 66.3 us -> 89.2 us
  local copies, waits for them, and re-layouts: 44 us -> 57.3 us
    reduce_scatter x10 -> x0, waiting for transfers between devices: 642 us -> none  [the longest x1 211 us: local(): lax.psum_scatter(back_inputs[:, :P_SEQ], 'tensor', scatter_dimension=1, t...]
    pallas_call x0 -> x8, Pallas kernels: none -> 625 us  [the longest x4 579 us: place(): pl.pallas_call(partial(place_kernel, n_dp, n_t, offsets), out_shape=jax.S...]
    ppermute x0 -> x68, waiting for transfers between devices: none -> 255 us  [the longest x35 128 us: swap(): return lax.ppermute(x, axis, [(i, i ^ 1 << bit) for i in range(count)])]
    all_gather x5 -> x0, waiting for transfers between devices: 206 us -> none  [the longest x1 114 us: local(): lax.all_gather(media_normed.astype(jnp.bfloat16), 'tensor', axis=1, tiled...]
    ppermute x0 -> x68, starting transfers between devices: none -> 148 us  [the longest x33 116 us: rotate(): lax.ppermute(x, 'tensor', [(i, (i + shift) % count) for i in range(count)])]
    dot_general x21 -> x18, matrix products: 162 us -> 75.1 us  [dot(): return jnp.einsum(equation, a, b, preferred_element_type=F32)]
    psum x2 -> x0, blocking collectives: 83.1 us -> none  [local(): lax.psum((entropy_part, count_part), ('dp', 'tensor'))]
    unnamed x17 -> x0, waiting for transfers between devices: 69.2 us -> none
  transfers between devices with their start and end apart: 16 -> 68, of which waited for: 14 -> 27; matrix products, arithmetic and copies ran while one was open for 9% -> 15% of each run, Pallas kernels for 0% -> 50%
where the time goes in v1:
time: 1270 us; the launch traced here: 1250 us
  Pallas kernels  625 us (49%)
  waiting for transfers between devices  255 us (20%)
  starting transfers between devices  148 us (12%)
  other arithmetic  89.2 us (7%)
  matrix products  75.1 us (6%)
  local copies, waits for them, and re-layouts  57.3 us (5%)
    pallas_call x4, Pallas kernels, place(): pl.pallas_call(partial(place_kernel, n_dp, n_t, offsets), out_shape=jax.S...  579 us
    ppermute x35, waiting for transfers between devices, swap(): return lax.ppermute(x, axis, [(i, i ^ 1 << bit) for i in range(count)])  128 us
    ppermute x33, waiting for transfers between devices, rotate(): lax.ppermute(x, 'tensor', [(i, (i + shift) % count) for i in range(count)])  126 us
    ppermute x33, starting transfers between devices, rotate(): lax.ppermute(x, 'tensor', [(i, (i + shift) % count) for i in range(count)])  116 us
    dot_general x18, matrix products, dot(): return jnp.einsum(equation, a, b, preferred_element_type=F32)  75.1 us
    ppermute x35, starting transfers between devices, swap(): return lax.ppermute(x, axis, [(i, i ^ 1 << bit) for i in range(count)])  31.3 us
  transfers between devices with their start and end apart: 68, of which 27 were waited for; matrix products, arithmetic and copies ran while one was open for 15% of the time, Pallas kernels for 50%

profile of v1, /device:TPU:0, one launch (start us, length us, event | category | flops | bytes accessed | tf_op | source)
XLA Modules:
  0.0 1254.2 jit_solution(14692265919025027163)
XLA Ops:
  2.2 8.0 fusion.79
  10.3 5.5 copy.114
  16.6 5.0 collective-permute-start.2
  22.7 5.6 copy.115
  41.5 8.0 collective-permute-done.1
  49.4 7.5 collective-permute-start.8
  59.8 7.6 collective-permute-start.7
  67.5 14.5 %collective-permute-done.13 = bf16[2,48,1536]{2,1,0:T(8,128)(2,1)} collective-permute-done((bf16[2,48,1536]{2,1,0:T(8,128)(2,1)}, bf16[2,48,1536]{2,1,0:T(8,128)(2,1)}, u32[]{:S(2)}, u32[]{:S(2)}) %collective-permute-start.13) | collective-permute-done | bytes 294944 | tf_op jit(solution)/shard_map/ppermute | solution.py:21
  88.0 9.8 collective-permute-done.9
  100.0 6.0 collective-permute-done.7
  110.0 6.7 collective-permute-done.4
  117.0 10.8 collective-permute-done.10
  131.4 10.8 collective-permute-done.16
  143.7 4.2 fusion.18
  148.7 3.3 collective-permute-done.22
  154.6 144.7 %shard_map.271 = bf16[4,8,48,1536]{3,2,1,0:T(8,128)(2,1)} custom-call(s32[2]{0:T(128)} %pad_add_fusion.1.at_ref, bf16[8,48,1536]{2,1,0:T(8,128)(2,1)} %bitcast.304, bf16[4,3,48,1536]{3,2,1,0:T(8,128)(2,1)} %copy-done.21, bf16[4,3,48,1536]{3,2,1,0:T(8,128)(2,1)} %copy-done.39), custom_call_target="tpu_custom_call" | custom-call | tf_op jit(solution)/shard_map/pallas_call | solution.py:106
  299.3 144.8 %shard_map.272 = bf16[4,8,48,1536]{3,2,1,0:T(8,128)(2,1)} custom-call(s32[2]{0:T(128)} %pad_add_fusion.1.at_ref, bf16[8,48,1536]{2,1,0:T(8,128)(2,1)} %bitcast.306, bf16[4,3,48,1536]{3,2,1,0:T(8,128)(2,1)} %pad_maximum_fusion.3.even_ref, bf16[4,3,48,1536]{3,2,1,0:T(8,128)(2,1)} %collective-permute-done.11.odd_ref), custom_call_target="tpu_custom_call" | custom-call | tf_op jit(solution)/shard_map/pallas_call | solution.py:106
  444.2 6.3 convolution_convert_fusion.7.k_ref
  450.5 144.7 %shard_map.273 = bf16[4,8,48,1536]{3,2,1,0:T(8,128)(2,1)} custom-call(s32[2]{0:T(128)} %pad_add_fusion.1.at_ref, bf16[8,48,1536]{2,1,0:T(8,128)(2,1)} %bitcast.308, bf16[4,3,48,1536]{3,2,1,0:T(8,128)(2,1)} %pad_maximum_fusion.4.even_ref, bf16[4,3,48,1536]{3,2,1,0:T(8,128)(2,1)} %collective-permute-done.17.odd_ref), custom_call_target="tpu_custom_call" | custom-call | tf_op jit(solution)/shard_map/pallas_call | solution.py:106
  595.2 7.7 convolution_convert_fusion.6.v_ref
  602.9 5.0 convolution_convert_fusion.10.q_ref
  608.0 20.0 %shard_map.274 = (bf16[1632,128]{1,0:T(8,128)(2,1)S(1)}, bf16[1632,128]{1,0:T(8,128)(2,1)}, bf16[1632,128]{1,0:T(8,128)(2,1)}, bf16[1632,128]{1,0:T(8,128)(2,1)}) custom-call(bf16[1536,512]{1,0:T(8,128)(2,1)S(1)} %convolution_convert_fusion.10.q_ref, bf16[1536,640]{1,0:T(8,128)(2,1)S(1)} %convolution_convert_fusion.7.k_ref, ...), custom_call_target="tpu_custom_call" | custom-call | tf_op jit(solution)/shard_map/pallas_call | solution.py:184
  629.1 5.3 collective-permute-start.19
  647.7 144.8 %shard_map.276 = bf16[4,8,48,1536]{3,2,1,0:T(8,128)(2,1)} custom-call(s32[2]{0:T(128)} %pad_add_fusion.1.at_ref, bf16[8,48,1536]{2,1,0:T(8,128)(2,1)} %bitcast.329, bf16[4,3,48,1536]{3,2,1,0:T(8,128)(2,1)} %pad_maximum_fusion.5.even_ref, bf16[4,3,48,1536]{3,2,1,0:T(8,128)(2,1)} %collective-permute-done.23.odd_ref), custom_call_target="tpu_custom_call" | custom-call | tf_op jit(solution)/shard_map/pallas_call | solution.py:106
  793.0 3.4 fusion.85
  803.7 5.3 collective-permute-done.26
  809.0 26.6 %collective-permute-start.33 = (bf16[128,1536]{1,0:T(8,128)(2,1)S(1)}, bf16[128,1536]{1,0:T(8,128)(2,1)S(1)}, u32[]{:S(2)}, u32[]{:S(2)}) collective-permute-start(bf16[128,1536]{1,0:T(8,128)(2,1)S(1)} %bitcast.341), channel_id=1, source_target_pairs={{0,1},{1,2},{2,3},{3,0},{4,5},{5,6},{6,7},{7,4},{8,9},{9,10},{10,1... | collective-permute-start | bytes 1179656 | tf_op jit(solution)/shard_map/ppermute | solution.py:21
  835.6 4.5 collective-permute-done.25
  840.2 5.2 multiply_convert_fusion
  845.5 4.0 fusion.40
  852.5 3.7 collective-permute-start.36
  861.1 4.2 convolution_convert_fusion.1
  865.3 4.4 convolution_convert_fusion
  869.6 3.0 collective-permute-start.27
  872.6 19.2 %collective-permute-done.37 = bf16[128,1536]{1,0:T(8,128)(2,1)S(1)} collective-permute-done((bf16[128,1536]{1,0:T(8,128)(2,1)S(1)}, bf16[128,1536]{1,0:T(8,128)(2,1)S(1)}, u32[]{:S(2)}, u32[]{:S(2)}) %collective-permute-start.37) | collective-permute-done | bytes 393248 | tf_op jit(solution)/shard_map/ppermute | solution.py:21
  892.4 20.3 %collective-permute-done.28 = bf16[128,1536]{1,0:T(8,128)(2,1)S(1)} collective-permute-done((bf16[128,1536]{1,0:T(8,128)(2,1)S(1)}, bf16[128,1536]{1,0:T(8,128)(2,1)S(1)}, u32[]{:S(2)}, u32[]{:S(2)}) %collective-permute-start.28) | collective-permute-done | bytes 393248 | tf_op jit(solution)/shard_map/ppermute | solution.py:21
  915.7 17.0 %collective-permute-start.39 = (bf16[1632,128]{1,0:T(8,128)(2,1)S(1)}, bf16[1632,128]{1,0:T(8,128)(2,1)S(1)}, u32[]{:S(2)}, u32[]{:S(2)}) collective-permute-start(bf16[1632,128]{1,0:T(8,128)(2,1)S(1)} %shard_map.277.rest_0_.rest_4_), channel_id=1, source_target_pairs={{0,1},{1,2},{2,3},{3,0},{4,5},{5,6},{6,7},{7,4},{8,9},{9,10},{10,1... | collective-permute-start | bytes 1253384 | tf_op jit(solution)/shard_map/ppermute | solution.py:21
  935.2 4.2 fusion.7
  939.5 3.6 convolution_convert_fusion.5
  943.1 7.4 collective-permute-done.40.rest_2_.rest_6_
  950.5 3.9 collective-permute-done.41.rest_3_.rest_7_
  954.4 24.9 %shard_map.278 = (bf16[1536,512]{1,0:T(8,128)(2,1)S(1)}, bf16[1536,640]{1,0:T(8,128)(2,1)}, bf16[1536,640]{1,0:T(8,128)(2,1)}) custom-call(bf16[1536,512]{1,0:T(8,128)(2,1)S(1)} %convolution_convert_fusion.10.q_ref, bf16[1536,640]{1,0:T(8,128)(2,1)} %copy-done, bf16[1536,640]{1,0:T(8,128)(2,1)} %convolution_convert_fusion.6.v_ref, s32[640,1]{1,0:T(8,128)S(1)} %copy-done.2, ...), custom_call_target="tpu_custom_call" | custom-call | tf_op jit(solution)/shard_map/pallas_call | solution.py:297
  979.3 6.0 fusion.86
  985.4 3.3 convolution_add_fusion
  995.2 4.4 convolution_convert_fusion.4
  1001.5 3.2 multiply_reduce_fusion
  1007.4 9.3 collective-permute-start.49
  1016.7 3.4 collective-permute-start.48
  1020.1 5.1 fusion.15
  1034.6 4.2 convolution_convert_fusion.3
  1038.8 4.2 collective-permute-done.45
  1043.1 4.2 convolution_convert_fusion.2
  1054.7 4.8 collective-permute-done.47
  1063.9 5.7 fusion.5
  1075.6 3.9 fusion.3
  1081.6 4.6 fusion.4
  1088.9 11.5 collective-permute-done.64
  1108.6 20.0 %collective-permute-done.51 = bf16[2,1,192,1536]{3,2,0,1:T(8,128)(2,1)} collective-permute-done((bf16[2,1,192,1536]{3,2,0,1:T(8,128)(2,1)}, bf16[2,1,192,1536]{3,2,0,1:T(8,128)(2,1)}, u32[]{:S(2)}, u32[]{:S(2)}) %collective-permute-start.51) | collective-permute-done | bytes 1179680 | tf_op jit(solution)/shard_map/ppermute | solution.py:37
  1130.9 22.9 %collective-permute-done.54 = bf16[2,1,192,1536]{3,2,0,1:T(8,128)(2,1)S(1)} collective-permute-done((bf16[2,1,192,1536]{3,2,0,1:T(8,128)(2,1)S(1)}, bf16[2,1,192,1536]{3,2,0,1:T(8,128)(2,1)S(1)}, u32[]{:S(2)}, u32[]{:S(2)}) %collective-permute-start.54) | collective-permute-done | bytes 1179680 | tf_op jit(solution)/shard_map/ppermute | solution.py:37
  1161.1 15.1 %collective-permute-done.52 = bf16[1,1,192,1536]{3,2,0,1:T(8,128)(2,1)S(1)} collective-permute-done((bf16[1,1,192,1536]{3,2,0,1:T(8,128)(2,1)S(1)}, bf16[1,1,192,1536]{3,2,0,1:T(8,128)(2,1)S(1)}, u32[]{:S(2)}, u32[]{:S(2)}) %collective-permute-start.52) | collective-permute-done | bytes 589856 | tf_op jit(solution)/shard_map/ppermute | solution.py:37
  1181.0 6.1 collective-permute-done.55
  1204.8 4.6 constant_dynamic-slice_fusion.8
  1218.2 9.5 collective-permute-done.62
  1227.7 22.7 %collective-permute-done.61 = bf16[4,192,384]{2,1,0:T(8,128)(2,1)S(1)} collective-permute-done((bf16[4,192,384]{2,1,0:T(8,128)(2,1)S(1)}, bf16[4,192,384]{2,1,0:T(8,128)(2,1)S(1)}, u32[]{:S(2)}, u32[]{:S(2)}) %collective-permute-start.61) | collective-permute-done | bytes 589856 | tf_op jit(solution)/shard_map/ppermute | solution.py:21
  (406 shorter events, 168.2 us)
Async XLA Ops:
  16.6 24.1 %collective-permute-start.2 = (bf16[2,48,1536]{2,1,0:T(8,128)(2,1)}, bf16[2,48,1536]{2,1,0:T(8,128)(2,1)}, u32[]{:S(2)}, u32[]{:S(2)}) collective-permute-start(bf16[2,48,1536]{2,1,0:T(8,128)(2,1)} %fusion.54), channel_id=1, source_target_pairs={{0,3},{1,0},{2,1},{3,2},{4,7},{5,4},{6,5},{7,6},{8,11},{9,8},{10,9... | collective-permute-start | bytes 884744 | tf_op jit(solution)/shard_map/ppermute | solution.py:21
  21.6 27.8 %collective-permute-start.1 = (bf16[2,48,1536]{2,1,0:T(8,128)(2,1)}, bf16[2,48,1536]{2,1,0:T(8,128)(2,1)}, u32[]{:S(2)}, u32[]{:S(2)}) collective-permute-start(bf16[2,48,1536]{2,1,0:T(8,128)(2,1)} %fusion.54), channel_id=1, source_target_pairs={{0,2},{1,3},{2,0},{3,1},{4,6},{5,7},{6,4},{7,5},{8,10},{9,11},{10,... | collective-permute-start | bytes 884744 | tf_op jit(solution)/shard_map/ppermute | solution.py:21
  21.7 35.3 %collective-permute-start = (bf16[2,48,1536]{2,1,0:T(8,128)(2,1)}, bf16[2,48,1536]{2,1,0:T(8,128)(2,1)}, u32[]{:S(2)}, u32[]{:S(2)}) collective-permute-start(bf16[2,48,1536]{2,1,0:T(8,128)(2,1)} %fusion.54), channel_id=1, source_target_pairs={{0,1},{1,2},{2,3},{3,0},{4,5},{5,6},{6,7},{7,4},{8,9},{9,10},{10,1... | collective-permute-start | bytes 884744 | tf_op jit(solution)/shard_map/ppermute | solution.py:21
  30.2 29.6 %collective-permute-start.14 = (bf16[2,48,1536]{2,1,0:T(8,128)(2,1)}, bf16[2,48,1536]{2,1,0:T(8,128)(2,1)S(1)}, u32[]{:S(2)}, u32[]{:S(2)}) collective-permute-start(bf16[2,48,1536]{2,1,0:T(8,128)(2,1)} %fusion.55), channel_id=1, source_target_pairs={{0,3},{1,0},{2,1},{3,2},{4,7},{5,4},{6,5},{7,6},{8,11},{9,8},{10,9... | collective-permute-start | bytes 884744 | tf_op jit(solution)/shard_map/ppermute | solution.py:21
  33.0 49.0 %collective-permute-start.13 = (bf16[2,48,1536]{2,1,0:T(8,128)(2,1)}, bf16[2,48,1536]{2,1,0:T(8,128)(2,1)}, u32[]{:S(2)}, u32[]{:S(2)}) collective-permute-start(bf16[2,48,1536]{2,1,0:T(8,128)(2,1)} %fusion.55), channel_id=1, source_target_pairs={{0,2},{1,3},{2,0},{3,1},{4,6},{5,7},{6,4},{7,5},{8,10},{9,11},{10,... | collective-permute-start | bytes 884744 | tf_op jit(solution)/shard_map/ppermute | solution.py:21
  40.7 44.0 %collective-permute-start.12 = (bf16[2,48,1536]{2,1,0:T(8,128)(2,1)}, bf16[2,48,1536]{2,1,0:T(8,128)(2,1)S(1)}, u32[]{:S(2)}, u32[]{:S(2)}) collective-permute-start(bf16[2,48,1536]{2,1,0:T(8,128)(2,1)} %fusion.55), channel_id=1, source_target_pairs={{0,1},{1,2},{2,3},{3,0},{4,5},{5,6},{6,7},{7,4},{8,9},{9,10},{10,1... | collective-permute-start | bytes 884744 | tf_op jit(solution)/shard_map/ppermute | solution.py:21
  49.4 49.9 %collective-permute-start.8 = (bf16[128,1536]{1,0:T(8,128)(2,1)S(1)}, bf16[128,1536]{1,0:T(8,128)(2,1)S(1)}, u32[]{:S(2)}, u32[]{:S(2)}) collective-permute-start(bf16[128,1536]{1,0:T(8,128)(2,1)S(1)} %bitcast.309), channel_id=1, source_target_pairs={{0,3},{1,0},{2,1},{3,2},{4,7},{5,4},{6,5},{7,6},{8,11},{9,8},{10,9... | collective-permute-start | bytes 1179656 | tf_op jit(solution)/shard_map/ppermute | solution.py:21
  58.3 29.0 %collective-permute-start.3 = (bf16[1,3,48,1536]{3,2,1,0:T(8,128)(2,1)S(1)}, bf16[1,3,48,1536]{3,2,1,0:T(8,128)(2,1)S(1)}, u32[]{:S(2)}, u32[]{:S(2)}) collective-permute-start(bf16[1,3,48,1536]{3,2,1,0:T(8,128)(2,1)S(1)} %get-tuple-element.141), channel_id=1, source_target_pairs={{0,8},{4,12},{8,0},{12,4},{16,24},{20,28},{24,16},{28,20},{1,9},{5... | collective-permute-start | bytes 1327112 | tf_op jit(solution)/shard_map/ppermute | solution.py:37
  59.8 46.2 %collective-permute-start.7 = (bf16[128,1536]{1,0:T(8,128)(2,1)S(1)}, bf16[128,1536]{1,0:T(8,128)(2,1)S(1)}, u32[]{:S(2)}, u32[]{:S(2)}) collective-permute-start(bf16[128,1536]{1,0:T(8,128)(2,1)S(1)} %bitcast.310), channel_id=1, source_target_pairs={{0,2},{1,3},{2,0},{3,1},{4,6},{5,7},{6,4},{7,5},{8,10},{9,11},{10,... | collective-permute-start | bytes 1179656 | tf_op jit(solution)/shard_map/ppermute | solution.py:21
  82.0 25.6 %collective-permute-start.6 = (bf16[128,1536]{1,0:T(8,128)(2,1)S(1)}, bf16[128,1536]{1,0:T(8,128)(2,1)S(1)}, u32[]{:S(2)}, u32[]{:S(2)}) collective-permute-start(bf16[128,1536]{1,0:T(8,128)(2,1)S(1)} %bitcast.311), channel_id=1, source_target_pairs={{0,1},{1,2},{2,3},{3,0},{4,5},{5,6},{6,7},{7,4},{8,9},{9,10},{10,1... | collective-permute-start | bytes 1179656 | tf_op jit(solution)/shard_map/ppermute | solution.py:21
  84.7 13.1 %collective-permute-start.9 = (bf16[1,3,48,1536]{3,2,1,0:T(8,128)(2,1)S(1)}, bf16[1,3,48,1536]{3,2,1,0:T(8,128)(2,1)S(1)}, u32[]{:S(2)}, u32[]{:S(2)}) collective-permute-start(bf16[1,3,48,1536]{3,2,1,0:T(8,128)(2,1)S(1)} %get-tuple-element.140), channel_id=1, source_target_pairs={{0,16},{4,20},{8,24},{12,28},{16,0},{20,4},{24,8},{28,12},{1,17},{... | collective-permute-start | bytes 1327112 | tf_op jit(solution)/shard_map/ppermute | solution.py:37
  87.3 29.4 %collective-permute-start.4 = (bf16[2,3,48,1536]{3,2,1,0:T(8,128)(2,1)S(1)}, bf16[2,3,48,1536]{3,2,1,0:T(8,128)(2,1)S(1)}, u32[]{:S(2)}, u32[]{:S(2)}) collective-permute-start(bf16[2,3,48,1536]{3,2,1,0:T(8,128)(2,1)S(1)} %pad_maximum_fusion.10), channel_id=1, source_target_pairs={{0,16},{4,20},{8,24},{12,28},{16,0},{20,4},{24,8},{28,12},{1,17},{... | collective-permute-start | bytes 2654216 | tf_op jit(solution)/shard_map/ppermute | solution.py:37
  97.8 11.6 collective-permute-start.15
  100.0 536.4 %collective-permute-start.30 = (f32[8,128]{1,0:T(8,128)}, f32[8,128]{1,0:T(8,128)}, u32[]{:S(2)}, u32[]{:S(2)}) collective-permute-start(f32[8,128]{1,0:T(8,128)} %broadcast_in_dim.91), channel_id=1, source_target_pairs={{0,4},{4,0},{8,12},{12,8},{16,20},{20,16},{24,28},{28,24},{1,5},{5... | collective-permute-start | bytes 12296 | tf_op jit(solution)/shard_map/ppermute | solution.py:37
  106.0 23.7 %collective-permute-start.21 = (bf16[1,3,48,1536]{3,2,1,0:T(8,128)(2,1)S(1)}, bf16[1,3,48,1536]{3,2,1,0:T(8,128)(2,1)S(1)}, u32[]{:S(2)}, u32[]{:S(2)}) collective-permute-start(bf16[1,3,48,1536]{3,2,1,0:T(8,128)(2,1)S(1)} %get-tuple-element.138), channel_id=1, source_target_pairs={{0,16},{4,20},{8,24},{12,28},{16,0},{20,4},{24,8},{28,12},{1,17},{... | collective-permute-start | bytes 1327112 | tf_op jit(solution)/shard_map/ppermute | solution.py:37
  107.5 20.2 %collective-permute-start.10 = (bf16[2,3,48,1536]{3,2,1,0:T(8,128)(2,1)S(1)}, bf16[2,3,48,1536]{3,2,1,0:T(8,128)(2,1)S(1)}, u32[]{:S(2)}, u32[]{:S(2)}) collective-permute-start(bf16[2,3,48,1536]{3,2,1,0:T(8,128)(2,1)S(1)} %pad_maximum_fusion.11), channel_id=1, source_target_pairs={{0,8},{4,12},{8,0},{12,4},{16,24},{20,28},{24,16},{28,20},{1,9},{5... | collective-permute-start | bytes 2654216 | tf_op jit(solution)/shard_map/ppermute | solution.py:37
  109.4 32.8 %collective-permute-start.16 = (bf16[2,3,48,1536]{3,2,1,0:T(8,128)(2,1)S(1)}, bf16[2,3,48,1536]{3,2,1,0:T(8,128)(2,1)S(1)}, u32[]{:S(2)}, u32[]{:S(2)}) collective-permute-start(bf16[2,3,48,1536]{3,2,1,0:T(8,128)(2,1)S(1)} %pad_maximum_fusion.13), channel_id=1, source_target_pairs={{0,16},{4,20},{8,24},{12,28},{16,0},{20,4},{24,8},{28,12},{1,17},{... | collective-permute-start | bytes 2654216 | tf_op jit(solution)/shard_map/ppermute | solution.py:37
  116.9 36.4 %collective-permute-start.5 = (bf16[4,3,48,1536]{3,2,1,0:T(8,128)(2,1)S(1)}, bf16[4,3,48,1536]{3,2,1,0:T(8,128)(2,1)S(1)}, u32[]{:S(2)}, u32[]{:S(2)}) collective-permute-start(bf16[4,3,48,1536]{3,2,1,0:T(8,128)(2,1)S(1)} %pad_maximum_fusion.2.even_ref), channel_id=1, source_target_pairs={{0,4},{4,0},{8,12},{12,8},{16,20},{20,16},{24,28},{28,24},{1,5},{5... | collective-permute-start | bytes 5308424 | tf_op jit(solution)/shard_map/ppermute | solution.py:37
  129.1 170.1 %collective-permute-start.11 = (bf16[4,3,48,1536]{3,2,1,0:T(8,128)(2,1)}, bf16[4,3,48,1536]{3,2,1,0:T(8,128)(2,1)}, u32[]{:S(2)}, u32[]{:S(2)}) collective-permute-start(bf16[4,3,48,1536]{3,2,1,0:T(8,128)(2,1)} %pad_maximum_fusion.3.even_ref), channel_id=1, source_target_pairs={{0,4},{4,0},{8,12},{12,8},{16,20},{20,16},{24,28},{28,24},{1,5},{5... | collective-permute-start | bytes 5308424 | tf_op jit(solution)/shard_map/ppermute | solution.py:37
  129.8 22.1 %collective-permute-start.22 = (bf16[2,3,48,1536]{3,2,1,0:T(8,128)(2,1)S(1)}, bf16[2,3,48,1536]{3,2,1,0:T(8,128)(2,1)S(1)}, u32[]{:S(2)}, u32[]{:S(2)}) collective-permute-start(bf16[2,3,48,1536]{3,2,1,0:T(8,128)(2,1)S(1)} %pad_maximum_fusion.14), channel_id=1, source_target_pairs={{0,8},{4,12},{8,0},{12,4},{16,24},{20,28},{24,16},{28,20},{1,9},{5... | collective-permute-start | bytes 2654216 | tf_op jit(solution)/shard_map/ppermute | solution.py:37
  143.6 306.9 %collective-permute-start.17 = (bf16[4,3,48,1536]{3,2,1,0:T(8,128)(2,1)}, bf16[4,3,48,1536]{3,2,1,0:T(8,128)(2,1)}, u32[]{:S(2)}, u32[]{:S(2)}) collective-permute-start(bf16[4,3,48,1536]{3,2,1,0:T(8,128)(2,1)} %pad_maximum_fusion.4.even_ref), channel_id=1, source_target_pairs={{0,4},{4,0},{8,12},{12,8},{16,20},{20,16},{24,28},{28,24},{1,5},{5... | collective-permute-start | bytes 5308424 | tf_op jit(solution)/shard_map/ppermute | solution.py:37
  153.3 494.3 %collective-permute-start.23 = (bf16[4,3,48,1536]{3,2,1,0:T(8,128)(2,1)}, bf16[4,3,48,1536]{3,2,1,0:T(8,128)(2,1)}, u32[]{:S(2)}, u32[]{:S(2)}) collective-permute-start(bf16[4,3,48,1536]{3,2,1,0:T(8,128)(2,1)} %pad_maximum_fusion.5.even_ref), channel_id=1, source_target_pairs={{0,4},{4,0},{8,12},{12,8},{16,20},{20,16},{24,28},{28,24},{1,5},{5... | collective-permute-start | bytes 5308424 | tf_op jit(solution)/shard_map/ppermute | solution.py:37
  628.7 163.8 %collective-permute-start.18 = (bf16[1632,128]{1,0:T(8,128)(2,1)}, bf16[1632,128]{1,0:T(8,128)(2,1)S(1)}, u32[]{:S(2)}, u32[]{:S(2)}) collective-permute-start(bf16[1632,128]{1,0:T(8,128)(2,1)} %get-tuple-element.25), channel_id=1, source_target_pairs={{0,3},{1,0},{2,1},{3,2},{4,7},{5,4},{6,5},{7,6},{8,11},{9,8},{10,9... | collective-permute-start | bytes 1253384 | tf_op jit(solution)/shard_map/ppermute | solution.py:21
  629.1 163.5 %collective-permute-start.19 = (bf16[1632,128]{1,0:T(8,128)(2,1)}, bf16[1632,128]{1,0:T(8,128)(2,1)S(1)}, u32[]{:S(2)}, u32[]{:S(2)}) collective-permute-start(bf16[1632,128]{1,0:T(8,128)(2,1)} %get-tuple-element.26), channel_id=1, source_target_pairs={{0,2},{1,3},{2,0},{3,1},{4,6},{5,7},{6,4},{7,5},{8,10},{9,11},{10,... | collective-permute-start | bytes 1253384 | tf_op jit(solution)/shard_map/ppermute | solution.py:21
  634.4 158.2 %collective-permute-start.20 = (bf16[1632,128]{1,0:T(8,128)(2,1)}, bf16[1632,128]{1,0:T(8,128)(2,1)S(1)}, u32[]{:S(2)}, u32[]{:S(2)}) collective-permute-start(bf16[1632,128]{1,0:T(8,128)(2,1)} %get-tuple-element.27), channel_id=1, source_target_pairs={{0,1},{1,2},{2,3},{3,0},{4,5},{5,6},{6,7},{7,4},{8,9},{9,10},{10,1... | collective-permute-start | bytes 1253384 | tf_op jit(solution)/shard_map/ppermute | solution.py:21
  645.0 200.5 %collective-permute-start.35 = (bf16[128,1536]{1,0:T(8,128)(2,1)}, bf16[128,1536]{1,0:T(8,128)(2,1)}, u32[]{:S(2)}, u32[]{:S(2)}) collective-permute-start(bf16[128,1536]{1,0:T(8,128)(2,1)} %bitcast.339), channel_id=1, source_target_pairs={{0,3},{1,0},{2,1},{3,2},{4,7},{5,4},{6,5},{7,6},{8,11},{9,8},{10,9... | collective-permute-start | bytes 1179656 | tf_op jit(solution)/shard_map/ppermute | solution.py:21
  647.7 197.8 %collective-permute-start.34 = (bf16[128,1536]{1,0:T(8,128)(2,1)}, bf16[128,1536]{1,0:T(8,128)(2,1)}, u32[]{:S(2)}, u32[]{:S(2)}) collective-permute-start(bf16[128,1536]{1,0:T(8,128)(2,1)} %bitcast.340), channel_id=1, source_target_pairs={{0,2},{1,3},{2,0},{3,1},{4,6},{5,7},{6,4},{7,5},{8,10},{9,11},{10,... | collective-permute-start | bytes 1179656 | tf_op jit(solution)/shard_map/ppermute | solution.py:21
  796.8 12.2 collective-permute-start.26
  799.4 40.7 %collective-permute-start.25 = (bf16[128,1536]{1,0:T(8,128)(2,1)S(1)}, bf16[128,1536]{1,0:T(8,128)(2,1)S(1)}, u32[]{:S(2)}, u32[]{:S(2)}) collective-permute-start(bf16[128,1536]{1,0:T(8,128)(2,1)S(1)} %add_convert_fusion.6), channel_id=1, source_target_pairs={{0,2},{1,3},{2,0},{3,1},{4,6},{5,7},{6,4},{7,5},{8,10},{9,11},{10,... | collective-permute-start | bytes 1179656 | tf_op jit(solution)/shard_map/ppermute | solution.py:21
  799.8 40.3 %collective-permute-start.24 = (bf16[128,1536]{1,0:T(8,128)(2,1)S(1)}, bf16[128,1536]{1,0:T(8,128)(2,1)S(1)}, u32[]{:S(2)}, u32[]{:S(2)}) collective-permute-start(bf16[128,1536]{1,0:T(8,128)(2,1)S(1)} %add_convert_fusion.6), channel_id=1, source_target_pairs={{0,1},{1,2},{2,3},{3,0},{4,5},{5,6},{6,7},{7,4},{8,9},{9,10},{10,1... | collective-permute-start | bytes 1179656 | tf_op jit(solution)/shard_map/ppermute | solution.py:21
  809.0 36.4 %collective-permute-start.33 = (bf16[128,1536]{1,0:T(8,128)(2,1)S(1)}, bf16[128,1536]{1,0:T(8,128)(2,1)S(1)}, u32[]{:S(2)}, u32[]{:S(2)}) collective-permute-start(bf16[128,1536]{1,0:T(8,128)(2,1)S(1)} %bitcast.341), channel_id=1, source_target_pairs={{0,1},{1,2},{2,3},{3,0},{4,5},{5,6},{6,7},{7,4},{8,9},{9,10},{10,1... | collective-permute-start | bytes 1179656 | tf_op jit(solution)/shard_map/ppermute | solution.py:21
  852.3 17.3 %collective-permute-start.38 = (bf16[128,1536]{1,0:T(8,128)(2,1)S(1)}, bf16[128,1536]{1,0:T(8,128)(2,1)S(1)}, u32[]{:S(2)}, u32[]{:S(2)}) collective-permute-start(bf16[128,1536]{1,0:T(8,128)(2,1)S(1)} %get-tuple-element.129), channel_id=1, source_target_pairs={{0,1},{1,2},{2,3},{3,0},{4,5},{5,6},{6,7},{7,4},{8,9},{9,10},{10,1... | collective-permute-start | bytes 1179656 | tf_op jit(solution)/shard_map/ppermute | solution.py:21
  852.4 39.5 %collective-permute-start.37 = (bf16[128,1536]{1,0:T(8,128)(2,1)S(1)}, bf16[128,1536]{1,0:T(8,128)(2,1)S(1)}, u32[]{:S(2)}, u32[]{:S(2)}) collective-permute-start(bf16[128,1536]{1,0:T(8,128)(2,1)S(1)} %get-tuple-element.130), channel_id=1, source_target_pairs={{0,2},{1,3},{2,0},{3,1},{4,6},{5,7},{6,4},{7,5},{8,10},{9,11},{10,... | collective-permute-start | bytes 1179656 | tf_op jit(solution)/shard_map/ppermute | solution.py:21
  852.5 39.4 %collective-permute-start.36 = (bf16[128,1536]{1,0:T(8,128)(2,1)S(1)}, bf16[128,1536]{1,0:T(8,128)(2,1)S(1)}, u32[]{:S(2)}, u32[]{:S(2)}) collective-permute-start(bf16[128,1536]{1,0:T(8,128)(2,1)S(1)} %get-tuple-element.128), channel_id=1, source_target_pairs={{0,3},{1,0},{2,1},{3,2},{4,7},{5,4},{6,5},{7,6},{8,11},{9,8},{10,9... | collective-permute-start | bytes 1179656 | tf_op jit(solution)/shard_map/ppermute | solution.py:21
  858.9 33.5 %collective-permute-start.29 = (bf16[128,1536]{1,0:T(8,128)(2,1)S(1)}, bf16[128,1536]{1,0:T(8,128)(2,1)S(1)}, u32[]{:S(2)}, u32[]{:S(2)}) collective-permute-start(bf16[128,1536]{1,0:T(8,128)(2,1)S(1)} %get-tuple-element.132), channel_id=1, source_target_pairs={{0,1},{1,2},{2,3},{3,0},{4,5},{5,6},{6,7},{7,4},{8,9},{9,10},{10,1... | collective-permute-start | bytes 1179656 | tf_op jit(solution)/shard_map/ppermute | solution.py:21
  859.5 53.2 %collective-permute-start.28 = (bf16[128,1536]{1,0:T(8,128)(2,1)S(1)}, bf16[128,1536]{1,0:T(8,128)(2,1)S(1)}, u32[]{:S(2)}, u32[]{:S(2)}) collective-permute-start(bf16[128,1536]{1,0:T(8,128)(2,1)S(1)} %get-tuple-element.133), channel_id=1, source_target_pairs={{0,2},{1,3},{2,0},{3,1},{4,6},{5,7},{6,4},{7,5},{8,10},{9,11},{10,... | collective-permute-start | bytes 1179656 | tf_op jit(solution)/shard_map/ppermute | solution.py:21
  869.6 43.1 %collective-permute-start.27 = (bf16[128,1536]{1,0:T(8,128)(2,1)S(1)}, bf16[128,1536]{1,0:T(8,128)(2,1)S(1)}, u32[]{:S(2)}, u32[]{:S(2)}) collective-permute-start(bf16[128,1536]{1,0:T(8,128)(2,1)S(1)} %get-tuple-element.131), channel_id=1, source_target_pairs={{0,3},{1,0},{2,1},{3,2},{4,7},{5,4},{6,5},{7,6},{8,11},{9,8},{10,9... | collective-permute-start | bytes 1179656 | tf_op jit(solution)/shard_map/ppermute | solution.py:21
  915.7 27.4 %collective-permute-start.39 = (bf16[1632,128]{1,0:T(8,128)(2,1)S(1)}, bf16[1632,128]{1,0:T(8,128)(2,1)S(1)}, u32[]{:S(2)}, u32[]{:S(2)}) collective-permute-start(bf16[1632,128]{1,0:T(8,128)(2,1)S(1)} %shard_map.277.rest_0_.rest_4_), channel_id=1, source_target_pairs={{0,1},{1,2},{2,3},{3,0},{4,5},{5,6},{6,7},{7,4},{8,9},{9,10},{10,1... | collective-permute-start | bytes 1253384 | tf_op jit(solution)/shard_map/ppermute | solution.py:21
  932.8 17.7 %collective-permute-start.40 = (bf16[1632,128]{1,0:T(8,128)(2,1)S(1)}, bf16[1632,128]{1,0:T(8,128)(2,1)S(1)}, u32[]{:S(2)}, u32[]{:S(2)}) collective-permute-start(bf16[1632,128]{1,0:T(8,128)(2,1)S(1)} %shard_map.277.rest_0_.rest_4_), channel_id=1, source_target_pairs={{0,2},{1,3},{2,0},{3,1},{4,6},{5,7},{6,4},{7,5},{8,10},{9,11},{10,... | collective-permute-start | bytes 1253384 | tf_op jit(solution)/shard_map/ppermute | solution.py:21
  932.8 21.7 %collective-permute-start.41 = (bf16[1632,128]{1,0:T(8,128)(2,1)S(1)}, bf16[1632,128]{1,0:T(8,128)(2,1)S(1)}, u32[]{:S(2)}, u32[]{:S(2)}) collective-permute-start(bf16[1632,128]{1,0:T(8,128)(2,1)S(1)} %shard_map.277.rest_0_.rest_4_), channel_id=1, source_target_pairs={{0,3},{1,0},{2,1},{3,2},{4,7},{5,4},{6,5},{7,6},{8,11},{9,8},{10,9... | collective-permute-start | bytes 1253384 | tf_op jit(solution)/shard_map/ppermute | solution.py:21
  939.4 124.4 %collective-permute-start.63 = (bf16[4,1,2,192,1536]{4,3,0,2,1:T(8,128)(2,1)}, bf16[4,1,2,192,1536]{4,3,0,2,1:T(8,128)(2,1)}, u32[]{:S(2)}, u32[]{:S(2)}) collective-permute-start(bf16[4,1,2,192,1536]{4,3,0,2,1:T(8,128)(2,1)} %fusion.7), channel_id=1, source_target_pairs={{0,4},{4,0},{8,12},{12,8},{16,20},{20,16},{24,28},{28,24},{1,5},{5... | collective-permute-start | bytes 14155784 | tf_op jit(solution)/shard_map/ppermute | solution.py:37
  1006.1 19.1 %collective-permute-start.42 = (f32[8,1536]{1,0:T(8,128)}, f32[8,1536]{1,0:T(8,128)S(1)}, u32[]{:S(2)}, u32[]{:S(2)}) collective-permute-start(f32[8,1536]{1,0:T(8,128)} %stack.127), channel_id=1, source_target_pairs={{0,4},{4,0},{8,12},{12,8},{16,20},{20,16},{24,28},{28,24},{1,5},{5... | collective-permute-start | bytes 147464 | tf_op jit(solution)/shard_map/ppermute | solution.py:37
  1007.4 47.2 %collective-permute-start.49 = (bf16[128,1536]{1,0:T(8,128)(2,1)S(1)}, bf16[128,1536]{1,0:T(8,128)(2,1)}, u32[]{:S(2)}, u32[]{:S(2)}) collective-permute-start(bf16[128,1536]{1,0:T(8,128)(2,1)S(1)} %get-tuple-element.126), channel_id=1, source_target_pairs={{0,1},{1,2},{2,3},{3,0},{4,5},{5,6},{6,7},{7,4},{8,9},{9,10},{10,1... | collective-permute-start | bytes 1179656 | tf_op jit(solution)/shard_map/ppermute | solution.py:21
  1016.7 38.0 %collective-permute-start.48 = (bf16[128,1536]{1,0:T(8,128)(2,1)S(1)}, bf16[128,1536]{1,0:T(8,128)(2,1)}, u32[]{:S(2)}, u32[]{:S(2)}) collective-permute-start(bf16[128,1536]{1,0:T(8,128)(2,1)S(1)} %get-tuple-element.127), channel_id=1, source_target_pairs={{0,2},{1,3},{2,0},{3,1},{4,6},{5,7},{6,4},{7,5},{8,10},{9,11},{10,... | collective-permute-start | bytes 1179656 | tf_op jit(solution)/shard_map/ppermute | solution.py:21
  1027.5 48.1 %collective-permute-start.50 = (bf16[4,1,2,192,1536]{4,3,0,2,1:T(8,128)(2,1)}, bf16[4,1,2,192,1536]{4,3,0,2,1:T(8,128)(2,1)}, u32[]{:S(2)}, u32[]{:S(2)}) collective-permute-start(bf16[4,1,2,192,1536]{4,3,0,2,1:T(8,128)(2,1)} %fusion.15), channel_id=1, source_target_pairs={{0,4},{4,0},{8,12},{12,8},{16,20},{20,16},{24,28},{28,24},{1,5},{5... | collective-permute-start | bytes 14155784 | tf_op jit(solution)/shard_map/ppermute | solution.py:37
  1034.5 8.5 collective-permute-start.45
  1043.0 5.3 collective-permute-start.46
  1048.3 11.2 collective-permute-start.47
  1054.6 27.0 %collective-permute-start.53 = (bf16[4,1,2,192,1536]{4,3,0,2,1:T(8,128)(2,1)}, bf16[4,1,2,192,1536]{4,3,0,2,1:T(8,128)(2,1)}, u32[]{:S(2)}, u32[]{:S(2)}) collective-permute-start(bf16[4,1,2,192,1536]{4,3,0,2,1:T(8,128)(2,1)} %fusion.11), channel_id=1, source_target_pairs={{0,4},{4,0},{8,12},{12,8},{16,20},{20,16},{24,28},{28,24},{1,5},{5... | collective-permute-start | bytes 14155784 | tf_op jit(solution)/shard_map/ppermute | solution.py:37
  1071.2 29.2 %collective-permute-start.64 = (bf16[1,2,192,1536]{3,2,1,0:T(8,128)(2,1)}, bf16[1,2,192,1536]{3,2,1,0:T(8,128)(2,1)}, u32[]{:S(2)}, u32[]{:S(2)}) collective-permute-start(bf16[1,2,192,1536]{3,2,1,0:T(8,128)(2,1)} %dynamic-slice_bitcast_fusion.1), channel_id=1, source_target_pairs={{0,16},{4,20},{8,24},{12,28},{16,0},{20,4},{24,8},{28,12},{1,17},{... | collective-permute-start | bytes 3538952 | tf_op jit(solution)/shard_map/ppermute | solution.py:37
  1074.1 30.6 %collective-permute-start.66 = (bf16[2,1,192,1536]{3,2,0,1:T(8,128)(2,1)}, bf16[2,1,192,1536]{3,2,0,1:T(8,128)(2,1)}, u32[]{:S(2)}, u32[]{:S(2)}) collective-permute-start(bf16[2,1,192,1536]{3,2,0,1:T(8,128)(2,1)} %dynamic-slice_bitcast_fusion), channel_id=1, source_target_pairs={{0,8},{4,12},{8,0},{12,4},{16,24},{20,28},{24,16},{28,20},{1,9},{5... | collective-permute-start | bytes 3538952 | tf_op jit(solution)/shard_map/ppermute | solution.py:37
  1081.0 47.7 %collective-permute-start.51 = (bf16[2,1,192,1536]{3,2,0,1:T(8,128)(2,1)}, bf16[2,1,192,1536]{3,2,0,1:T(8,128)(2,1)}, u32[]{:S(2)}, u32[]{:S(2)}) collective-permute-start(bf16[2,1,192,1536]{3,2,0,1:T(8,128)(2,1)} %dynamic-slice_bitcast_fusion.5), channel_id=1, source_target_pairs={{0,8},{4,12},{8,0},{12,4},{16,24},{20,28},{24,16},{28,20},{1,9},{5... | collective-permute-start | bytes 3538952 | tf_op jit(solution)/shard_map/ppermute | solution.py:37
  1086.6 67.2 %collective-permute-start.54 = (bf16[2,1,192,1536]{3,2,0,1:T(8,128)(2,1)S(1)}, bf16[2,1,192,1536]{3,2,0,1:T(8,128)(2,1)S(1)}, u32[]{:S(2)}, u32[]{:S(2)}) collective-permute-start(bf16[2,1,192,1536]{3,2,0,1:T(8,128)(2,1)S(1)} %dynamic-slice_bitcast_fusion.4), channel_id=1, source_target_pairs={{0,8},{4,12},{8,0},{12,4},{16,24},{20,28},{24,16},{28,20},{1,9},{5... | collective-permute-start | bytes 3538952 | tf_op jit(solution)/shard_map/ppermute | solution.py:37
  1088.2 67.4 %collective-permute-start.56 = (bf16[1,2,192,1536]{3,2,1,0:T(8,128)(2,1)S(1)}, bf16[1,2,192,1536]{3,2,1,0:T(8,128)(2,1)S(1)}, u32[]{:S(2)}, u32[]{:S(2)}) collective-permute-start(bf16[1,2,192,1536]{3,2,1,0:T(8,128)(2,1)S(1)} %dynamic-slice_bitcast_fusion.3), channel_id=1, source_target_pairs={{0,16},{4,20},{8,24},{12,28},{16,0},{20,4},{24,8},{28,12},{1,17},{... | collective-permute-start | bytes 3538952 | tf_op jit(solution)/shard_map/ppermute | solution.py:37
  1100.4 57.9 %collective-permute-start.58 = (bf16[1,2,192,1536]{3,2,1,0:T(8,128)(2,1)S(1)}, bf16[1,2,192,1536]{3,2,1,0:T(8,128)(2,1)S(1)}, u32[]{:S(2)}, u32[]{:S(2)}) collective-permute-start(bf16[1,2,192,1536]{3,2,1,0:T(8,128)(2,1)S(1)} %dynamic-slice_bitcast_fusion.2), channel_id=1, source_target_pairs={{0,16},{4,20},{8,24},{12,28},{16,0},{20,4},{24,8},{28,12},{1,17},{... | collective-permute-start | bytes 3538952 | tf_op jit(solution)/shard_map/ppermute | solution.py:37
  1104.7 109.0 %collective-permute-start.65 = (bf16[1,1,192,1536]{3,2,1,0:T(8,128)(2,1)}, bf16[1,1,192,1536]{3,2,1,0:T(8,128)(2,1)}, u32[]{:S(2)}, u32[]{:S(2)}) collective-permute-start(bf16[1,1,192,1536]{3,2,1,0:T(8,128)(2,1)} %constant_dynamic-slice_fusion.5), channel_id=1, source_target_pairs={{0,8},{4,12},{8,0},{12,4},{16,24},{20,28},{24,16},{28,20},{1,9},{5... | collective-permute-start | bytes 1769480 | tf_op jit(solution)/shard_map/ppermute | solution.py:37
  1128.6 87.3 %collective-permute-start.67 = (bf16[1,1,192,1536]{3,2,0,1:T(8,128)(2,1)}, bf16[1,1,192,1536]{3,2,0,1:T(8,128)(2,1)}, u32[]{:S(2)}, u32[]{:S(2)}) collective-permute-start(bf16[1,1,192,1536]{3,2,0,1:T(8,128)(2,1)} %constant_dynamic-slice_fusion.4), channel_id=1, source_target_pairs={{0,16},{4,20},{8,24},{12,28},{16,0},{20,4},{24,8},{28,12},{1,17},{... | collective-permute-start | bytes 1769480 | tf_op jit(solution)/shard_map/ppermute | solution.py:37
  1153.8 22.3 %collective-permute-start.52 = (bf16[1,1,192,1536]{3,2,0,1:T(8,128)(2,1)S(1)}, bf16[1,1,192,1536]{3,2,0,1:T(8,128)(2,1)S(1)}, u32[]{:S(2)}, u32[]{:S(2)}) collective-permute-start(bf16[1,1,192,1536]{3,2,0,1:T(8,128)(2,1)S(1)} %constant_dynamic-slice_fusion.12), channel_id=1, source_target_pairs={{0,16},{4,20},{8,24},{12,28},{16,0},{20,4},{24,8},{28,12},{1,17},{... | collective-permute-start | bytes 1769480 | tf_op jit(solution)/shard_map/ppermute | solution.py:37
  1155.5 31.6 %collective-permute-start.55 = (bf16[1,1,192,1536]{3,2,0,1:T(8,128)(2,1)}, bf16[1,1,192,1536]{3,2,0,1:T(8,128)(2,1)}, u32[]{:S(2)}, u32[]{:S(2)}) collective-permute-start(bf16[1,1,192,1536]{3,2,0,1:T(8,128)(2,1)} %constant_dynamic-slice_fusion.11), channel_id=1, source_target_pairs={{0,16},{4,20},{8,24},{12,28},{16,0},{20,4},{24,8},{28,12},{1,17},{... | collective-permute-start | bytes 1769480 | tf_op jit(solution)/shard_map/ppermute | solution.py:37
  1158.3 34.6 %collective-permute-start.57 = (bf16[1,1,192,1536]{3,2,1,0:T(8,128)(2,1)}, bf16[1,1,192,1536]{3,2,1,0:T(8,128)(2,1)}, u32[]{:S(2)}, u32[]{:S(2)}) collective-permute-start(bf16[1,1,192,1536]{3,2,1,0:T(8,128)(2,1)} %constant_dynamic-slice_fusion.10), channel_id=1, source_target_pairs={{0,8},{4,12},{8,0},{12,4},{16,24},{20,28},{24,16},{28,20},{1,9},{5... | collective-permute-start | bytes 1769480 | tf_op jit(solution)/shard_map/ppermute | solution.py:37
  1176.1 19.0 %collective-permute-start.59 = (bf16[1,1,192,1536]{3,2,1,0:T(8,128)(2,1)}, bf16[1,1,192,1536]{3,2,1,0:T(8,128)(2,1)}, u32[]{:S(2)}, u32[]{:S(2)}) collective-permute-start(bf16[1,1,192,1536]{3,2,1,0:T(8,128)(2,1)} %constant_dynamic-slice_fusion.9), channel_id=1, source_target_pairs={{0,8},{4,12},{8,0},{12,4},{16,24},{20,28},{24,16},{28,20},{1,9},{5... | collective-permute-start | bytes 1769480 | tf_op jit(solution)/shard_map/ppermute | solution.py:37
  1209.5 18.2 %collective-permute-start.62 = (bf16[4,192,384]{2,1,0:T(8,128)(2,1)S(1)}, bf16[4,192,384]{2,1,0:T(8,128)(2,1)S(1)}, u32[]{:S(2)}, u32[]{:S(2)}) collective-permute-start(bf16[4,192,384]{2,1,0:T(8,128)(2,1)S(1)} %bitcast.336), channel_id=1, source_target_pairs={{0,1},{1,2},{2,3},{3,0},{4,5},{5,6},{6,7},{7,4},{8,9},{9,10},{10,1... | collective-permute-start | bytes 1769480 | tf_op jit(solution)/shard_map/ppermute | solution.py:21
  1209.7 40.7 %collective-permute-start.61 = (bf16[4,192,384]{2,1,0:T(8,128)(2,1)S(1)}, bf16[4,192,384]{2,1,0:T(8,128)(2,1)S(1)}, u32[]{:S(2)}, u32[]{:S(2)}) collective-permute-start(bf16[4,192,384]{2,1,0:T(8,128)(2,1)S(1)} %bitcast.337), channel_id=1, source_target_pairs={{0,2},{1,3},{2,0},{3,1},{4,6},{5,7},{6,4},{7,5},{8,10},{9,11},{10,... | collective-permute-start | bytes 1769480 | tf_op jit(solution)/shard_map/ppermute | solution.py:21
  1212.5 37.9 %collective-permute-start.60 = (bf16[4,192,384]{2,1,0:T(8,128)(2,1)S(1)}, bf16[4,192,384]{2,1,0:T(8,128)(2,1)S(1)}, u32[]{:S(2)}, u32[]{:S(2)}) collective-permute-start(bf16[4,192,384]{2,1,0:T(8,128)(2,1)S(1)} %bitcast.338), channel_id=1, source_target_pairs={{0,3},{1,0},{2,1},{3,2},{4,7},{5,4},{6,5},{7,6},{8,11},{9,8},{10,9... | collective-permute-start | bytes 1769480 | tf_op jit(solution)/shard_map/ppermute | solution.py:21
  (84 other events, 1448.4 us)

commit v2 on v1

--- a/solution.py
+++ b/solution.py
@@ -21,8 +21,19 @@
     return lax.ppermute(x, "tensor", [(i, (i + shift) % count) for i in range(count)])
 
 
+def after(x, *done):
+    return lax.optimization_barrier((x, *done))[0]
+
+
 def gather_blocks(x, count):
-    return [x] + [rotate(x, count, k) for k in range(1, count)]
+    if count != 4:
+        return [x] + [rotate(x, count, k) for k in range(1, count)]
+    z = lax.axis_index("tensor")
+    two = rotate(x, 4, 2)
+    up = lax.ppermute(x, "tensor", [(0, 1), (1, 2), (2, 3)])
+    down = lax.ppermute(x, "tensor", [(1, 0), (2, 1), (3, 2)])
+    ends = lax.ppermute(two, "tensor", [(2, 3), (1, 0)])
+    return [x, jnp.where(z == 0, ends, up), two, jnp.where(z == 3, ends, down)]
 
 
 def scatter_blocks(blocks, count):
@@ -41,36 +52,89 @@
     return count.bit_length() - 1
 
 
-def halve(parts, left, bit, count):
-    place = left.index(bit)
-    rest = parts.shape[1:]
-    split = parts.reshape((1 << place, 2, 1 << (len(left) - place - 1)) + rest)
-    mine = (lax.axis_index("dp") >> bit) & 1
-    send = lax.dynamic_index_in_dim(split, 1 - mine, 1, keepdims=False)
-    keep = lax.dynamic_index_in_dim(split, mine, 1, keepdims=False)
-    got = swap(send, "dp", count, bit)
-    total = keep.astype(F32) + got.astype(F32)
-    left = [b for b in left if b != bit]
-    return total.reshape((1 << len(left),) + rest), left
-
-
 def bit_orders(count):
     outer = list(range(1, bits_of(count)))
     half = (len(outer) + 1) // 2
     return outer, outer[half:] + outer[:half]
 
 
-def reduce_pair(one, two, count):
-    left = list(range(bits_of(count) - 1, -1, -1))
-    both, left = halve(jnp.stack([one, two], axis=1), left, 0, count)
-    both = both.astype(BF)
-    out = []
-    for which, order in enumerate(bit_orders(count)):
-        part, still = both[:, which], left
-        for bit in order:
-            part, still = halve(part.astype(BF), still, bit, count)
-        out.append(part[0])
-    return out
+def gradient_kernel(natural, at_ref, even_ref, odd_ref, y_ref, keep_ref, send_ref):
+    dims = (((1,), (0,)), ((), ())) if natural else (((1,), (1,)), ((), ()))
+    keep_ref[0] = lax.dot_general(
+        even_ref[...], y_ref[...], dims, preferred_element_type=F32
+    ).astype(BF)
+    send_ref[0] = lax.dot_general(
+        odd_ref[...], y_ref[...], dims, preferred_element_type=F32
+    ).astype(BF)
+
+
+def gradient(xt, y, natural, at, n_dp):
+    unit, rows = xt.shape[0] // n_dp, xt.shape[1]
+    wide = y.shape[1] if natural else y.shape[0]
+    half = n_dp // 2
+    return pl.pallas_call(
+        partial(gradient_kernel, natural),
+        grid_spec=pltpu.PrefetchScalarGridSpec(
+            num_scalar_prefetch=1,
+            grid=(half,),
+            in_specs=[
+                pl.BlockSpec((unit, rows), lambda i, at: (at[1] ^ (2 * i), 0)),
+                pl.BlockSpec((unit, rows), lambda i, at: (at[1] ^ (2 * i + 1), 0)),
+                pl.BlockSpec(y.shape, lambda i, at: (0, 0)),
+            ],
+            out_specs=[pl.BlockSpec((1, unit, wide), lambda i, at: (i, 0, 0))] * 2,
+        ),
+        out_shape=[jax.ShapeDtypeStruct((half, unit, wide), BF)] * 2,
+        compiler_params=pltpu.CompilerParams(vmem_limit_bytes=VMEM_LIMIT),
+        cost_estimate=pl.CostEstimate(
+            flops=2 * n_dp * unit * rows * wide,
+            bytes_accessed=2 * (n_dp * unit * (rows + wide) + rows * wide),
+            transcendentals=0,
+        ),
+    )(at, xt, xt, y)
+
+
+def reduce_step(keep, got, order, step, n_dp):
+    left = [b for b in range(bits_of(n_dp) - 1, 0, -1) if b not in order[:step]]
+    place = left.index(order[step])
+    shape = (1 << place, 2, 1 << (len(left) - place - 1)) + keep.shape[1:]
+    flat = (1 << (len(left) - 1),) + keep.shape[1:]
+    keep, got = keep.reshape(shape), got.reshape(shape)
+    send = (keep[:, 1].astype(F32) + got[:, 1].astype(F32)).astype(BF)
+    keep = (keep[:, 0].astype(F32) + got[:, 0].astype(F32)).astype(BF)
+    return keep.reshape(flat), swap(send.reshape(flat), "dp", n_dp, order[step])
+
+
+def reduce_outer(keep, got, order, n_dp):
+    for step in range(len(order)):
+        keep, got = reduce_step(keep, got, order, step, n_dp)
+    return keep[0], got[0]
+
+
+def blocks_kernel(n_t, pairs, at_ref, *refs):
+    ins, outs = refs[: 2 * pairs], refs[2 * pairs :]
+    z = at_ref[0]
+    part = outs[0].shape[-1]
+    for k in range(n_t):
+        start = pl.multiple_of(lax.rem(z - k + n_t, n_t) * part, part)
+        for m in range(pairs):
+            cols = pl.ds(start, part)
+            total = ins[2 * m][:, cols].astype(F32) + ins[2 * m + 1][:, cols].astype(F32)
+            outs[k][m] = total.astype(outs[k].dtype)
+
+
+def tensor_blocks(pairs, at, n_t):
+    rows, columns = pairs[0][0].shape
+    part = columns // n_t
+    count = len(pairs)
+    flat = [x for pair in pairs for x in pair]
+    return pl.pallas_call(
+        partial(blocks_kernel, n_t, count),
+        in_specs=[pl.BlockSpec(memory_space=pltpu.SMEM)]
+        + [pl.BlockSpec(memory_space=pltpu.VMEM)] * len(flat),
+        out_shape=[jax.ShapeDtypeStruct((count, rows, part), F32 if k == 0 else BF) for k in range(n_t)],
+        compiler_params=pltpu.CompilerParams(vmem_limit_bytes=VMEM_LIMIT),
+    )(at, *flat)
 
 
 def all_sum(x, axes):
@@ -80,54 +144,78 @@
     return x
 
 
-def place_kernel(n_dp, n_t, offsets, at_ref, own_ref, even_ref, odd_ref, out_ref, sem):
+def place_kernel(n_t, unit, z_rows, z_cols, offsets, parts, at_ref, own_ref, *refs):
+    out_ref = refs[-1]
     z, p = at_ref[0], at_ref[1]
-    copies = [pltpu.make_async_copy(own_ref, out_ref.at[z], sem)]
+    rows, cols = own_ref.shape
+    if z_rows:
+        out_ref[pl.ds(pl.multiple_of(z * z_rows, z_rows), rows), :] = own_ref[...]
+    else:
+        out_ref[:, pl.ds(pl.multiple_of(z * z_cols, z_cols), cols)] = own_ref[...]
     for k in range(1, n_t):
         shard = lax.rem(z - k + n_t, n_t)
-        for i, off in enumerate(offsets):
-            copies.append(
-                pltpu.make_async_copy(even_ref.at[i, k - 1], out_ref.at[shard, p ^ off], sem)
-            )
-            copies.append(
-                pltpu.make_async_copy(
-                    odd_ref.at[i, k - 1], out_ref.at[shard, p ^ (off ^ 1)], sem
-                )
-            )
-    for copy in copies:
-        copy.start()
-    for copy in copies:
-        copy.wait()
-
-
-def place(own, even, odd, offsets, at, n_dp, n_t):
-    unit = own.shape[0] // n_dp
-    width = own.shape[1]
-    out = pl.pallas_call(
-        partial(place_kernel, n_dp, n_t, offsets),
-        out_shape=jax.ShapeDtypeStruct((n_t, n_dp, unit, width), own.dtype),
-        in_specs=[pl.BlockSpec(memory_space=pltpu.SMEM)] + [pl.BlockSpec(memory_space=pl.ANY)] * 3,
-        out_specs=pl.BlockSpec(memory_space=pl.ANY),
-        scratch_shapes=[pltpu.SemaphoreType.DMA],
-    )(at, own.reshape(n_dp, unit, width), even, odd)
-    return out.reshape(n_t * own.shape[0], width)
-
-
-def gather_pair(one, two, at, n_dp, n_t):
-    unit = one.shape[0] // n_dp
-    width = one.shape[1]
-    slices = jnp.stack([one, two]).reshape(2, n_dp, unit, width)
-    mine = lax.dynamic_index_in_dim(slices, lax.axis_index("dp"), 1, keepdims=False)
-    arrived = jnp.stack([rotate(mine, n_t, k) for k in range(1, n_t)], axis=1)
-    out = []
-    for which, (own, order) in enumerate(zip((one, two), bit_orders(n_dp))):
-        held, offsets = arrived[which][None], [0]
+        for which, (row_at, col_at) in enumerate(parts):
+            for odd in range(2):
+                src = refs[2 * which + odd]
+                height, wide = src.shape[2:]
+                for i, off in enumerate(offsets[which]):
+                    base = shard * z_rows + (p ^ (off ^ odd)) * unit + row_at
+                    where = pl.ds(pl.multiple_of(base, 16), height)
+                    if z_cols:
+                        at = pl.ds(pl.multiple_of(shard * z_cols, z_cols), wide)
+                    else:
+                        at = slice(col_at, col_at + wide)
+                    out_ref[where, at] = src[i, k - 1]
+
+
+def reorder(x, places):
+    return jnp.stack([lax.dynamic_index_in_dim(x, i, 0, keepdims=False) for i in places])
+
+
+def place(own, pieces, offsets, parts, unit, by_rows, at, n_dp, n_t):
+    rows, cols = own.shape
+    shape = (n_t * rows, cols) if by_rows else (rows, n_t * cols)
+    if unit % 16 or any(row_at % 16 for row_at, _ in parts):
+        z, p = at[0], at[1]
+        across = []
+        for (even, odd), offs in zip(pieces, offsets):
+            ordered = [None] * n_dp
+            for i, off in enumerate(offs):
+                ordered[off], ordered[off ^ 1] = even[i], odd[i]
+            across.append(reorder(jnp.stack(ordered), [p ^ d for d in range(n_dp)]))
+        axis = 2 if parts[-1][1] == 0 else 3
+        whole = jnp.concatenate(across, axis=axis).transpose(1, 0, 2, 3)
+        whole = whole.reshape((n_t - 1, rows, cols))
+        whole = jnp.concatenate([own[None], whole], axis=0)
+        whole = reorder(whole, [(z - k + n_t) % n_t for k in range(n_t)])
+        return whole.reshape(shape) if by_rows else whole.transpose(1, 0, 2).reshape(shape)
+    flat = [x for pair in pieces for x in pair]
+    return pl.pallas_call(
+        partial(place_kernel, n_t, unit, rows if by_rows else 0, 0 if by_rows else cols, offsets, parts),
+        out_shape=jax.ShapeDtypeStruct(shape, own.dtype),
+        in_specs=[pl.BlockSpec(memory_space=pltpu.SMEM)]
+        + [pl.BlockSpec(memory_space=pltpu.VMEM)] * (1 + len(flat)),
+        out_specs=pl.BlockSpec(memory_space=pltpu.VMEM),
+        compiler_params=pltpu.CompilerParams(vmem_limit_bytes=VMEM_LIMIT),
+    )(at, own, *flat)
+
+
+def spread(slices, n_dp, n_t):
+    arrived = gather_blocks(slices, n_t)[1:]
+    pieces, offsets = [], []
+    for which, order in enumerate(bit_orders(n_dp)):
+        held, offs = jnp.stack([x[which] for x in arrived])[None], [0]
         for bit in order:
             held = jnp.concatenate([held, swap(held, "dp", n_dp, bit)], axis=0)
-            offsets = offsets + [o ^ (1 << bit) for o in offsets]
-        other = swap(held, "dp", n_dp, 0)
-        out.append(place(own, held, other, offsets, at, n_dp, n_t))
-    return out
+            offs = offs + [o ^ (1 << bit) for o in offs]
+        pieces.append((held, swap(held, "dp", n_dp, 0)))
+        offsets.append(offs)
+    return pieces, offsets, arrived[0]
+
+
+def share_of(x, axis, count):
+    size = x.shape[axis] // count
+    return lax.dynamic_slice_in_dim(x, lax.axis_index("dp") * size, size, axis)
 
 
 def three(x):
@@ -377,10 +465,21 @@
     heads = inner // HD
     images = lengths.shape[0]
 
-    latent_blocks = gather_blocks(latents, n_t)
-    wq, wk = gather_pair(query_weight.T, key_value_weight[:, 0].T, at, n_dp, n_t)
-    wv, wo = gather_pair(key_value_weight[:, 1].T, output_weight, at, n_dp, n_t)
-    cot_all = jnp.concatenate(gather_blocks(cotangent, n_t), axis=0)
+    unit = width // n_dp
+    keyval = jnp.moveaxis(share_of(key_value_weight, 0, n_dp), 1, 0)
+    kv_pieces, kv_offsets, near = spread(keyval, n_dp, n_t)
+    q_share = share_of(query_weight, 0, n_dp).reshape(2, unit // 2, -1)
+    q_pieces, q_offsets, near = spread(after(q_share, near), n_dp, n_t)
+    latent_blocks = gather_blocks(after(latents, near), n_t)
+    out_unit = output_weight.shape[0] // n_dp
+    out_share = share_of(output_weight, 0, n_dp)
+    out_share = jnp.stack([out_share[:, : width // 2], out_share[:, width // 2 :]])
+    o_pieces, o_offsets, near = spread(after(out_share, latent_blocks[1]), n_dp, n_t)
+    wk = place(key_value_weight[:, 0], kv_pieces[:1], kv_offsets[:1], [(0, 0)], unit, False, at, n_dp, n_t)
+    wv = place(key_value_weight[:, 1], kv_pieces[1:], kv_offsets[1:], [(0, 0)], unit, False, at, n_dp, n_t)
+    wq = place(query_weight, q_pieces, q_offsets, [(0, 0), (unit // 2, 0)], unit, False, at, n_dp, n_t)
+    wo = place(output_weight, o_pieces, o_offsets, [(0, 0), (0, width // 2)], out_unit, True, at, n_dp, n_t)
+    cot_all = jnp.concatenate(gather_blocks(after(cotangent, near), n_t), axis=0)
 
     count_part = jnp.full((8, 128), jnp.sum(valid).astype(F32))
     count_total = all_sum(count_part, [("dp", n_dp)])[0, 0]
@@ -410,9 +509,9 @@
     latent_hat, latent_root = norm_parts(latent_all)
     latent_normed = (latent_hat * latent_gain + latent_shift).astype(BF)
     key_input = jnp.concatenate([media_normed, latent_normed[:own_rows]], axis=0)
-    queries = dot("hd,rd->hr", wq, latent_normed).astype(BF)
-    keys = dot("hd,rd->hr", wk, key_input).astype(BF)
-    values = dot("hd,rd->hr", wv, key_input).astype(BF)
+    queries = dot("dh,rd->hr", wq, latent_normed).astype(BF)
+    keys = dot("dh,rd->hr", wk, key_input).astype(BF)
+    values = dot("dh,rd->hr", wv, key_input).astype(BF)
     sent = attend_forward(queries, keys, values, key_image, row_image, n_t)
     got = [sent[0]] + [rotate(sent[k], n_t, -k) for k in range(1, n_t)]
     attended, stat = combine(got, heads)
@@ -432,39 +531,56 @@
     back_activation = dot("rd,fd->rf", cot_all, down_weight)
     back_hidden = (back_activation * slope).astype(BF)
     back_terms = dot("rf,df->rd", back_hidden, up_weight).astype(BF)
-    back_feed = scatter_blocks(
-        [back_terms[k * own_rows : (k + 1) * own_rows] for k in range(n_t)], n_t
-    )
+    back_blocks = [back_terms[k * own_rows : (k + 1) * own_rows] for k in range(n_t)]
+    down_keep, down_send = gradient(cot_all.T, activation, True, at, n_dp)
+    up_keep, up_send = gradient(feed_all.T, back_hidden, True, at, n_dp)
+    down_got = swap(down_send, "dp", n_dp, 0)
+    up_got = swap(up_send, "dp", n_dp, 0)
+    back_feed = after(scatter_blocks(back_blocks, n_t), down_got, up_got)
+    orders = bit_orders(n_dp)
     feed_terms = dot("rf,fd->rd", activation, down_weight).astype(BF)
-    result = middle + scatter_blocks(
-        [feed_terms[k * own_rows : (k + 1) * own_rows] for k in range(n_t)], n_t
-    )
-    grad_down = dot("rd,rf->df", cot_all, activation).astype(BF)
-    grad_up = dot("rd,rf->df", feed_all, back_hidden).astype(BF)
-    down_share, up_share = reduce_pair(
-        grad_down.reshape(n_dp, width // n_dp, -1), grad_up.reshape(n_dp, width // n_dp, -1), n_dp
-    )
 
     back_middle = cotangent.astype(F32) + norm_backward(back_feed, feed_hat, feed_root, feed_gain)
     back_branch = back_middle.astype(BF)
     back_attended = dot("hd,rd->hr", wo, back_branch).astype(BF)
     own_coef = own_valid / count_total
     message = make_message(back_attended, attended, stat, own_coef, heads)
+    down_keep, down_got = reduce_step(down_keep, down_got, orders[0], 0, n_dp)
+    up_keep, up_got = reduce_step(up_keep, up_got, orders[1], 0, n_dp)
     messages = gather_blocks(message, n_t)
+    feed_terms = after(feed_terms, messages[1])
+    messages = [after(m, down_got, up_got) if k else m for k, m in enumerate(messages)]
+    result = middle + scatter_blocks(
+        [feed_terms[k * own_rows : (k + 1) * own_rows] for k in range(n_t)], n_t
+    )
     back_q, back_k, back_v = attend_backward(
         queries, keys, values, key_image, row_image, row_valid / count_total, messages
     )
-
-    def shares(a, b):
-        return dot("rd,hr->dh", a, b).astype(BF).reshape(n_dp, width // n_dp, inner)
-
-    key_share, value_share = reduce_pair(shares(key_input, back_k), shares(key_input, back_v), n_dp)
-    query_share, output_share = reduce_pair(
-        shares(latent_normed, back_q), shares(back_branch, attended), n_dp
-    )
-    back_inputs = dot("hr,hd->rd", back_k, wk) + dot("hr,hd->rd", back_v, wv)
+    for i in range(1, len(orders[0])):
+        down_keep, down_got = reduce_step(down_keep, down_got, orders[0], i, n_dp)
+        up_keep, up_got = reduce_step(up_keep, up_got, orders[1], i, n_dp)
+    down_share = down_keep[0].astype(F32) + down_got[0].astype(F32)
+    up_share = up_keep[0].astype(F32) + up_got[0].astype(F32)
+
+    def halves(keep, send):
+        got = swap(send, "dp", n_dp, 0)
+        cut = inner // 2
+        one = reduce_outer(keep[..., :cut], got[..., :cut], orders[0], n_dp)
+        two = reduce_outer(keep[..., cut:], got[..., cut:], orders[1], n_dp)
+        return tuple(jnp.concatenate([x, y], axis=1) for x, y in zip(one, two))
+
+    out_terms = halves(*gradient(back_branch.T, attended, False, at, n_dp))
+    back_q, back_k, back_v = lax.optimization_barrier(
+        (back_q, back_k, back_v, down_got, up_got)
+    )[:3]
+    v_keep, v_send = gradient(key_input.T, back_v, False, at, n_dp)
+    k_keep, k_send = gradient(key_input.T, back_k, False, at, n_dp)
+    value_terms = reduce_outer(v_keep, swap(v_send, "dp", n_dp, 0), orders[0], n_dp)
+    key_terms = reduce_outer(k_keep, swap(k_send, "dp", n_dp, 0), orders[1], n_dp)
+    query_terms = halves(*gradient(latent_normed.T, back_q, False, at, n_dp))
+    back_inputs = dot("hr,dh->rd", back_k, wk) + dot("hr,dh->rd", back_v, wv)
     back_media = back_inputs[:own_patches]
-    latent_terms = dot("hr,hd->rd", back_q, wq)
+    latent_terms = dot("hr,dh->rd", back_q, wq)
     latent_terms = jnp.concatenate(
         [latent_terms[:own_rows] + back_inputs[own_patches:], latent_terms[own_rows:]], axis=0
     )
@@ -477,13 +593,9 @@
         back_latent, latent_hat[:own_rows], latent_root[:own_rows], latent_gain
     )
 
-    part = inner // n_t
-    four = jnp.stack([query_share, key_share, value_share, output_share]).astype(BF)
-    four = four.reshape(4, width // n_dp, n_t, part).transpose(2, 0, 1, 3)
-    blocks = [
-        lax.dynamic_index_in_dim(four, (z - k + n_t) % n_t, 0, keepdims=False) for k in range(n_t)
-    ]
-    four = scatter_blocks(blocks, n_t)
+    grad_o = scatter_blocks(tensor_blocks([out_terms], at, n_t), n_t)[0]
+    grad_kv = scatter_blocks(tensor_blocks([key_terms, value_terms], at, n_t), n_t)
+    grad_q = scatter_blocks(tensor_blocks([query_terms], at, n_t), n_t)[0]
 
     sums = (
         gain_shift(back_media, media_hat)
@@ -508,9 +620,9 @@
         mine[3],
         mine[4],
         mine[5],
-        four[0],
-        jnp.stack([four[1], four[2]], axis=1),
-        four[3].T,
+        grad_q,
+        jnp.moveaxis(grad_kv, 0, 1),
+        grad_o.T,
         up_share,
         down_share.T,
     )

time: 1270 us -> 669 us (0.53)
  Pallas kernels: 625 us -> 98.2 us
  other arithmetic: 89.2 us -> 61.8 us
  starting transfers between devices: 148 us -> 135 us
  matrix products: 75.1 us -> 62.2 us
    pallas_call x4 -> x13, Pallas kernels: 579 us -> 53.1 us  [the longest x6 33.8 us: gradient(): pl.pallas_call(partial(gradient_kernel, natural), grid_spec=pltpu.Prefetc...]
    ppermute x33 -> x28, starting transfers between devices: 116 us -> 53.3 us  [rotate(): lax.ppermute(x, 'tensor', [(i, (i + shift) % count) for i in range(count)])]
    ppermute x0 -> x21, waiting for transfers between devices: none -> 49.1 us  [the longest x7 32.9 us: gather_blocks(): ends = lax.ppermute(two, 'tensor', [(2, 3), (1, 0)])]
    ppermute x35 -> x48, waiting for transfers between devices: 128 us -> 86.9 us  [swap(): return lax.ppermute(x, axis, [(i, i ^ 1 << bit) for i in range(count)])]
    ppermute x0 -> x21, starting transfers between devices: none -> 38.3 us  [the longest x7 19.6 us: gather_blocks(): up = lax.ppermute(x, 'tensor', [(0, 1), (1, 2), (2, 3)])]
    ppermute x33 -> x28, waiting for transfers between devices: 126 us -> 107 us  [rotate(): lax.ppermute(x, 'tensor', [(i, (i + shift) % count) for i in range(count)])]
    another operation x9 -> x1, other arithmetic: 16.4 us -> 0.68 us  [local(): jnp.stack([out_share[:, :width // 2], out_share[:, width // 2:]])]
    squeeze x5 -> x1, other arithmetic: 14.6 us -> 1.7 us  [local(): grad_q = scatter_blocks(tensor_blocks([query_terms], at, n_t), n_t)[0]]
  transfers between devices with their start and end apart: 68 -> 97, of which waited for: 27 -> 37; matrix products, arithmetic and copies ran while one was open for 15% -> 24% of each run, Pallas kernels for 50% -> 14%
where the time goes in v2:
time: 669 us; the launch traced here: 658 us
  waiting for transfers between devices  243 us (36%)
  starting transfers between devices  135 us (20%)
  Pallas kernels  98.2 us (15%)
  matrix products  62.2 us (9%)
  other arithmetic  61.8 us (9%)
  local copies, waits for them, and re-layouts  52 us (8%)
    ppermute x28, waiting for transfers between devices, rotate(): lax.ppermute(x, 'tensor', [(i, (i + shift) % count) for i in range(count)])  107 us
    ppermute x48, waiting for transfers between devices, swap(): return lax.ppermute(x, axis, [(i, i ^ 1 << bit) for i in range(count)])  86.9 us
    dot_general x12, matrix products, dot(): return jnp.einsum(equation, a, b, preferred_element_type=F32)  62.2 us
    ppermute x28, starting transfers between devices, rotate(): lax.ppermute(x, 'tensor', [(i, (i + shift) % count) for i in range(count)])  53.3 us
    ppermute x48, starting transfers between devices, swap(): return lax.ppermute(x, axis, [(i, i ^ 1 << bit) for i in range(count)])  43.4 us
    pallas_call x6, Pallas kernels, gradient(): pl.pallas_call(partial(gradient_kernel, natural), grid_spec=pltpu.Prefetc...  33.8 us
    ppermute x7, waiting for transfers between devices, gather_blocks(): ends = lax.ppermute(two, 'tensor', [(2, 3), (1, 0)])  32.9 us
    pallas_call x1, Pallas kernels, attend_backward(): pl.pallas_call(partial(backward_kernel, heads, n_t), grid=(heads,), out_s...  24.6 us
  transfers between devices with their start and end apart: 97, of which 37 were waited for; matrix products, arithmetic and copies ran while one was open for 24% of the time, Pallas kernels for 14%

profile of v2, /device:TPU:0, one launch (start us, length us, event | category | flops | bytes accessed | tf_op | source)
XLA Modules:
  0.0 658.1 jit_solution(14713230596043798328)
XLA Ops:
  2.6 4.0 collective-permute-start
  7.9 5.3 collective-permute-start.2
  15.2 7.9 %fusion.85 = (bf16[1536,1,384]{2,1,0:T(2,128)(2,1)}, bf16[1536,1,384]{2,1,0:T(2,128)(2,1)}) fusion(bf16[1536,2,384]{2,1,0:T(2,128)(2,1)} %param.27), kind=kLoop, calls=%fused_computation.274 | loop fusion | bytes 4718592 | tf_op jit(solution)/shard_map/slice | solution.py:479
  38.1 7.6 %collective-permute-done.1 = bf16[2,192,384]{2,1,0:T(8,128)(2,1)S(1)} collective-permute-done((bf16[2,192,384]{2,1,0:T(8,128)(2,1)}, bf16[2,192,384]{2,1,0:T(8,128)(2,1)S(1)}, u32[]{:S(2)}, u32[]{:S(2)}) %collective-permute-start.1) | collective-permute-done | bytes 294944 | tf_op jit(solution)/shard_map/ppermute | solution.py:35
  45.8 2.8 collective-permute-start.5
  51.7 3.8 collective-permute-done.3
  58.5 4.5 collective-permute-done.4
  76.9 5.7 collective-permute-done.21
  83.9 3.7 collective-permute-done.13
  92.5 4.1 collective-permute-done.16
  96.5 7.7 %collective-permute-done.14 = bf16[128,1536]{0,1:T(8,128)(2,1)S(1)} collective-permute-done((bf16[128,1536]{0,1:T(8,128)(2,1)S(1)}, bf16[128,1536]{0,1:T(8,128)(2,1)S(1)}, u32[]{:S(2)}, u32[]{:S(2)}) %collective-permute-start.14) | collective-permute-done | bytes 393248 | tf_op jit(solution)/shard_map/ppermute | solution.py:35
  109.8 2.8 collective-permute-done.27
  116.0 5.2 collective-permute-done.30
  127.6 2.9 collective-permute-done.31
  135.2 3.1 shard_map.271
  138.3 5.0 convolution_convert_fusion.4.q_ref
  148.2 4.2 shard_map.272
  152.5 6.3 convolution_convert_fusion.1.k_ref
  158.7 4.7 shard_map.273
  163.4 7.7 %convolution_convert_fusion.v_ref = bf16[1536,640]{1,0:T(8,128)(2,1)} fusion(bf16[1536,1536]{1,0:T(8,128)(2,1)} %shard_map.273, bf16[128,1536]{0,1:T(8,128)(2,1)S(1)} %copy-done.47, bf16[512,1536]{0,1:T(8,128)(2,1)S(1)} %copy-done.30), kind=kOutput, calls=%fused_computation.9 | convolution fusion | flops 3024814080 | bytes 8650752 | tf_op jit(solution)/shard_map/dh,rd->hr/dot_general | solution.py:435
  171.2 20.1 %shard_map.274 = (bf16[1632,128]{1,0:T(8,128)(2,1)S(1)}, bf16[1632,128]{1,0:T(8,128)(2,1)}, bf16[1632,128]{1,0:T(8,128)(2,1)}, bf16[1632,128]{1,0:T(8,128)(2,1)}) custom-call(bf16[1536,512]{1,0:T(8,128)(2,1)S(1)} %convolution_convert_fusion.4.q_ref, bf16[1536,640]{1,0:T(8,128)(2,1)S(1)} %convolution_convert_fusion.1.k_ref, ...), custom_call_target="tpu_custom_call" | custom-call | tf_op jit(solution)/shard_map/pallas_call | solution.py:272
  196.0 2.9 collective-permute-start.41
  204.4 4.5 shard_map.276
  208.9 37.7 %collective-permute-done.41 = bf16[128,1536]{0,1:T(8,128)(2,1)} collective-permute-done((bf16[128,1536]{0,1:T(8,128)(2,1)}, bf16[128,1536]{0,1:T(8,128)(2,1)}, u32[]{:S(2)}, u32[]{:S(2)}) %collective-permute-start.41) | collective-permute-done | bytes 393248 | tf_op jit(solution)/shard_map/ppermute | solution.py:21
  249.6 4.3 fusion.98
  254.6 4.6 collective-permute-start.37
  263.1 14.1 %collective-permute-done.37 = bf16[128,1536]{0,1:T(8,128)(2,1)S(1)} collective-permute-done((bf16[128,1536]{0,1:T(8,128)(2,1)S(1)}, bf16[128,1536]{0,1:T(8,128)(2,1)S(1)}, u32[]{:S(2)}, u32[]{:S(2)}) %collective-permute-start.37) | collective-permute-done | bytes 393248 | tf_op jit(solution)/shard_map/ppermute | solution.py:21
  280.7 5.3 collective-permute-done.40
  286.0 6.6 collective-permute-done.38
  292.7 4.4 multiply_convert_fusion
  297.1 4.6 shard_map.277
  303.6 5.9 fusion.22.y_ref
  309.5 4.6 shard_map.278
  314.1 5.0 convolution_convert_fusion.2
  319.5 3.9 collective-permute-start.45
  323.4 7.3 %convolution_convert_fusion.3 = bf16[512,1536]{0,1:T(8,128)(2,1)} fusion(bf16[512,1536]{1,0:T(8,128)(2,1)S(1)} %get-tuple-element.262.y_ref, bf16[1536,1536]{1,0:T(8,128)(2,1)} %param.30), kind=kOutput, calls=%fused_computation.37 | convolution fusion | flops 2416705536 | bytes 7864320 | tf_op jit(solution)/shard_map/rf,fd->rd/dot_general | solution.py:435
  333.2 15.9 %collective-permute-done.46 = bf16[128,1536]{0,1:T(8,128)(2,1)S(1)} collective-permute-done((bf16[128,1536]{0,1:T(8,128)(2,1)S(1)}, bf16[128,1536]{0,1:T(8,128)(2,1)S(1)}, u32[]{:S(2)}, u32[]{:S(2)}) %collective-permute-start.46) | collective-permute-done | bytes 393248 | tf_op jit(solution)/shard_map/ppermute | solution.py:21
  353.2 7.6 %collective-permute-start.53 = (bf16[1632,128]{1,0:T(8,128)(2,1)S(1)}, bf16[1632,128]{1,0:T(8,128)(2,1)S(1)}, u32[]{:S(2)}, u32[]{:S(2)}) collective-permute-start(bf16[1632,128]{1,0:T(8,128)(2,1)S(1)} %shard_map.279.rest_0_.rest_4_), channel_id=1, source_target_pairs={{0,2},{1,3},{2,0},{3,1},{4,6},{5,7},{6,4},{7,5},{8,10},{9,11},{10,... | collective-permute-start | bytes 1253384 | tf_op jit(solution)/shard_map/ppermute | solution.py:21
  362.1 4.6 collective-permute-start.55
  366.7 3.5 fusion.27
  372.0 8.3 %collective-permute-done.53.rest_2_.rest_6_ = bf16[1632,128]{1,0:T(8,128)(2,1)S(1)} collective-permute-done((bf16[1632,128]{1,0:T(8,128)(2,1)S(1)}, bf16[1632,128]{1,0:T(8,128)(2,1)S(1)}, u32[]{:S(2)}, u32[]{:S(2)}) %collective-permute-start.53) | collective-permute-done | bytes 417824 | tf_op jit(solution)/shard_map/ppermute | solution.py:21
  384.1 3.6 shard_map.286
  387.7 4.3 collective-permute-done.54
  393.4 4.7 collective-permute-start.57
  401.7 10.8 %collective-permute-done.60 = bf16[2,192,1536]{2,1,0:T(8,128)(2,1)} collective-permute-done((bf16[2,192,1536]{2,1,0:T(8,128)(2,1)}, bf16[2,192,1536]{2,1,0:T(8,128)(2,1)}, u32[]{:S(2)}, u32[]{:S(2)}) %collective-permute-start.60) | collective-permute-done | bytes 1179680 | tf_op jit(solution)/shard_map/ppermute | solution.py:48
  419.1 24.6 %shard_map.280 = (bf16[1536,512]{1,0:T(8,128)(2,1)S(1)}, bf16[1536,640]{1,0:T(8,128)(2,1)}, bf16[1536,640]{1,0:T(8,128)(2,1)}) custom-call(bf16[1536,512]{1,0:T(8,128)(2,1)S(1)} %convolution_convert_fusion.4.q_ref, bf16[1536,640]{1,0:T(8,128)(2,1)} %copy-done, bf16[1536,640]{1,0:T(8,128)(2,1)} %convolution_convert_fusion.v_ref, s32[640,1]{1,0:T(8,128)S(1)} %copy-done.2, ...), custom_call_target="tpu_custom_call" | custom-call | tf_op jit(solution)/shard_map/pallas_call | solution.py:385
  446.1 6.4 fusion.99
  452.6 5.8 convolution_add_fusion
  461.0 2.7 fusion.100
  474.8 3.4 collective-permute-start.71
  479.4 3.1 collective-permute-start.69
  483.8 4.5 fusion.16
  493.9 6.2 shard_map.281
  504.4 7.4 %shard_map.284 = (bf16[4,192,1536]{2,1,0:T(8,128)(2,1)}, bf16[4,192,1536]{2,1,0:T(8,128)(2,1)}) custom-call(s32[2]{0:T(128)S(1)} %pad_add_fusion.1.at_ref, bf16[1536,640]{1,0:T(8,128)(2,1)S(1)} %fusion.50.even_ref.odd_ref, bf16[1536,640]{1,0:T(8,128)(2,1)S(1)} %fusion.50.even_ref.odd_ref, bf16[1536,640]{1,0:T(8,128)(2,1)S(1)} %copy-done.11), custom_call_target="tpu_custom_call" | custom-call | flops 3019898880 | bytes 8650752 | tf_op jit(solution)/shard_map/pallas_call | solution.py:75
  513.8 7.4 %shard_map.283 = (bf16[4,192,1536]{2,1,0:T(8,128)(2,1)}, bf16[4,192,1536]{2,1,0:T(8,128)(2,1)}) custom-call(s32[2]{0:T(128)S(1)} %pad_add_fusion.1.at_ref, bf16[1536,640]{1,0:T(8,128)(2,1)S(1)} %fusion.50.even_ref.odd_ref, bf16[1536,640]{1,0:T(8,128)(2,1)S(1)} %fusion.50.even_ref.odd_ref, bf16[1536,640]{1,0:T(8,128)(2,1)S(1)} %copy-done.10), custom_call_target="tpu_custom_call" | custom-call | flops 3019898880 | bytes 8650752 | tf_op jit(solution)/shard_map/pallas_call | solution.py:75
  521.2 3.5 copy.120
  534.9 10.5 %collective-permute-done.91 = bf16[2,192,768]{2,1,0:T(8,128)(2,1)S(1)} collective-permute-done((bf16[2,192,768]{2,1,0:T(8,128)(2,1)S(1)}, bf16[2,192,768]{2,1,0:T(8,128)(2,1)S(1)}, u32[]{:S(2)}, u32[]{:S(2)}) %collective-permute-start.91) | collective-permute-done | bytes 589856 | tf_op jit(solution)/shard_map/ppermute | solution.py:48
  548.3 5.9 collective-permute-done.93
  571.0 7.1 %collective-permute-done.74 = bf16[2,192,768]{2,1,0:T(8,128)(2,1)S(1)} collective-permute-done((bf16[2,192,768]{2,1,0:T(8,128)(2,1)S(1)}, bf16[2,192,768]{2,1,0:T(8,128)(2,1)S(1)}, u32[]{:S(2)}, u32[]{:S(2)}) %collective-permute-start.74) | collective-permute-done | bytes 589856 | tf_op jit(solution)/shard_map/ppermute | solution.py:48
  580.6 20.1 %collective-permute-done.81 = bf16[2,192,1536]{2,1,0:T(8,128)(2,1)S(1)} collective-permute-done((bf16[2,192,1536]{2,1,0:T(8,128)(2,1)S(1)}, bf16[2,192,1536]{2,1,0:T(8,128)(2,1)S(1)}, u32[]{:S(2)}, u32[]{:S(2)}) %collective-permute-start.81) | collective-permute-done | bytes 1179680 | tf_op jit(solution)/shard_map/ppermute | solution.py:48
  601.6 5.4 collective-permute-done.84
  609.9 3.5 collective-permute-done.76
  635.5 6.8 %collective-permute-done.78 = bf16[1,192,384]{2,1,0:T(8,128)(2,1)S(1)} collective-permute-done((bf16[1,192,384]{2,1,0:T(8,128)(2,1)}, bf16[1,192,384]{2,1,0:T(8,128)(2,1)S(1)}, u32[]{:S(2)}, u32[]{:S(2)}) %collective-permute-start.78) | collective-permute-done | bytes 147488 | tf_op jit(solution)/shard_map/ppermute | solution.py:21
  644.0 11.4 %collective-permute-done.87 = bf16[2,192,384]{2,1,0:T(8,128)(2,1)S(1)} collective-permute-done((bf16[2,192,384]{2,1,0:T(8,128)(2,1)S(1)}, bf16[2,192,384]{2,1,0:T(8,128)(2,1)S(1)}, u32[]{:S(2)}, u32[]{:S(2)}) %collective-permute-start.87) | collective-permute-done | bytes 294944 | tf_op jit(solution)/shard_map/ppermute | solution.py:21
  (476 shorter events, 208.4 us)
Async XLA Ops:
  2.6 31.6 %collective-permute-start = (bf16[2,192,384]{2,1,0:T(8,128)(2,1)}, bf16[2,192,384]{2,1,0:T(8,128)(2,1)}, u32[]{:S(2)}, u32[]{:S(2)}) collective-permute-start(bf16[2,192,384]{2,1,0:T(8,128)(2,1)} %bitcast.316), channel_id=1, source_target_pairs={{0,2},{1,3},{2,0},{3,1},{4,6},{5,7},{6,4},{7,5},{8,10},{9,11},{10,... | collective-permute-start | bytes 884744 | tf_op jit(solution)/shard_map/ppermute | solution.py:21
  6.6 31.5 %collective-permute-start.17 = (bf16[2,192,384]{2,1,0:T(8,128)(2,1)}, bf16[2,192,384]{2,1,0:T(8,128)(2,1)S(1)}, u32[]{:S(2)}, u32[]{:S(2)}) collective-permute-start(bf16[2,192,384]{2,1,0:T(8,128)(2,1)} %bitcast.316), channel_id=1, source_target_pairs={{1,0},{2,1},{3,2},{5,4},{6,5},{7,6},{9,8},{10,9},{11,10},{13,12},{... | collective-permute-start | bytes 884744 | tf_op jit(solution)/shard_map/ppermute | solution.py:34
  7.9 30.2 %collective-permute-start.2 = (bf16[2,192,384]{2,1,0:T(8,128)(2,1)}, bf16[2,192,384]{2,1,0:T(8,128)(2,1)}, u32[]{:S(2)}, u32[]{:S(2)}) collective-permute-start(bf16[2,192,384]{2,1,0:T(8,128)(2,1)} %bitcast.316), channel_id=1, source_target_pairs={{0,1},{1,2},{2,3},{4,5},{5,6},{6,7},{8,9},{9,10},{10,11},{12,13},{... | collective-permute-start | bytes 884744 | tf_op jit(solution)/shard_map/ppermute | solution.py:33
  15.1 20.4 %collective-permute-start.50 = (f32[8,128]{1,0:T(8,128)S(1)}, f32[8,128]{1,0:T(8,128)S(1)}, u32[]{:S(2)}, u32[]{:S(2)}) collective-permute-start(f32[8,128]{1,0:T(8,128)S(1)} %broadcast_in_dim.114), channel_id=1, source_target_pairs={{0,4},{4,0},{8,12},{12,8},{16,20},{20,16},{24,28},{28,24},{1,5},{5... | collective-permute-start | bytes 12296 | tf_op jit(solution)/shard_map/ppermute | solution.py:48
  35.5 39.2 %collective-permute-start.51 = (f32[8,128]{1,0:T(8,128)S(1)}, f32[8,128]{1,0:T(8,128)S(1)}, u32[]{:S(2)}, u32[]{:S(2)}) collective-permute-start(f32[8,128]{1,0:T(8,128)S(1)} %broadcast_add_fusion), channel_id=1, source_target_pairs={{0,8},{4,12},{8,0},{12,4},{16,24},{20,28},{24,16},{28,20},{1,9},{5... | collective-permute-start | bytes 12296 | tf_op jit(solution)/shard_map/ppermute | solution.py:48
  50.1 25.2 %collective-permute-start.18 = (bf16[1,3,192,384]{3,2,1,0:T(8,128)(2,1)S(1)}, bf16[1,3,192,384]{3,2,1,0:T(8,128)(2,1)S(1)}, u32[]{:S(2)}, u32[]{:S(2)}) collective-permute-start(bf16[1,3,192,384]{3,2,1,0:T(8,128)(2,1)S(1)} %maximum_bitcast_fusion), channel_id=1, source_target_pairs={{0,8},{4,12},{8,0},{12,4},{16,24},{20,28},{24,16},{28,20},{1,9},{5... | collective-permute-start | bytes 1327112 | tf_op jit(solution)/shard_map/ppermute | solution.py:48
  66.3 16.3 %collective-permute-start.21 = (bf16[1,3,192,384]{3,2,1,0:T(8,128)(2,1)S(1)}, bf16[1,3,192,384]{3,2,1,0:T(8,128)(2,1)S(1)}, u32[]{:S(2)}, u32[]{:S(2)}) collective-permute-start(bf16[1,3,192,384]{3,2,1,0:T(8,128)(2,1)S(1)} %maximum_bitcast_fusion.1), channel_id=1, source_target_pairs={{0,16},{4,20},{8,24},{12,28},{16,0},{20,4},{24,8},{28,12},{1,17},{... | collective-permute-start | bytes 1327112 | tf_op jit(solution)/shard_map/ppermute | solution.py:48
  69.4 18.1 %collective-permute-start.13 = (bf16[128,1536]{0,1:T(8,128)(2,1)S(1)}, bf16[128,1536]{0,1:T(8,128)(2,1)S(1)}, u32[]{:S(2)}, u32[]{:S(2)}) collective-permute-start(bf16[128,1536]{0,1:T(8,128)(2,1)S(1)} %bitcast.327), channel_id=1, source_target_pairs={{0,2},{1,3},{2,0},{3,1},{4,6},{5,7},{6,4},{7,5},{8,10},{9,11},{10,... | collective-permute-start | bytes 1179656 | tf_op jit(solution)/shard_map/ppermute | solution.py:21
  73.1 16.6 %collective-permute-start.8 = (bf16[2,3,96,384]{3,2,1,0:T(8,128)(2,1)S(1)}, bf16[2,3,96,384]{3,2,1,0:T(8,128)(2,1)S(1)}, u32[]{:S(2)}, u32[]{:S(2)}) collective-permute-start(bf16[2,3,96,384]{3,2,1,0:T(8,128)(2,1)S(1)} %pad_maximum_fusion.19), channel_id=1, source_target_pairs={{0,16},{4,20},{8,24},{12,28},{16,0},{20,4},{24,8},{28,12},{1,17},{... | collective-permute-start | bytes 1327112 | tf_op jit(solution)/shard_map/ppermute | solution.py:48
  74.7 16.7 %collective-permute-start.11 = (bf16[2,3,96,384]{3,2,1,0:T(8,128)(2,1)S(1)}, bf16[2,3,96,384]{3,2,1,0:T(8,128)(2,1)S(1)}, u32[]{:S(2)}, u32[]{:S(2)}) collective-permute-start(bf16[2,3,96,384]{3,2,1,0:T(8,128)(2,1)S(1)} %pad_maximum_fusion.20), channel_id=1, source_target_pairs={{0,8},{4,12},{8,0},{12,4},{16,24},{20,28},{24,16},{28,20},{1,9},{5... | collective-permute-start | bytes 1327112 | tf_op jit(solution)/shard_map/ppermute | solution.py:48
  75.3 17.1 %collective-permute-start.15 = (bf16[128,1536]{0,1:T(8,128)(2,1)S(1)}, bf16[128,1536]{0,1:T(8,128)(2,1)S(1)}, u32[]{:S(2)}, u32[]{:S(2)}) collective-permute-start(bf16[128,1536]{0,1:T(8,128)(2,1)S(1)} %bitcast.328), channel_id=1, source_target_pairs={{0,1},{1,2},{2,3},{4,5},{5,6},{6,7},{8,9},{9,10},{10,11},{12,13},{... | collective-permute-start | bytes 1179656 | tf_op jit(solution)/shard_map/ppermute | solution.py:33
  87.6 16.7 %collective-permute-start.14 = (bf16[128,1536]{0,1:T(8,128)(2,1)S(1)}, bf16[128,1536]{0,1:T(8,128)(2,1)S(1)}, u32[]{:S(2)}, u32[]{:S(2)}) collective-permute-start(bf16[128,1536]{0,1:T(8,128)(2,1)S(1)} %collective-permute-done.13), channel_id=1, source_target_pairs={{2,3},{1,0},{6,7},{5,4},{10,11},{9,8},{14,15},{13,12},{18,19},{17,... | collective-permute-start | bytes 1179656 | tf_op jit(solution)/shard_map/ppermute | solution.py:35
  89.7 24.2 %collective-permute-start.19 = (bf16[2,3,192,384]{3,2,1,0:T(8,128)(2,1)S(1)}, bf16[2,3,192,384]{3,2,1,0:T(8,128)(2,1)S(1)}, u32[]{:S(2)}, u32[]{:S(2)}) collective-permute-start(bf16[2,3,192,384]{3,2,1,0:T(8,128)(2,1)S(1)} %pad_maximum_fusion.9), channel_id=1, source_target_pairs={{0,16},{4,20},{8,24},{12,28},{16,0},{20,4},{24,8},{28,12},{1,17},{... | collective-permute-start | bytes 2654216 | tf_op jit(solution)/shard_map/ppermute | solution.py:48
  91.4 34.4 %collective-permute-start.22 = (bf16[2,3,192,384]{3,2,1,0:T(8,128)(2,1)S(1)}, bf16[2,3,192,384]{3,2,1,0:T(8,128)(2,1)S(1)}, u32[]{:S(2)}, u32[]{:S(2)}) collective-permute-start(bf16[2,3,192,384]{3,2,1,0:T(8,128)(2,1)S(1)} %pad_maximum_fusion.10), channel_id=1, source_target_pairs={{0,8},{4,12},{8,0},{12,4},{16,24},{20,28},{24,16},{28,20},{1,9},{5... | collective-permute-start | bytes 2654216 | tf_op jit(solution)/shard_map/ppermute | solution.py:48
  92.4 40.5 %collective-permute-start.9 = (bf16[4,3,96,384]{3,2,1,0:T(8,128)(2,1)S(1)}, bf16[4,3,96,384]{3,2,1,0:T(8,128)(2,1)S(1)}, u32[]{:S(2)}, u32[]{:S(2)}) collective-permute-start(bf16[4,3,96,384]{3,2,1,0:T(8,128)(2,1)S(1)} %pad_maximum_fusion.7.refs_0_), channel_id=1, source_target_pairs={{0,4},{4,0},{8,12},{12,8},{16,20},{20,16},{24,28},{28,24},{1,5},{5... | collective-permute-start | bytes 2654216 | tf_op jit(solution)/shard_map/ppermute | solution.py:48
  116.0 17.8 %collective-permute-start.12 = (bf16[4,3,96,384]{3,2,1,0:T(8,128)(2,1)S(1)}, bf16[4,3,96,384]{3,2,1,0:T(8,128)(2,1)S(1)}, u32[]{:S(2)}, u32[]{:S(2)}) collective-permute-start(bf16[4,3,96,384]{3,2,1,0:T(8,128)(2,1)S(1)} %pad_maximum_fusion.8.refs_2_), channel_id=1, source_target_pairs={{0,4},{4,0},{8,12},{12,8},{16,20},{20,16},{24,28},{28,24},{1,5},{5... | collective-permute-start | bytes 2654216 | tf_op jit(solution)/shard_map/ppermute | solution.py:48
  121.2 27.0 %collective-permute-start.20 = (bf16[4,3,192,384]{3,2,1,0:T(8,128)(2,1)S(1)}, bf16[4,3,192,384]{3,2,1,0:T(8,128)(2,1)}, u32[]{:S(2)}, u32[]{:S(2)}) collective-permute-start(bf16[4,3,192,384]{3,2,1,0:T(8,128)(2,1)S(1)} %pad_maximum_fusion.2.refs_0_), channel_id=1, source_target_pairs={{0,4},{4,0},{8,12},{12,8},{16,20},{20,16},{24,28},{28,24},{1,5},{5... | collective-permute-start | bytes 5308424 | tf_op jit(solution)/shard_map/ppermute | solution.py:48
  130.5 62.5 %collective-permute-start.52 = (f32[8,128]{1,0:T(8,128)S(1)}, f32[8,128]{1,0:T(8,128)S(1)}, u32[]{:S(2)}, u32[]{:S(2)}) collective-permute-start(f32[8,128]{1,0:T(8,128)S(1)} %fusion.120), channel_id=1, source_target_pairs={{0,16},{4,20},{8,24},{12,28},{16,0},{20,4},{24,8},{28,12},{1,17},{... | collective-permute-start | bytes 12296 | tf_op jit(solution)/shard_map/ppermute | solution.py:48
  132.8 25.9 %collective-permute-start.23 = (bf16[4,3,192,384]{3,2,1,0:T(8,128)(2,1)S(1)}, bf16[4,3,192,384]{3,2,1,0:T(8,128)(2,1)}, u32[]{:S(2)}, u32[]{:S(2)}) collective-permute-start(bf16[4,3,192,384]{3,2,1,0:T(8,128)(2,1)S(1)} %pad_maximum_fusion.3.refs_0_), channel_id=1, source_target_pairs={{0,4},{4,0},{8,12},{12,8},{16,20},{20,16},{24,28},{28,24},{1,5},{5... | collective-permute-start | bytes 5308424 | tf_op jit(solution)/shard_map/ppermute | solution.py:48
  146.7 49.3 %collective-permute-start.33 = (bf16[4,3,48,768]{3,2,1,0:T(8,128)(2,1)}, bf16[4,3,48,768]{3,2,1,0:T(8,128)(2,1)}, u32[]{:S(2)}, u32[]{:S(2)}) collective-permute-start(bf16[4,3,48,768]{3,2,1,0:T(8,128)(2,1)} %pad_maximum_fusion.11.refs_0_), channel_id=1, source_target_pairs={{0,4},{4,0},{8,12},{12,8},{16,20},{20,16},{24,28},{28,24},{1,5},{5... | collective-permute-start | bytes 2654216 | tf_op jit(solution)/shard_map/ppermute | solution.py:48
  147.7 53.0 %collective-permute-start.36 = (bf16[4,3,48,768]{3,2,1,0:T(8,128)(2,1)}, bf16[4,3,48,768]{3,2,1,0:T(8,128)(2,1)}, u32[]{:S(2)}, u32[]{:S(2)}) collective-permute-start(bf16[4,3,48,768]{3,2,1,0:T(8,128)(2,1)} %pad_maximum_fusion.12.refs_2_), channel_id=1, source_target_pairs={{0,4},{4,0},{8,12},{12,8},{16,20},{20,16},{24,28},{28,24},{1,5},{5... | collective-permute-start | bytes 2654216 | tf_op jit(solution)/shard_map/ppermute | solution.py:48
  192.0 55.9 %collective-permute-start.24 = (bf16[1632,128]{1,0:T(8,128)(2,1)}, bf16[1632,128]{1,0:T(8,128)(2,1)S(1)}, u32[]{:S(2)}, u32[]{:S(2)}) collective-permute-start(bf16[1632,128]{1,0:T(8,128)(2,1)} %get-tuple-element.63), channel_id=1, source_target_pairs={{0,3},{1,0},{2,1},{3,2},{4,7},{5,4},{6,5},{7,6},{8,11},{9,8},{10,9... | collective-permute-start | bytes 1253384 | tf_op jit(solution)/shard_map/ppermute | solution.py:21
  192.0 57.2 %collective-permute-start.25 = (bf16[1632,128]{1,0:T(8,128)(2,1)}, bf16[1632,128]{1,0:T(8,128)(2,1)S(1)}, u32[]{:S(2)}, u32[]{:S(2)}) collective-permute-start(bf16[1632,128]{1,0:T(8,128)(2,1)} %get-tuple-element.64), channel_id=1, source_target_pairs={{0,2},{1,3},{2,0},{3,1},{4,6},{5,7},{6,4},{7,5},{8,10},{9,11},{10,... | collective-permute-start | bytes 1253384 | tf_op jit(solution)/shard_map/ppermute | solution.py:21
  193.0 56.2 %collective-permute-start.26 = (bf16[1632,128]{1,0:T(8,128)(2,1)}, bf16[1632,128]{1,0:T(8,128)(2,1)S(1)}, u32[]{:S(2)}, u32[]{:S(2)}) collective-permute-start(bf16[1632,128]{1,0:T(8,128)(2,1)} %get-tuple-element.65), channel_id=1, source_target_pairs={{0,1},{1,2},{2,3},{3,0},{4,5},{5,6},{6,7},{7,4},{8,9},{9,10},{10,1... | collective-permute-start | bytes 1253384 | tf_op jit(solution)/shard_map/ppermute | solution.py:21
  196.0 50.6 %collective-permute-start.41 = (bf16[128,1536]{0,1:T(8,128)(2,1)}, bf16[128,1536]{0,1:T(8,128)(2,1)}, u32[]{:S(2)}, u32[]{:S(2)}) collective-permute-start(bf16[128,1536]{0,1:T(8,128)(2,1)} %bitcast.19), channel_id=1, source_target_pairs={{0,2},{1,3},{2,0},{3,1},{4,6},{5,7},{6,4},{7,5},{8,10},{9,11},{10,... | collective-permute-start | bytes 1179656 | tf_op jit(solution)/shard_map/ppermute | solution.py:21
  200.8 61.0 %collective-permute-start.43 = (bf16[128,1536]{0,1:T(8,128)(2,1)}, bf16[128,1536]{0,1:T(8,128)(2,1)S(1)}, u32[]{:S(2)}, u32[]{:S(2)}) collective-permute-start(bf16[128,1536]{0,1:T(8,128)(2,1)} %bitcast.19), channel_id=1, source_target_pairs={{0,1},{1,2},{2,3},{4,5},{5,6},{6,7},{8,9},{9,10},{10,11},{12,13},{... | collective-permute-start | bytes 1179656 | tf_op jit(solution)/shard_map/ppermute | solution.py:33
  246.6 32.1 %collective-permute-start.44 = (bf16[128,1536]{0,1:T(8,128)(2,1)}, bf16[128,1536]{0,1:T(8,128)(2,1)S(1)}, u32[]{:S(2)}, u32[]{:S(2)}) collective-permute-start(bf16[128,1536]{0,1:T(8,128)(2,1)} %bitcast.19), channel_id=1, source_target_pairs={{1,0},{2,1},{3,2},{5,4},{6,5},{7,6},{9,8},{10,9},{11,10},{13,12},{... | collective-permute-start | bytes 1179656 | tf_op jit(solution)/shard_map/ppermute | solution.py:34
  247.9 30.8 %collective-permute-start.42 = (bf16[128,1536]{0,1:T(8,128)(2,1)}, bf16[128,1536]{0,1:T(8,128)(2,1)S(1)}, u32[]{:S(2)}, u32[]{:S(2)}) collective-permute-start(bf16[128,1536]{0,1:T(8,128)(2,1)} %collective-permute-done.41), channel_id=1, source_target_pairs={{2,3},{1,0},{6,7},{5,4},{10,11},{9,8},{14,15},{13,12},{18,19},{17,... | collective-permute-start | bytes 1179656 | tf_op jit(solution)/shard_map/ppermute | solution.py:35
  254.6 22.6 %collective-permute-start.37 = (bf16[128,1536]{0,1:T(8,128)(2,1)S(1)}, bf16[128,1536]{0,1:T(8,128)(2,1)S(1)}, u32[]{:S(2)}, u32[]{:S(2)}) collective-permute-start(bf16[128,1536]{0,1:T(8,128)(2,1)S(1)} %add_convert_fusion.26), channel_id=1, source_target_pairs={{0,2},{1,3},{2,0},{3,1},{4,6},{5,7},{6,4},{7,5},{8,10},{9,11},{10,... | collective-permute-start | bytes 1179656 | tf_op jit(solution)/shard_map/ppermute | solution.py:21
  260.1 20.6 %collective-permute-start.39 = (bf16[128,1536]{0,1:T(8,128)(2,1)S(1)}, bf16[128,1536]{0,1:T(8,128)(2,1)S(1)}, u32[]{:S(2)}, u32[]{:S(2)}) collective-permute-start(bf16[128,1536]{0,1:T(8,128)(2,1)S(1)} %add_convert_fusion.26), channel_id=1, source_target_pairs={{0,1},{1,2},{2,3},{4,5},{5,6},{6,7},{8,9},{9,10},{10,11},{12,13},{... | collective-permute-start | bytes 1179656 | tf_op jit(solution)/shard_map/ppermute | solution.py:33
  261.8 24.2 %collective-permute-start.40 = (bf16[128,1536]{0,1:T(8,128)(2,1)S(1)}, bf16[128,1536]{0,1:T(8,128)(2,1)S(1)}, u32[]{:S(2)}, u32[]{:S(2)}) collective-permute-start(bf16[128,1536]{0,1:T(8,128)(2,1)S(1)} %add_convert_fusion.26), channel_id=1, source_target_pairs={{1,0},{2,1},{3,2},{5,4},{6,5},{7,6},{9,8},{10,9},{11,10},{13,12},{... | collective-permute-start | bytes 1179656 | tf_op jit(solution)/shard_map/ppermute | solution.py:34
  301.7 47.6 %collective-permute-start.48 = (bf16[4,192,1536]{2,1,0:T(8,128)(2,1)}, bf16[4,192,1536]{2,1,0:T(8,128)(2,1)}, u32[]{:S(2)}, u32[]{:S(2)}) collective-permute-start(bf16[4,192,1536]{2,1,0:T(8,128)(2,1)} %get-tuple-element.69), channel_id=1, source_target_pairs={{0,4},{4,0},{8,12},{12,8},{16,20},{20,16},{24,28},{28,24},{1,5},{5... | collective-permute-start | bytes 7077896 | tf_op jit(solution)/shard_map/ppermute | solution.py:48
  314.1 35.3 %collective-permute-start.49 = (bf16[4,192,1536]{2,1,0:T(8,128)(2,1)}, bf16[4,192,1536]{2,1,0:T(8,128)(2,1)S(1)}, u32[]{:S(2)}, u32[]{:S(2)}) collective-permute-start(bf16[4,192,1536]{2,1,0:T(8,128)(2,1)} %get-tuple-element.70), channel_id=1, source_target_pairs={{0,4},{4,0},{8,12},{12,8},{16,20},{20,16},{24,28},{28,24},{1,5},{5... | collective-permute-start | bytes 7077896 | tf_op jit(solution)/shard_map/ppermute | solution.py:48
  319.4 29.8 %collective-permute-start.46 = (bf16[128,1536]{0,1:T(8,128)(2,1)S(1)}, bf16[128,1536]{0,1:T(8,128)(2,1)S(1)}, u32[]{:S(2)}, u32[]{:S(2)}) collective-permute-start(bf16[128,1536]{0,1:T(8,128)(2,1)S(1)} %get-tuple-element.209), channel_id=1, source_target_pairs={{0,2},{1,3},{2,0},{3,1},{4,6},{5,7},{6,4},{7,5},{8,10},{9,11},{10,... | collective-permute-start | bytes 1179656 | tf_op jit(solution)/shard_map/ppermute | solution.py:21
  319.5 29.7 %collective-permute-start.45 = (bf16[128,1536]{0,1:T(8,128)(2,1)S(1)}, bf16[128,1536]{0,1:T(8,128)(2,1)S(1)}, u32[]{:S(2)}, u32[]{:S(2)}) collective-permute-start(bf16[128,1536]{0,1:T(8,128)(2,1)S(1)} %get-tuple-element.207), channel_id=1, source_target_pairs={{0,3},{1,0},{2,1},{3,2},{4,7},{5,4},{6,5},{7,6},{8,11},{9,8},{10,9... | collective-permute-start | bytes 1179656 | tf_op jit(solution)/shard_map/ppermute | solution.py:21
  353.2 27.1 %collective-permute-start.53 = (bf16[1632,128]{1,0:T(8,128)(2,1)S(1)}, bf16[1632,128]{1,0:T(8,128)(2,1)S(1)}, u32[]{:S(2)}, u32[]{:S(2)}) collective-permute-start(bf16[1632,128]{1,0:T(8,128)(2,1)S(1)} %shard_map.279.rest_0_.rest_4_), channel_id=1, source_target_pairs={{0,2},{1,3},{2,0},{3,1},{4,6},{5,7},{6,4},{7,5},{8,10},{9,11},{10,... | collective-permute-start | bytes 1253384 | tf_op jit(solution)/shard_map/ppermute | solution.py:21
  360.8 26.9 %collective-permute-start.61 = (bf16[1632,128]{1,0:T(8,128)(2,1)S(1)}, bf16[1632,128]{1,0:T(8,128)(2,1)S(1)}, u32[]{:S(2)}, u32[]{:S(2)}) collective-permute-start(bf16[1632,128]{1,0:T(8,128)(2,1)S(1)} %shard_map.279.rest_0_.rest_4_), channel_id=1, source_target_pairs={{1,0},{2,1},{3,2},{5,4},{6,5},{7,6},{9,8},{10,9},{11,10},{13,12},{... | collective-permute-start | bytes 1253384 | tf_op jit(solution)/shard_map/ppermute | solution.py:34
  362.1 25.6 %collective-permute-start.55 = (bf16[1632,128]{1,0:T(8,128)(2,1)S(1)}, bf16[1632,128]{1,0:T(8,128)(2,1)S(1)}, u32[]{:S(2)}, u32[]{:S(2)}) collective-permute-start(bf16[1632,128]{1,0:T(8,128)(2,1)S(1)} %shard_map.279.rest_0_.rest_4_), channel_id=1, source_target_pairs={{0,1},{1,2},{2,3},{4,5},{5,6},{6,7},{8,9},{9,10},{10,11},{12,13},{... | collective-permute-start | bytes 1253384 | tf_op jit(solution)/shard_map/ppermute | solution.py:33
  370.2 28.6 %collective-permute-start.59 = (bf16[2,192,1536]{2,1,0:T(8,128)(2,1)}, bf16[2,192,1536]{2,1,0:T(8,128)(2,1)}, u32[]{:S(2)}, u32[]{:S(2)}) collective-permute-start(bf16[2,192,1536]{2,1,0:T(8,128)(2,1)} %get-tuple-element.174), channel_id=1, source_target_pairs={{0,8},{4,12},{8,0},{12,4},{16,24},{20,28},{24,16},{28,20},{1,9},{5... | collective-permute-start | bytes 3538952 | tf_op jit(solution)/shard_map/ppermute | solution.py:48
  383.3 29.2 %collective-permute-start.60 = (bf16[2,192,1536]{2,1,0:T(8,128)(2,1)}, bf16[2,192,1536]{2,1,0:T(8,128)(2,1)}, u32[]{:S(2)}, u32[]{:S(2)}) collective-permute-start(bf16[2,192,1536]{2,1,0:T(8,128)(2,1)} %get-tuple-element.172), channel_id=1, source_target_pairs={{0,16},{4,20},{8,24},{12,28},{16,0},{20,4},{24,8},{28,12},{1,17},{... | collective-permute-start | bytes 3538952 | tf_op jit(solution)/shard_map/ppermute | solution.py:48
  393.3 51.5 %collective-permute-start.58 = (bf16[128,1536]{0,1:T(8,128)(2,1)S(1)}, bf16[128,1536]{0,1:T(8,128)(2,1)S(1)}, u32[]{:S(2)}, u32[]{:S(2)}) collective-permute-start(bf16[128,1536]{0,1:T(8,128)(2,1)S(1)} %get-tuple-element.205), channel_id=1, source_target_pairs={{0,1},{1,2},{2,3},{3,0},{4,5},{5,6},{6,7},{7,4},{8,9},{9,10},{10,1... | collective-permute-start | bytes 1179656 | tf_op jit(solution)/shard_map/ppermute | solution.py:21
  393.4 51.5 %collective-permute-start.57 = (bf16[128,1536]{0,1:T(8,128)(2,1)S(1)}, bf16[128,1536]{0,1:T(8,128)(2,1)S(1)}, u32[]{:S(2)}, u32[]{:S(2)}) collective-permute-start(bf16[128,1536]{0,1:T(8,128)(2,1)S(1)} %get-tuple-element.206), channel_id=1, source_target_pairs={{0,2},{1,3},{2,0},{3,1},{4,6},{5,7},{6,4},{7,5},{8,10},{9,11},{10,... | collective-permute-start | bytes 1179656 | tf_op jit(solution)/shard_map/ppermute | solution.py:21
  398.1 46.8 %collective-permute-start.56 = (bf16[128,1536]{0,1:T(8,128)(2,1)S(1)}, bf16[128,1536]{0,1:T(8,128)(2,1)S(1)}, u32[]{:S(2)}, u32[]{:S(2)}) collective-permute-start(bf16[128,1536]{0,1:T(8,128)(2,1)S(1)} %get-tuple-element.204), channel_id=1, source_target_pairs={{0,3},{1,0},{2,1},{3,2},{4,7},{5,4},{6,5},{7,6},{8,11},{9,8},{10,9... | collective-permute-start | bytes 1179656 | tf_op jit(solution)/shard_map/ppermute | solution.py:21
  400.9 45.2 %collective-permute-start.62 = (bf16[1,192,1536]{2,1,0:T(8,128)(2,1)}, bf16[1,192,1536]{2,1,0:T(8,128)(2,1)}, u32[]{:S(2)}, u32[]{:S(2)}) collective-permute-start(bf16[1,192,1536]{2,1,0:T(8,128)(2,1)} %fusion.34), channel_id=1, source_target_pairs={{0,16},{4,20},{8,24},{12,28},{16,0},{20,4},{24,8},{28,12},{1,17},{... | collective-permute-start | bytes 1769480 | tf_op jit(solution)/shard_map/ppermute | solution.py:48
  414.6 31.5 %collective-permute-start.63 = (bf16[1,192,1536]{2,1,0:T(8,128)(2,1)}, bf16[1,192,1536]{2,1,0:T(8,128)(2,1)}, u32[]{:S(2)}, u32[]{:S(2)}) collective-permute-start(bf16[1,192,1536]{2,1,0:T(8,128)(2,1)} %fusion.35), channel_id=1, source_target_pairs={{0,8},{4,12},{8,0},{12,4},{16,24},{20,28},{24,16},{28,20},{1,9},{5... | collective-permute-start | bytes 1769480 | tf_op jit(solution)/shard_map/ppermute | solution.py:48
  444.8 82.5 %collective-permute-start.89 = (bf16[4,192,1536]{2,1,0:T(8,128)(2,1)}, bf16[4,192,1536]{2,1,0:T(8,128)(2,1)}, u32[]{:S(2)}, u32[]{:S(2)}) collective-permute-start(bf16[4,192,1536]{2,1,0:T(8,128)(2,1)} %get-tuple-element.100), channel_id=1, source_target_pairs={{0,4},{4,0},{8,12},{12,8},{16,20},{20,16},{24,28},{28,24},{1,5},{5... | collective-permute-start | bytes 7077896 | tf_op jit(solution)/shard_map/ppermute | solution.py:48
  472.0 21.5 %collective-permute-start.64 = (f32[8,1536]{1,0:T(8,128)}, f32[8,1536]{1,0:T(8,128)S(1)}, u32[]{:S(2)}, u32[]{:S(2)}) collective-permute-start(f32[8,1536]{1,0:T(8,128)} %stack.72), channel_id=1, source_target_pairs={{0,4},{4,0},{8,12},{12,8},{16,20},{20,16},{24,28},{28,24},{1,5},{5... | collective-permute-start | bytes 147464 | tf_op jit(solution)/shard_map/ppermute | solution.py:48
  474.8 56.0 %collective-permute-start.71 = (bf16[128,1536]{0,1:T(8,128)(2,1)}, bf16[128,1536]{0,1:T(8,128)(2,1)}, u32[]{:S(2)}, u32[]{:S(2)}) collective-permute-start(bf16[128,1536]{0,1:T(8,128)(2,1)} %get-tuple-element.202), channel_id=1, source_target_pairs={{0,1},{1,2},{2,3},{3,0},{4,5},{5,6},{6,7},{7,4},{8,9},{9,10},{10,1... | collective-permute-start | bytes 1179656 | tf_op jit(solution)/shard_map/ppermute | solution.py:21
  478.2 53.2 %collective-permute-start.70 = (bf16[128,1536]{0,1:T(8,128)(2,1)}, bf16[128,1536]{0,1:T(8,128)(2,1)}, u32[]{:S(2)}, u32[]{:S(2)}) collective-permute-start(bf16[128,1536]{0,1:T(8,128)(2,1)} %get-tuple-element.203), channel_id=1, source_target_pairs={{0,2},{1,3},{2,0},{3,1},{4,6},{5,7},{6,4},{7,5},{8,10},{9,11},{10,... | collective-permute-start | bytes 1179656 | tf_op jit(solution)/shard_map/ppermute | solution.py:21
  479.4 52.0 %collective-permute-start.69 = (bf16[128,1536]{0,1:T(8,128)(2,1)}, bf16[128,1536]{0,1:T(8,128)(2,1)}, u32[]{:S(2)}, u32[]{:S(2)}) collective-permute-start(bf16[128,1536]{0,1:T(8,128)(2,1)} %get-tuple-element.201), channel_id=1, source_target_pairs={{0,3},{1,0},{2,1},{3,2},{4,7},{5,4},{6,5},{7,6},{8,11},{9,8},{10,9... | collective-permute-start | bytes 1179656 | tf_op jit(solution)/shard_map/ppermute | solution.py:21
  524.8 34.9 %collective-permute-start.72 = (bf16[4,192,1536]{2,1,0:T(8,128)(2,1)}, bf16[4,192,1536]{2,1,0:T(8,128)(2,1)}, u32[]{:S(2)}, u32[]{:S(2)}) collective-permute-start(bf16[4,192,1536]{2,1,0:T(8,128)(2,1)} %get-tuple-element.86), channel_id=1, source_target_pairs={{0,4},{4,0},{8,12},{12,8},{16,20},{20,16},{24,28},{28,24},{1,5},{5... | collective-permute-start | bytes 7077896 | tf_op jit(solution)/shard_map/ppermute | solution.py:48
  530.8 32.1 %collective-permute-start.80 = (bf16[4,192,1536]{2,1,0:T(8,128)(2,1)}, bf16[4,192,1536]{2,1,0:T(8,128)(2,1)S(1)}, u32[]{:S(2)}, u32[]{:S(2)}) collective-permute-start(bf16[4,192,1536]{2,1,0:T(8,128)(2,1)} %get-tuple-element.92), channel_id=1, source_target_pairs={{0,4},{4,0},{8,12},{12,8},{16,20},{20,16},{24,28},{28,24},{1,5},{5... | collective-permute-start | bytes 7077896 | tf_op jit(solution)/shard_map/ppermute | solution.py:48
  531.4 35.9 %collective-permute-start.83 = (bf16[4,192,1536]{2,1,0:T(8,128)(2,1)}, bf16[4,192,1536]{2,1,0:T(8,128)(2,1)}, u32[]{:S(2)}, u32[]{:S(2)}) collective-permute-start(bf16[4,192,1536]{2,1,0:T(8,128)(2,1)} %get-tuple-element.94), channel_id=1, source_target_pairs={{0,4},{4,0},{8,12},{12,8},{16,20},{20,16},{24,28},{28,24},{1,5},{5... | collective-permute-start | bytes 7077896 | tf_op jit(solution)/shard_map/ppermute | solution.py:48
  556.7 70.5 %collective-permute-start.96 = (bf16[1,192,384]{2,1,0:T(8,128)(2,1)S(1)}, bf16[1,192,384]{2,1,0:T(8,128)(2,1)}, u32[]{:S(2)}, u32[]{:S(2)}) collective-permute-start(bf16[1,192,384]{2,1,0:T(8,128)(2,1)S(1)} %get-tuple-element.104), channel_id=1, source_target_pairs={{0,1},{1,2},{2,3},{3,0},{4,5},{5,6},{6,7},{7,4},{8,9},{9,10},{10,1... | collective-permute-start | bytes 442376 | tf_op jit(solution)/shard_map/ppermute | solution.py:21
  559.3 70.5 %collective-permute-start.95 = (bf16[1,192,384]{2,1,0:T(8,128)(2,1)S(1)}, bf16[1,192,384]{2,1,0:T(8,128)(2,1)}, u32[]{:S(2)}, u32[]{:S(2)}) collective-permute-start(bf16[1,192,384]{2,1,0:T(8,128)(2,1)S(1)} %get-tuple-element.103), channel_id=1, source_target_pairs={{0,2},{1,3},{2,0},{3,1},{4,6},{5,7},{6,4},{7,5},{8,10},{9,11},{10,... | collective-permute-start | bytes 442376 | tf_op jit(solution)/shard_map/ppermute | solution.py:21
  561.8 16.3 %collective-permute-start.74 = (bf16[2,192,768]{2,1,0:T(8,128)(2,1)S(1)}, bf16[2,192,768]{2,1,0:T(8,128)(2,1)S(1)}, u32[]{:S(2)}, u32[]{:S(2)}) collective-permute-start(bf16[2,192,768]{2,1,0:T(8,128)(2,1)S(1)} %get-tuple-element.196), channel_id=1, source_target_pairs={{0,16},{4,20},{8,24},{12,28},{16,0},{20,4},{24,8},{28,12},{1,17},{... | collective-permute-start | bytes 1769480 | tf_op jit(solution)/shard_map/ppermute | solution.py:48
  562.9 17.1 %collective-permute-start.73 = (bf16[2,192,768]{2,1,0:T(8,128)(2,1)S(1)}, bf16[2,192,768]{2,1,0:T(8,128)(2,1)S(1)}, u32[]{:S(2)}, u32[]{:S(2)}) collective-permute-start(bf16[2,192,768]{2,1,0:T(8,128)(2,1)S(1)} %get-tuple-element.190), channel_id=1, source_target_pairs={{0,8},{4,12},{8,0},{12,4},{16,24},{20,28},{24,16},{28,20},{1,9},{5... | collective-permute-start | bytes 1769480 | tf_op jit(solution)/shard_map/ppermute | solution.py:48
  567.2 33.4 %collective-permute-start.81 = (bf16[2,192,1536]{2,1,0:T(8,128)(2,1)S(1)}, bf16[2,192,1536]{2,1,0:T(8,128)(2,1)S(1)}, u32[]{:S(2)}, u32[]{:S(2)}) collective-permute-start(bf16[2,192,1536]{2,1,0:T(8,128)(2,1)S(1)} %get-tuple-element.170), channel_id=1, source_target_pairs={{0,16},{4,20},{8,24},{12,28},{16,0},{20,4},{24,8},{28,12},{1,17},{... | collective-permute-start | bytes 3538952 | tf_op jit(solution)/shard_map/ppermute | solution.py:48
  578.1 28.9 %collective-permute-start.84 = (bf16[2,192,1536]{2,1,0:T(8,128)(2,1)S(1)}, bf16[2,192,1536]{2,1,0:T(8,128)(2,1)S(1)}, u32[]{:S(2)}, u32[]{:S(2)}) collective-permute-start(bf16[2,192,1536]{2,1,0:T(8,128)(2,1)S(1)} %get-tuple-element.168), channel_id=1, source_target_pairs={{0,8},{4,12},{8,0},{12,4},{16,24},{20,28},{24,16},{28,20},{1,9},{5... | collective-permute-start | bytes 3538952 | tf_op jit(solution)/shard_map/ppermute | solution.py:48
  580.0 33.4 %collective-permute-start.76 = (bf16[1,192,768]{2,1,0:T(8,128)(2,1)S(1)}, bf16[1,192,768]{2,1,0:T(8,128)(2,1)S(1)}, u32[]{:S(2)}, u32[]{:S(2)}) collective-permute-start(bf16[1,192,768]{2,1,0:T(8,128)(2,1)S(1)} %get-tuple-element.216), channel_id=1, source_target_pairs={{0,8},{4,12},{8,0},{12,4},{16,24},{20,28},{24,16},{28,20},{1,9},{5... | collective-permute-start | bytes 884744 | tf_op jit(solution)/shard_map/ppermute | solution.py:48
  613.4 16.4 %collective-permute-start.94 = (bf16[1,192,384]{2,1,0:T(8,128)(2,1)S(1)}, bf16[1,192,384]{2,1,0:T(8,128)(2,1)}, u32[]{:S(2)}, u32[]{:S(2)}) collective-permute-start(bf16[1,192,384]{2,1,0:T(8,128)(2,1)S(1)} %get-tuple-element.102), channel_id=1, source_target_pairs={{0,3},{1,0},{2,1},{3,2},{4,7},{5,4},{6,5},{7,6},{8,11},{9,8},{10,9... | collective-permute-start | bytes 442376 | tf_op jit(solution)/shard_map/ppermute | solution.py:21
  625.5 16.8 %collective-permute-start.78 = (bf16[1,192,384]{2,1,0:T(8,128)(2,1)}, bf16[1,192,384]{2,1,0:T(8,128)(2,1)S(1)}, u32[]{:S(2)}, u32[]{:S(2)}) collective-permute-start(bf16[1,192,384]{2,1,0:T(8,128)(2,1)} %copy-done.14), channel_id=1, source_target_pairs={{0,2},{1,3},{2,0},{3,1},{4,6},{5,7},{6,4},{7,5},{8,10},{9,11},{10,... | collective-permute-start | bytes 442376 | tf_op jit(solution)/shard_map/ppermute | solution.py:21
  629.8 25.6 %collective-permute-start.87 = (bf16[2,192,384]{2,1,0:T(8,128)(2,1)S(1)}, bf16[2,192,384]{2,1,0:T(8,128)(2,1)S(1)}, u32[]{:S(2)}, u32[]{:S(2)}) collective-permute-start(bf16[2,192,384]{2,1,0:T(8,128)(2,1)S(1)} %get-tuple-element.97), channel_id=1, source_target_pairs={{0,2},{1,3},{2,0},{3,1},{4,6},{5,7},{6,4},{7,5},{8,10},{9,11},{10,... | collective-permute-start | bytes 884744 | tf_op jit(solution)/shard_map/ppermute | solution.py:21
  631.3 24.1 %collective-permute-start.86 = (bf16[2,192,384]{2,1,0:T(8,128)(2,1)S(1)}, bf16[2,192,384]{2,1,0:T(8,128)(2,1)S(1)}, u32[]{:S(2)}, u32[]{:S(2)}) collective-permute-start(bf16[2,192,384]{2,1,0:T(8,128)(2,1)S(1)} %get-tuple-element.96), channel_id=1, source_target_pairs={{0,3},{1,0},{2,1},{3,2},{4,7},{5,4},{6,5},{7,6},{8,11},{9,8},{10,9... | collective-permute-start | bytes 884744 | tf_op jit(solution)/shard_map/ppermute | solution.py:21
  (113 other events, 1436.0 us)

commit v3 on v1

--- a/solution.py
+++ b/solution.py
@@ -21,37 +21,65 @@
     return lax.ppermute(x, "tensor", [(i, (i + shift) % count) for i in range(count)])
 
 
+def after(x, *done):
+    many = isinstance(x, (list, tuple))
+    held = lax.optimization_barrier((*x, *done) if many else (x, *done))
+    return list(held[: len(x)]) if many else held[0]
+
+
 def gather_blocks(x, count):
     return [x] + [rotate(x, count, k) for k in range(1, count)]
 
 
+def send_blocks(blocks, count):
+    return [blocks[0]] + [rotate(blocks[k], count, -k) for k in range(1, count)]
+
+
 def scatter_blocks(blocks, count):
-    arrived = [rotate(blocks[k], count, -k) for k in range(1, count)]
-    total = blocks[0].astype(F32)
-    for part in arrived:
-        total = total + part.astype(F32)
-    return total
-
-
-def swap(x, axis, count, bit):
-    return lax.ppermute(x, axis, [(i, i ^ (1 << bit)) for i in range(count)])
+    return add_up(send_blocks(blocks, count))
+
+
+def partner(x, axis, count, offset):
+    return lax.ppermute(x, axis, [(i, i ^ offset) for i in range(count)])
 
 
 def bits_of(count):
     return count.bit_length() - 1
 
 
-def halve(parts, left, bit, count):
-    place = left.index(bit)
-    rest = parts.shape[1:]
-    split = parts.reshape((1 << place, 2, 1 << (len(left) - place - 1)) + rest)
-    mine = (lax.axis_index("dp") >> bit) & 1
-    send = lax.dynamic_index_in_dim(split, 1 - mine, 1, keepdims=False)
-    keep = lax.dynamic_index_in_dim(split, mine, 1, keepdims=False)
-    got = swap(send, "dp", count, bit)
-    total = keep.astype(F32) + got.astype(F32)
-    left = [b for b in left if b != bit]
-    return total.reshape((1 << len(left),) + rest), left
+def gradient_kernel(natural, n_dp, at_ref, xt_ref, y_ref, keep_ref, send_ref, total_ref):
+    dims = (((1,), (0,)), ((), ())) if natural else (((1,), (1,)), ((), ()))
+    total_ref[...] = lax.dot_general(xt_ref[...], y_ref[...], dims, preferred_element_type=F32)
+    p, unit = at_ref[1], keep_ref.shape[1]
+    for i in range(n_dp // 2):
+        for odd, out in enumerate((keep_ref, send_ref)):
+            first = pl.multiple_of((p ^ (2 * i + odd)) * unit, unit)
+            out[i] = total_ref[pl.ds(first, unit), :].astype(BF)
+
+
+def gradient(xt, y, natural, at, n_dp):
+    width, rows = xt.shape
+    unit = width // n_dp
+    wide = y.shape[1] if natural else y.shape[0]
+    step = wide // 3
+    half = n_dp // 2
+    if natural:
+        y_spec = pl.BlockSpec((rows, step), lambda i: (0, i))
+    else:
+        y_spec = pl.BlockSpec((step, rows), lambda i: (i, 0))
+    return pl.pallas_call(
+        partial(gradient_kernel, natural, n_dp),
+        grid=(3,),
+        in_specs=[
+            pl.BlockSpec(memory_space=pltpu.SMEM),
+            pl.BlockSpec((width, rows), lambda i: (0, 0)),
+            y_spec,
+        ],
+        out_specs=[pl.BlockSpec((half, unit, step), lambda i: (0, 0, i))] * 2,
+        out_shape=[jax.ShapeDtypeStruct((half, unit, wide), BF)] * 2,
+        scratch_shapes=[pltpu.VMEM((width, step), F32)],
+        compiler_params=pltpu.CompilerParams(vmem_limit_bytes=VMEM_LIMIT),
+    )(at, xt, y)
 
 
 def bit_orders(count):
@@ -60,74 +88,217 @@
     return outer, outer[half:] + outer[:half]
 
 
-def reduce_pair(one, two, count):
-    left = list(range(bits_of(count) - 1, -1, -1))
-    both, left = halve(jnp.stack([one, two], axis=1), left, 0, count)
-    both = both.astype(BF)
+def cut_kernel(widths, *refs):
+    ins, (keep_ref, send_ref) = refs[:-2], refs[-2:]
+    start = 0
+    for i, wide in enumerate(widths):
+        lanes = slice(start, start + wide)
+        keep_a, got_a, keep_b, got_b = ins[4 * i : 4 * i + 4]
+        keep_ref[:, :, lanes] = (keep_a[...].astype(F32) + got_a[...].astype(F32)).astype(BF)
+        send_ref[:, :, lanes] = (keep_b[...].astype(F32) + got_b[...].astype(F32)).astype(BF)
+        start += wide
+
+
+def reduce_cut(parts, order, step, n_dp):
+    left = [b for b in range(bits_of(n_dp) - 1, 0, -1) if b not in order[:step]]
+    low = 1 << (len(left) - left.index(order[step]) - 1)
+    count, rows, _ = parts[0][0].shape
+    widths, specs, flat = [], [], []
+    for keep, got, half in parts:
+        wide = keep.shape[2] if half is None else keep.shape[2] // 2
+
+        def at(bit, wide=wide, lane=half or 0):
+            return pl.BlockSpec(
+                (1, rows, wide), lambda i: (i // low * (2 * low) + bit * low + i % low, 0, lane)
+            )
+
+        widths.append(wide)
+        specs += [at(0), at(0), at(1), at(1)]
+        flat += [keep, got, keep, got]
+    total = sum(widths)
+    return pl.pallas_call(
+        partial(cut_kernel, widths),
+        grid=(count // 2,),
+        in_specs=specs,
+        out_specs=[pl.BlockSpec((1, rows, total), lambda i: (i, 0, 0))] * 2,
+        out_shape=[jax.ShapeDtypeStruct((count // 2, rows, total), BF)] * 2,
+        compiler_params=pltpu.CompilerParams(vmem_limit_bytes=VMEM_LIMIT),
+    )(*flat)
+
+
+def first_cut(one, two, split, orders, n_dp):
     out = []
-    for which, order in enumerate(bit_orders(count)):
-        part, still = both[:, which], left
-        for bit in order:
-            part, still = halve(part.astype(BF), still, bit, count)
-        out.append(part[0])
+    for h, full in enumerate((one, two)):
+        parts = [(*full, None)] if full else []
+        parts += [(*split, h)] if split else []
+        out.append(reduce_cut(parts, orders[h], 0, n_dp))
     return out
+
+
+def next_cut(pair, orders, step, n_dp):
+    return [reduce_cut([(*x, None)], order, step, n_dp) for x, order in zip(pair, orders)]
+
+
+def cross(pair, orders, step, n_dp):
+    return [
+        (keep, partner(send, "dp", n_dp, 1 << order[step])) for (keep, send), order in zip(pair, orders)
+    ]
+
+
+def add_up(terms):
+    total = terms[0].astype(F32)
+    for term in terms[1:]:
+        total = total + term.astype(F32)
+    return total
+
+
+def blocks_kernel(n_t, weights, at_ref, *refs):
+    (a_keep, a_got, b_keep, b_got), outs = refs[:4], refs[4:]
+    pairs = (a_keep, a_got), (b_keep, b_got)
+    z = at_ref[0]
+    columns = outs[0].shape[-1]
+    half = n_t // 2
+
+    def piece(which, lane):
+        lanes = pl.ds(pl.multiple_of(lane, columns), columns)
+        keep, got = pairs[which]
+        return keep[0, :, lanes].astype(F32) + got[0, :, lanes].astype(F32)
+
+    for k in range(n_t):
+        block = lax.rem(z - k + n_t, n_t)
+        for m, which in enumerate(weights):
+            if which is None:
+                lane = (a_keep.shape[2] - columns * half) + lax.rem(block, half) * columns
+                value = jnp.where(block >= half, piece(1, lane), piece(0, lane))
+            else:
+                value = piece(which, block * columns)
+            outs[k][m] = value.astype(outs[k].dtype)
+
+
+def tensor_blocks(pair, weights, columns, at, n_t):
+    flat = [x for terms in pair for x in terms]
+    rows = flat[0].shape[1]
+    return pl.pallas_call(
+        partial(blocks_kernel, n_t, weights),
+        in_specs=[pl.BlockSpec(memory_space=pltpu.SMEM)]
+        + [pl.BlockSpec(memory_space=pltpu.VMEM)] * len(flat),
+        out_shape=[
+            jax.ShapeDtypeStruct((len(weights), rows, columns // n_t), F32 if k == 0 else BF)
+            for k in range(n_t)
+        ],
+        compiler_params=pltpu.CompilerParams(vmem_limit_bytes=VMEM_LIMIT),
+    )(at, *flat)
 
 
 def all_sum(x, axes):
     for axis, count in axes:
         for bit in range(bits_of(count)):
-            x = x + swap(x, axis, count, bit)
+            x = x + partner(x, axis, count, 1 << bit)
     return x
 
 
-def place_kernel(n_dp, n_t, offsets, at_ref, own_ref, even_ref, odd_ref, out_ref, sem):
+def place_kernel(n_t, unit, z_rows, z_cols, offsets, parts, at_ref, own_ref, *refs):
+    out_ref = refs[-1]
     z, p = at_ref[0], at_ref[1]
-    copies = [pltpu.make_async_copy(own_ref, out_ref.at[z], sem)]
+    rows, cols = own_ref.shape
+    if z_rows:
+        out_ref[pl.ds(pl.multiple_of(z * z_rows, z_rows), rows), :] = own_ref[...]
+    else:
+        out_ref[:, pl.ds(pl.multiple_of(z * z_cols, z_cols), cols)] = own_ref[...]
     for k in range(1, n_t):
         shard = lax.rem(z - k + n_t, n_t)
-        for i, off in enumerate(offsets):
-            copies.append(
-                pltpu.make_async_copy(even_ref.at[i, k - 1], out_ref.at[shard, p ^ off], sem)
-            )
-            copies.append(
-                pltpu.make_async_copy(
-                    odd_ref.at[i, k - 1], out_ref.at[shard, p ^ (off ^ 1)], sem
-                )
-            )
-    for copy in copies:
-        copy.start()
-    for copy in copies:
-        copy.wait()
-
-
-def place(own, even, odd, offsets, at, n_dp, n_t):
-    unit = own.shape[0] // n_dp
-    width = own.shape[1]
-    out = pl.pallas_call(
-        partial(place_kernel, n_dp, n_t, offsets),
-        out_shape=jax.ShapeDtypeStruct((n_t, n_dp, unit, width), own.dtype),
-        in_specs=[pl.BlockSpec(memory_space=pltpu.SMEM)] + [pl.BlockSpec(memory_space=pl.ANY)] * 3,
-        out_specs=pl.BlockSpec(memory_space=pl.ANY),
-        scratch_shapes=[pltpu.SemaphoreType.DMA],
-    )(at, own.reshape(n_dp, unit, width), even, odd)
-    return out.reshape(n_t * own.shape[0], width)
-
-
-def gather_pair(one, two, at, n_dp, n_t):
-    unit = one.shape[0] // n_dp
-    width = one.shape[1]
-    slices = jnp.stack([one, two]).reshape(2, n_dp, unit, width)
-    mine = lax.dynamic_index_in_dim(slices, lax.axis_index("dp"), 1, keepdims=False)
-    arrived = jnp.stack([rotate(mine, n_t, k) for k in range(1, n_t)], axis=1)
-    out = []
-    for which, (own, order) in enumerate(zip((one, two), bit_orders(n_dp))):
-        held, offsets = arrived[which][None], [0]
-        for bit in order:
-            held = jnp.concatenate([held, swap(held, "dp", n_dp, bit)], axis=0)
-            offsets = offsets + [o ^ (1 << bit) for o in offsets]
-        other = swap(held, "dp", n_dp, 0)
-        out.append(place(own, held, other, offsets, at, n_dp, n_t))
-    return out
+        for which, first, height, row_at, col_at in parts:
+            for odd in range(2):
+                src = refs[2 * which + odd]
+                wide = src.shape[3]
+                for i, off in enumerate(offsets[which]):
+                    base = shard * z_rows + (p ^ (off ^ odd)) * unit + row_at
+                    where = pl.ds(pl.multiple_of(base, 16), height)
+                    if z_cols:
+                        at = pl.ds(pl.multiple_of(shard * z_cols, z_cols), wide)
+                    else:
+                        at = slice(col_at, col_at + wide)
+                    out_ref[where, at] = src[i, k - 1, first : first + height, :]
+
+
+def reorder(x, places):
+    return jnp.stack([lax.dynamic_index_in_dim(x, i, 0, keepdims=False) for i in places])
+
+
+def project_kernel(place_kernel, count, at_ref, x_ref, *refs):
+    place_kernel(at_ref, *refs[:-2])
+    weight_ref, out_ref, turned_ref = refs[-3:]
+    turned_ref[...] = x_ref[...].T
+    step = weight_ref.shape[1] // count
+    for c in range(count):
+        cols = slice(c * step, (c + 1) * step)
+        block = jnp.dot(x_ref[...], weight_ref[:, cols], preferred_element_type=F32)
+        out_ref[cols, :] = block.T.astype(BF)
+
+
+def place(own, pieces, offsets, parts, unit, by_rows, at, n_dp, n_t, x=None):
+    rows, cols = own.shape
+    shape = (n_t * rows, cols) if by_rows else (rows, n_t * cols)
+    if unit % 16 or any(part[2] % 16 for part in parts):
+        z, p = at[0], at[1]
+        across = []
+        for which, first, height, _, _ in parts:
+            ordered = [None] * n_dp
+            for i, off in enumerate(offsets[which]):
+                for odd in range(2):
+                    ordered[off ^ odd] = pieces[which][odd][i, :, first : first + height]
+            across.append(reorder(jnp.stack(ordered), [p ^ d for d in range(n_dp)]))
+        whole = jnp.concatenate(across, axis=3 if by_rows else 2).transpose(1, 0, 2, 3)
+        whole = whole.reshape((n_t - 1, rows, cols))
+        whole = jnp.concatenate([own[None], whole], axis=0)
+        whole = reorder(whole, [(z - k + n_t) % n_t for k in range(n_t)])
+        whole = whole.reshape(shape) if by_rows else whole.transpose(1, 0, 2).reshape(shape)
+        return whole if x is None else (whole, dot("dh,rd->hr", whole, x).astype(BF), x.T)
+    flat = [x for pair in pieces for x in pair]
+    kernel = partial(
+        place_kernel, n_t, unit, rows if by_rows else 0, 0 if by_rows else cols, offsets, parts
+    )
+    out = jax.ShapeDtypeStruct(shape, own.dtype)
+    if x is None:
+        first, outs = [], out
+    else:
+        kernel, first = partial(project_kernel, kernel, n_t), [x]
+        outs = [out] + [jax.ShapeDtypeStruct((n, x.shape[0]), BF) for n in (shape[1], x.shape[1])]
+    ins = [*first, own, *flat]
+    return pl.pallas_call(
+        kernel,
+        out_shape=outs,
+        in_specs=[pl.BlockSpec(memory_space=pltpu.SMEM)]
+        + [pl.BlockSpec(memory_space=pltpu.VMEM)] * len(ins),
+        compiler_params=pltpu.CompilerParams(vmem_limit_bytes=VMEM_LIMIT),
+    )(at, *ins)
+
+
+def rotations(x, count):
+    return [rotate(x, count, k) for k in range(1, count)]
+
+
+def widen(one, two, step, orders, n_dp):
+    return [
+        jnp.concatenate([x, partner(x, "dp", n_dp, 1 << order[step])], axis=0)
+        for x, order in zip((one, two), orders)
+    ]
+
+
+def widen_offsets(order):
+    offsets = [0]
+    for bit in order:
+        offsets = offsets + [o ^ (1 << bit) for o in offsets]
+    return offsets
+
+
+def cores(one, two, n_dp):
+    return [(x, partner(x, "dp", n_dp, 1)) for x in (one, two)]
+
+
+def share_of(x, axis, count):
+    size = x.shape[axis] // count
+    return lax.dynamic_slice_in_dim(x, lax.axis_index("dp") * size, size, axis)
 
 
 def three(x):
@@ -319,6 +490,11 @@
         ],
         scratch_shapes=[pltpu.VMEM((2 * heads, rows), F32)],
         compiler_params=pltpu.CompilerParams(vmem_limit_bytes=VMEM_LIMIT),
+        cost_estimate=pl.CostEstimate(
+            flops=60 * heads * HD * rows * keys,
+            bytes_accessed=60 * 1024 * 1024,
+            transcendentals=heads * rows * keys,
+        ),
     )(q, k, v, seg, img, coef, *msgs, *msgs)
 
 
@@ -341,6 +517,107 @@
 
 def gain_shift(grad_rows, normal):
     return [jnp.sum(grad_rows * normal, axis=0), jnp.sum(grad_rows, axis=0)]
+
+
+def rows_back(grads, weights):
+    total = None
+    for grad, weight in zip(grads, weights):
+        term = lax.dot_general(grad, weight, (((0,), (1,)), ((), ())), preferred_element_type=F32)
+        total = term if total is None else total + term
+    return total
+
+
+def media_back_kernel(dk_ref, dv_ref, wk_ref, wv_ref, x_ref, gain_ref, out_ref, sums_ref):
+    back = rows_back((dk_ref[...], dv_ref[...]), (wk_ref[...], wv_ref[...]))
+    normal, root = norm_parts(x_ref[...])
+    out_ref[...] = norm_backward(back, normal, root, gain_ref[...])
+
+    @pl.when(pl.program_id(0) == 0)
+    def _():
+        sums_ref[...] = jnp.zeros_like(sums_ref)
+
+    sums_ref[0:1] += jnp.sum(back * normal, axis=0, keepdims=True)
+    sums_ref[1:2] += jnp.sum(back, axis=0, keepdims=True)
+
+
+def media_back(back_k, back_v, wk, wv, features, gain, block):
+    rows, width = features.shape
+    inner = back_k.shape[0]
+    whole = pl.BlockSpec((width, inner), lambda i: (0, 0))
+    return pl.pallas_call(
+        media_back_kernel,
+        grid=(rows // block,),
+        in_specs=[pl.BlockSpec((inner, block), lambda i: (0, i))] * 2
+        + [whole] * 2
+        + [pl.BlockSpec((block, width), lambda i: (i, 0)), pl.BlockSpec((1, width), lambda i: (0, 0))],
+        out_specs=[
+            pl.BlockSpec((block, width), lambda i: (i, 0)),
+            pl.BlockSpec((8, width), lambda i: (0, 0)),
+        ],
+        out_shape=[
+            jax.ShapeDtypeStruct((rows, width), F32),
+            jax.ShapeDtypeStruct((8, width), F32),
+        ],
+        compiler_params=pltpu.CompilerParams(vmem_limit_bytes=VMEM_LIMIT),
+    )(back_k, back_v, wk, wv, features, gain[None])
+
+
+def latent_back_kernel(n_t, dq_ref, dk_ref, dv_ref, wq_ref, wk_ref, wv_ref, *refs):
+    xs, outs, sums_ref = refs[:n_t], refs[n_t:-1], refs[-1]
+    rows = xs[0].shape[0]
+    gain_sum = shift_sum = None
+    total = rows_back((dq_ref[...],), (wq_ref[...],))
+    own = rows_back((dk_ref[...], dv_ref[...]), (wk_ref[...], wv_ref[...]))
+    for k in range(n_t):
+        back = total[k * rows : (k + 1) * rows]
+        if k == 0:
+            back = back + own
+        outs[k][...] = back.astype(outs[k].dtype)
+        normal, _ = norm_parts(xs[k][...])
+        gain_part = jnp.sum(back * normal, axis=0, keepdims=True)
+        shift_part = jnp.sum(back, axis=0, keepdims=True)
+        gain_sum = gain_part if gain_sum is None else gain_sum + gain_part
+        shift_sum = shift_part if shift_sum is None else shift_sum + shift_part
+    sums_ref[...] = jnp.zeros_like(sums_ref)
+    sums_ref[0:1] = gain_sum
+    sums_ref[1:2] = shift_sum
+
+
+def latent_back(back_q, back_k, back_v, wq, wk, wv, blocks):
+    n_t = len(blocks)
+    rows, width = blocks[0].shape
+    inner, keys = back_k.shape
+    tail = pl.BlockSpec((inner, rows), lambda i: (0, keys // rows - 1))
+    whole = pl.BlockSpec((width, inner), lambda i: (0, 0))
+    return pl.pallas_call(
+        partial(latent_back_kernel, n_t),
+        grid=(1,),
+        in_specs=[pl.BlockSpec(back_q.shape, lambda i: (0, 0)), tail, tail, whole, whole, whole]
+        + [pl.BlockSpec((rows, width), lambda i: (0, 0))] * n_t,
+        out_specs=[pl.BlockSpec((rows, width), lambda i: (0, 0))] * n_t
+        + [pl.BlockSpec((8, width), lambda i: (0, 0))],
+        out_shape=[jax.ShapeDtypeStruct((rows, width), BF if k else F32) for k in range(n_t)]
+        + [jax.ShapeDtypeStruct((8, width), F32)],
+        compiler_params=pltpu.CompilerParams(vmem_limit_bytes=VMEM_LIMIT),
+    )(back_q, back_k, back_v, wq, wk, wv, *blocks)
+
+
+def blocks_of_product_kernel(n_t, a_ref, b_ref, *outs):
+    total = jnp.dot(a_ref[...], b_ref[...], preferred_element_type=F32)
+    rows = outs[0].shape[0]
+    for k in range(n_t):
+        outs[k][...] = total[k * rows : (k + 1) * rows].astype(outs[k].dtype)
+
+
+def blocks_of_product(a, b, n_t):
+    shape = a.shape[0] // n_t, b.shape[1]
+    return list(
+        pl.pallas_call(
+            partial(blocks_of_product_kernel, n_t),
+            out_shape=[jax.ShapeDtypeStruct(shape, BF if k else F32) for k in range(n_t)],
+            compiler_params=pltpu.CompilerParams(vmem_limit_bytes=VMEM_LIMIT),
+        )(a, b)
+    )
 
 
 def dot(equation, a, b):
@@ -377,11 +654,6 @@
     heads = inner // HD
     images = lengths.shape[0]
 
-    latent_blocks = gather_blocks(latents, n_t)
-    wq, wk = gather_pair(query_weight.T, key_value_weight[:, 0].T, at, n_dp, n_t)
-    wv, wo = gather_pair(key_value_weight[:, 1].T, output_weight, at, n_dp, n_t)
-    cot_all = jnp.concatenate(gather_blocks(cotangent, n_t), axis=0)
-
     count_part = jnp.full((8, 128), jnp.sum(valid).astype(F32))
     count_total = all_sum(count_part, [("dp", n_dp)])[0, 0]
 
@@ -404,16 +676,58 @@
         axis=1,
     ).astype(F32)[None, :]
 
+    orders = bit_orders(n_dp)
+    steps = range(len(orders[0]))
+    offsets = [widen_offsets(order) for order in orders]
+    unit, part = width // n_dp, query_weight.shape[1]
+    keyval = jnp.moveaxis(share_of(key_value_weight, 0, n_dp), 1, 0)
+    kv_z = rotations(keyval, n_t)
     media_hat, media_root = norm_parts(features)
     media_normed = (media_hat * media_gain + media_shift).astype(BF)
+    own_hat, own_root = norm_parts(latents)
+    own_normed = (own_hat * latent_gain + latent_shift).astype(BF)
+    key_input = jnp.concatenate([media_normed, own_normed], axis=0)
+    kv_own = [key_value_weight[:, 0], key_value_weight[:, 1]]
+    *kv_z, key_input, count_total, k_own, v_own = after([*kv_z, key_input, count_total, *kv_own])
+    q_share = share_of(query_weight, 0, n_dp).reshape(2, unit // 2, part)
+    o_share = share_of(output_weight, 0, n_dp)
+    o_unit = o_share.shape[0]
+    o_share = o_share.reshape(o_unit, 2, -1, part).transpose(1, 2, 0, 3).reshape(2, -1, part)
+    qo_share = jnp.concatenate([q_share, o_share], axis=1)
+    qo_z = rotations(after(qo_share, *kv_z), n_t)
+    k_held, v_held = [jnp.stack([x[m] for x in kv_z])[None] for m in range(2)]
+    for step in steps[:-1]:
+        k_held, v_held = widen(k_held, v_held, step, orders, n_dp)
+    k_held, v_held, late_latents = after([k_held, v_held, latents], *qo_z)
+    latent_blocks = [latents] + rotations(late_latents, n_t)
+    k_held, v_held = widen(k_held, v_held, steps[-1], orders, n_dp)
+    k_pieces, v_pieces = cores(k_held, v_held, n_dp)
+    qo_held = [jnp.stack([x[m] for x in qo_z])[None] for m in range(2)]
+    qo_held = after(qo_held, k_held, v_held)
+    for step in steps[:-1]:
+        qo_held = widen(*qo_held, step, orders, n_dp)
+    whole = [(0, 0, unit, 0, 0)]
+    wk, keys, key_input_t = place(k_own, [k_pieces], offsets[:1], whole, unit, False, at, n_dp, n_t, key_input)
+    wv, values, _ = place(v_own, [v_pieces], offsets[1:], whole, unit, False, at, n_dp, n_t, key_input)
+    qo_held = widen(*after(qo_held, keys), steps[-1], orders, n_dp)
+    qo_held = after(qo_held, values)
+    qo_pieces = cores(*qo_held, n_dp)
     latent_all = jnp.concatenate(latent_blocks, axis=0)
     latent_hat, latent_root = norm_parts(latent_all)
     latent_normed = (latent_hat * latent_gain + latent_shift).astype(BF)
-    key_input = jnp.concatenate([media_normed, latent_normed[:own_rows]], axis=0)
-    queries = dot("hd,rd->hr", wq, latent_normed).astype(BF)
-    keys = dot("hd,rd->hr", wk, key_input).astype(BF)
-    values = dot("hd,rd->hr", wv, key_input).astype(BF)
+    cot_blocks = [cotangent] + rotations(after(cotangent, values, latent_normed), n_t)
+    cuts = [(h, 0, unit // 2, h * unit // 2, 0) for h in range(2)]
+    wq, queries, latent_t = place(
+        query_weight, qo_pieces, offsets, cuts, unit, False, at, n_dp, n_t, latent_normed
+    )
+    cuts = [
+        (h, unit // 2 + c * o_unit, o_unit, 0, h * width // 2 + c * part)
+        for h in range(2)
+        for c in range(width // 2 // part)
+    ]
+    wo = place(output_weight, qo_pieces, offsets, cuts, o_unit, True, at, n_dp, n_t)
     sent = attend_forward(queries, keys, values, key_image, row_image, n_t)
+    sent = after(sent, wo, *cot_blocks[1:])
     got = [sent[0]] + [rotate(sent[k], n_t, -k) for k in range(1, n_t)]
     attended, stat = combine(got, heads)
     entropy = stat[:heads] - stat[heads:]
@@ -425,6 +739,7 @@
     feed_hat, feed_root = norm_parts(middle)
     feed_normed = (feed_hat * feed_gain + feed_shift).astype(BF)
     feed_all = jnp.concatenate(gather_blocks(feed_normed, n_t), axis=0)
+    cot_all = jnp.concatenate(after(cot_blocks, feed_normed), axis=0)
     hidden = dot("rd,df->rf", feed_all, up_weight)
     cdf = 0.5 * (1.0 + lax.erf(hidden * (0.5**0.5)))
     slope = cdf + hidden * jnp.exp(-0.5 * hidden * hidden) * (0.5 / jnp.pi) ** 0.5
@@ -432,18 +747,14 @@
     back_activation = dot("rd,fd->rf", cot_all, down_weight)
     back_hidden = (back_activation * slope).astype(BF)
     back_terms = dot("rf,df->rd", back_hidden, up_weight).astype(BF)
-    back_feed = scatter_blocks(
-        [back_terms[k * own_rows : (k + 1) * own_rows] for k in range(n_t)], n_t
-    )
-    feed_terms = dot("rf,fd->rd", activation, down_weight).astype(BF)
-    result = middle + scatter_blocks(
-        [feed_terms[k * own_rows : (k + 1) * own_rows] for k in range(n_t)], n_t
-    )
-    grad_down = dot("rd,rf->df", cot_all, activation).astype(BF)
-    grad_up = dot("rd,rf->df", feed_all, back_hidden).astype(BF)
-    down_share, up_share = reduce_pair(
-        grad_down.reshape(n_dp, width // n_dp, -1), grad_up.reshape(n_dp, width // n_dp, -1), n_dp
-    )
+    back_blocks = [back_terms[k * own_rows : (k + 1) * own_rows] for k in range(n_t)]
+    back_arrived = send_blocks(back_blocks, n_t)
+    late_activation, late_hidden = after([activation, back_hidden], back_terms)
+    down_keep, down_send = gradient(cot_all.T, late_activation, True, at, n_dp)
+    up_keep, up_send = gradient(feed_all.T, late_hidden, True, at, n_dp)
+    result_terms = blocks_of_product(late_activation, down_weight, n_t)
+    back_feed = add_up(after(back_arrived, down_send, up_send, *result_terms))
+    down_got, up_got = partner(down_send, "dp", n_dp, 1), partner(up_send, "dp", n_dp, 1)
 
     back_middle = cotangent.astype(F32) + norm_backward(back_feed, feed_hat, feed_root, feed_gain)
     back_branch = back_middle.astype(BF)
@@ -451,46 +762,75 @@
     own_coef = own_valid / count_total
     message = make_message(back_attended, attended, stat, own_coef, heads)
     messages = gather_blocks(message, n_t)
+    out_keep, out_send = gradient(back_branch.T, attended, False, at, n_dp)
+    out_got = partner(out_send, "dp", n_dp, 1)
+    down_got, up_got, out_got = after([down_got, up_got, out_got], message)
+    feed_pair = first_cut((down_keep, down_got), (up_keep, up_got), (out_keep, out_got), orders, n_dp)
+    messages = after(messages, *[send for _, send in feed_pair])
+    result_terms[1:] = after(result_terms[1:], *messages)
+    result_terms = send_blocks(result_terms, n_t)
     back_q, back_k, back_v = attend_backward(
         queries, keys, values, key_image, row_image, row_valid / count_total, messages
     )
-
-    def shares(a, b):
-        return dot("rd,hr->dh", a, b).astype(BF).reshape(n_dp, width // n_dp, inner)
-
-    key_share, value_share = reduce_pair(shares(key_input, back_k), shares(key_input, back_v), n_dp)
-    query_share, output_share = reduce_pair(
-        shares(latent_normed, back_q), shares(back_branch, attended), n_dp
-    )
-    back_inputs = dot("hr,hd->rd", back_k, wk) + dot("hr,hd->rd", back_v, wv)
-    back_media = back_inputs[:own_patches]
-    latent_terms = dot("hr,hd->rd", back_q, wq)
-    latent_terms = jnp.concatenate(
-        [latent_terms[:own_rows] + back_inputs[own_patches:], latent_terms[own_rows:]], axis=0
-    )
-    terms_low = latent_terms.astype(BF)
-    back_latent = scatter_blocks(
-        [terms_low[k * own_rows : (k + 1) * own_rows] for k in range(n_t)], n_t
-    )
-    features_grad = norm_backward(back_media, media_hat, media_root, media_gain)
+    feed_pair = cross(feed_pair, orders, 0, n_dp)
+    for i in steps[1:]:
+        feed_pair = next_cut(feed_pair, orders, i, n_dp)
+        if i == steps[1]:
+            back_q, back_k, back_v = after([back_q, back_k, back_v], *[send for _, send in feed_pair])
+        feed_pair = cross(feed_pair, orders, i, n_dp)
+
+    v_keep, v_send = gradient(key_input_t, back_v, False, at, n_dp)
+    k_keep, k_send = gradient(key_input_t, after(back_k, v_send), False, at, n_dp)
+    q_keep, q_send = gradient(latent_t, after(back_q, k_send, *result_terms[1:]), False, at, n_dp)
+    v_send, k_send = after([v_send, k_send], q_send)
+    v_got, k_got, q_got = [partner(x, "dp", n_dp, 1) for x in (v_send, k_send, q_send)]
+    latent_q = after(back_q, q_send)
+    *latent_terms, latent_sums = latent_back(latent_q, back_k, back_v, wq, wk, wv, latent_blocks)
+    v_got, k_got, q_got = after([v_got, k_got, q_got], latent_sums)
+    pair = first_cut((v_keep, v_got), (k_keep, k_got), None, orders, n_dp)
+    sends = [send for _, send in pair]
+    latent_terms[1:] = after(latent_terms[1:], *sends)
+    latent_terms = send_blocks(latent_terms, n_t)
+    pair = cross(pair, orders, 0, n_dp)
+    q_pair = first_cut(None, None, (q_keep, after(q_got, *sends)), orders, n_dp)
+    out_blocks = tensor_blocks(feed_pair, [None], inner, at, n_t)
+    features_grad, media_sums = media_back(
+        after(back_k, latent_sums, *out_blocks, *[send for _, send in q_pair]),
+        back_v, wk, wv, features, media_gain, own_patches,
+    )
+    for i in steps[1:]:
+        gots = after([got for _, got in pair], features_grad)
+        pair = [(keep, got) for (keep, _), got in zip(pair, gots)]
+        pair = next_cut(pair, orders, i, n_dp)
+        if i == steps[1]:
+            q_sends = after([send for _, send in q_pair], *[send for _, send in pair], *latent_terms[1:])
+            q_pair = [(keep, send) for (keep, _), send in zip(q_pair, q_sends)]
+        pair = cross(pair, orders, i, n_dp)
+    q_pair = cross(q_pair, orders, 0, n_dp)
+    blocks = tensor_blocks(pair, [1, 0], inner, at, n_t)
+    for i in steps[1:]:
+        gots = after([got for _, got in q_pair], *blocks)
+        q_pair = [(keep, got) for (keep, _), got in zip(q_pair, gots)]
+        q_pair = cross(next_cut(q_pair, orders, i, n_dp), orders, i, n_dp)
+    blocks = send_blocks(blocks, n_t)
+    q_blocks = tensor_blocks(q_pair, [None], inner, at, n_t)
+    grad_kv = add_up(after(blocks, *q_blocks))
+    back_latent = add_up(after(latent_terms, *q_blocks))
+    late = after([x for terms in feed_pair for x in terms], *q_blocks)
+    (down_keep, down_got), (up_keep, up_got) = late[:2], late[2:]
+    down_share = down_keep[0, :, :inner].astype(F32) + down_got[0, :, :inner].astype(F32)
+    up_share = up_keep[0, :, :inner].astype(F32) + up_got[0, :, :inner].astype(F32)
+    result = middle + add_up(after(result_terms, *q_blocks))
     latents_grad = back_middle + norm_backward(
-        back_latent, latent_hat[:own_rows], latent_root[:own_rows], latent_gain
-    )
-
-    part = inner // n_t
-    four = jnp.stack([query_share, key_share, value_share, output_share]).astype(BF)
-    four = four.reshape(4, width // n_dp, n_t, part).transpose(2, 0, 1, 3)
-    blocks = [
-        lax.dynamic_index_in_dim(four, (z - k + n_t) % n_t, 0, keepdims=False) for k in range(n_t)
-    ]
-    four = scatter_blocks(blocks, n_t)
-
-    sums = (
-        gain_shift(back_media, media_hat)
-        + gain_shift(latent_terms, latent_hat)
-        + gain_shift(back_feed, feed_hat)
-    )
+        back_latent, own_hat, own_root, latent_gain
+    )
+
+    grad_qo = scatter_blocks([jnp.concatenate(x, axis=0) for x in zip(q_blocks, out_blocks)], n_t)
+    grad_q, grad_o = grad_qo[0], grad_qo[1]
+
+    sums = [media_sums[0], media_sums[1], latent_sums[0], latent_sums[1]] + gain_shift(back_feed, feed_hat)
     sums = jnp.stack(sums + [jnp.full((width,), penalty_part)] * 2)
+    sums = after(sums, features_grad)
     sums = all_sum(sums, [("dp", n_dp), ("tensor", n_t)])
     penalty = sums[6, 0] / count_total
     share = width // (n_dp * n_t)
@@ -508,9 +848,9 @@
         mine[3],
         mine[4],
         mine[5],
-        four[0],
-        jnp.stack([four[1], four[2]], axis=1),
-        four[3].T,
+        grad_q,
+        jnp.moveaxis(grad_kv, 0, 1),
+        grad_o.T,
         up_share,
         down_share.T,
     )

time: 1270 us -> 598 us (0.47)
  Pallas kernels: 625 us -> 161 us
  starting transfers between devices: 148 us -> 78.9 us
  matrix products: 75.1 us -> 20.2 us
  other arithmetic: 89.2 us -> 34.8 us
  waiting for transfers between devices: 255 us -> 227 us
    pallas_call x4 -> x28, Pallas kernels: 579 us -> 117 us  [the longest x6 31.6 us: gradient(): pl.pallas_call(partial(gradient_kernel, natural, n_dp), grid=(3,), in_spe...]
    ppermute x33 -> x36, starting transfers between devices: 116 us -> 48.4 us  [rotate(): lax.ppermute(x, 'tensor', [(i, (i + shift) % count) for i in range(count)])]
    ppermute x35 -> x38, waiting for transfers between devices: 128 us -> 69.2 us  [partner(): return lax.ppermute(x, axis, [(i, i ^ offset) for i in range(count)])]
    dot_general x18 -> x5, matrix products: 75.1 us -> 20.2 us  [dot(): return jnp.einsum(equation, a, b, preferred_element_type=F32)]
    ppermute x33 -> x36, waiting for transfers between devices: 126 us -> 158 us  [rotate(): lax.ppermute(x, 'tensor', [(i, (i + shift) % count) for i in range(count)])]
    unnamed x166 -> x281, local copies, waits for them, and re-layouts: 10.2 us -> 35.1 us
    convert_element_type x10 -> x2, other arithmetic: 21.3 us -> 0.96 us  [the longest x1 0.65 us: local(): latent_normed = (latent_hat * latent_gain + latent_shift).astype(BF)]
    another operation x9 -> x0, other arithmetic: 16.4 us -> none
  transfers between devices with their start and end apart: 68 -> 74, of which waited for: 27 -> 29; matrix products, arithmetic and copies ran while one was open for 15% -> 10% of each run, Pallas kernels for 50% -> 26%
where the time goes in v3:
time: 598 us; the launch traced here: 589 us
  waiting for transfers between devices  227 us (38%)
  Pallas kernels  161 us (27%)
  starting transfers between devices  78.9 us (13%)
  local copies, waits for them, and re-layouts  60.5 us (10%)
  other arithmetic  34.8 us (6%)
  matrix products  20.2 us (3%)
    ppermute x36, waiting for transfers between devices, rotate(): lax.ppermute(x, 'tensor', [(i, (i + shift) % count) for i in range(count)])  158 us
    ppermute x38, waiting for transfers between devices, partner(): return lax.ppermute(x, axis, [(i, i ^ offset) for i in range(count)])  69.2 us
    ppermute x36, starting transfers between devices, rotate(): lax.ppermute(x, 'tensor', [(i, (i + shift) % count) for i in range(count)])  48.4 us
    unnamed x281, local copies, waits for them, and re-layouts  35.1 us
    pallas_call x6, Pallas kernels, gradient(): pl.pallas_call(partial(gradient_kernel, natural, n_dp), grid=(3,), in_spe...  31.6 us
    ppermute x38, starting transfers between devices, partner(): return lax.ppermute(x, axis, [(i, i ^ offset) for i in range(count)])  30.5 us
    pallas_call x4, Pallas kernels, place(): pl.pallas_call(kernel, out_shape=outs, in_specs=[pl.BlockSpec(memory_spac...  28.1 us
    pallas_call x1, Pallas kernels, attend_backward(): pl.pallas_call(partial(backward_kernel, heads, n_t), grid=(heads,), out_s...  24.7 us
  transfers between devices with their start and end apart: 74, of which 29 were waited for; matrix products, arithmetic and copies ran while one was open for 10% of the time, Pallas kernels for 26%

profile of v3, /device:TPU:0, one launch (start us, length us, event | category | flops | bytes accessed | tf_op | source)
XLA Modules:
  0.0 588.8 jit_solution(9853665372743877850)
XLA Ops:
  2.6 5.0 collective-permute-start.2
  10.7 6.6 %fusion.49 = (bf16[1536,1,384]{2,1,0:T(2,128)(2,1)S(1)}, bf16[1536,1,384]{2,1,0:T(2,128)(2,1)S(1)}) fusion(bf16[1536,2,384]{2,1,0:T(2,128)(2,1)} %param.27), kind=kLoop, calls=%fused_computation.162 | loop fusion | bytes 4718592 | tf_op jit(solution)/shard_map/slice | solution.py:690
  28.5 4.5 collective-permute-done.1
  41.8 2.9 collective-permute-start.9
  47.3 2.2 pad_maximum_fusion.5
  49.5 2.2 pad_maximum_fusion.6
  51.7 17.8 %collective-permute-done.9 = bf16[2,192,384]{2,1,0:T(8,128)(2,1)S(1)} collective-permute-done((bf16[2,192,384]{2,1,0:T(8,128)(2,1)S(1)}, bf16[2,192,384]{2,1,0:T(8,128)(2,1)S(1)}, u32[]{:S(2)}, u32[]{:S(2)}) %collective-permute-start.9) | collective-permute-done | bytes 294944 | tf_op jit(solution)/shard_map/ppermute | solution.py:21
  72.5 17.5 %collective-permute-done.14 = bf16[2,3,192,384]{3,2,1,0:T(8,128)(2,1)} collective-permute-done((bf16[2,3,192,384]{3,2,1,0:T(8,128)(2,1)}, bf16[2,3,192,384]{3,2,1,0:T(8,128)(2,1)}, u32[]{:S(2)}, u32[]{:S(2)}) %collective-permute-start.14) | collective-permute-done | bytes 884768 | tf_op jit(solution)/shard_map/ppermute | solution.py:43
  96.3 10.8 %collective-permute-done.16 = bf16[1,3,192,384]{3,2,1,0:T(8,128)(2,1)S(1)} collective-permute-done((bf16[1,3,192,384]{3,2,1,0:T(8,128)(2,1)S(1)}, bf16[1,3,192,384]{3,2,1,0:T(8,128)(2,1)S(1)}, u32[]{:S(2)}, u32[]{:S(2)}) %collective-permute-start.16) | collective-permute-done | bytes 442400 | tf_op jit(solution)/shard_map/ppermute | solution.py:43
  107.5 8.2 %shard_map.271 = (bf16[1536,1536]{1,0:T(8,128)(2,1)}, bf16[1536,640]{1,0:T(8,128)(2,1)}, bf16[1536,640]{1,0:T(8,128)(2,1)}) custom-call(s32[2]{0:T(128)S(1)} %pad_add_fusion.1.at_ref, bf16[640,1536]{1,0:T(8,128)(2,1)} %pad_maximum_fusion.x_ref, bf16[1536,384]{1,0:T(8,128)(2,1)S(1)} %copy-done.31, ...), custom_call_target="tpu_custom_call" | custom-call | tf_op jit(solution)/shard_map/pallas_call | solution.py:268
  119.7 2.2 collective-permute-start.11
  122.0 8.3 %shard_map.272 = (bf16[1536,1536]{1,0:T(8,128)(2,1)}, bf16[1536,640]{1,0:T(8,128)(2,1)}, bf16[1536,640]{1,0:T(8,128)(2,1)}) custom-call(s32[2]{0:T(128)S(1)} %pad_add_fusion.1.at_ref, bf16[640,1536]{1,0:T(8,128)(2,1)} %pad_maximum_fusion.x_ref, bf16[1536,384]{1,0:T(8,128)(2,1)S(1)} %get-tuple-element.186.refs_0_, ...), custom_call_target="tpu_custom_call" | custom-call | tf_op jit(solution)/shard_map/pallas_call | solution.py:268
  130.4 5.8 collective-permute-done.19
  137.3 15.2 %collective-permute-done.12.refs_2_ = bf16[128,1536]{1,0:T(8,128)(2,1)S(1)} collective-permute-done((bf16[128,1536]{1,0:T(8,128)(2,1)S(1)}, bf16[128,1536]{1,0:T(8,128)(2,1)S(1)}, u32[]{:S(2)}, u32[]{:S(2)}) %collective-permute-start.12) | collective-permute-done | bytes 393248 | tf_op jit(solution)/shard_map/ppermute | solution.py:21
  159.3 7.0 %shard_map.273 = (bf16[1536,1536]{1,0:T(8,128)(2,1)}, bf16[1536,512]{1,0:T(8,128)(2,1)S(1)}, bf16[1536,512]{1,0:T(8,128)(2,1)S(1)}) custom-call(s32[2]{0:T(128)S(1)} %pad_add_fusion.1.at_ref, bf16[512,1536]{1,0:T(8,128)(2,1)S(1)} %fusion.7.x_ref, bf16[1536,384]{1,0:T(8,128)(2,1)S(1)} %copy-done.53, bf16[4,3,192,384]{3,2,1,0:T(8,128)(2,1)} %copy-done.7, ...), custom_call_target="tpu_custom_call" | custom-call | tf_op jit(solution)/shard_map/pallas_call | solution.py:268
  166.4 19.3 %shard_map.274 = (bf16[1632,128]{1,0:T(8,128)(2,1)S(1)}, bf16[1632,128]{1,0:T(8,128)(2,1)S(1)}, bf16[1632,128]{1,0:T(8,128)(2,1)S(1)}, bf16[1632,128]{1,0:T(8,128)(2,1)S(1)}) custom-call(bf16[1536,512]{1,0:T(8,128)(2,1)S(1)} %get-tuple-element.190.q_ref, bf16[1536,640]{1,0:T(8,128)(2,1)S(1)} %copy-done.46, bf16[1536,640]{1,0:T(8,128)(2,1)} %get-tuple-element.187.v_ref, ...), custom_call_target="tpu_custom_call" | custom-call | tf_op jit(solution)/shard_map/pallas_call | solution.py:355
  185.8 4.5 shard_map.275
  194.0 8.5 %collective-permute-done.27.refs_1_ = bf16[1632,128]{1,0:T(8,128)(2,1)S(1)} collective-permute-done((bf16[1632,128]{1,0:T(8,128)(2,1)S(1)}, bf16[1632,128]{1,0:T(8,128)(2,1)S(1)}, u32[]{:S(2)}, u32[]{:S(2)}) %collective-permute-start.27) | collective-permute-done | bytes 417824 | tf_op jit(solution)/shard_map/ppermute | solution.py:21
  202.5 25.2 %collective-permute-done.28.refs_2_ = bf16[1632,128]{1,0:T(8,128)(2,1)S(1)} collective-permute-done((bf16[1632,128]{1,0:T(8,128)(2,1)S(1)}, bf16[1632,128]{1,0:T(8,128)(2,1)S(1)}, u32[]{:S(2)}, u32[]{:S(2)}) %collective-permute-start.28) | collective-permute-done | bytes 417824 | tf_op jit(solution)/shard_map/ppermute | solution.py:21
  228.1 3.4 fusion.57
  232.2 2.6 collective-permute-start.31
  237.0 4.9 collective-permute-done.32
  241.9 26.5 %collective-permute-done.31 = bf16[128,1536]{1,0:T(8,128)(2,1)S(1)} collective-permute-done((bf16[128,1536]{1,0:T(8,128)(2,1)S(1)}, bf16[128,1536]{1,0:T(8,128)(2,1)S(1)}, u32[]{:S(2)}, u32[]{:S(2)}) %collective-permute-start.31) | collective-permute-done | bytes 393248 | tf_op jit(solution)/shard_map/ppermute | solution.py:21
  268.4 6.6 %multiply_convert_fusion = (bf16[512,1536]{1,0:T(8,128)(2,1)}, f32[512,1536]{1,0:T(8,128)S(1)}) fusion(bf16[1536,1536]{1,0:T(8,128)(2,1)} %param.29, bf16[128,1536]{1,0:T(8,128)(2,1)S(1)} %collective-permute-done.32, bf16[128,1536]{1,0:T(8,128)(2,1)S(1)} %collective-permute-done.31, bf16[128,1536]{1,0:T(8,128)(2,1)S(1)} %collective-permute-done.30, ...), kind=kOutput, calls=%fused_computation.22 | convolution fusion | flops 2426142720 | bytes 11010048 | tf_op jit(solution)/shard_map/rd,df->rf/dot_general | solution.py:624
  275.1 3.7 fusion.16.y_ref
  278.8 2.6 convolution_convert_fusion
  282.7 4.0 collective-permute-start.33
  288.2 2.6 fusion.33
  294.0 5.1 shard_map.277
  302.2 5.1 shard_map.278
  308.9 5.2 shard_map.279
  314.6 2.8 multiply_reduce_fusion
  320.1 3.1 shard_map.281
  325.1 3.9 convolution_convert_fusion.1.do_ref
  329.2 4.5 collective-permute-start.38
  336.6 3.0 shard_map.282
  340.4 3.0 shard_map.283
  346.2 25.1 %collective-permute-done.37.rest_2_.rest_6_ = bf16[1632,128]{1,0:T(8,128)(2,1)S(1)} collective-permute-done((bf16[1632,128]{1,0:T(8,128)(2,1)S(1)}, bf16[1632,128]{1,0:T(8,128)(2,1)S(1)}, u32[]{:S(2)}, u32[]{:S(2)}) %collective-permute-start.37) | collective-permute-done | bytes 417824 | tf_op jit(solution)/shard_map/ppermute | solution.py:21
  372.7 2.2 collective-permute-start.44
  374.9 24.7 %shard_map.284 = (bf16[1536,512]{1,0:T(8,128)(2,1)S(1)}, bf16[1536,640]{1,0:T(8,128)(2,1)}, bf16[1536,640]{1,0:T(8,128)(2,1)}) custom-call(bf16[1536,512]{1,0:T(8,128)(2,1)S(1)} %copy-done.50, bf16[1536,640]{1,0:T(8,128)(2,1)} %get-tuple-element.183.k_ref, bf16[1536,640]{1,0:T(8,128)(2,1)} %get-tuple-element.187.v_ref, s32[640,1]{1,0:T(8,128)S(1)} %copy-done.56, ...), custom_call_target="tpu_custom_call" | custom-call | flops 30198988800 | bytes 62914560 | tf_op jit(solution)/shard_map/pallas_call | solution.py:468
  399.6 2.7 shard_map.285
  408.8 6.5 %shard_map.287 = (bf16[4,192,1536]{2,1,0:T(8,128)(2,1)}, bf16[4,192,1536]{2,1,0:T(8,128)(2,1)}) custom-call(s32[2]{0:T(128)S(1)} %pad_add_fusion.1.at_ref, bf16[1536,640]{1,0:T(8,128)(2,1)S(1)} %copy-done.15, bf16[1536,640]{1,0:T(8,128)(2,1)S(1)} %copy-done.5), custom_call_target="tpu_custom_call" | custom-call | tf_op jit(solution)/shard_map/pallas_call | solution.py:70
  415.3 6.5 %shard_map.288 = (bf16[4,192,1536]{2,1,0:T(8,128)(2,1)}, bf16[4,192,1536]{2,1,0:T(8,128)(2,1)}) custom-call(s32[2]{0:T(128)S(1)} %pad_add_fusion.1.at_ref, bf16[1536,640]{1,0:T(8,128)(2,1)S(1)} %copy-done.15, bf16[1536,640]{1,0:T(8,128)(2,1)S(1)} %copy-done.3), custom_call_target="tpu_custom_call" | custom-call | tf_op jit(solution)/shard_map/pallas_call | solution.py:70
  421.9 5.2 shard_map.289
  429.8 11.5 %shard_map.290 = (f32[128,1536]{1,0:T(8,128)S(1)}, bf16[128,1536]{1,0:T(8,128)(2,1)S(1)}, bf16[128,1536]{1,0:T(8,128)(2,1)S(1)}, bf16[128,1536]{1,0:T(8,128)(2,1)S(1)}, f32[8,1536]{1,0:T(8,128)S(1)}) custom-call(bf16[1536,512]{1,0:T(8,128)(2,1)S(1)} %get-tuple-element.255.y_ref.dq_ref, bf16[1536,640]{1,0:T(8,128)(2,1)} %get-tuple-element.278.y_ref.dk_ref, ...), custom_call_target="tpu_custom_call" | custom-call | tf_op jit(solution)/shard_map/pallas_call | solution.py:592
  445.1 2.9 shard_map.292
  448.6 2.9 shard_map.291
  455.6 2.1 collective-permute-start.56
  466.1 12.0 %shard_map.296 = (f32[512,1536]{1,0:T(8,128)}, f32[8,1536]{1,0:T(8,128)S(1)}) custom-call(bf16[1536,640]{1,0:T(8,128)(2,1)S(1)} %copy-done.4, bf16[1536,640]{1,0:T(8,128)(2,1)S(1)} %copy-done.6, bf16[1536,1536]{1,0:T(8,128)(2,1)} %get-tuple-element.257.wk_ref, bf16[1536,1536]{1,0:T(8,128)(2,1)} %get-tuple-element.258.wv_ref, ...), custom_call_target="tpu_custom_call" | custom-call | tf_op jit(solution)/shard_map/pallas_call | solution.py:547
  478.1 2.3 collective-permute-done.50.refs_1_.refs_3_
  480.3 2.4 shard_map.298
  484.9 2.2 shard_map.297
  496.0 4.1 collective-permute-done.60.refs_3_
  500.1 4.4 collective-permute-done.59.refs_1_
  509.0 2.0 collective-permute-done.57.refs_1_.refs_3_
  510.9 3.6 collective-permute-done.58.refs_1_.refs_3_
  519.7 5.4 collective-permute-done.65
  525.4 4.3 collective-permute-done.66
  531.0 4.4 collective-permute-done.67
  547.0 9.5 %collective-permute-done.71 = bf16[2,192,384]{2,1,0:T(8,128)(2,1)S(1)} collective-permute-done((bf16[2,192,384]{2,1,0:T(8,128)(2,1)}, bf16[2,192,384]{2,1,0:T(8,128)(2,1)S(1)}, u32[]{:S(2)}, u32[]{:S(2)}) %collective-permute-start.71) | collective-permute-done | bytes 294944 | tf_op jit(solution)/shard_map/ppermute | solution.py:21
  556.5 20.3 %collective-permute-done.72 = bf16[2,192,384]{2,1,0:T(8,128)(2,1)S(1)} collective-permute-done((bf16[2,192,384]{2,1,0:T(8,128)(2,1)}, bf16[2,192,384]{2,1,0:T(8,128)(2,1)S(1)}, u32[]{:S(2)}, u32[]{:S(2)}) %collective-permute-start.72) | collective-permute-done | bytes 294944 | tf_op jit(solution)/shard_map/ppermute | solution.py:21
  578.2 2.4 add_bitcast_fusion.1
  581.9 2.1 fusion.32
  584.0 2.2 add_bitcast_fusion
  (511 shorter events, 140.6 us)
Async XLA Ops:
  2.6 25.9 %collective-permute-start.2 = (bf16[2,192,384]{2,1,0:T(8,128)(2,1)}, bf16[2,192,384]{2,1,0:T(8,128)(2,1)S(1)}, u32[]{:S(2)}, u32[]{:S(2)}) collective-permute-start(bf16[2,192,384]{2,1,0:T(8,128)(2,1)} %bitcast.103), channel_id=1, source_target_pairs={{0,3},{1,0},{2,1},{3,2},{4,7},{5,4},{6,5},{7,6},{8,11},{9,8},{10,9... | collective-permute-start | bytes 884744 | tf_op jit(solution)/shard_map/ppermute | solution.py:21
  7.6 25.4 %collective-permute-start.1 = (bf16[2,192,384]{2,1,0:T(8,128)(2,1)}, bf16[2,192,384]{2,1,0:T(8,128)(2,1)}, u32[]{:S(2)}, u32[]{:S(2)}) collective-permute-start(bf16[2,192,384]{2,1,0:T(8,128)(2,1)} %bitcast.103), channel_id=1, source_target_pairs={{0,2},{1,3},{2,0},{3,1},{4,6},{5,7},{6,4},{7,5},{8,10},{9,11},{10,... | collective-permute-start | bytes 884744 | tf_op jit(solution)/shard_map/ppermute | solution.py:21
  7.6 25.4 %collective-permute-start = (bf16[2,192,384]{2,1,0:T(8,128)(2,1)}, bf16[2,192,384]{2,1,0:T(8,128)(2,1)}, u32[]{:S(2)}, u32[]{:S(2)}) collective-permute-start(bf16[2,192,384]{2,1,0:T(8,128)(2,1)} %bitcast.103), channel_id=1, source_target_pairs={{0,1},{1,2},{2,3},{3,0},{4,5},{5,6},{6,7},{7,4},{8,9},{9,10},{10,1... | collective-permute-start | bytes 884744 | tf_op jit(solution)/shard_map/ppermute | solution.py:21
  36.0 11.4 %collective-permute-start.6 = (bf16[1,3,192,384]{3,2,1,0:T(8,128)(2,1)}, bf16[1,3,192,384]{3,2,1,0:T(8,128)(2,1)}, u32[]{:S(2)}, u32[]{:S(2)}) collective-permute-start(bf16[1,3,192,384]{3,2,1,0:T(8,128)(2,1)} %maximum_bitcast_fusion), channel_id=1, source_target_pairs={{0,8},{4,12},{8,0},{12,4},{16,24},{20,28},{24,16},{28,20},{1,9},{5... | collective-permute-start | bytes 1327112 | tf_op jit(solution)/shard_map/ppermute | solution.py:43
  41.8 27.6 %collective-permute-start.9 = (bf16[2,192,384]{2,1,0:T(8,128)(2,1)S(1)}, bf16[2,192,384]{2,1,0:T(8,128)(2,1)S(1)}, u32[]{:S(2)}, u32[]{:S(2)}) collective-permute-start(bf16[2,192,384]{2,1,0:T(8,128)(2,1)S(1)} %pad_maximum_fusion.9), channel_id=1, source_target_pairs={{0,2},{1,3},{2,0},{3,1},{4,6},{5,7},{6,4},{7,5},{8,10},{9,11},{10,... | collective-permute-start | bytes 884744 | tf_op jit(solution)/shard_map/ppermute | solution.py:21
  44.7 24.7 %collective-permute-start.8 = (bf16[2,192,384]{2,1,0:T(8,128)(2,1)S(1)}, bf16[2,192,384]{2,1,0:T(8,128)(2,1)S(1)}, u32[]{:S(2)}, u32[]{:S(2)}) collective-permute-start(bf16[2,192,384]{2,1,0:T(8,128)(2,1)S(1)} %pad_maximum_fusion.9), channel_id=1, source_target_pairs={{0,1},{1,2},{2,3},{3,0},{4,5},{5,6},{6,7},{7,4},{8,9},{9,10},{10,1... | collective-permute-start | bytes 884744 | tf_op jit(solution)/shard_map/ppermute | solution.py:21
  70.1 19.9 %collective-permute-start.14 = (bf16[2,3,192,384]{3,2,1,0:T(8,128)(2,1)}, bf16[2,3,192,384]{3,2,1,0:T(8,128)(2,1)}, u32[]{:S(2)}, u32[]{:S(2)}) collective-permute-start(bf16[2,3,192,384]{3,2,1,0:T(8,128)(2,1)} %pad_maximum_fusion.5), channel_id=1, source_target_pairs={{0,16},{4,20},{8,24},{12,28},{16,0},{20,4},{24,8},{28,12},{1,17},{... | collective-permute-start | bytes 2654216 | tf_op jit(solution)/shard_map/ppermute | solution.py:43
  70.6 22.2 %collective-permute-start.15 = (bf16[2,3,192,384]{3,2,1,0:T(8,128)(2,1)}, bf16[2,3,192,384]{3,2,1,0:T(8,128)(2,1)}, u32[]{:S(2)}, u32[]{:S(2)}) collective-permute-start(bf16[2,3,192,384]{3,2,1,0:T(8,128)(2,1)} %pad_maximum_fusion.6), channel_id=1, source_target_pairs={{0,8},{4,12},{8,0},{12,4},{16,24},{20,28},{24,16},{28,20},{1,9},{5... | collective-permute-start | bytes 2654216 | tf_op jit(solution)/shard_map/ppermute | solution.py:43
  91.4 16.1 %collective-permute-start.18 = (bf16[4,3,192,384]{3,2,1,0:T(8,128)(2,1)S(1)}, bf16[4,3,192,384]{3,2,1,0:T(8,128)(2,1)S(1)}, u32[]{:S(2)}, u32[]{:S(2)}) collective-permute-start(bf16[4,3,192,384]{3,2,1,0:T(8,128)(2,1)S(1)} %constant_dynamic-update-slice_fusion.refs_1_), channel_id=1, source_target_pairs={{0,4},{4,0},{8,12},{12,8},{16,20},{20,16},{24,28},{28,24},{1,5},{5... | collective-permute-start | bytes 5308424 | tf_op jit(solution)/shard_map/ppermute | solution.py:43
  94.2 25.5 %collective-permute-start.21 = (bf16[4,3,192,384]{3,2,1,0:T(8,128)(2,1)S(1)}, bf16[4,3,192,384]{3,2,1,0:T(8,128)(2,1)S(1)}, u32[]{:S(2)}, u32[]{:S(2)}) collective-permute-start(bf16[4,3,192,384]{3,2,1,0:T(8,128)(2,1)S(1)} %constant_dynamic-update-slice_fusion.2.refs_1_), channel_id=1, source_target_pairs={{0,4},{4,0},{8,12},{12,8},{16,20},{20,16},{24,28},{28,24},{1,5},{5... | collective-permute-start | bytes 5308424 | tf_op jit(solution)/shard_map/ppermute | solution.py:43
  94.9 12.2 %collective-permute-start.16 = (bf16[1,3,192,384]{3,2,1,0:T(8,128)(2,1)S(1)}, bf16[1,3,192,384]{3,2,1,0:T(8,128)(2,1)S(1)}, u32[]{:S(2)}, u32[]{:S(2)}) collective-permute-start(bf16[1,3,192,384]{3,2,1,0:T(8,128)(2,1)S(1)} %maximum_bitcast_fusion.2), channel_id=1, source_target_pairs={{0,8},{4,12},{8,0},{12,4},{16,24},{20,28},{24,16},{28,20},{1,9},{5... | collective-permute-start | bytes 1327112 | tf_op jit(solution)/shard_map/ppermute | solution.py:43
  95.5 11.8 %collective-permute-start.17 = (bf16[1,3,192,384]{3,2,1,0:T(8,128)(2,1)S(1)}, bf16[1,3,192,384]{3,2,1,0:T(8,128)(2,1)S(1)}, u32[]{:S(2)}, u32[]{:S(2)}) collective-permute-start(bf16[1,3,192,384]{3,2,1,0:T(8,128)(2,1)S(1)} %maximum_bitcast_fusion.3), channel_id=1, source_target_pairs={{0,16},{4,20},{8,24},{12,28},{16,0},{20,4},{24,8},{28,12},{1,17},{... | collective-permute-start | bytes 1327112 | tf_op jit(solution)/shard_map/ppermute | solution.py:43
  115.6 20.6 %collective-permute-start.19 = (bf16[2,3,192,384]{3,2,1,0:T(8,128)(2,1)S(1)}, bf16[2,3,192,384]{3,2,1,0:T(8,128)(2,1)S(1)}, u32[]{:S(2)}, u32[]{:S(2)}) collective-permute-start(bf16[2,3,192,384]{3,2,1,0:T(8,128)(2,1)S(1)} %pad_maximum_fusion.7), channel_id=1, source_target_pairs={{0,16},{4,20},{8,24},{12,28},{16,0},{20,4},{24,8},{28,12},{1,17},{... | collective-permute-start | bytes 2654216 | tf_op jit(solution)/shard_map/ppermute | solution.py:43
  116.2 20.4 %collective-permute-start.20 = (bf16[2,3,192,384]{3,2,1,0:T(8,128)(2,1)S(1)}, bf16[2,3,192,384]{3,2,1,0:T(8,128)(2,1)S(1)}, u32[]{:S(2)}, u32[]{:S(2)}) collective-permute-start(bf16[2,3,192,384]{3,2,1,0:T(8,128)(2,1)S(1)} %pad_maximum_fusion.8), channel_id=1, source_target_pairs={{0,8},{4,12},{8,0},{12,4},{16,24},{20,28},{24,16},{28,20},{1,9},{5... | collective-permute-start | bytes 2654216 | tf_op jit(solution)/shard_map/ppermute | solution.py:43
  118.5 18.8 %collective-permute-start.13 = (bf16[128,1536]{1,0:T(8,128)(2,1)S(1)}, bf16[128,1536]{1,0:T(8,128)(2,1)S(1)}, u32[]{:S(2)}, u32[]{:S(2)}) collective-permute-start(bf16[128,1536]{1,0:T(8,128)(2,1)S(1)} %bitcast.104), channel_id=1, source_target_pairs={{0,3},{1,0},{2,1},{3,2},{4,7},{5,4},{6,5},{7,6},{8,11},{9,8},{10,9... | collective-permute-start | bytes 1179656 | tf_op jit(solution)/shard_map/ppermute | solution.py:21
  118.5 34.0 %collective-permute-start.12 = (bf16[128,1536]{1,0:T(8,128)(2,1)S(1)}, bf16[128,1536]{1,0:T(8,128)(2,1)S(1)}, u32[]{:S(2)}, u32[]{:S(2)}) collective-permute-start(bf16[128,1536]{1,0:T(8,128)(2,1)S(1)} %bitcast.105), channel_id=1, source_target_pairs={{0,2},{1,3},{2,0},{3,1},{4,6},{5,7},{6,4},{7,5},{8,10},{9,11},{10,... | collective-permute-start | bytes 1179656 | tf_op jit(solution)/shard_map/ppermute | solution.py:21
  119.7 32.9 %collective-permute-start.11 = (bf16[128,1536]{1,0:T(8,128)(2,1)S(1)}, bf16[128,1536]{1,0:T(8,128)(2,1)S(1)}, u32[]{:S(2)}, u32[]{:S(2)}) collective-permute-start(bf16[128,1536]{1,0:T(8,128)(2,1)S(1)} %bitcast.106), channel_id=1, source_target_pairs={{0,1},{1,2},{2,3},{3,0},{4,5},{5,6},{6,7},{7,4},{8,9},{9,10},{10,1... | collective-permute-start | bytes 1179656 | tf_op jit(solution)/shard_map/ppermute | solution.py:21
  136.7 21.3 %collective-permute-start.22 = (bf16[4,3,192,384]{3,2,1,0:T(8,128)(2,1)S(1)}, bf16[4,3,192,384]{3,2,1,0:T(8,128)(2,1)S(1)}, u32[]{:S(2)}, u32[]{:S(2)}) collective-permute-start(bf16[4,3,192,384]{3,2,1,0:T(8,128)(2,1)S(1)} %pad_maximum_fusion.1.refs_1_.refs_0_), channel_id=1, source_target_pairs={{0,4},{4,0},{8,12},{12,8},{16,20},{20,16},{24,28},{28,24},{1,5},{5... | collective-permute-start | bytes 5308424 | tf_op jit(solution)/shard_map/ppermute | solution.py:43
  136.8 21.3 %collective-permute-start.23 = (bf16[4,3,192,384]{3,2,1,0:T(8,128)(2,1)S(1)}, bf16[4,3,192,384]{3,2,1,0:T(8,128)(2,1)}, u32[]{:S(2)}, u32[]{:S(2)}) collective-permute-start(bf16[4,3,192,384]{3,2,1,0:T(8,128)(2,1)S(1)} %pad_maximum_fusion.2.refs_3_.refs_2_), channel_id=1, source_target_pairs={{0,4},{4,0},{8,12},{12,8},{16,20},{20,16},{24,28},{28,24},{1,5},{5... | collective-permute-start | bytes 5308424 | tf_op jit(solution)/shard_map/ppermute | solution.py:43
  154.1 36.2 %collective-permute-start.26 = (bf16[128,1536]{1,0:T(8,128)(2,1)S(1)}, bf16[128,1536]{1,0:T(8,128)(2,1)S(1)}, u32[]{:S(2)}, u32[]{:S(2)}) collective-permute-start(bf16[128,1536]{1,0:T(8,128)(2,1)S(1)} %bitcast.115), channel_id=1, source_target_pairs={{0,3},{1,0},{2,1},{3,2},{4,7},{5,4},{6,5},{7,6},{8,11},{9,8},{10,9... | collective-permute-start | bytes 1179656 | tf_op jit(solution)/shard_map/ppermute | solution.py:21
  154.2 36.3 %collective-permute-start.25 = (bf16[128,1536]{1,0:T(8,128)(2,1)S(1)}, bf16[128,1536]{1,0:T(8,128)(2,1)S(1)}, u32[]{:S(2)}, u32[]{:S(2)}) collective-permute-start(bf16[128,1536]{1,0:T(8,128)(2,1)S(1)} %bitcast.116), channel_id=1, source_target_pairs={{0,2},{1,3},{2,0},{3,1},{4,6},{5,7},{6,4},{7,5},{8,10},{9,11},{10,... | collective-permute-start | bytes 1179656 | tf_op jit(solution)/shard_map/ppermute | solution.py:21
  156.0 34.5 %collective-permute-start.24 = (bf16[128,1536]{1,0:T(8,128)(2,1)S(1)}, bf16[128,1536]{1,0:T(8,128)(2,1)S(1)}, u32[]{:S(2)}, u32[]{:S(2)}) collective-permute-start(bf16[128,1536]{1,0:T(8,128)(2,1)S(1)} %bitcast.117), channel_id=1, source_target_pairs={{0,1},{1,2},{2,3},{3,0},{4,5},{5,6},{6,7},{7,4},{8,9},{9,10},{10,1... | collective-permute-start | bytes 1179656 | tf_op jit(solution)/shard_map/ppermute | solution.py:21
  190.5 12.0 %collective-permute-start.27 = (bf16[1632,128]{1,0:T(8,128)(2,1)S(1)}, bf16[1632,128]{1,0:T(8,128)(2,1)S(1)}, u32[]{:S(2)}, u32[]{:S(2)}) collective-permute-start(bf16[1632,128]{1,0:T(8,128)(2,1)S(1)} %get-tuple-element.197), channel_id=1, source_target_pairs={{0,3},{1,0},{2,1},{3,2},{4,7},{5,4},{6,5},{7,6},{8,11},{9,8},{10,9... | collective-permute-start | bytes 1253384 | tf_op jit(solution)/shard_map/ppermute | solution.py:21
  192.3 35.4 %collective-permute-start.28 = (bf16[1632,128]{1,0:T(8,128)(2,1)S(1)}, bf16[1632,128]{1,0:T(8,128)(2,1)S(1)}, u32[]{:S(2)}, u32[]{:S(2)}) collective-permute-start(bf16[1632,128]{1,0:T(8,128)(2,1)S(1)} %get-tuple-element.198), channel_id=1, source_target_pairs={{0,2},{1,3},{2,0},{3,1},{4,6},{5,7},{6,4},{7,5},{8,10},{9,11},{10,... | collective-permute-start | bytes 1253384 | tf_op jit(solution)/shard_map/ppermute | solution.py:21
  192.3 35.4 %collective-permute-start.29 = (bf16[1632,128]{1,0:T(8,128)(2,1)S(1)}, bf16[1632,128]{1,0:T(8,128)(2,1)S(1)}, u32[]{:S(2)}, u32[]{:S(2)}) collective-permute-start(bf16[1632,128]{1,0:T(8,128)(2,1)S(1)} %get-tuple-element.199), channel_id=1, source_target_pairs={{0,1},{1,2},{2,3},{3,0},{4,5},{5,6},{6,7},{7,4},{8,9},{9,10},{10,1... | collective-permute-start | bytes 1253384 | tf_op jit(solution)/shard_map/ppermute | solution.py:21
  232.2 36.2 %collective-permute-start.31 = (bf16[128,1536]{1,0:T(8,128)(2,1)S(1)}, bf16[128,1536]{1,0:T(8,128)(2,1)S(1)}, u32[]{:S(2)}, u32[]{:S(2)}) collective-permute-start(bf16[128,1536]{1,0:T(8,128)(2,1)S(1)} %add_convert_fusion.1), channel_id=1, source_target_pairs={{0,2},{1,3},{2,0},{3,1},{4,6},{5,7},{6,4},{7,5},{8,10},{9,11},{10,... | collective-permute-start | bytes 1179656 | tf_op jit(solution)/shard_map/ppermute | solution.py:21
  234.8 33.6 %collective-permute-start.30 = (bf16[128,1536]{1,0:T(8,128)(2,1)S(1)}, bf16[128,1536]{1,0:T(8,128)(2,1)S(1)}, u32[]{:S(2)}, u32[]{:S(2)}) collective-permute-start(bf16[128,1536]{1,0:T(8,128)(2,1)S(1)} %add_convert_fusion.1), channel_id=1, source_target_pairs={{0,1},{1,2},{2,3},{3,0},{4,5},{5,6},{6,7},{7,4},{8,9},{9,10},{10,1... | collective-permute-start | bytes 1179656 | tf_op jit(solution)/shard_map/ppermute | solution.py:21
  282.7 31.9 %collective-permute-start.35 = (bf16[128,1536]{1,0:T(8,128)(2,1)}, bf16[128,1536]{1,0:T(8,128)(2,1)}, u32[]{:S(2)}, u32[]{:S(2)}) collective-permute-start(bf16[128,1536]{1,0:T(8,128)(2,1)} %get-tuple-element.388), channel_id=1, source_target_pairs={{0,1},{1,2},{2,3},{3,0},{4,5},{5,6},{6,7},{7,4},{8,9},{9,10},{10,1... | collective-permute-start | bytes 1179656 | tf_op jit(solution)/shard_map/ppermute | solution.py:21
  282.7 31.9 %collective-permute-start.34 = (bf16[128,1536]{1,0:T(8,128)(2,1)}, bf16[128,1536]{1,0:T(8,128)(2,1)}, u32[]{:S(2)}, u32[]{:S(2)}) collective-permute-start(bf16[128,1536]{1,0:T(8,128)(2,1)} %get-tuple-element.389), channel_id=1, source_target_pairs={{0,2},{1,3},{2,0},{3,1},{4,6},{5,7},{6,4},{7,5},{8,10},{9,11},{10,... | collective-permute-start | bytes 1179656 | tf_op jit(solution)/shard_map/ppermute | solution.py:21
  282.7 31.9 %collective-permute-start.33 = (bf16[128,1536]{1,0:T(8,128)(2,1)}, bf16[128,1536]{1,0:T(8,128)(2,1)}, u32[]{:S(2)}, u32[]{:S(2)}) collective-permute-start(bf16[128,1536]{1,0:T(8,128)(2,1)} %get-tuple-element.390), channel_id=1, source_target_pairs={{0,3},{1,0},{2,1},{3,2},{4,7},{5,4},{6,5},{7,6},{8,11},{9,8},{10,9... | collective-permute-start | bytes 1179656 | tf_op jit(solution)/shard_map/ppermute | solution.py:21
  308.8 25.7 %collective-permute-start.39 = (bf16[4,192,1536]{2,1,0:T(8,128)(2,1)}, bf16[4,192,1536]{2,1,0:T(8,128)(2,1)}, u32[]{:S(2)}, u32[]{:S(2)}) collective-permute-start(bf16[4,192,1536]{2,1,0:T(8,128)(2,1)} %get-tuple-element.210), channel_id=1, source_target_pairs={{0,4},{4,0},{8,12},{12,8},{16,20},{20,16},{24,28},{28,24},{1,5},{5... | collective-permute-start | bytes 7077896 | tf_op jit(solution)/shard_map/ppermute | solution.py:43
  314.1 21.1 %collective-permute-start.40 = (bf16[4,192,1536]{2,1,0:T(8,128)(2,1)}, bf16[4,192,1536]{2,1,0:T(8,128)(2,1)}, u32[]{:S(2)}, u32[]{:S(2)}) collective-permute-start(bf16[4,192,1536]{2,1,0:T(8,128)(2,1)} %get-tuple-element.212), channel_id=1, source_target_pairs={{0,4},{4,0},{8,12},{12,8},{16,20},{20,16},{24,28},{28,24},{1,5},{5... | collective-permute-start | bytes 7077896 | tf_op jit(solution)/shard_map/ppermute | solution.py:43
  323.2 12.0 %collective-permute-start.41 = (bf16[4,192,1536]{2,1,0:T(8,128)(2,1)S(1)}, bf16[4,192,1536]{2,1,0:T(8,128)(2,1)S(1)}, u32[]{:S(2)}, u32[]{:S(2)}) collective-permute-start(bf16[4,192,1536]{2,1,0:T(8,128)(2,1)S(1)} %get-tuple-element.220), channel_id=1, source_target_pairs={{0,4},{4,0},{8,12},{12,8},{16,20},{20,16},{24,28},{28,24},{1,5},{5... | collective-permute-start | bytes 7077896 | tf_op jit(solution)/shard_map/ppermute | solution.py:43
  329.2 17.1 %collective-permute-start.38 = (bf16[1632,128]{1,0:T(8,128)(2,1)S(1)}, bf16[1632,128]{1,0:T(8,128)(2,1)S(1)}, u32[]{:S(2)}, u32[]{:S(2)}) collective-permute-start(bf16[1632,128]{1,0:T(8,128)(2,1)S(1)} %shard_map.280.rest_0_.rest_4_), channel_id=1, source_target_pairs={{0,3},{1,0},{2,1},{3,2},{4,7},{5,4},{6,5},{7,6},{8,11},{9,8},{10,9... | collective-permute-start | bytes 1253384 | tf_op jit(solution)/shard_map/ppermute | solution.py:21
  333.7 37.7 %collective-permute-start.37 = (bf16[1632,128]{1,0:T(8,128)(2,1)S(1)}, bf16[1632,128]{1,0:T(8,128)(2,1)S(1)}, u32[]{:S(2)}, u32[]{:S(2)}) collective-permute-start(bf16[1632,128]{1,0:T(8,128)(2,1)S(1)} %shard_map.280.rest_0_.rest_4_), channel_id=1, source_target_pairs={{0,2},{1,3},{2,0},{3,1},{4,6},{5,7},{6,4},{7,5},{8,10},{9,11},{10,... | collective-permute-start | bytes 1253384 | tf_op jit(solution)/shard_map/ppermute | solution.py:21
  334.5 36.8 %collective-permute-start.36 = (bf16[1632,128]{1,0:T(8,128)(2,1)S(1)}, bf16[1632,128]{1,0:T(8,128)(2,1)S(1)}, u32[]{:S(2)}, u32[]{:S(2)}) collective-permute-start(bf16[1632,128]{1,0:T(8,128)(2,1)S(1)} %shard_map.280.rest_0_.rest_4_), channel_id=1, source_target_pairs={{0,1},{1,2},{2,3},{3,0},{4,5},{5,6},{6,7},{7,4},{8,9},{9,10},{10,1... | collective-permute-start | bytes 1253384 | tf_op jit(solution)/shard_map/ppermute | solution.py:21
  339.6 60.0 %collective-permute-start.45 = (bf16[2,192,2304]{2,1,0:T(8,128)(2,1)S(1)}, bf16[2,192,2304]{2,1,0:T(8,128)(2,1)}, u32[]{:S(2)}, u32[]{:S(2)}) collective-permute-start(bf16[2,192,2304]{2,1,0:T(8,128)(2,1)S(1)} %get-tuple-element.224), channel_id=1, source_target_pairs={{0,8},{4,12},{8,0},{12,4},{16,24},{20,28},{24,16},{28,20},{1,9},{5... | collective-permute-start | bytes 5308424 | tf_op jit(solution)/shard_map/ppermute | solution.py:43
  344.7 58.6 %collective-permute-start.46 = (bf16[2,192,2304]{2,1,0:T(8,128)(2,1)}, bf16[2,192,2304]{2,1,0:T(8,128)(2,1)S(1)}, u32[]{:S(2)}, u32[]{:S(2)}) collective-permute-start(bf16[2,192,2304]{2,1,0:T(8,128)(2,1)} %copy-done.74), channel_id=1, source_target_pairs={{0,16},{4,20},{8,24},{12,28},{16,0},{20,4},{24,8},{28,12},{1,17},{... | collective-permute-start | bytes 5308424 | tf_op jit(solution)/shard_map/ppermute | solution.py:43
  371.4 50.5 %collective-permute-start.42 = (bf16[128,1536]{1,0:T(8,128)(2,1)}, bf16[128,1536]{1,0:T(8,128)(2,1)S(1)}, u32[]{:S(2)}, u32[]{:S(2)}) collective-permute-start(bf16[128,1536]{1,0:T(8,128)(2,1)} %copy-done.79), channel_id=1, source_target_pairs={{0,3},{1,0},{2,1},{3,2},{4,7},{5,4},{6,5},{7,6},{8,11},{9,8},{10,9... | collective-permute-start | bytes 1179656 | tf_op jit(solution)/shard_map/ppermute | solution.py:21
  371.4 50.5 %collective-permute-start.43 = (bf16[128,1536]{1,0:T(8,128)(2,1)S(1)}, bf16[128,1536]{1,0:T(8,128)(2,1)}, u32[]{:S(2)}, u32[]{:S(2)}) collective-permute-start(bf16[128,1536]{1,0:T(8,128)(2,1)S(1)} %copy-done.78), channel_id=1, source_target_pairs={{0,2},{1,3},{2,0},{3,1},{4,6},{5,7},{6,4},{7,5},{8,10},{9,11},{10,... | collective-permute-start | bytes 1179656 | tf_op jit(solution)/shard_map/ppermute | solution.py:21
  372.7 49.2 %collective-permute-start.44 = (bf16[128,1536]{1,0:T(8,128)(2,1)S(1)}, bf16[128,1536]{1,0:T(8,128)(2,1)}, u32[]{:S(2)}, u32[]{:S(2)}) collective-permute-start(bf16[128,1536]{1,0:T(8,128)(2,1)S(1)} %copy-done.76), channel_id=1, source_target_pairs={{0,1},{1,2},{2,3},{3,0},{4,5},{5,6},{6,7},{7,4},{8,9},{9,10},{10,1... | collective-permute-start | bytes 1179656 | tf_op jit(solution)/shard_map/ppermute | solution.py:21
  427.1 15.0 %collective-permute-start.47 = (bf16[4,192,1536]{2,1,0:T(8,128)(2,1)}, bf16[4,192,1536]{2,1,0:T(8,128)(2,1)S(1)}, u32[]{:S(2)}, u32[]{:S(2)}) collective-permute-start(bf16[4,192,1536]{2,1,0:T(8,128)(2,1)} %get-tuple-element.253), channel_id=1, source_target_pairs={{0,4},{4,0},{8,12},{12,8},{16,20},{20,16},{24,28},{28,24},{1,5},{5... | collective-permute-start | bytes 7077896 | tf_op jit(solution)/shard_map/ppermute | solution.py:43
  427.1 15.0 %collective-permute-start.48 = (bf16[4,192,1536]{2,1,0:T(8,128)(2,1)}, bf16[4,192,1536]{2,1,0:T(8,128)(2,1)}, u32[]{:S(2)}, u32[]{:S(2)}) collective-permute-start(bf16[4,192,1536]{2,1,0:T(8,128)(2,1)} %get-tuple-element.254), channel_id=1, source_target_pairs={{0,4},{4,0},{8,12},{12,8},{16,20},{20,16},{24,28},{28,24},{1,5},{5... | collective-permute-start | bytes 7077896 | tf_op jit(solution)/shard_map/ppermute | solution.py:43
  427.6 14.5 %collective-permute-start.49 = (bf16[4,192,1536]{2,1,0:T(8,128)(2,1)}, bf16[4,192,1536]{2,1,0:T(8,128)(2,1)S(1)}, u32[]{:S(2)}, u32[]{:S(2)}) collective-permute-start(bf16[4,192,1536]{2,1,0:T(8,128)(2,1)} %get-tuple-element.252), channel_id=1, source_target_pairs={{0,4},{4,0},{8,12},{12,8},{16,20},{20,16},{24,28},{28,24},{1,5},{5... | collective-permute-start | bytes 7077896 | tf_op jit(solution)/shard_map/ppermute | solution.py:43
  427.6 28.0 %collective-permute-start.52 = (bf16[1,192,2304]{2,1,0:T(8,128)(2,1)}, bf16[1,192,2304]{2,1,0:T(8,128)(2,1)}, u32[]{:S(2)}, u32[]{:S(2)}) collective-permute-start(bf16[1,192,2304]{2,1,0:T(8,128)(2,1)} %get-tuple-element.240), channel_id=1, source_target_pairs={{0,16},{4,20},{8,24},{12,28},{16,0},{20,4},{24,8},{28,12},{1,17},{... | collective-permute-start | bytes 2654216 | tf_op jit(solution)/shard_map/ppermute | solution.py:43
  429.1 26.5 %collective-permute-start.53 = (bf16[1,192,2304]{2,1,0:T(8,128)(2,1)}, bf16[1,192,2304]{2,1,0:T(8,128)(2,1)}, u32[]{:S(2)}, u32[]{:S(2)}) collective-permute-start(bf16[1,192,2304]{2,1,0:T(8,128)(2,1)} %get-tuple-element.242), channel_id=1, source_target_pairs={{0,8},{4,12},{8,0},{12,4},{16,24},{20,28},{24,16},{28,20},{1,9},{5... | collective-permute-start | bytes 2654216 | tf_op jit(solution)/shard_map/ppermute | solution.py:43
  448.1 30.0 %collective-permute-start.51 = (bf16[2,192,1536]{2,1,0:T(8,128)(2,1)}, bf16[2,192,1536]{2,1,0:T(8,128)(2,1)}, u32[]{:S(2)}, u32[]{:S(2)}) collective-permute-start(bf16[2,192,1536]{2,1,0:T(8,128)(2,1)} %get-tuple-element.266), channel_id=1, source_target_pairs={{0,16},{4,20},{8,24},{12,28},{16,0},{20,4},{24,8},{28,12},{1,17},{... | collective-permute-start | bytes 3538952 | tf_op jit(solution)/shard_map/ppermute | solution.py:43
  452.5 27.9 %collective-permute-start.50 = (bf16[2,192,1536]{2,1,0:T(8,128)(2,1)}, bf16[2,192,1536]{2,1,0:T(8,128)(2,1)}, u32[]{:S(2)}, u32[]{:S(2)}) collective-permute-start(bf16[2,192,1536]{2,1,0:T(8,128)(2,1)} %get-tuple-element.263), channel_id=1, source_target_pairs={{0,8},{4,12},{8,0},{12,4},{16,24},{20,28},{24,16},{28,20},{1,9},{5... | collective-permute-start | bytes 3538952 | tf_op jit(solution)/shard_map/ppermute | solution.py:43
  453.8 35.6 %collective-permute-start.54 = (bf16[128,1536]{1,0:T(8,128)(2,1)}, bf16[128,1536]{1,0:T(8,128)(2,1)S(1)}, u32[]{:S(2)}, u32[]{:S(2)}) collective-permute-start(bf16[128,1536]{1,0:T(8,128)(2,1)} %copy-done.80), channel_id=1, source_target_pairs={{0,3},{1,0},{2,1},{3,2},{4,7},{5,4},{6,5},{7,6},{8,11},{9,8},{10,9... | collective-permute-start | bytes 1179656 | tf_op jit(solution)/shard_map/ppermute | solution.py:21
  455.6 34.1 %collective-permute-start.55 = (bf16[128,1536]{1,0:T(8,128)(2,1)S(1)}, bf16[128,1536]{1,0:T(8,128)(2,1)}, u32[]{:S(2)}, u32[]{:S(2)}) collective-permute-start(bf16[128,1536]{1,0:T(8,128)(2,1)S(1)} %get-tuple-element.289), channel_id=1, source_target_pairs={{0,2},{1,3},{2,0},{3,1},{4,6},{5,7},{6,4},{7,5},{8,10},{9,11},{10,... | collective-permute-start | bytes 1179656 | tf_op jit(solution)/shard_map/ppermute | solution.py:21
  455.6 34.1 %collective-permute-start.56 = (bf16[128,1536]{1,0:T(8,128)(2,1)S(1)}, bf16[128,1536]{1,0:T(8,128)(2,1)}, u32[]{:S(2)}, u32[]{:S(2)}) collective-permute-start(bf16[128,1536]{1,0:T(8,128)(2,1)S(1)} %get-tuple-element.290), channel_id=1, source_target_pairs={{0,1},{1,2},{2,3},{3,0},{4,5},{5,6},{6,7},{7,4},{8,9},{9,10},{10,1... | collective-permute-start | bytes 1179656 | tf_op jit(solution)/shard_map/ppermute | solution.py:21
  483.6 16.6 %collective-permute-start.60 = (bf16[1,192,1536]{2,1,0:T(8,128)(2,1)}, bf16[1,192,1536]{2,1,0:T(8,128)(2,1)}, u32[]{:S(2)}, u32[]{:S(2)}) collective-permute-start(bf16[1,192,1536]{2,1,0:T(8,128)(2,1)} %get-tuple-element.284), channel_id=1, source_target_pairs={{0,8},{4,12},{8,0},{12,4},{16,24},{20,28},{24,16},{28,20},{1,9},{5... | collective-permute-start | bytes 1769480 | tf_op jit(solution)/shard_map/ppermute | solution.py:43
  487.9 16.6 %collective-permute-start.59 = (bf16[1,192,1536]{2,1,0:T(8,128)(2,1)}, bf16[1,192,1536]{2,1,0:T(8,128)(2,1)}, u32[]{:S(2)}, u32[]{:S(2)}) collective-permute-start(bf16[1,192,1536]{2,1,0:T(8,128)(2,1)} %get-tuple-element.281), channel_id=1, source_target_pairs={{0,16},{4,20},{8,24},{12,28},{16,0},{20,4},{24,8},{28,12},{1,17},{... | collective-permute-start | bytes 1769480 | tf_op jit(solution)/shard_map/ppermute | solution.py:43
  489.7 21.2 %collective-permute-start.57 = (bf16[2,192,768]{2,1,0:T(8,128)(2,1)}, bf16[2,192,768]{2,1,0:T(8,128)(2,1)S(1)}, u32[]{:S(2)}, u32[]{:S(2)}) collective-permute-start(bf16[2,192,768]{2,1,0:T(8,128)(2,1)} %get-tuple-element.291), channel_id=1, source_target_pairs={{0,8},{4,12},{8,0},{12,4},{16,24},{20,28},{24,16},{28,20},{1,9},{5... | collective-permute-start | bytes 1769480 | tf_op jit(solution)/shard_map/ppermute | solution.py:43
  490.4 24.1 %collective-permute-start.58 = (bf16[2,192,768]{2,1,0:T(8,128)(2,1)}, bf16[2,192,768]{2,1,0:T(8,128)(2,1)S(1)}, u32[]{:S(2)}, u32[]{:S(2)}) collective-permute-start(bf16[2,192,768]{2,1,0:T(8,128)(2,1)} %get-tuple-element.292), channel_id=1, source_target_pairs={{0,16},{4,20},{8,24},{12,28},{16,0},{20,4},{24,8},{28,12},{1,17},{... | collective-permute-start | bytes 1769480 | tf_op jit(solution)/shard_map/ppermute | solution.py:43
  494.6 24.5 %collective-permute-start.64 = (f32[8,1536]{1,0:T(8,128)S(1)}, f32[8,1536]{1,0:T(8,128)S(1)}, u32[]{:S(2)}, u32[]{:S(2)}) collective-permute-start(f32[8,1536]{1,0:T(8,128)S(1)} %add.296), channel_id=1, source_target_pairs={{0,8},{4,12},{8,0},{12,4},{16,24},{20,28},{24,16},{28,20},{1,9},{5... | collective-permute-start | bytes 147464 | tf_op jit(solution)/shard_map/ppermute | solution.py:43
  516.0 24.5 %collective-permute-start.62 = (bf16[1,192,768]{2,1,0:T(8,128)(2,1)}, bf16[1,192,768]{2,1,0:T(8,128)(2,1)S(1)}, u32[]{:S(2)}, u32[]{:S(2)}) collective-permute-start(bf16[1,192,768]{2,1,0:T(8,128)(2,1)} %get-tuple-element.305), channel_id=1, source_target_pairs={{0,8},{4,12},{8,0},{12,4},{16,24},{20,28},{24,16},{28,20},{1,9},{5... | collective-permute-start | bytes 884744 | tf_op jit(solution)/shard_map/ppermute | solution.py:43
  517.5 23.0 %collective-permute-start.61 = (bf16[1,192,768]{2,1,0:T(8,128)(2,1)}, bf16[1,192,768]{2,1,0:T(8,128)(2,1)S(1)}, u32[]{:S(2)}, u32[]{:S(2)}) collective-permute-start(bf16[1,192,768]{2,1,0:T(8,128)(2,1)} %get-tuple-element.301), channel_id=1, source_target_pairs={{0,16},{4,20},{8,24},{12,28},{16,0},{20,4},{24,8},{28,12},{1,17},{... | collective-permute-start | bytes 884744 | tf_op jit(solution)/shard_map/ppermute | solution.py:43
  537.9 18.6 %collective-permute-start.71 = (bf16[2,192,384]{2,1,0:T(8,128)(2,1)}, bf16[2,192,384]{2,1,0:T(8,128)(2,1)S(1)}, u32[]{:S(2)}, u32[]{:S(2)}) collective-permute-start(bf16[2,192,384]{2,1,0:T(8,128)(2,1)} %copy-done.83), channel_id=1, source_target_pairs={{0,3},{1,0},{2,1},{3,2},{4,7},{5,4},{6,5},{7,6},{8,11},{9,8},{10,9... | collective-permute-start | bytes 884744 | tf_op jit(solution)/shard_map/ppermute | solution.py:21
  538.8 38.0 %collective-permute-start.72 = (bf16[2,192,384]{2,1,0:T(8,128)(2,1)}, bf16[2,192,384]{2,1,0:T(8,128)(2,1)S(1)}, u32[]{:S(2)}, u32[]{:S(2)}) collective-permute-start(bf16[2,192,384]{2,1,0:T(8,128)(2,1)} %copy-done.82), channel_id=1, source_target_pairs={{0,2},{1,3},{2,0},{3,1},{4,6},{5,7},{6,4},{7,5},{8,10},{9,11},{10,... | collective-permute-start | bytes 884744 | tf_op jit(solution)/shard_map/ppermute | solution.py:21
  538.9 37.9 %collective-permute-start.73 = (bf16[2,192,384]{2,1,0:T(8,128)(2,1)}, bf16[2,192,384]{2,1,0:T(8,128)(2,1)S(1)}, u32[]{:S(2)}, u32[]{:S(2)}) collective-permute-start(bf16[2,192,384]{2,1,0:T(8,128)(2,1)} %copy-done.81), channel_id=1, source_target_pairs={{0,1},{1,2},{2,3},{3,0},{4,5},{5,6},{6,7},{7,4},{8,9},{9,10},{10,1... | collective-permute-start | bytes 884744 | tf_op jit(solution)/shard_map/ppermute | solution.py:21
  544.0 42.2 %collective-permute-start.70 = (bf16[2,192,384]{2,1,0:T(8,128)(2,1)S(1)}, bf16[2,192,384]{2,1,0:T(8,128)(2,1)S(1)}, u32[]{:S(2)}, u32[]{:S(2)}) collective-permute-start(bf16[2,192,384]{2,1,0:T(8,128)(2,1)S(1)} %pad_maximum_fusion.12), channel_id=1, source_target_pairs={{0,1},{1,2},{2,3},{3,0},{4,5},{5,6},{6,7},{7,4},{8,9},{9,10},{10,1... | collective-permute-start | bytes 884744 | tf_op jit(solution)/shard_map/ppermute | solution.py:21
  545.9 40.3 %collective-permute-start.69 = (bf16[2,192,384]{2,1,0:T(8,128)(2,1)S(1)}, bf16[2,192,384]{2,1,0:T(8,128)(2,1)S(1)}, u32[]{:S(2)}, u32[]{:S(2)}) collective-permute-start(bf16[2,192,384]{2,1,0:T(8,128)(2,1)S(1)} %pad_maximum_fusion.11), channel_id=1, source_target_pairs={{0,2},{1,3},{2,0},{3,1},{4,6},{5,7},{6,4},{7,5},{8,10},{9,11},{10,... | collective-permute-start | bytes 884744 | tf_op jit(solution)/shard_map/ppermute | solution.py:21
  556.5 29.8 %collective-permute-start.68 = (bf16[2,192,384]{2,1,0:T(8,128)(2,1)S(1)}, bf16[2,192,384]{2,1,0:T(8,128)(2,1)S(1)}, u32[]{:S(2)}, u32[]{:S(2)}) collective-permute-start(bf16[2,192,384]{2,1,0:T(8,128)(2,1)S(1)} %pad_maximum_fusion.10), channel_id=1, source_target_pairs={{0,3},{1,0},{2,1},{3,2},{4,7},{5,4},{6,5},{7,6},{8,11},{9,8},{10,9... | collective-permute-start | bytes 884744 | tf_op jit(solution)/shard_map/ppermute | solution.py:21
  (147 other events, 1522.3 us)

commit v4 on v3

--- a/solution.py
+++ b/solution.py
@@ -278,11 +278,11 @@
     return [rotate(x, count, k) for k in range(1, count)]
 
 
-def widen(one, two, step, orders, n_dp):
-    return [
-        jnp.concatenate([x, partner(x, "dp", n_dp, 1 << order[step])], axis=0)
-        for x, order in zip((one, two), orders)
-    ]
+def widen(one, two, step, orders, n_dp, *done):
+    arrived = [partner(x, "dp", n_dp, 1 << order[step]) for x, order in zip((one, two), orders)]
+    if done:
+        arrived = after(arrived, *done)
+    return [jnp.concatenate(x, axis=0) for x in zip((one, two), arrived)]
 
 
 def widen_offsets(order):
@@ -314,59 +314,111 @@
     return x[:count] + x[count : 2 * count] + x[2 * count :]
 
 
-def forward_kernel(heads, n_t, q_ref, k_ref, v_ref, seg_ref, img_ref, *rest):
-    msgs, stat = rest[:n_t], rest[n_t]
-    h = pl.program_id(0)
+GROUP = 8
+CHUNK = 128
+TN = (((0,), (0,)), ((), ()))
+NT = (((1,), (1,)), ((), ()))
+
+
+def forward_kernel(heads, n_t, span_ref, q_ref, k_ref, v_ref, seg_ref, img_ref, *rest):
+    msgs, stat, acc, run = rest[:n_t], rest[n_t], rest[n_t + 1], rest[n_t + 2]
+    g = pl.program_id(0)
     rows = q_ref.shape[1] // n_t
-    scores = (
-        lax.dot_general(
-            k_ref[...], q_ref[...], (((0,), (0,)), ((), ())), preferred_element_type=F32
-        )
-        * SCALE
-    )
-    allowed = seg_ref[...] == img_ref[...]
-    masked = jnp.where(allowed, scores, NEGATIVE)
-    top = jnp.max(masked, axis=0, keepdims=True)
-    weight = jnp.where(allowed, jnp.exp(masked - top), 0.0)
-    total = jnp.sum(weight, axis=0, keepdims=True)
-    mean = jnp.sum(weight * scores, axis=0, keepdims=True)
-    some = total > 0.0
-    inverse = jnp.where(some, 1.0 / jnp.where(some, total, 1.0), 0.0)
-    out = jnp.dot(v_ref[...], weight.astype(BF), preferred_element_type=F32) * inverse
-    stat[pl.ds(h, 1)] = jnp.where(some, top + jnp.log(jnp.where(some, total, 1.0)), NEGATIVE)
-    stat[pl.ds(heads + h, 1)] = mean * inverse
-    at = pl.ds(pl.multiple_of(h * HD, HD), HD)
+    keys = k_ref.shape[1]
     for k in range(n_t):
-        msgs[k][at, :] = out[:, k * rows : (k + 1) * rows].astype(BF)
-
-    @pl.when(h == heads - 1)
+        cols = slice(k * rows, (k + 1) * rows)
+        image = img_ref[:, cols]
+        acc[...] = jnp.zeros_like(acc)
+        run[...] = jnp.zeros_like(run)
+        run[0] = jnp.full(run.shape[1:], NEGATIVE)
+
+        def step(at, cols=cols, image=image):
+            allowed = seg_ref[at, :] == image
+            bands = [slice(h * HD, (h + 1) * HD) for h in range(GROUP)]
+            scores = [
+                SCALE
+                * lax.dot_general(k_ref[b, at], q_ref[b, cols], TN, preferred_element_type=F32)
+                for b in bands
+            ]
+            scores = [jnp.where(allowed, x, NEGATIVE) for x in scores]
+            old = [run[0, h : h + 1] for h in range(GROUP)]
+            tops = [
+                jnp.maximum(m, jnp.max(x, axis=0, keepdims=True)) for m, x in zip(old, scores)
+            ]
+            weights = [jnp.where(allowed, jnp.exp(x - m), 0.0) for x, m in zip(scores, tops)]
+            outs = [
+                jnp.dot(v_ref[b, at], w.astype(BF), preferred_element_type=F32)
+                for b, w in zip(bands, weights)
+            ]
+            fades = [jnp.exp(m - n) for m, n in zip(old, tops)]
+            for h in range(GROUP):
+                run[0, h : h + 1] = tops[h]
+                run[1, h : h + 1] = run[1, h : h + 1] * fades[h] + jnp.sum(
+                    weights[h], axis=0, keepdims=True
+                )
+                run[2, h : h + 1] = run[2, h : h + 1] * fades[h] + jnp.sum(
+                    weights[h] * scores[h], axis=0, keepdims=True
+                )
+            for b, f, o in zip(bands, fades, outs):
+                acc[b, :] = acc[b, :] * f + o
+
+        if k == 0:
+            step(slice(keys - rows, keys))
+
+        @pl.loop(span_ref[0, k], span_ref[1, k])
+        def _(c, step=step):
+            step(pl.ds(pl.multiple_of(c * CHUNK, CHUNK), CHUNK))
+
+        total = run[1, :GROUP]
+        some = total > 0.0
+        safe = jnp.where(some, total, 1.0)
+        inverse = jnp.where(some, 1.0 / safe, 0.0)
+        stat[0, pl.ds(g, 1), :, cols] = jnp.where(some, run[0, :GROUP] + jnp.log(safe), NEGATIVE)[None]
+        stat[1, pl.ds(g, 1), :, cols] = (run[2, :GROUP] * inverse)[None]
+        for h in range(GROUP):
+            band = slice(h * HD, (h + 1) * HD)
+            first = pl.multiple_of((g * GROUP + h) * HD, HD)
+            msgs[k][pl.ds(first, HD), :] = (acc[band, :] * inverse[h : h + 1]).astype(BF)
+
+    @pl.when(g == heads // GROUP - 1)
     def _():
         for k in range(n_t):
             cols = slice(k * rows, (k + 1) * rows)
-            msgs[k][heads * HD : heads * (HD + 3), :] = three(stat[:heads, cols])
-            msgs[k][heads * (HD + 3) :, :] = three(stat[heads:, cols])
-
-
-def attend_forward(q, k, v, seg, img, n_t):
+            for i in range(2):
+                first = heads * (HD + 3 * i)
+                msgs[k][first : first + 3 * heads, :] = three(
+                    stat[i, :, :, cols].reshape(heads, rows)
+                )
+
+
+def attend_forward(q, k, v, seg, img, span, n_t):
     heads = q.shape[0] // HD
     rows, keys = q.shape[1], k.shape[1]
     one = rows // n_t
     tall = heads * (HD + 6)
+    band = GROUP * HD
     return pl.pallas_call(
         partial(forward_kernel, heads, n_t),
-        grid=(heads,),
+        grid_spec=pltpu.PrefetchScalarGridSpec(
+            num_scalar_prefetch=1,
+            grid=(heads // GROUP,),
+            in_specs=[
+                pl.BlockSpec((band, rows), lambda g, s: (g, 0)),
+                pl.BlockSpec((band, keys), lambda g, s: (g, 0)),
+                pl.BlockSpec((band, keys), lambda g, s: (g, 0)),
+                pl.BlockSpec((keys, 1), lambda g, s: (0, 0)),
+                pl.BlockSpec((1, rows), lambda g, s: (0, 0)),
+            ],
+            out_specs=[pl.BlockSpec((tall, one), lambda g, s: (0, 0))] * n_t,
+            scratch_shapes=[
+                pltpu.VMEM((2, heads // GROUP, GROUP, rows), F32),
+                pltpu.VMEM((band, one), F32),
+                pltpu.VMEM((3, 8, one), F32),
+            ],
+        ),
         out_shape=[jax.ShapeDtypeStruct((tall, one), BF)] * n_t,
-        in_specs=[
-            pl.BlockSpec((HD, rows), lambda h: (h, 0)),
-            pl.BlockSpec((HD, keys), lambda h: (h, 0)),
-            pl.BlockSpec((HD, keys), lambda h: (h, 0)),
-            pl.BlockSpec((keys, 1), lambda h: (0, 0)),
-            pl.BlockSpec((1, rows), lambda h: (0, 0)),
-        ],
-        out_specs=[pl.BlockSpec((tall, one), lambda h: (0, 0))] * n_t,
-        scratch_shapes=[pltpu.VMEM((2 * heads, rows), F32)],
         compiler_params=pltpu.CompilerParams(vmem_limit_bytes=VMEM_LIMIT),
-    )(q, k, v, seg, img)
+    )(span, q, k, v, seg, img)
 
 
 def combine_kernel(heads, n_t, *refs):
@@ -428,74 +480,110 @@
     )(do, out, stat, coef)
 
 
-def backward_kernel(heads, n_t, q_ref, k_ref, v_ref, seg_ref, img_ref, coef_ref, *rest):
+def backward_kernel(heads, n_t, span_ref, q_ref, k_ref, v_ref, seg_ref, img_ref, coef_ref, *rest):
     grads, stats = rest[:n_t], rest[n_t : 2 * n_t]
-    dq_ref, dk_ref, dv_ref, stat = rest[2 * n_t :]
-    h = pl.program_id(0)
-
-    @pl.when(h == 0)
+    dq_ref, dk_ref, dv_ref, stat, dq, dk, dv = rest[2 * n_t :]
+    g = pl.program_id(0)
+    rows = q_ref.shape[1] // n_t
+    keys = k_ref.shape[1]
+
+    @pl.when(g == 0)
     def _():
-        rows = q_ref.shape[1] // n_t
         for i in range(n_t):
             cols = slice(i * rows, (i + 1) * rows)
-            stat[:heads, cols] = join(stats[i][: 3 * heads, :], heads)
-            stat[heads:, cols] = join(stats[i][3 * heads :, :], heads)
-
-    q, k, v = q_ref[...], k_ref[...], v_ref[...]
-    grad = jnp.concatenate([g[...] for g in grads], axis=1)
-    scores = (
-        lax.dot_general(k, q, (((0,), (0,)), ((), ())), preferred_element_type=F32) * SCALE
-    )
-    allowed = seg_ref[...] == img_ref[...]
-    log_total = stat[pl.ds(h, 1)]
-    delta = stat[pl.ds(heads + h, 1)]
-    prob = jnp.where(allowed, jnp.exp(jnp.where(allowed, scores - log_total, 0.0)), 0.0)
-    back_prob = lax.dot_general(v, grad, (((0,), (0,)), ((), ())), preferred_element_type=F32)
-    back = (prob * (back_prob - coef_ref[...] * scores - delta)).astype(BF)
-    dq_ref[...] = (jnp.dot(k, back, preferred_element_type=F32) * SCALE).astype(BF)
-    nt = (((1,), (1,)), ((), ()))
-    dk_ref[...] = (lax.dot_general(q, back, nt, preferred_element_type=F32) * SCALE).astype(BF)
-    dv_ref[...] = lax.dot_general(
-        grad, prob.astype(BF), nt, preferred_element_type=F32
-    ).astype(BF)
-
-
-def attend_backward(q, k, v, seg, img, coef, msgs):
+            for j in range(2):
+                part = join(stats[i][3 * j * heads : 3 * (j + 1) * heads, :], heads)
+                stat[j, :, :, cols] = part.reshape(heads // GROUP, GROUP, rows)
+
+    dk[...] = jnp.zeros_like(dk)
+    dv[...] = jnp.zeros_like(dv)
+    for i in range(n_t):
+        cols = slice(i * rows, (i + 1) * rows)
+        image, coef = img_ref[:, cols], coef_ref[:, cols]
+        logs = stat[0, pl.ds(g, 1), :, cols][0]
+        deltas = stat[1, pl.ds(g, 1), :, cols][0]
+        dq[...] = jnp.zeros_like(dq)
+
+        def step(at, cols=cols, image=image, coef=coef, logs=logs, deltas=deltas, grad_ref=grads[i]):
+            allowed = seg_ref[at, :] == image
+            bands = [slice(h * HD, (h + 1) * HD) for h in range(GROUP)]
+            scores = [
+                SCALE
+                * lax.dot_general(k_ref[b, at], q_ref[b, cols], TN, preferred_element_type=F32)
+                for b in bands
+            ]
+            back_probs = [
+                lax.dot_general(v_ref[b, at], grad_ref[b, :], TN, preferred_element_type=F32)
+                for b in bands
+            ]
+            probs = [
+                jnp.where(allowed, jnp.exp(jnp.where(allowed, x - logs[h : h + 1], 0.0)), 0.0)
+                for h, x in enumerate(scores)
+            ]
+            backs = [
+                (p * (y - coef * x - deltas[h : h + 1])).astype(BF)
+                for h, (x, y, p) in enumerate(zip(scores, back_probs, probs))
+            ]
+            probs = [p.astype(BF) for p in probs]
+            for b, p in zip(bands, probs):
+                dv[b, at] += lax.dot_general(grad_ref[b, :], p, NT, preferred_element_type=F32)
+            for b, x in zip(bands, backs):
+                dq[b, :] += jnp.dot(k_ref[b, at], x, preferred_element_type=F32)
+            for b, x in zip(bands, backs):
+                dk[b, at] += lax.dot_general(q_ref[b, cols], x, NT, preferred_element_type=F32)
+
+        if i == 0:
+            step(slice(keys - rows, keys))
+
+        @pl.loop(span_ref[0, i], span_ref[1, i])
+        def _(c, step=step):
+            step(pl.ds(pl.multiple_of(c * CHUNK, CHUNK), CHUNK))
+
+        dq_ref[:, cols] = (dq[...] * SCALE).astype(BF)
+    dk_ref[...] = (dk[...] * SCALE).astype(BF)
+    dv_ref[...] = dv[...].astype(BF)
+
+
+def attend_backward(q, k, v, seg, img, coef, span, msgs):
     n_t = len(msgs)
     heads = q.shape[0] // HD
     rows, keys = q.shape[1], k.shape[1]
     one = rows // n_t
+    band = GROUP * HD
+    wide = [pl.BlockSpec((band, n), lambda g, s: (g, 0)) for n in (rows, keys, keys)]
     return pl.pallas_call(
         partial(backward_kernel, heads, n_t),
-        grid=(heads,),
+        grid_spec=pltpu.PrefetchScalarGridSpec(
+            num_scalar_prefetch=1,
+            grid=(heads // GROUP,),
+            in_specs=wide
+            + [
+                pl.BlockSpec((keys, 1), lambda g, s: (0, 0)),
+                pl.BlockSpec((1, rows), lambda g, s: (0, 0)),
+                pl.BlockSpec((1, rows), lambda g, s: (0, 0)),
+            ]
+            + [pl.BlockSpec((band, one), lambda g, s: (g, 0))] * n_t
+            + [pl.BlockSpec((6 * heads, one), lambda g, s: (HD // 6, 0))] * n_t,
+            out_specs=wide,
+            scratch_shapes=[
+                pltpu.VMEM((2, heads // GROUP, GROUP, rows), F32),
+                pltpu.VMEM((band, one), F32),
+                pltpu.VMEM((band, keys), F32),
+                pltpu.VMEM((band, keys), F32),
+            ],
+        ),
         out_shape=[
             jax.ShapeDtypeStruct(q.shape, BF),
             jax.ShapeDtypeStruct(k.shape, BF),
             jax.ShapeDtypeStruct(v.shape, BF),
         ],
-        in_specs=[
-            pl.BlockSpec((HD, rows), lambda h: (h, 0)),
-            pl.BlockSpec((HD, keys), lambda h: (h, 0)),
-            pl.BlockSpec((HD, keys), lambda h: (h, 0)),
-            pl.BlockSpec((keys, 1), lambda h: (0, 0)),
-            pl.BlockSpec((1, rows), lambda h: (0, 0)),
-            pl.BlockSpec((1, rows), lambda h: (0, 0)),
-        ]
-        + [pl.BlockSpec((HD, one), lambda h: (h, 0))] * n_t
-        + [pl.BlockSpec((6 * heads, one), lambda h: (HD // 6, 0))] * n_t,
-        out_specs=[
-            pl.BlockSpec((HD, rows), lambda h: (h, 0)),
-            pl.BlockSpec((HD, keys), lambda h: (h, 0)),
-            pl.BlockSpec((HD, keys), lambda h: (h, 0)),
-        ],
-        scratch_shapes=[pltpu.VMEM((2 * heads, rows), F32)],
         compiler_params=pltpu.CompilerParams(vmem_limit_bytes=VMEM_LIMIT),
         cost_estimate=pl.CostEstimate(
             flops=60 * heads * HD * rows * keys,
             bytes_accessed=60 * 1024 * 1024,
             transcendentals=heads * rows * keys,
         ),
-    )(q, k, v, seg, img, coef, *msgs, *msgs)
+    )(span, q, k, v, seg, img, coef, *msgs, *msgs)
 
 
 def norm_parts(values):
@@ -618,6 +706,33 @@
             compiler_params=pltpu.CompilerParams(vmem_limit_bytes=VMEM_LIMIT),
         )(a, b)
     )
+
+
+def finish_kernel(n_t, columns, *refs):
+    results, latent_terms, feeds = refs[:n_t], refs[n_t : 2 * n_t], refs[2 * n_t : 2 * n_t + 4]
+    middle_ref, back_ref, x_ref, gain_ref, *outs = refs[2 * n_t + 4 :]
+    outs[0][...] = (middle_ref[...] + add_up([r[...] for r in results])).astype(BF)
+    normal, root = norm_parts(x_ref[...])
+    back = add_up([r[...] for r in latent_terms])
+    outs[1][...] = back_ref[...] + norm_backward(back, normal, root, gain_ref[...])
+    for m in range(2):
+        keep, got = feeds[2 * m], feeds[2 * m + 1]
+        outs[2 + m][...] = keep[0, :, :columns].astype(F32) + got[0, :, :columns].astype(F32)
+
+
+def finish(result_terms, latent_terms, feed_pair, middle, back_middle, latents, gain, columns):
+    feeds = [x for pair in feed_pair for x in pair]
+    unit, width = feeds[0].shape[1], middle.shape[1]
+    return pl.pallas_call(
+        partial(finish_kernel, len(result_terms), columns),
+        out_shape=[
+            jax.ShapeDtypeStruct(middle.shape, BF),
+            jax.ShapeDtypeStruct(middle.shape, F32),
+            jax.ShapeDtypeStruct((unit, columns), F32),
+            jax.ShapeDtypeStruct((unit, columns), F32),
+        ],
+        compiler_params=pltpu.CompilerParams(vmem_limit_bytes=VMEM_LIMIT),
+    )(*result_terms, *latent_terms, *feeds, middle, back_middle, latents, gain[None])
 
 
 def dot(equation, a, b):
@@ -671,6 +786,16 @@
     block_of = (z - jnp.arange(n_t, dtype=jnp.int32) + n_t) % n_t
     row_index = block_of[:, None] * own_rows + jnp.arange(own_rows, dtype=jnp.int32)[None, :]
     row_image = (row_index // LAT).reshape(1, -1)
+    rows_each = own_rows // LAT
+    local_ends = jnp.clip(ends - z * own_patches, 0, own_patches)
+    local_starts = jnp.clip(ends - lengths - z * own_patches, 0, own_patches)
+    block_image = block_of * rows_each
+    at_image = jnp.arange(images, dtype=jnp.int32)[None, :]
+    low = jnp.sum(jnp.where(at_image == block_image[:, None], local_starts[None, :], 0), axis=1)
+    high = jnp.sum(
+        jnp.where(at_image == block_image[:, None] + rows_each - 1, local_ends[None, :], 0), axis=1
+    )
+    span = jnp.stack([low // CHUNK, (high + CHUNK - 1) // CHUNK]).astype(jnp.int32)
     row_valid = jnp.sum(
         jnp.where(row_image.T == jnp.arange(images, dtype=jnp.int32)[None, :], valid[None, :], 0),
         axis=1,
@@ -698,24 +823,28 @@
     k_held, v_held = [jnp.stack([x[m] for x in kv_z])[None] for m in range(2)]
     for step in steps[:-1]:
         k_held, v_held = widen(k_held, v_held, step, orders, n_dp)
-    k_held, v_held, late_latents = after([k_held, v_held, latents], *qo_z)
-    latent_blocks = [latents] + rotations(late_latents, n_t)
+    k_held, v_held = after([k_held, v_held], *qo_z)
+    gathered = lax.all_gather(jnp.stack(after([latents, cotangent], *qo_z)), "tensor", axis=0)
+    others = [
+        lax.dynamic_index_in_dim(gathered, (z - k + n_t) % n_t, 0, keepdims=False)
+        for k in range(1, n_t)
+    ]
+    latent_blocks = [latents] + [x[0] for x in others]
+    cot_blocks = [cotangent] + [x[1] for x in others]
     k_held, v_held = widen(k_held, v_held, steps[-1], orders, n_dp)
     k_pieces, v_pieces = cores(k_held, v_held, n_dp)
     qo_held = [jnp.stack([x[m] for x in qo_z])[None] for m in range(2)]
     qo_held = after(qo_held, k_held, v_held)
-    for step in steps[:-1]:
-        qo_held = widen(*qo_held, step, orders, n_dp)
     whole = [(0, 0, unit, 0, 0)]
     wk, keys, key_input_t = place(k_own, [k_pieces], offsets[:1], whole, unit, False, at, n_dp, n_t, key_input)
     wv, values, _ = place(v_own, [v_pieces], offsets[1:], whole, unit, False, at, n_dp, n_t, key_input)
-    qo_held = widen(*after(qo_held, keys), steps[-1], orders, n_dp)
-    qo_held = after(qo_held, values)
+    for step in steps[:-1]:
+        qo_held = widen(*qo_held, step, orders, n_dp, keys)
+    qo_held = widen(*qo_held, steps[-1], orders, n_dp, values)
     qo_pieces = cores(*qo_held, n_dp)
     latent_all = jnp.concatenate(latent_blocks, axis=0)
     latent_hat, latent_root = norm_parts(latent_all)
     latent_normed = (latent_hat * latent_gain + latent_shift).astype(BF)
-    cot_blocks = [cotangent] + rotations(after(cotangent, values, latent_normed), n_t)
     cuts = [(h, 0, unit // 2, h * unit // 2, 0) for h in range(2)]
     wq, queries, latent_t = place(
         query_weight, qo_pieces, offsets, cuts, unit, False, at, n_dp, n_t, latent_normed
@@ -726,8 +855,8 @@
         for c in range(width // 2 // part)
     ]
     wo = place(output_weight, qo_pieces, offsets, cuts, o_unit, True, at, n_dp, n_t)
-    sent = attend_forward(queries, keys, values, key_image, row_image, n_t)
-    sent = after(sent, wo, *cot_blocks[1:])
+    sent = attend_forward(queries, keys, values, key_image, row_image, span, n_t)
+    sent = after(sent, wo)
     got = [sent[0]] + [rotate(sent[k], n_t, -k) for k in range(1, n_t)]
     attended, stat = combine(got, heads)
     entropy = stat[:heads] - stat[heads:]
@@ -770,7 +899,7 @@
     result_terms[1:] = after(result_terms[1:], *messages)
     result_terms = send_blocks(result_terms, n_t)
     back_q, back_k, back_v = attend_backward(
-        queries, keys, values, key_image, row_image, row_valid / count_total, messages
+        queries, keys, values, key_image, row_image, row_valid / count_total, span, messages
     )
     feed_pair = cross(feed_pair, orders, 0, n_dp)
     for i in steps[1:]:
@@ -787,6 +916,7 @@
     latent_q = after(back_q, q_send)
     *latent_terms, latent_sums = latent_back(latent_q, back_k, back_v, wq, wk, wv, latent_blocks)
     v_got, k_got, q_got = after([v_got, k_got, q_got], latent_sums)
+    k_got = after(k_got, *[got for _, got in feed_pair])
     pair = first_cut((v_keep, v_got), (k_keep, k_got), None, orders, n_dp)
     sends = [send for _, send in pair]
     latent_terms[1:] = after(latent_terms[1:], *sends)
@@ -807,25 +937,19 @@
             q_pair = [(keep, send) for (keep, _), send in zip(q_pair, q_sends)]
         pair = cross(pair, orders, i, n_dp)
     q_pair = cross(q_pair, orders, 0, n_dp)
-    blocks = tensor_blocks(pair, [1, 0], inner, at, n_t)
+    blocks = send_blocks(tensor_blocks(pair, [1, 0], inner, at, n_t), n_t)
     for i in steps[1:]:
-        gots = after([got for _, got in q_pair], *blocks)
+        gots = after([got for _, got in q_pair], blocks[1], blocks[-1])
         q_pair = [(keep, got) for (keep, _), got in zip(q_pair, gots)]
         q_pair = cross(next_cut(q_pair, orders, i, n_dp), orders, i, n_dp)
-    blocks = send_blocks(blocks, n_t)
     q_blocks = tensor_blocks(q_pair, [None], inner, at, n_t)
     grad_kv = add_up(after(blocks, *q_blocks))
-    back_latent = add_up(after(latent_terms, *q_blocks))
-    late = after([x for terms in feed_pair for x in terms], *q_blocks)
-    (down_keep, down_got), (up_keep, up_got) = late[:2], late[2:]
-    down_share = down_keep[0, :, :inner].astype(F32) + down_got[0, :, :inner].astype(F32)
-    up_share = up_keep[0, :, :inner].astype(F32) + up_got[0, :, :inner].astype(F32)
-    result = middle + add_up(after(result_terms, *q_blocks))
-    latents_grad = back_middle + norm_backward(
-        back_latent, own_hat, own_root, latent_gain
-    )
-
-    grad_qo = scatter_blocks([jnp.concatenate(x, axis=0) for x in zip(q_blocks, out_blocks)], n_t)
+    result, latents_grad, down_share, up_share = finish(
+        after(result_terms, *q_blocks), latent_terms, feed_pair, middle, back_middle, latents, latent_gain, inner
+    )
+
+    qo_blocks = [jnp.concatenate(x, axis=0) for x in zip(q_blocks, out_blocks)]
+    grad_qo = add_up(after(send_blocks(qo_blocks, n_t), result))
     grad_q, grad_o = grad_qo[0], grad_qo[1]
 
     sums = [media_sums[0], media_sums[1], latent_sums[0], latent_sums[1]] + gain_shift(back_feed, feed_hat)
@@ -838,7 +962,7 @@
         sums.reshape(8, n_dp * n_t, share), p * n_t + z, 1, keepdims=False
     )
     return (
-        result.astype(BF)[None],
+        result[None],
         penalty,
         latents_grad[None],
         features_grad[None],

time: 598 us -> 576 us (0.963)
  waiting for transfers between devices: 227 us -> 193 us
  local copies, waits for them, and re-layouts: 60.5 us -> 82.6 us
  between operations: 5.93 us -> 18.8 us
  Pallas kernels: 161 us -> 149 us
  other arithmetic: 34.8 us -> 26.9 us
    ppermute x36 -> x30, waiting for transfers between devices: 158 us -> 127 us  [rotate(): lax.ppermute(x, 'tensor', [(i, (i + shift) % count) for i in range(count)])]
    pallas_call x2 -> x3, Pallas kernels: 44 us -> 30 us  [the longest x1 15.3 us: attend_backward(): pl.pallas_call(partial(backward_kernel, heads, n_t), grid_spec=pltpu.Pref...]
    unnamed x281 -> x243, local copies, waits for them, and re-layouts: 35.1 us -> 42.9 us
    ppermute x36 -> x30, starting transfers between devices: 48.4 us -> 45.2 us  [rotate(): lax.ppermute(x, 'tensor', [(i, (i + shift) % count) for i in range(count)])]
  transfers between devices with their start and end apart: 74 -> 69, of which waited for: 29 -> 28; matrix products, arithmetic and copies ran while one was open for 10% -> 12% of each run, Pallas kernels for 26% -> 21%
where the time goes in v4:
time: 576 us; the launch traced here: 570 us
  waiting for transfers between devices  193 us (34%)
  Pallas kernels  149 us (26%)
  local copies, waits for them, and re-layouts  82.6 us (14%)
  starting transfers between devices  80.9 us (14%)
  other arithmetic  26.9 us (5%)
  between operations  18.8 us (3%)
  matrix products  18.5 us (3%)
    ppermute x30, waiting for transfers between devices, rotate(): lax.ppermute(x, 'tensor', [(i, (i + shift) % count) for i in range(count)])  127 us
    ppermute x38, waiting for transfers between devices, partner(): return lax.ppermute(x, axis, [(i, i ^ offset) for i in range(count)])  66 us
    ppermute x30, starting transfers between devices, rotate(): lax.ppermute(x, 'tensor', [(i, (i + shift) % count) for i in range(count)])  45.2 us
    unnamed x243, local copies, waits for them, and re-layouts  42.9 us
    ppermute x38, starting transfers between devices, partner(): return lax.ppermute(x, axis, [(i, i ^ offset) for i in range(count)])  35.6 us
    pallas_call x6, Pallas kernels, gradient(): pl.pallas_call(partial(gradient_kernel, natural, n_dp), grid=(3,), in_spe...  31.5 us
    pallas_call x4, Pallas kernels, place(): pl.pallas_call(kernel, out_shape=outs, in_specs=[pl.BlockSpec(memory_spac...  29.1 us
    pallas_call x12, Pallas kernels, reduce_cut(): pl.pallas_call(partial(cut_kernel, widths), grid=(count // 2,), in_specs=...  25 us
  transfers between devices with their start and end apart: 69, of which 28 were waited for; matrix products, arithmetic and copies ran while one was open for 12% of the time, Pallas kernels for 21%

profile of v4, /device:TPU:0, one launch (start us, length us, event | category | flops | bytes accessed | tf_op | source)
XLA Modules:
  0.0 569.6 jit_solution(4954430930774392745)
XLA Ops:
  9.2 5.0 collective-permute-start.2
  17.3 7.9 %fusion.40 = (bf16[1536,1,384]{2,1,0:T(2,128)(2,1)}, bf16[1536,1,384]{2,1,0:T(2,128)(2,1)}) fusion(bf16[1536,2,384]{2,1,0:T(2,128)(2,1)} %param.27), kind=kLoop, calls=%fused_computation.179 | loop fusion | bytes 4718592 | tf_op jit(solution)/shard_map/slice | solution.py:815
  48.3 2.9 collective-permute-start.8
  59.0 17.8 %collective-permute-done.7 = bf16[2,192,384]{2,1,0:T(8,128)(2,1)} collective-permute-done((bf16[2,192,384]{2,1,0:T(8,128)(2,1)}, bf16[2,192,384]{2,1,0:T(8,128)(2,1)}, u32[]{:S(2)}, u32[]{:S(2)}) %collective-permute-start.7) | collective-permute-done | bytes 294944 | tf_op jit(solution)/shard_map/ppermute | solution.py:21
  84.6 15.7 %collective-permute-done.11 = bf16[2,3,192,384]{3,2,1,0:T(8,128)(2,1)S(1)} collective-permute-done((bf16[2,3,192,384]{3,2,1,0:T(8,128)(2,1)S(1)}, bf16[2,3,192,384]{3,2,1,0:T(8,128)(2,1)S(1)}, u32[]{:S(2)}, u32[]{:S(2)}) %collective-permute-start.11) | collective-permute-done | bytes 884768 | tf_op jit(solution)/shard_map/ppermute | solution.py:43
  107.5 8.2 %shard_map.271 = (bf16[1536,1536]{1,0:T(8,128)(2,1)}, bf16[1536,640]{1,0:T(8,128)(2,1)}, bf16[1536,640]{1,0:T(8,128)(2,1)}) custom-call(s32[2]{0:T(128)S(1)} %pad_add_fusion.2.at_ref, bf16[640,1536]{1,0:T(8,128)(2,1)} %pad_maximum_fusion.x_ref, bf16[1536,384]{1,0:T(8,128)(2,1)S(1)} %copy-done.25, ...), custom_call_target="tpu_custom_call" | custom-call | tf_op jit(solution)/shard_map/pallas_call | solution.py:268
  122.3 8.2 %shard_map.272 = (bf16[1536,1536]{1,0:T(8,128)(2,1)}, bf16[1536,640]{1,0:T(8,128)(2,1)}, bf16[1536,640]{1,0:T(8,128)(2,1)}) custom-call(s32[2]{0:T(128)S(1)} %pad_add_fusion.2.at_ref, bf16[640,1536]{1,0:T(8,128)(2,1)} %pad_maximum_fusion.x_ref, bf16[1536,384]{1,0:T(8,128)(2,1)S(1)} %get-tuple-element.188.refs_0_, ...), custom_call_target="tpu_custom_call" | custom-call | tf_op jit(solution)/shard_map/pallas_call | solution.py:268
  132.2 6.4 %collective-permute-done.17 = bf16[2,3,192,384]{3,2,1,0:T(8,128)(2,1)S(1)} collective-permute-done((bf16[2,3,192,384]{3,2,1,0:T(8,128)(2,1)S(1)}, bf16[2,3,192,384]{3,2,1,0:T(8,128)(2,1)S(1)}, u32[]{:S(2)}, u32[]{:S(2)}) %collective-permute-start.17) | collective-permute-done | bytes 884768 | tf_op jit(solution)/shard_map/ppermute | solution.py:43
  147.0 7.2 %shard_map.273 = (bf16[1536,1536]{1,0:T(8,128)(2,1)}, bf16[1536,512]{1,0:T(8,128)(2,1)S(1)}, bf16[1536,512]{1,0:T(8,128)(2,1)S(1)}) custom-call(s32[2]{0:T(128)S(1)} %pad_add_fusion.2.at_ref, bf16[512,1536]{1,0:T(8,128)(2,1)S(1)} %fusion.7.x_ref, bf16[1536,384]{1,0:T(8,128)(2,1)S(1)} %copy-done.47, ...), custom_call_target="tpu_custom_call" | custom-call | tf_op jit(solution)/shard_map/pallas_call | solution.py:268
  155.3 9.4 %shard_map.274 = (bf16[1632,128]{1,0:T(8,128)(2,1)S(1)}, bf16[1632,128]{1,0:T(8,128)(2,1)S(1)}, bf16[1632,128]{1,0:T(8,128)(2,1)S(1)}, bf16[1632,128]{1,0:T(8,128)(2,1)S(1)}) custom-call(s32[2,4]{1,0:T(2,128)S(1)} %pad_add_fusion.1.span_ref, bf16[1536,512]{1,0:T(8,128)(2,1)S(1)} %get-tuple-element.192.q_ref, bf16[1536,640]{1,0:T(8,128)(2,1)S(1)} %copy-done.39, ...), custom_call_target="tpu_custom_call" | custom-call | tf_op jit(solution)/shard_map/pallas_call | solution.py:400
  165.9 5.6 shard_map.275
  171.5 3.1 collective-permute-start.22
  174.6 2.0 collective-permute-start.23
  176.6 6.6 %collective-permute-done.21.refs_1_ = bf16[1632,128]{1,0:T(8,128)(2,1)S(1)} collective-permute-done((bf16[1632,128]{1,0:T(8,128)(2,1)S(1)}, bf16[1632,128]{1,0:T(8,128)(2,1)S(1)}, u32[]{:S(2)}, u32[]{:S(2)}) %collective-permute-start.21) | collective-permute-done | bytes 417824 | tf_op jit(solution)/shard_map/ppermute | solution.py:21
  183.2 28.2 %collective-permute-done.22.refs_2_ = bf16[1632,128]{1,0:T(8,128)(2,1)S(1)} collective-permute-done((bf16[1632,128]{1,0:T(8,128)(2,1)S(1)}, bf16[1632,128]{1,0:T(8,128)(2,1)S(1)}, u32[]{:S(2)}, u32[]{:S(2)}) %collective-permute-start.22) | collective-permute-done | bytes 417824 | tf_op jit(solution)/shard_map/ppermute | solution.py:21
  212.4 3.4 fusion.48
  217.2 2.1 collective-permute-start.24
  219.5 9.5 %collective-permute-done.26 = bf16[128,1536]{1,0:T(8,128)(2,1)S(1)} collective-permute-done((bf16[128,1536]{1,0:T(8,128)(2,1)S(1)}, bf16[128,1536]{1,0:T(8,128)(2,1)S(1)}, u32[]{:S(2)}, u32[]{:S(2)}) %collective-permute-start.26) | collective-permute-done | bytes 393248 | tf_op jit(solution)/shard_map/ppermute | solution.py:21
  229.0 22.6 %collective-permute-done.25 = bf16[128,1536]{1,0:T(8,128)(2,1)S(1)} collective-permute-done((bf16[128,1536]{1,0:T(8,128)(2,1)S(1)}, bf16[128,1536]{1,0:T(8,128)(2,1)S(1)}, u32[]{:S(2)}, u32[]{:S(2)}) %collective-permute-start.25) | collective-permute-done | bytes 393248 | tf_op jit(solution)/shard_map/ppermute | solution.py:21
  251.6 4.7 multiply_convert_fusion
  256.4 3.7 fusion.16.y_ref
  260.1 2.6 convolution_convert_fusion
  264.6 1.9 collective-permute-start.28
  266.6 2.9 collective-permute-start.27
  269.5 2.6 copy.63.xt_ref
  272.1 2.6 fusion.23
  274.7 2.6 copy.64.xt_ref
  278.7 6.1 %shard_map.277 = (f32[128,1536]{1,0:T(8,128)S(1)}, bf16[128,1536]{1,0:T(8,128)(2,1)}, bf16[128,1536]{1,0:T(8,128)(2,1)}, bf16[128,1536]{1,0:T(8,128)(2,1)}) custom-call(bf16[512,1536]{1,0:T(8,128)(2,1)S(1)} %copy-done.23, bf16[1536,1536]{1,0:T(8,128)(2,1)} %b_ref.1), custom_call_target="tpu_custom_call" | custom-call | tf_op jit(solution)/shard_map/pallas_call | solution.py:703
  285.6 5.1 shard_map.278
  292.3 5.2 shard_map.279
  298.0 2.8 multiply_reduce_fusion
  302.2 1.9 copy.65.xt_ref
  306.1 3.1 shard_map.281
  310.4 4.1 convolution_convert_fusion.1.do_ref
  314.7 5.8 %collective-permute-start.32 = (bf16[1632,128]{1,0:T(8,128)(2,1)S(1)}, bf16[1632,128]{1,0:T(8,128)(2,1)S(1)}, u32[]{:S(2)}, u32[]{:S(2)}) collective-permute-start(bf16[1632,128]{1,0:T(8,128)(2,1)S(1)} %shard_map.280.rest_0_.rest_4_), channel_id=1, source_target_pairs={{0,3},{1,0},{2,1},{3,2},{4,7},{5,4},{6,5},{7,6},{8,11},{9,8},{10,9... | collective-permute-start | bytes 1253384 | tf_op jit(solution)/shard_map/ppermute | solution.py:21
  321.8 3.7 shard_map.282
  325.6 3.7 shard_map.283
  329.3 3.6 collective-permute-start.40
  333.6 23.5 %collective-permute-done.31.rest_2_.rest_6_ = bf16[1632,128]{1,0:T(8,128)(2,1)S(1)} collective-permute-done((bf16[1632,128]{1,0:T(8,128)(2,1)S(1)}, bf16[1632,128]{1,0:T(8,128)(2,1)S(1)}, u32[]{:S(2)}, u32[]{:S(2)}) %collective-permute-start.31) | collective-permute-done | bytes 417824 | tf_op jit(solution)/shard_map/ppermute | solution.py:21
  360.2 2.0 collective-permute-start.38
  366.7 15.3 %shard_map.284 = (bf16[1536,512]{1,0:T(8,128)(2,1)S(1)}, bf16[1536,640]{1,0:T(8,128)(2,1)}, bf16[1536,640]{1,0:T(8,128)(2,1)}) custom-call(s32[2,4]{1,0:T(2,128)S(1)} %pad_add_fusion.1.span_ref, bf16[1536,512]{1,0:T(8,128)(2,1)S(1)} %copy-done.44, bf16[1536,640]{1,0:T(8,128)(2,1)} %get-tuple-element.185.k_ref, bf16[1536,640]{1,0:T(8,128)(2,1)} %get-tuple-element.189.v_ref, ...), custom_call_target="tpu_custom_call" | custom-call | flops 30198988800 | bytes 62914560 | tf_op jit(solution)/shard_map/pallas_call | solution.py:554
  381.9 2.7 shard_map.285
  391.1 6.5 %shard_map.287 = (bf16[4,192,1536]{2,1,0:T(8,128)(2,1)}, bf16[4,192,1536]{2,1,0:T(8,128)(2,1)}) custom-call(s32[2]{0:T(128)S(1)} %pad_add_fusion.2.at_ref, bf16[1536,640]{1,0:T(8,128)(2,1)S(1)} %copy-done.15, bf16[1536,640]{1,0:T(8,128)(2,1)S(1)} %copy-done.5), custom_call_target="tpu_custom_call" | custom-call | tf_op jit(solution)/shard_map/pallas_call | solution.py:70
  397.5 6.5 %shard_map.288 = (bf16[4,192,1536]{2,1,0:T(8,128)(2,1)}, bf16[4,192,1536]{2,1,0:T(8,128)(2,1)}) custom-call(s32[2]{0:T(128)S(1)} %pad_add_fusion.2.at_ref, bf16[1536,640]{1,0:T(8,128)(2,1)S(1)} %copy-done.15, bf16[1536,640]{1,0:T(8,128)(2,1)S(1)} %copy-done.3), custom_call_target="tpu_custom_call" | custom-call | tf_op jit(solution)/shard_map/pallas_call | solution.py:70
  404.1 5.2 shard_map.289
  409.8 2.4 collective-permute-start.44
  413.4 11.5 %shard_map.290 = (f32[128,1536]{1,0:T(8,128)S(1)}, bf16[128,1536]{1,0:T(8,128)(2,1)}, bf16[128,1536]{1,0:T(8,128)(2,1)}, bf16[128,1536]{1,0:T(8,128)(2,1)}, f32[8,1536]{1,0:T(8,128)S(1)}) custom-call(bf16[1536,512]{1,0:T(8,128)(2,1)S(1)} %get-tuple-element.256.y_ref.dq_ref, bf16[1536,640]{1,0:T(8,128)(2,1)} %get-tuple-element.280.y_ref.dk_ref, ...), custom_call_target="tpu_custom_call" | custom-call | tf_op jit(solution)/shard_map/pallas_call | solution.py:680
  426.4 6.3 %collective-permute-done.44.refs_1_.refs_9_ = bf16[1,192,2304]{2,1,0:T(8,128)(2,1)S(1)} collective-permute-done((bf16[1,192,2304]{2,1,0:T(8,128)(2,1)}, bf16[1,192,2304]{2,1,0:T(8,128)(2,1)S(1)}, u32[]{:S(2)}, u32[]{:S(2)}) %collective-permute-start.44) | collective-permute-done | bytes 884768 | tf_op jit(solution)/shard_map/ppermute | solution.py:43
  436.7 2.8 shard_map.292
  440.7 2.7 shard_map.291
  446.1 2.0 collective-permute-start.50
  458.4 12.0 %shard_map.296 = (f32[512,1536]{1,0:T(8,128)}, f32[8,1536]{1,0:T(8,128)S(1)}) custom-call(bf16[1536,640]{1,0:T(8,128)(2,1)S(1)} %copy-done.4, bf16[1536,640]{1,0:T(8,128)(2,1)S(1)} %copy-done.6, bf16[1536,1536]{1,0:T(8,128)(2,1)} %get-tuple-element.258.wk_ref, bf16[1536,1536]{1,0:T(8,128)(2,1)} %get-tuple-element.259.wv_ref, ...), custom_call_target="tpu_custom_call" | custom-call | tf_op jit(solution)/shard_map/pallas_call | solution.py:635
  476.0 3.9 collective-permute-done.49.refs_6_
  481.2 7.8 %collective-permute-done.54.refs_3_ = bf16[1,192,1536]{2,1,0:T(8,128)(2,1)S(1)} collective-permute-done((bf16[1,192,1536]{2,1,0:T(8,128)(2,1)S(1)}, bf16[1,192,1536]{2,1,0:T(8,128)(2,1)S(1)}, u32[]{:S(2)}, u32[]{:S(2)}) %collective-permute-start.54) | collective-permute-done | bytes 589856 | tf_op jit(solution)/shard_map/ppermute | solution.py:43
  488.9 2.8 collective-permute-done.53.refs_1_
  501.7 2.8 collective-permute-done.56
  504.5 1.8 shard_map.301
  510.7 5.4 collective-permute-done.61
  517.1 3.1 collective-permute-done.62
  521.3 7.8 %collective-permute-done.63 = f32[8,1536]{1,0:T(8,128)S(1)} collective-permute-done((f32[8,1536]{1,0:T(8,128)S(1)}, f32[8,1536]{1,0:T(8,128)S(1)}, u32[]{:S(2)}, u32[]{:S(2)}) %collective-permute-start.63) | collective-permute-done | bytes 49184 | tf_op jit(solution)/shard_map/ppermute | solution.py:43
  534.9 2.7 collective-permute-start.66
  538.1 3.2 collective-permute-start.64
  541.2 11.3 %collective-permute-done.67 = bf16[2,192,384]{2,1,0:T(8,128)(2,1)S(1)} collective-permute-done((bf16[2,192,384]{2,1,0:T(8,128)(2,1)}, bf16[2,192,384]{2,1,0:T(8,128)(2,1)S(1)}, u32[]{:S(2)}, u32[]{:S(2)}) %collective-permute-start.67) | collective-permute-done | bytes 294944 | tf_op jit(solution)/shard_map/ppermute | solution.py:21
  555.0 5.3 shard_map.303
  (470 shorter events, 151.1 us)
Async XLA Ops:
  7.2 134.8 %all-gather.3.cloned.1.call-start = ((), (), s32[]{:S(2)}) async-start(), calls=%async_computation | async-start | bytes 3932160 | tf_op jit(solution)/shard_map/all_gather | solution.py:827
  9.2 37.1 %collective-permute-start.2 = (bf16[2,192,384]{2,1,0:T(8,128)(2,1)}, bf16[2,192,384]{2,1,0:T(8,128)(2,1)}, u32[]{:S(2)}, u32[]{:S(2)}) collective-permute-start(bf16[2,192,384]{2,1,0:T(8,128)(2,1)} %bitcast.135), channel_id=1, source_target_pairs={{0,3},{1,0},{2,1},{3,2},{4,7},{5,4},{6,5},{7,6},{8,11},{9,8},{10,9... | collective-permute-start | bytes 884744 | tf_op jit(solution)/shard_map/ppermute | solution.py:21
  14.2 32.1 %collective-permute-start.1 = (bf16[2,192,384]{2,1,0:T(8,128)(2,1)}, bf16[2,192,384]{2,1,0:T(8,128)(2,1)}, u32[]{:S(2)}, u32[]{:S(2)}) collective-permute-start(bf16[2,192,384]{2,1,0:T(8,128)(2,1)} %bitcast.135), channel_id=1, source_target_pairs={{0,2},{1,3},{2,0},{3,1},{4,6},{5,7},{6,4},{7,5},{8,10},{9,11},{10,... | collective-permute-start | bytes 884744 | tf_op jit(solution)/shard_map/ppermute | solution.py:21
  14.2 32.1 %collective-permute-start = (bf16[2,192,384]{2,1,0:T(8,128)(2,1)}, bf16[2,192,384]{2,1,0:T(8,128)(2,1)}, u32[]{:S(2)}, u32[]{:S(2)}) collective-permute-start(bf16[2,192,384]{2,1,0:T(8,128)(2,1)} %bitcast.135), channel_id=1, source_target_pairs={{0,1},{1,2},{2,3},{3,0},{4,5},{5,6},{6,7},{7,4},{8,9},{9,10},{10,1... | collective-permute-start | bytes 884744 | tf_op jit(solution)/shard_map/ppermute | solution.py:21
  17.2 20.5 %collective-permute-start.3 = (f32[8,128]{1,0:T(8,128)S(1)}, f32[8,128]{1,0:T(8,128)S(1)}, u32[]{:S(2)}, u32[]{:S(2)}) collective-permute-start(f32[8,128]{1,0:T(8,128)S(1)} %broadcast_in_dim.130), channel_id=1, source_target_pairs={{0,4},{4,0},{8,12},{12,8},{16,20},{20,16},{24,28},{28,24},{1,5},{5... | collective-permute-start | bytes 12296 | tf_op jit(solution)/shard_map/ppermute | solution.py:43
  48.3 10.7 %collective-permute-start.8 = (bf16[2,192,384]{2,1,0:T(8,128)(2,1)}, bf16[2,192,384]{2,1,0:T(8,128)(2,1)}, u32[]{:S(2)}, u32[]{:S(2)}) collective-permute-start(bf16[2,192,384]{2,1,0:T(8,128)(2,1)} %pad_maximum_fusion.9), channel_id=1, source_target_pairs={{0,3},{1,0},{2,1},{3,2},{4,7},{5,4},{6,5},{7,6},{8,11},{9,8},{10,9... | collective-permute-start | bytes 884744 | tf_op jit(solution)/shard_map/ppermute | solution.py:21
  51.2 25.7 %collective-permute-start.7 = (bf16[2,192,384]{2,1,0:T(8,128)(2,1)}, bf16[2,192,384]{2,1,0:T(8,128)(2,1)}, u32[]{:S(2)}, u32[]{:S(2)}) collective-permute-start(bf16[2,192,384]{2,1,0:T(8,128)(2,1)} %pad_maximum_fusion.9), channel_id=1, source_target_pairs={{0,2},{1,3},{2,0},{3,1},{4,6},{5,7},{6,4},{7,5},{8,10},{9,11},{10,... | collective-permute-start | bytes 884744 | tf_op jit(solution)/shard_map/ppermute | solution.py:21
  52.3 24.5 %collective-permute-start.6 = (bf16[2,192,384]{2,1,0:T(8,128)(2,1)}, bf16[2,192,384]{2,1,0:T(8,128)(2,1)}, u32[]{:S(2)}, u32[]{:S(2)}) collective-permute-start(bf16[2,192,384]{2,1,0:T(8,128)(2,1)} %pad_maximum_fusion.9), channel_id=1, source_target_pairs={{0,1},{1,2},{2,3},{3,0},{4,5},{5,6},{6,7},{7,4},{8,9},{9,10},{10,1... | collective-permute-start | bytes 884744 | tf_op jit(solution)/shard_map/ppermute | solution.py:21
  54.7 24.1 %collective-permute-start.9 = (bf16[1,3,192,384]{3,2,1,0:T(8,128)(2,1)}, bf16[1,3,192,384]{3,2,1,0:T(8,128)(2,1)}, u32[]{:S(2)}, u32[]{:S(2)}) collective-permute-start(bf16[1,3,192,384]{3,2,1,0:T(8,128)(2,1)} %maximum_bitcast_fusion.2), channel_id=1, source_target_pairs={{0,8},{4,12},{8,0},{12,4},{16,24},{20,28},{24,16},{28,20},{1,9},{5... | collective-permute-start | bytes 1327112 | tf_op jit(solution)/shard_map/ppermute | solution.py:43
  57.0 23.0 %collective-permute-start.10 = (bf16[1,3,192,384]{3,2,1,0:T(8,128)(2,1)}, bf16[1,3,192,384]{3,2,1,0:T(8,128)(2,1)}, u32[]{:S(2)}, u32[]{:S(2)}) collective-permute-start(bf16[1,3,192,384]{3,2,1,0:T(8,128)(2,1)} %maximum_bitcast_fusion.3), channel_id=1, source_target_pairs={{0,16},{4,20},{8,24},{12,28},{16,0},{20,4},{24,8},{28,12},{1,17},{... | collective-permute-start | bytes 1327112 | tf_op jit(solution)/shard_map/ppermute | solution.py:43
  81.3 19.1 %collective-permute-start.11 = (bf16[2,3,192,384]{3,2,1,0:T(8,128)(2,1)S(1)}, bf16[2,3,192,384]{3,2,1,0:T(8,128)(2,1)S(1)}, u32[]{:S(2)}, u32[]{:S(2)}) collective-permute-start(bf16[2,3,192,384]{3,2,1,0:T(8,128)(2,1)S(1)} %pad_maximum_fusion.3), channel_id=1, source_target_pairs={{0,16},{4,20},{8,24},{12,28},{16,0},{20,4},{24,8},{28,12},{1,17},{... | collective-permute-start | bytes 2654216 | tf_op jit(solution)/shard_map/ppermute | solution.py:43
  83.1 19.7 %collective-permute-start.12 = (bf16[2,3,192,384]{3,2,1,0:T(8,128)(2,1)S(1)}, bf16[2,3,192,384]{3,2,1,0:T(8,128)(2,1)S(1)}, u32[]{:S(2)}, u32[]{:S(2)}) collective-permute-start(bf16[2,3,192,384]{3,2,1,0:T(8,128)(2,1)S(1)} %pad_maximum_fusion.4), channel_id=1, source_target_pairs={{0,8},{4,12},{8,0},{12,4},{16,24},{20,28},{24,16},{28,20},{1,9},{5... | collective-permute-start | bytes 2654216 | tf_op jit(solution)/shard_map/ppermute | solution.py:43
  100.5 7.0 %collective-permute-start.15 = (bf16[4,3,192,384]{3,2,1,0:T(8,128)(2,1)S(1)}, bf16[4,3,192,384]{3,2,1,0:T(8,128)(2,1)S(1)}, u32[]{:S(2)}, u32[]{:S(2)}) collective-permute-start(bf16[4,3,192,384]{3,2,1,0:T(8,128)(2,1)S(1)} %constant_dynamic-update-slice_fusion.refs_1_), channel_id=1, source_target_pairs={{0,4},{4,0},{8,12},{12,8},{16,20},{20,16},{24,28},{28,24},{1,5},{5... | collective-permute-start | bytes 5308424 | tf_op jit(solution)/shard_map/ppermute | solution.py:43
  103.0 19.3 %collective-permute-start.18 = (bf16[4,3,192,384]{3,2,1,0:T(8,128)(2,1)S(1)}, bf16[4,3,192,384]{3,2,1,0:T(8,128)(2,1)S(1)}, u32[]{:S(2)}, u32[]{:S(2)}) collective-permute-start(bf16[4,3,192,384]{3,2,1,0:T(8,128)(2,1)S(1)} %constant_dynamic-update-slice_fusion.2.refs_1_), channel_id=1, source_target_pairs={{0,4},{4,0},{8,12},{12,8},{16,20},{20,16},{24,28},{28,24},{1,5},{5... | collective-permute-start | bytes 5308424 | tf_op jit(solution)/shard_map/ppermute | solution.py:43
  104.8 12.2 %collective-permute-start.13 = (bf16[1,3,192,384]{3,2,1,0:T(8,128)(2,1)S(1)}, bf16[1,3,192,384]{3,2,1,0:T(8,128)(2,1)S(1)}, u32[]{:S(2)}, u32[]{:S(2)}) collective-permute-start(bf16[1,3,192,384]{3,2,1,0:T(8,128)(2,1)S(1)} %maximum_bitcast_fusion), channel_id=1, source_target_pairs={{0,8},{4,12},{8,0},{12,4},{16,24},{20,28},{24,16},{28,20},{1,9},{5... | collective-permute-start | bytes 1327112 | tf_op jit(solution)/shard_map/ppermute | solution.py:43
  105.9 11.9 %collective-permute-start.14 = (bf16[1,3,192,384]{3,2,1,0:T(8,128)(2,1)S(1)}, bf16[1,3,192,384]{3,2,1,0:T(8,128)(2,1)S(1)}, u32[]{:S(2)}, u32[]{:S(2)}) collective-permute-start(bf16[1,3,192,384]{3,2,1,0:T(8,128)(2,1)S(1)} %maximum_bitcast_fusion.1), channel_id=1, source_target_pairs={{0,16},{4,20},{8,24},{12,28},{16,0},{20,4},{24,8},{28,12},{1,17},{... | collective-permute-start | bytes 1327112 | tf_op jit(solution)/shard_map/ppermute | solution.py:43
  117.9 20.7 %collective-permute-start.17 = (bf16[2,3,192,384]{3,2,1,0:T(8,128)(2,1)S(1)}, bf16[2,3,192,384]{3,2,1,0:T(8,128)(2,1)S(1)}, u32[]{:S(2)}, u32[]{:S(2)}) collective-permute-start(bf16[2,3,192,384]{3,2,1,0:T(8,128)(2,1)S(1)} %pad_maximum_fusion.6), channel_id=1, source_target_pairs={{0,8},{4,12},{8,0},{12,4},{16,24},{20,28},{24,16},{28,20},{1,9},{5... | collective-permute-start | bytes 2654216 | tf_op jit(solution)/shard_map/ppermute | solution.py:43
  119.0 20.4 %collective-permute-start.16 = (bf16[2,3,192,384]{3,2,1,0:T(8,128)(2,1)S(1)}, bf16[2,3,192,384]{3,2,1,0:T(8,128)(2,1)S(1)}, u32[]{:S(2)}, u32[]{:S(2)}) collective-permute-start(bf16[2,3,192,384]{3,2,1,0:T(8,128)(2,1)S(1)} %pad_maximum_fusion.5), channel_id=1, source_target_pairs={{0,16},{4,20},{8,24},{12,28},{16,0},{20,4},{24,8},{28,12},{1,17},{... | collective-permute-start | bytes 2654216 | tf_op jit(solution)/shard_map/ppermute | solution.py:43
  141.4 5.6 collective-permute-start.19
  171.5 11.7 %collective-permute-start.21 = (bf16[1632,128]{1,0:T(8,128)(2,1)S(1)}, bf16[1632,128]{1,0:T(8,128)(2,1)S(1)}, u32[]{:S(2)}, u32[]{:S(2)}) collective-permute-start(bf16[1632,128]{1,0:T(8,128)(2,1)S(1)} %get-tuple-element.198), channel_id=1, source_target_pairs={{0,3},{1,0},{2,1},{3,2},{4,7},{5,4},{6,5},{7,6},{8,11},{9,8},{10,9... | collective-permute-start | bytes 1253384 | tf_op jit(solution)/shard_map/ppermute | solution.py:21
  171.5 39.9 %collective-permute-start.22 = (bf16[1632,128]{1,0:T(8,128)(2,1)S(1)}, bf16[1632,128]{1,0:T(8,128)(2,1)S(1)}, u32[]{:S(2)}, u32[]{:S(2)}) collective-permute-start(bf16[1632,128]{1,0:T(8,128)(2,1)S(1)} %get-tuple-element.199), channel_id=1, source_target_pairs={{0,2},{1,3},{2,0},{3,1},{4,6},{5,7},{6,4},{7,5},{8,10},{9,11},{10,... | collective-permute-start | bytes 1253384 | tf_op jit(solution)/shard_map/ppermute | solution.py:21
  174.6 36.8 %collective-permute-start.23 = (bf16[1632,128]{1,0:T(8,128)(2,1)S(1)}, bf16[1632,128]{1,0:T(8,128)(2,1)S(1)}, u32[]{:S(2)}, u32[]{:S(2)}) collective-permute-start(bf16[1632,128]{1,0:T(8,128)(2,1)S(1)} %get-tuple-element.200), channel_id=1, source_target_pairs={{0,1},{1,2},{2,3},{3,0},{4,5},{5,6},{6,7},{7,4},{8,9},{9,10},{10,1... | collective-permute-start | bytes 1253384 | tf_op jit(solution)/shard_map/ppermute | solution.py:21
  217.0 12.0 %collective-permute-start.26 = (bf16[128,1536]{1,0:T(8,128)(2,1)S(1)}, bf16[128,1536]{1,0:T(8,128)(2,1)S(1)}, u32[]{:S(2)}, u32[]{:S(2)}) collective-permute-start(bf16[128,1536]{1,0:T(8,128)(2,1)S(1)} %add_convert_fusion), channel_id=1, source_target_pairs={{0,3},{1,0},{2,1},{3,2},{4,7},{5,4},{6,5},{7,6},{8,11},{9,8},{10,9... | collective-permute-start | bytes 1179656 | tf_op jit(solution)/shard_map/ppermute | solution.py:21
  217.1 34.5 %collective-permute-start.25 = (bf16[128,1536]{1,0:T(8,128)(2,1)S(1)}, bf16[128,1536]{1,0:T(8,128)(2,1)S(1)}, u32[]{:S(2)}, u32[]{:S(2)}) collective-permute-start(bf16[128,1536]{1,0:T(8,128)(2,1)S(1)} %add_convert_fusion), channel_id=1, source_target_pairs={{0,2},{1,3},{2,0},{3,1},{4,6},{5,7},{6,4},{7,5},{8,10},{9,11},{10,... | collective-permute-start | bytes 1179656 | tf_op jit(solution)/shard_map/ppermute | solution.py:21
  217.2 34.4 %collective-permute-start.24 = (bf16[128,1536]{1,0:T(8,128)(2,1)S(1)}, bf16[128,1536]{1,0:T(8,128)(2,1)S(1)}, u32[]{:S(2)}, u32[]{:S(2)}) collective-permute-start(bf16[128,1536]{1,0:T(8,128)(2,1)S(1)} %add_convert_fusion), channel_id=1, source_target_pairs={{0,1},{1,2},{2,3},{3,0},{4,5},{5,6},{6,7},{7,4},{8,9},{9,10},{10,1... | collective-permute-start | bytes 1179656 | tf_op jit(solution)/shard_map/ppermute | solution.py:21
  263.9 34.0 %collective-permute-start.29 = (bf16[128,1536]{1,0:T(8,128)(2,1)}, bf16[128,1536]{1,0:T(8,128)(2,1)}, u32[]{:S(2)}, u32[]{:S(2)}) collective-permute-start(bf16[128,1536]{1,0:T(8,128)(2,1)} %get-tuple-element.408), channel_id=1, source_target_pairs={{0,1},{1,2},{2,3},{3,0},{4,5},{5,6},{6,7},{7,4},{8,9},{9,10},{10,1... | collective-permute-start | bytes 1179656 | tf_op jit(solution)/shard_map/ppermute | solution.py:21
  264.6 33.3 %collective-permute-start.28 = (bf16[128,1536]{1,0:T(8,128)(2,1)}, bf16[128,1536]{1,0:T(8,128)(2,1)}, u32[]{:S(2)}, u32[]{:S(2)}) collective-permute-start(bf16[128,1536]{1,0:T(8,128)(2,1)} %get-tuple-element.409), channel_id=1, source_target_pairs={{0,2},{1,3},{2,0},{3,1},{4,6},{5,7},{6,4},{7,5},{8,10},{9,11},{10,... | collective-permute-start | bytes 1179656 | tf_op jit(solution)/shard_map/ppermute | solution.py:21
  266.6 31.4 %collective-permute-start.27 = (bf16[128,1536]{1,0:T(8,128)(2,1)}, bf16[128,1536]{1,0:T(8,128)(2,1)}, u32[]{:S(2)}, u32[]{:S(2)}) collective-permute-start(bf16[128,1536]{1,0:T(8,128)(2,1)} %get-tuple-element.410), channel_id=1, source_target_pairs={{0,3},{1,0},{2,1},{3,2},{4,7},{5,4},{6,5},{7,6},{8,11},{9,8},{10,9... | collective-permute-start | bytes 1179656 | tf_op jit(solution)/shard_map/ppermute | solution.py:21
  292.2 28.3 %collective-permute-start.33 = (bf16[4,192,1536]{2,1,0:T(8,128)(2,1)}, bf16[4,192,1536]{2,1,0:T(8,128)(2,1)}, u32[]{:S(2)}, u32[]{:S(2)}) collective-permute-start(bf16[4,192,1536]{2,1,0:T(8,128)(2,1)} %get-tuple-element.211), channel_id=1, source_target_pairs={{0,4},{4,0},{8,12},{12,8},{16,20},{20,16},{24,28},{28,24},{1,5},{5... | collective-permute-start | bytes 7077896 | tf_op jit(solution)/shard_map/ppermute | solution.py:43
  297.5 24.3 %collective-permute-start.34 = (bf16[4,192,1536]{2,1,0:T(8,128)(2,1)}, bf16[4,192,1536]{2,1,0:T(8,128)(2,1)}, u32[]{:S(2)}, u32[]{:S(2)}) collective-permute-start(bf16[4,192,1536]{2,1,0:T(8,128)(2,1)} %get-tuple-element.213), channel_id=1, source_target_pairs={{0,4},{4,0},{8,12},{12,8},{16,20},{20,16},{24,28},{28,24},{1,5},{5... | collective-permute-start | bytes 7077896 | tf_op jit(solution)/shard_map/ppermute | solution.py:43
  309.2 12.6 %collective-permute-start.35 = (bf16[4,192,1536]{2,1,0:T(8,128)(2,1)S(1)}, bf16[4,192,1536]{2,1,0:T(8,128)(2,1)}, u32[]{:S(2)}, u32[]{:S(2)}) collective-permute-start(bf16[4,192,1536]{2,1,0:T(8,128)(2,1)S(1)} %get-tuple-element.221), channel_id=1, source_target_pairs={{0,4},{4,0},{8,12},{12,8},{16,20},{20,16},{24,28},{28,24},{1,5},{5... | collective-permute-start | bytes 7077896 | tf_op jit(solution)/shard_map/ppermute | solution.py:43
  314.7 18.2 %collective-permute-start.32 = (bf16[1632,128]{1,0:T(8,128)(2,1)S(1)}, bf16[1632,128]{1,0:T(8,128)(2,1)S(1)}, u32[]{:S(2)}, u32[]{:S(2)}) collective-permute-start(bf16[1632,128]{1,0:T(8,128)(2,1)S(1)} %shard_map.280.rest_0_.rest_4_), channel_id=1, source_target_pairs={{0,3},{1,0},{2,1},{3,2},{4,7},{5,4},{6,5},{7,6},{8,11},{9,8},{10,9... | collective-permute-start | bytes 1253384 | tf_op jit(solution)/shard_map/ppermute | solution.py:21
  320.5 36.7 %collective-permute-start.31 = (bf16[1632,128]{1,0:T(8,128)(2,1)S(1)}, bf16[1632,128]{1,0:T(8,128)(2,1)S(1)}, u32[]{:S(2)}, u32[]{:S(2)}) collective-permute-start(bf16[1632,128]{1,0:T(8,128)(2,1)S(1)} %shard_map.280.rest_0_.rest_4_), channel_id=1, source_target_pairs={{0,2},{1,3},{2,0},{3,1},{4,6},{5,7},{6,4},{7,5},{8,10},{9,11},{10,... | collective-permute-start | bytes 1253384 | tf_op jit(solution)/shard_map/ppermute | solution.py:21
  320.5 37.4 %collective-permute-start.30 = (bf16[1632,128]{1,0:T(8,128)(2,1)S(1)}, bf16[1632,128]{1,0:T(8,128)(2,1)S(1)}, u32[]{:S(2)}, u32[]{:S(2)}) collective-permute-start(bf16[1632,128]{1,0:T(8,128)(2,1)S(1)} %shard_map.280.rest_0_.rest_4_), channel_id=1, source_target_pairs={{0,1},{1,2},{2,3},{3,0},{4,5},{5,6},{6,7},{7,4},{8,9},{9,10},{10,1... | collective-permute-start | bytes 1253384 | tf_op jit(solution)/shard_map/ppermute | solution.py:21
  325.5 56.4 %collective-permute-start.39 = (bf16[2,192,2304]{2,1,0:T(8,128)(2,1)}, bf16[2,192,2304]{2,1,0:T(8,128)(2,1)}, u32[]{:S(2)}, u32[]{:S(2)}) collective-permute-start(bf16[2,192,2304]{2,1,0:T(8,128)(2,1)} %get-tuple-element.225), channel_id=1, source_target_pairs={{0,8},{4,12},{8,0},{12,4},{16,24},{20,28},{24,16},{28,20},{1,9},{5... | collective-permute-start | bytes 5308424 | tf_op jit(solution)/shard_map/ppermute | solution.py:43
  329.3 56.3 %collective-permute-start.40 = (bf16[2,192,2304]{2,1,0:T(8,128)(2,1)}, bf16[2,192,2304]{2,1,0:T(8,128)(2,1)S(1)}, u32[]{:S(2)}, u32[]{:S(2)}) collective-permute-start(bf16[2,192,2304]{2,1,0:T(8,128)(2,1)} %get-tuple-element.228), channel_id=1, source_target_pairs={{0,16},{4,20},{8,24},{12,28},{16,0},{20,4},{24,8},{28,12},{1,17},{... | collective-permute-start | bytes 5308424 | tf_op jit(solution)/shard_map/ppermute | solution.py:43
  358.7 45.4 %collective-permute-start.36 = (bf16[128,1536]{1,0:T(8,128)(2,1)}, bf16[128,1536]{1,0:T(8,128)(2,1)S(1)}, u32[]{:S(2)}, u32[]{:S(2)}) collective-permute-start(bf16[128,1536]{1,0:T(8,128)(2,1)} %get-tuple-element.233), channel_id=1, source_target_pairs={{0,3},{1,0},{2,1},{3,2},{4,7},{5,4},{6,5},{7,6},{8,11},{9,8},{10,9... | collective-permute-start | bytes 1179656 | tf_op jit(solution)/shard_map/ppermute | solution.py:21
  358.7 45.4 %collective-permute-start.37 = (bf16[128,1536]{1,0:T(8,128)(2,1)}, bf16[128,1536]{1,0:T(8,128)(2,1)}, u32[]{:S(2)}, u32[]{:S(2)}) collective-permute-start(bf16[128,1536]{1,0:T(8,128)(2,1)} %get-tuple-element.234), channel_id=1, source_target_pairs={{0,2},{1,3},{2,0},{3,1},{4,6},{5,7},{6,4},{7,5},{8,10},{9,11},{10,... | collective-permute-start | bytes 1179656 | tf_op jit(solution)/shard_map/ppermute | solution.py:21
  360.2 43.9 %collective-permute-start.38 = (bf16[128,1536]{1,0:T(8,128)(2,1)}, bf16[128,1536]{1,0:T(8,128)(2,1)}, u32[]{:S(2)}, u32[]{:S(2)}) collective-permute-start(bf16[128,1536]{1,0:T(8,128)(2,1)} %get-tuple-element.235), channel_id=1, source_target_pairs={{0,1},{1,2},{2,3},{3,0},{4,5},{5,6},{6,7},{7,4},{8,9},{9,10},{10,1... | collective-permute-start | bytes 1179656 | tf_op jit(solution)/shard_map/ppermute | solution.py:21
  409.3 17.1 %collective-permute-start.41 = (bf16[4,192,1536]{2,1,0:T(8,128)(2,1)}, bf16[4,192,1536]{2,1,0:T(8,128)(2,1)}, u32[]{:S(2)}, u32[]{:S(2)}) collective-permute-start(bf16[4,192,1536]{2,1,0:T(8,128)(2,1)} %get-tuple-element.254), channel_id=1, source_target_pairs={{0,4},{4,0},{8,12},{12,8},{16,20},{20,16},{24,28},{28,24},{1,5},{5... | collective-permute-start | bytes 7077896 | tf_op jit(solution)/shard_map/ppermute | solution.py:43
  409.3 17.1 %collective-permute-start.42 = (bf16[4,192,1536]{2,1,0:T(8,128)(2,1)}, bf16[4,192,1536]{2,1,0:T(8,128)(2,1)}, u32[]{:S(2)}, u32[]{:S(2)}) collective-permute-start(bf16[4,192,1536]{2,1,0:T(8,128)(2,1)} %get-tuple-element.255), channel_id=1, source_target_pairs={{0,4},{4,0},{8,12},{12,8},{16,20},{20,16},{24,28},{28,24},{1,5},{5... | collective-permute-start | bytes 7077896 | tf_op jit(solution)/shard_map/ppermute | solution.py:43
  409.8 16.6 %collective-permute-start.43 = (bf16[4,192,1536]{2,1,0:T(8,128)(2,1)}, bf16[4,192,1536]{2,1,0:T(8,128)(2,1)S(1)}, u32[]{:S(2)}, u32[]{:S(2)}) collective-permute-start(bf16[4,192,1536]{2,1,0:T(8,128)(2,1)} %get-tuple-element.253), channel_id=1, source_target_pairs={{0,4},{4,0},{8,12},{12,8},{16,20},{20,16},{24,28},{28,24},{1,5},{5... | collective-permute-start | bytes 7077896 | tf_op jit(solution)/shard_map/ppermute | solution.py:43
  409.8 22.9 %collective-permute-start.44 = (bf16[1,192,2304]{2,1,0:T(8,128)(2,1)}, bf16[1,192,2304]{2,1,0:T(8,128)(2,1)S(1)}, u32[]{:S(2)}, u32[]{:S(2)}) collective-permute-start(bf16[1,192,2304]{2,1,0:T(8,128)(2,1)} %get-tuple-element.241), channel_id=1, source_target_pairs={{0,16},{4,20},{8,24},{12,28},{16,0},{20,4},{24,8},{28,12},{1,17},{... | collective-permute-start | bytes 2654216 | tf_op jit(solution)/shard_map/ppermute | solution.py:43
  412.2 22.0 %collective-permute-start.45 = (bf16[1,192,2304]{2,1,0:T(8,128)(2,1)}, bf16[1,192,2304]{2,1,0:T(8,128)(2,1)S(1)}, u32[]{:S(2)}, u32[]{:S(2)}) collective-permute-start(bf16[1,192,2304]{2,1,0:T(8,128)(2,1)} %get-tuple-element.243), channel_id=1, source_target_pairs={{0,8},{4,12},{8,0},{12,4},{16,24},{20,28},{24,16},{28,20},{1,9},{5... | collective-permute-start | bytes 2654216 | tf_op jit(solution)/shard_map/ppermute | solution.py:43
  439.5 30.9 %collective-permute-start.47 = (bf16[2,192,1536]{2,1,0:T(8,128)(2,1)}, bf16[2,192,1536]{2,1,0:T(8,128)(2,1)}, u32[]{:S(2)}, u32[]{:S(2)}) collective-permute-start(bf16[2,192,1536]{2,1,0:T(8,128)(2,1)} %get-tuple-element.268), channel_id=1, source_target_pairs={{0,16},{4,20},{8,24},{12,28},{16,0},{20,4},{24,8},{28,12},{1,17},{... | collective-permute-start | bytes 3538952 | tf_op jit(solution)/shard_map/ppermute | solution.py:43
  443.4 27.6 %collective-permute-start.46 = (bf16[2,192,1536]{2,1,0:T(8,128)(2,1)}, bf16[2,192,1536]{2,1,0:T(8,128)(2,1)}, u32[]{:S(2)}, u32[]{:S(2)}) collective-permute-start(bf16[2,192,1536]{2,1,0:T(8,128)(2,1)} %get-tuple-element.264), channel_id=1, source_target_pairs={{0,8},{4,12},{8,0},{12,4},{16,24},{20,28},{24,16},{28,20},{1,9},{5... | collective-permute-start | bytes 3538952 | tf_op jit(solution)/shard_map/ppermute | solution.py:43
  444.7 31.3 %collective-permute-start.48 = (bf16[128,1536]{1,0:T(8,128)(2,1)}, bf16[128,1536]{1,0:T(8,128)(2,1)}, u32[]{:S(2)}, u32[]{:S(2)}) collective-permute-start(bf16[128,1536]{1,0:T(8,128)(2,1)} %get-tuple-element.290), channel_id=1, source_target_pairs={{0,3},{1,0},{2,1},{3,2},{4,7},{5,4},{6,5},{7,6},{8,11},{9,8},{10,9... | collective-permute-start | bytes 1179656 | tf_op jit(solution)/shard_map/ppermute | solution.py:21
  444.7 35.2 %collective-permute-start.49 = (bf16[128,1536]{1,0:T(8,128)(2,1)}, bf16[128,1536]{1,0:T(8,128)(2,1)}, u32[]{:S(2)}, u32[]{:S(2)}) collective-permute-start(bf16[128,1536]{1,0:T(8,128)(2,1)} %get-tuple-element.291), channel_id=1, source_target_pairs={{0,2},{1,3},{2,0},{3,1},{4,6},{5,7},{6,4},{7,5},{8,10},{9,11},{10,... | collective-permute-start | bytes 1179656 | tf_op jit(solution)/shard_map/ppermute | solution.py:21
  446.1 33.8 %collective-permute-start.50 = (bf16[128,1536]{1,0:T(8,128)(2,1)}, bf16[128,1536]{1,0:T(8,128)(2,1)}, u32[]{:S(2)}, u32[]{:S(2)}) collective-permute-start(bf16[128,1536]{1,0:T(8,128)(2,1)} %get-tuple-element.292), channel_id=1, source_target_pairs={{0,1},{1,2},{2,3},{3,0},{4,5},{5,6},{6,7},{7,4},{8,9},{9,10},{10,1... | collective-permute-start | bytes 1179656 | tf_op jit(solution)/shard_map/ppermute | solution.py:21
  472.6 16.3 %collective-permute-start.54 = (bf16[1,192,1536]{2,1,0:T(8,128)(2,1)S(1)}, bf16[1,192,1536]{2,1,0:T(8,128)(2,1)S(1)}, u32[]{:S(2)}, u32[]{:S(2)}) collective-permute-start(bf16[1,192,1536]{2,1,0:T(8,128)(2,1)S(1)} %get-tuple-element.286), channel_id=1, source_target_pairs={{0,8},{4,12},{8,0},{12,4},{16,24},{20,28},{24,16},{28,20},{1,9},{5... | collective-permute-start | bytes 1769480 | tf_op jit(solution)/shard_map/ppermute | solution.py:43
  475.4 16.3 %collective-permute-start.53 = (bf16[1,192,1536]{2,1,0:T(8,128)(2,1)S(1)}, bf16[1,192,1536]{2,1,0:T(8,128)(2,1)S(1)}, u32[]{:S(2)}, u32[]{:S(2)}) collective-permute-start(bf16[1,192,1536]{2,1,0:T(8,128)(2,1)S(1)} %get-tuple-element.283), channel_id=1, source_target_pairs={{0,16},{4,20},{8,24},{12,28},{16,0},{20,4},{24,8},{28,12},{1,17},{... | collective-permute-start | bytes 1769480 | tf_op jit(solution)/shard_map/ppermute | solution.py:43
  479.9 20.5 %collective-permute-start.51 = (bf16[2,192,768]{2,1,0:T(8,128)(2,1)}, bf16[2,192,768]{2,1,0:T(8,128)(2,1)S(1)}, u32[]{:S(2)}, u32[]{:S(2)}) collective-permute-start(bf16[2,192,768]{2,1,0:T(8,128)(2,1)} %get-tuple-element.293), channel_id=1, source_target_pairs={{0,8},{4,12},{8,0},{12,4},{16,24},{20,28},{24,16},{28,20},{1,9},{5... | collective-permute-start | bytes 1769480 | tf_op jit(solution)/shard_map/ppermute | solution.py:43
  480.5 21.1 %collective-permute-start.52 = (bf16[2,192,768]{2,1,0:T(8,128)(2,1)}, bf16[2,192,768]{2,1,0:T(8,128)(2,1)}, u32[]{:S(2)}, u32[]{:S(2)}) collective-permute-start(bf16[2,192,768]{2,1,0:T(8,128)(2,1)} %get-tuple-element.294), channel_id=1, source_target_pairs={{0,16},{4,20},{8,24},{12,28},{16,0},{20,4},{24,8},{28,12},{1,17},{... | collective-permute-start | bytes 1769480 | tf_op jit(solution)/shard_map/ppermute | solution.py:43
  494.0 7.7 %collective-permute-start.55 = (bf16[2,192,384]{2,1,0:T(8,128)(2,1)}, bf16[2,192,384]{2,1,0:T(8,128)(2,1)}, u32[]{:S(2)}, u32[]{:S(2)}) collective-permute-start(bf16[2,192,384]{2,1,0:T(8,128)(2,1)} %get-tuple-element.297), channel_id=1, source_target_pairs={{0,3},{1,0},{2,1},{3,2},{4,7},{5,4},{6,5},{7,6},{8,11},{9,8},{10,9... | collective-permute-start | bytes 884744 | tf_op jit(solution)/shard_map/ppermute | solution.py:21
  495.2 9.3 %collective-permute-start.56 = (bf16[2,192,384]{2,1,0:T(8,128)(2,1)S(1)}, bf16[2,192,384]{2,1,0:T(8,128)(2,1)}, u32[]{:S(2)}, u32[]{:S(2)}) collective-permute-start(bf16[2,192,384]{2,1,0:T(8,128)(2,1)S(1)} %get-tuple-element.298), channel_id=1, source_target_pairs={{0,1},{1,2},{2,3},{3,0},{4,5},{5,6},{6,7},{7,4},{8,9},{9,10},{10,1... | collective-permute-start | bytes 884744 | tf_op jit(solution)/shard_map/ppermute | solution.py:21
  499.5 9.9 %collective-permute-start.60 = (f32[8,1536]{1,0:T(8,128)S(1)}, f32[8,1536]{1,0:T(8,128)S(1)}, u32[]{:S(2)}, u32[]{:S(2)}) collective-permute-start(f32[8,1536]{1,0:T(8,128)S(1)} %add.355), channel_id=1, source_target_pairs={{0,8},{4,12},{8,0},{12,4},{16,24},{20,28},{24,16},{28,20},{1,9},{5... | collective-permute-start | bytes 147464 | tf_op jit(solution)/shard_map/ppermute | solution.py:43
  506.4 25.3 %collective-permute-start.58 = (bf16[1,192,768]{2,1,0:T(8,128)(2,1)}, bf16[1,192,768]{2,1,0:T(8,128)(2,1)}, u32[]{:S(2)}, u32[]{:S(2)}) collective-permute-start(bf16[1,192,768]{2,1,0:T(8,128)(2,1)} %get-tuple-element.305), channel_id=1, source_target_pairs={{0,8},{4,12},{8,0},{12,4},{16,24},{20,28},{24,16},{28,20},{1,9},{5... | collective-permute-start | bytes 884744 | tf_op jit(solution)/shard_map/ppermute | solution.py:43
  508.6 23.1 %collective-permute-start.57 = (bf16[1,192,768]{2,1,0:T(8,128)(2,1)}, bf16[1,192,768]{2,1,0:T(8,128)(2,1)S(1)}, u32[]{:S(2)}, u32[]{:S(2)}) collective-permute-start(bf16[1,192,768]{2,1,0:T(8,128)(2,1)} %get-tuple-element.301), channel_id=1, source_target_pairs={{0,16},{4,20},{8,24},{12,28},{16,0},{20,4},{24,8},{28,12},{1,17},{... | collective-permute-start | bytes 884744 | tf_op jit(solution)/shard_map/ppermute | solution.py:43
  509.5 6.6 %collective-permute-start.61 = (f32[8,1536]{1,0:T(8,128)S(1)}, f32[8,1536]{1,0:T(8,128)S(1)}, u32[]{:S(2)}, u32[]{:S(2)}) collective-permute-start(f32[8,1536]{1,0:T(8,128)S(1)} %add.356), channel_id=1, source_target_pairs={{0,16},{4,20},{8,24},{12,28},{16,0},{20,4},{24,8},{28,12},{1,17},{... | collective-permute-start | bytes 147464 | tf_op jit(solution)/shard_map/ppermute | solution.py:43
  520.3 8.9 %collective-permute-start.63 = (f32[8,1536]{1,0:T(8,128)S(1)}, f32[8,1536]{1,0:T(8,128)S(1)}, u32[]{:S(2)}, u32[]{:S(2)}) collective-permute-start(f32[8,1536]{1,0:T(8,128)S(1)} %add.358), channel_id=1, source_target_pairs={{0,2},{1,3},{2,0},{3,1},{4,6},{5,7},{6,4},{7,5},{8,10},{9,11},{10,... | collective-permute-start | bytes 147464 | tf_op jit(solution)/shard_map/ppermute | solution.py:43
  531.7 20.9 %collective-permute-start.67 = (bf16[2,192,384]{2,1,0:T(8,128)(2,1)}, bf16[2,192,384]{2,1,0:T(8,128)(2,1)S(1)}, u32[]{:S(2)}, u32[]{:S(2)}) collective-permute-start(bf16[2,192,384]{2,1,0:T(8,128)(2,1)} %copy-done.75), channel_id=1, source_target_pairs={{0,2},{1,3},{2,0},{3,1},{4,6},{5,7},{6,4},{7,5},{8,10},{9,11},{10,... | collective-permute-start | bytes 884744 | tf_op jit(solution)/shard_map/ppermute | solution.py:21
  534.9 25.5 %collective-permute-start.66 = (bf16[2,192,384]{2,1,0:T(8,128)(2,1)S(1)}, bf16[2,192,384]{2,1,0:T(8,128)(2,1)S(1)}, u32[]{:S(2)}, u32[]{:S(2)}) collective-permute-start(bf16[2,192,384]{2,1,0:T(8,128)(2,1)S(1)} %pad_maximum_fusion.12), channel_id=1, source_target_pairs={{0,1},{1,2},{2,3},{3,0},{4,5},{5,6},{6,7},{7,4},{8,9},{9,10},{10,1... | collective-permute-start | bytes 884744 | tf_op jit(solution)/shard_map/ppermute | solution.py:21
  537.7 22.7 %collective-permute-start.65 = (bf16[2,192,384]{2,1,0:T(8,128)(2,1)S(1)}, bf16[2,192,384]{2,1,0:T(8,128)(2,1)S(1)}, u32[]{:S(2)}, u32[]{:S(2)}) collective-permute-start(bf16[2,192,384]{2,1,0:T(8,128)(2,1)S(1)} %pad_maximum_fusion.11), channel_id=1, source_target_pairs={{0,2},{1,3},{2,0},{3,1},{4,6},{5,7},{6,4},{7,5},{8,10},{9,11},{10,... | collective-permute-start | bytes 884744 | tf_op jit(solution)/shard_map/ppermute | solution.py:21
  538.1 22.4 %collective-permute-start.64 = (bf16[2,192,384]{2,1,0:T(8,128)(2,1)S(1)}, bf16[2,192,384]{2,1,0:T(8,128)(2,1)S(1)}, u32[]{:S(2)}, u32[]{:S(2)}) collective-permute-start(bf16[2,192,384]{2,1,0:T(8,128)(2,1)S(1)} %pad_maximum_fusion.10), channel_id=1, source_target_pairs={{0,3},{1,0},{2,1},{3,2},{4,7},{5,4},{6,5},{7,6},{8,11},{9,8},{10,9... | collective-permute-start | bytes 884744 | tf_op jit(solution)/shard_map/ppermute | solution.py:21
  (121 other events, 1019.1 us)
Sparse Core Ops, SparseCore 0:
  77.9 62.1 all-gather.2

commit v5 on v4

--- a/solution.py
+++ b/solution.py
@@ -47,9 +47,10 @@
     return count.bit_length() - 1
 
 
-def gradient_kernel(natural, n_dp, at_ref, xt_ref, y_ref, keep_ref, send_ref, total_ref):
+def gradient_kernel(natural, turned, n_dp, at_ref, xt_ref, y_ref, keep_ref, send_ref, total_ref):
     dims = (((1,), (0,)), ((), ())) if natural else (((1,), (1,)), ((), ()))
-    total_ref[...] = lax.dot_general(xt_ref[...], y_ref[...], dims, preferred_element_type=F32)
+    xt = xt_ref[...].T if turned else xt_ref[...]
+    total_ref[...] = lax.dot_general(xt, y_ref[...], dims, preferred_element_type=F32)
     p, unit = at_ref[1], keep_ref.shape[1]
     for i in range(n_dp // 2):
         for odd, out in enumerate((keep_ref, send_ref)):
@@ -57,8 +58,8 @@
             out[i] = total_ref[pl.ds(first, unit), :].astype(BF)
 
 
-def gradient(xt, y, natural, at, n_dp):
-    width, rows = xt.shape
+def gradient(xt, y, natural, at, n_dp, turned=False):
+    width, rows = xt.shape[::-1] if turned else xt.shape
     unit = width // n_dp
     wide = y.shape[1] if natural else y.shape[0]
     step = wide // 3
@@ -68,17 +69,17 @@
     else:
         y_spec = pl.BlockSpec((step, rows), lambda i: (i, 0))
     return pl.pallas_call(
-        partial(gradient_kernel, natural, n_dp),
+        partial(gradient_kernel, natural, turned, n_dp),
         grid=(3,),
         in_specs=[
             pl.BlockSpec(memory_space=pltpu.SMEM),
-            pl.BlockSpec((width, rows), lambda i: (0, 0)),
+            pl.BlockSpec(xt.shape, lambda i: (0, 0)),
             y_spec,
         ],
         out_specs=[pl.BlockSpec((half, unit, step), lambda i: (0, 0, i))] * 2,
-        out_shape=[jax.ShapeDtypeStruct((half, unit, wide), BF)] * 2,
+        out_shape=[pltpu.HBM((half, unit, wide), BF)] * 2,
         scratch_shapes=[pltpu.VMEM((width, step), F32)],
-        compiler_params=pltpu.CompilerParams(vmem_limit_bytes=VMEM_LIMIT),
+        compiler_params=pltpu.CompilerParams(vmem_limit_bytes=24 * 1024 * 1024),
     )(at, xt, y)
 
 
@@ -121,8 +122,8 @@
         grid=(count // 2,),
         in_specs=specs,
         out_specs=[pl.BlockSpec((1, rows, total), lambda i: (i, 0, 0))] * 2,
-        out_shape=[jax.ShapeDtypeStruct((count // 2, rows, total), BF)] * 2,
-        compiler_params=pltpu.CompilerParams(vmem_limit_bytes=VMEM_LIMIT),
+        out_shape=[pltpu.HBM((count // 2, rows, total), BF)] * 2,
+        compiler_params=pltpu.CompilerParams(vmem_limit_bytes=20 * 1024 * 1024),
     )(*flat)
 
 
@@ -186,7 +187,7 @@
             jax.ShapeDtypeStruct((len(weights), rows, columns // n_t), F32 if k == 0 else BF)
             for k in range(n_t)
         ],
-        compiler_params=pltpu.CompilerParams(vmem_limit_bytes=VMEM_LIMIT),
+        compiler_params=pltpu.CompilerParams(vmem_limit_bytes=14 * 1024 * 1024),
     )(at, *flat)
 
 
@@ -270,7 +271,7 @@
         out_shape=outs,
         in_specs=[pl.BlockSpec(memory_space=pltpu.SMEM)]
         + [pl.BlockSpec(memory_space=pltpu.VMEM)] * len(ins),
-        compiler_params=pltpu.CompilerParams(vmem_limit_bytes=VMEM_LIMIT),
+        compiler_params=pltpu.CompilerParams(vmem_limit_bytes=28 * 1024 * 1024),
     )(at, *ins)
 
 
@@ -417,7 +418,7 @@
             ],
         ),
         out_shape=[jax.ShapeDtypeStruct((tall, one), BF)] * n_t,
-        compiler_params=pltpu.CompilerParams(vmem_limit_bytes=VMEM_LIMIT),
+        compiler_params=pltpu.CompilerParams(vmem_limit_bytes=20 * 1024 * 1024),
     )(span, q, k, v, seg, img)
 
 
@@ -455,7 +456,7 @@
             jax.ShapeDtypeStruct((heads * HD, one), BF),
             jax.ShapeDtypeStruct((2 * heads, one), F32),
         ],
-        compiler_params=pltpu.CompilerParams(vmem_limit_bytes=VMEM_LIMIT),
+        compiler_params=pltpu.CompilerParams(vmem_limit_bytes=8 * 1024 * 1024),
     )(*msgs)
 
 
@@ -476,7 +477,7 @@
     return pl.pallas_call(
         partial(message_kernel, heads),
         out_shape=jax.ShapeDtypeStruct((heads * (HD + 6), do.shape[1]), BF),
-        compiler_params=pltpu.CompilerParams(vmem_limit_bytes=VMEM_LIMIT),
+        compiler_params=pltpu.CompilerParams(vmem_limit_bytes=6 * 1024 * 1024),
     )(do, out, stat, coef)
 
 
@@ -577,7 +578,7 @@
             jax.ShapeDtypeStruct(k.shape, BF),
             jax.ShapeDtypeStruct(v.shape, BF),
         ],
-        compiler_params=pltpu.CompilerParams(vmem_limit_bytes=VMEM_LIMIT),
+        compiler_params=pltpu.CompilerParams(vmem_limit_bytes=36 * 1024 * 1024),
         cost_estimate=pl.CostEstimate(
             flops=60 * heads * HD * rows * keys,
             bytes_accessed=60 * 1024 * 1024,
@@ -686,7 +687,7 @@
         + [pl.BlockSpec((8, width), lambda i: (0, 0))],
         out_shape=[jax.ShapeDtypeStruct((rows, width), BF if k else F32) for k in range(n_t)]
         + [jax.ShapeDtypeStruct((8, width), F32)],
-        compiler_params=pltpu.CompilerParams(vmem_limit_bytes=VMEM_LIMIT),
+        compiler_params=pltpu.CompilerParams(vmem_limit_bytes=50 * 1024 * 1024),
     )(back_q, back_k, back_v, wq, wk, wv, *blocks)
 
 
@@ -731,7 +732,7 @@
             jax.ShapeDtypeStruct((unit, columns), F32),
             jax.ShapeDtypeStruct((unit, columns), F32),
         ],
-        compiler_params=pltpu.CompilerParams(vmem_limit_bytes=VMEM_LIMIT),
+        compiler_params=pltpu.CompilerParams(vmem_limit_bytes=20 * 1024 * 1024),
     )(*result_terms, *latent_terms, *feeds, middle, back_middle, latents, gain[None])
 
 
@@ -769,8 +770,6 @@
     heads = inner // HD
     images = lengths.shape[0]
 
-    count_part = jnp.full((8, 128), jnp.sum(valid).astype(F32))
-    count_total = all_sum(count_part, [("dp", n_dp)])[0, 0]
 
     ends = jnp.sum(
         jnp.where(jnp.arange(images)[:, None] <= jnp.arange(images)[None, :], lengths[:, None], 0),
@@ -813,7 +812,7 @@
     own_normed = (own_hat * latent_gain + latent_shift).astype(BF)
     key_input = jnp.concatenate([media_normed, own_normed], axis=0)
     kv_own = [key_value_weight[:, 0], key_value_weight[:, 1]]
-    *kv_z, key_input, count_total, k_own, v_own = after([*kv_z, key_input, count_total, *kv_own])
+    *kv_z, key_input, k_own, v_own = after([*kv_z, key_input, *kv_own])
     q_share = share_of(query_weight, 0, n_dp).reshape(2, unit // 2, part)
     o_share = share_of(output_weight, 0, n_dp)
     o_unit = o_share.shape[0]
@@ -858,6 +857,9 @@
     sent = attend_forward(queries, keys, values, key_image, row_image, span, n_t)
     sent = after(sent, wo)
     got = [sent[0]] + [rotate(sent[k], n_t, -k) for k in range(1, n_t)]
+    count_part = after(jnp.full((8, 128), jnp.sum(valid).astype(F32)), *sent[1:])
+    count_total = all_sum(count_part, [("dp", n_dp)])[0, 0]
+    got = after(got, count_total)
     attended, stat = combine(got, heads)
     entropy = stat[:heads] - stat[heads:]
     own_valid = row_valid[:, :own_rows]
@@ -891,7 +893,7 @@
     own_coef = own_valid / count_total
     message = make_message(back_attended, attended, stat, own_coef, heads)
     messages = gather_blocks(message, n_t)
-    out_keep, out_send = gradient(back_branch.T, attended, False, at, n_dp)
+    out_keep, out_send = gradient(back_branch, attended, False, at, n_dp, True)
     out_got = partner(out_send, "dp", n_dp, 1)
     down_got, up_got, out_got = after([down_got, up_got, out_got], message)
     feed_pair = first_cut((down_keep, down_got), (up_keep, up_got), (out_keep, out_got), orders, n_dp)
@@ -955,7 +957,8 @@
     sums = [media_sums[0], media_sums[1], latent_sums[0], latent_sums[1]] + gain_shift(back_feed, feed_hat)
     sums = jnp.stack(sums + [jnp.full((width,), penalty_part)] * 2)
     sums = after(sums, features_grad)
-    sums = all_sum(sums, [("dp", n_dp), ("tensor", n_t)])
+    sums = after(all_sum(sums, [("dp", n_dp)]), *q_blocks)
+    sums = all_sum(sums, [("tensor", n_t)])
     penalty = sums[6, 0] / count_total
     share = width // (n_dp * n_t)
     mine = lax.dynamic_index_in_dim(

time: 576 us -> 546 us (0.948)
  local copies, waits for them, and re-layouts: 82.6 us -> 60.8 us
  Pallas kernels: 149 us -> 132 us
  waiting for transfers between devices: 193 us -> 210 us
    unnamed x243 -> x279, local copies, waits for them, and re-layouts: 42.9 us -> 30.5 us
    ppermute x30, waiting for transfers between devices: 127 us -> 136 us  [rotate(): lax.ppermute(x, 'tensor', [(i, (i + shift) % count) for i in range(count)])]
    ppermute x38, waiting for transfers between devices: 66 us -> 74.3 us  [partner(): return lax.ppermute(x, axis, [(i, i ^ offset) for i in range(count)])]
    pallas_call x4, Pallas kernels: 29.1 us -> 21.5 us  [place(): pl.pallas_call(kernel, out_shape=outs, in_specs=[pl.BlockSpec(memory_spac...]
  transfers between devices with their start and end apart: 69 -> 69, of which waited for: 28 -> 32; matrix products, arithmetic and copies ran while one was open for 12% -> 11% of each run, Pallas kernels for 21% -> 19%
where the time goes in v5:
time: 546 us; the launch traced here: 541 us
  waiting for transfers between devices  210 us (38%)
  Pallas kernels  132 us (24%)
  starting transfers between devices  75.9 us (14%)
  local copies, waits for them, and re-layouts  60.8 us (11%)
  other arithmetic  25 us (5%)
  between operations  19.1 us (3%)
  matrix products  17.7 us (3%)
    ppermute x30, waiting for transfers between devices, rotate(): lax.ppermute(x, 'tensor', [(i, (i + shift) % count) for i in range(count)])  136 us
    ppermute x38, waiting for transfers between devices, partner(): return lax.ppermute(x, axis, [(i, i ^ offset) for i in range(count)])  74.3 us
    ppermute x30, starting transfers between devices, rotate(): lax.ppermute(x, 'tensor', [(i, (i + shift) % count) for i in range(count)])  45.9 us
    pallas_call x6, Pallas kernels, gradient(): pl.pallas_call(partial(gradient_kernel, natural, turned, n_dp), grid=(3,)...  33.1 us
    unnamed x279, local copies, waits for them, and re-layouts  30.5 us
    ppermute x38, starting transfers between devices, partner(): return lax.ppermute(x, axis, [(i, i ^ offset) for i in range(count)])  29.9 us
    pallas_call x4, Pallas kernels, place(): pl.pallas_call(kernel, out_shape=outs, in_specs=[pl.BlockSpec(memory_spac...  21.5 us
    pallas_call x12, Pallas kernels, reduce_cut(): pl.pallas_call(partial(cut_kernel, widths), grid=(count // 2,), in_specs=...  19.6 us
  transfers between devices with their start and end apart: 69, of which 32 were waited for; matrix products, arithmetic and copies ran while one was open for 11% of the time, Pallas kernels for 19%

profile of v5, /device:TPU:0, one launch (start us, length us, event | category | flops | bytes accessed | tf_op | source)
XLA Modules:
  0.0 541.3 jit_solution(9763360589881249355)
XLA Ops:
  8.5 5.1 collective-permute-start.2
  14.6 7.9 %fusion.40 = (bf16[1536,1,384]{2,1,0:T(2,128)(2,1)}, bf16[1536,1,384]{2,1,0:T(2,128)(2,1)}) fusion(bf16[1536,2,384]{2,1,0:T(2,128)(2,1)} %param.27), kind=kLoop, calls=%fused_computation.177 | loop fusion | bytes 4718592 | tf_op jit(solution)/shard_map/slice | solution.py:814
  26.2 4.2 copy_bitcast_fusion
  32.8 5.9 %collective-permute-done.1 = bf16[2,192,384]{2,1,0:T(8,128)(2,1)S(1)} collective-permute-done((bf16[2,192,384]{2,1,0:T(8,128)(2,1)S(1)}, bf16[2,192,384]{2,1,0:T(8,128)(2,1)S(1)}, u32[]{:S(2)}, u32[]{:S(2)}) %collective-permute-start.1) | collective-permute-done | bytes 294944 | tf_op jit(solution)/shard_map/ppermute | solution.py:21
  38.8 2.9 collective-permute-start.4
  41.7 2.5 collective-permute-start.3
  47.5 19.5 %collective-permute-done.4 = bf16[2,192,384]{2,1,0:T(8,128)(2,1)S(1)} collective-permute-done((bf16[2,192,384]{2,1,0:T(8,128)(2,1)S(1)}, bf16[2,192,384]{2,1,0:T(8,128)(2,1)S(1)}, u32[]{:S(2)}, u32[]{:S(2)}) %collective-permute-start.4) | collective-permute-done | bytes 294944 | tf_op jit(solution)/shard_map/ppermute | solution.py:21
  74.9 16.7 %collective-permute-done.8 = bf16[2,3,192,384]{3,2,1,0:T(8,128)(2,1)S(1)} collective-permute-done((bf16[2,3,192,384]{3,2,1,0:T(8,128)(2,1)S(1)}, bf16[2,3,192,384]{3,2,1,0:T(8,128)(2,1)S(1)}, u32[]{:S(2)}, u32[]{:S(2)}) %collective-permute-start.8) | collective-permute-done | bytes 884768 | tf_op jit(solution)/shard_map/ppermute | solution.py:43
  96.2 5.3 shard_map.271
  104.1 2.1 collective-permute-done.10
  110.4 5.3 shard_map.272
  119.3 9.3 %collective-permute-done.14 = bf16[2,3,192,384]{3,2,1,0:T(8,128)(2,1)S(1)} collective-permute-done((bf16[2,3,192,384]{3,2,1,0:T(8,128)(2,1)S(1)}, bf16[2,3,192,384]{3,2,1,0:T(8,128)(2,1)S(1)}, u32[]{:S(2)}, u32[]{:S(2)}) %collective-permute-start.14) | collective-permute-done | bytes 884768 | tf_op jit(solution)/shard_map/ppermute | solution.py:43
  131.7 2.7 dynamic-slice_bitcast_fusion
  136.7 7.5 %shard_map.273 = (bf16[1536,1536]{1,0:T(8,128)(2,1)S(1)}, bf16[1536,512]{1,0:T(8,128)(2,1)S(1)}, bf16[1536,512]{1,0:T(8,128)(2,1)S(1)}) custom-call(s32[2]{0:T(128)S(1)} %pad_add_fusion.2.at_ref, bf16[512,1536]{1,0:T(8,128)(2,1)S(1)} %fusion.7.x_ref, bf16[1536,384]{1,0:T(8,128)(2,1)S(1)} %copy-done.56, ...), custom_call_target="tpu_custom_call" | custom-call | tf_op jit(solution)/shard_map/pallas_call | solution.py:269
  144.3 2.1 copy-done.30
  146.4 8.1 %shard_map.274 = (bf16[1632,128]{1,0:T(8,128)(2,1)S(1)}, bf16[1632,128]{1,0:T(8,128)(2,1)}, bf16[1632,128]{1,0:T(8,128)(2,1)}, bf16[1632,128]{1,0:T(8,128)(2,1)}) custom-call(s32[2,4]{1,0:T(2,128)S(1)} %pad_add_fusion.1.span_ref, bf16[1536,512]{1,0:T(8,128)(2,1)S(1)} %get-tuple-element.197.q_ref, bf16[1536,640]{1,0:T(8,128)(2,1)S(1)} %copy-done.45, ...), custom_call_target="tpu_custom_call" | custom-call | tf_op jit(solution)/shard_map/pallas_call | solution.py:401
  154.5 3.5 shard_map.275
  158.0 2.1 copy-done.6
  161.9 2.0 collective-permute-start.20
  167.3 2.8 collective-permute-done.22
  170.6 3.0 collective-permute-done.23
  174.2 24.7 %collective-permute-done.19.refs_2_ = bf16[1632,128]{1,0:T(8,128)(2,1)} collective-permute-done((bf16[1632,128]{1,0:T(8,128)(2,1)}, bf16[1632,128]{1,0:T(8,128)(2,1)}, u32[]{:S(2)}, u32[]{:S(2)}) %collective-permute-start.19) | collective-permute-done | bytes 417824 | tf_op jit(solution)/shard_map/ppermute | solution.py:21
  201.1 3.4 fusion.48
  207.0 2.1 collective-permute-start.24
  209.4 6.3 %collective-permute-done.26 = bf16[128,1536]{1,0:T(8,128)(2,1)S(1)} collective-permute-done((bf16[128,1536]{1,0:T(8,128)(2,1)S(1)}, bf16[128,1536]{1,0:T(8,128)(2,1)S(1)}, u32[]{:S(2)}, u32[]{:S(2)}) %collective-permute-start.26) | collective-permute-done | bytes 393248 | tf_op jit(solution)/shard_map/ppermute | solution.py:21
  215.7 25.9 %collective-permute-done.25 = bf16[128,1536]{1,0:T(8,128)(2,1)S(1)} collective-permute-done((bf16[128,1536]{1,0:T(8,128)(2,1)S(1)}, bf16[128,1536]{1,0:T(8,128)(2,1)S(1)}, u32[]{:S(2)}, u32[]{:S(2)}) %collective-permute-start.25) | collective-permute-done | bytes 393248 | tf_op jit(solution)/shard_map/ppermute | solution.py:21
  241.6 6.6 %multiply_convert_fusion = (bf16[512,1536]{1,0:T(8,128)(2,1)}, f32[512,1536]{1,0:T(8,128)S(1)}) fusion(bf16[1536,1536]{1,0:T(8,128)(2,1)} %param.29, bf16[128,1536]{1,0:T(8,128)(2,1)S(1)} %collective-permute-done.26, bf16[128,1536]{1,0:T(8,128)(2,1)S(1)} %collective-permute-done.25, bf16[128,1536]{1,0:T(8,128)(2,1)S(1)} %collective-permute-done.24, ...), kind=kOutput, calls=%fused_computation.22 | convolution fusion | flops 2426142720 | bytes 11010048 | tf_op jit(solution)/shard_map/rd,df->rf/dot_general | solution.py:740
  248.2 3.7 fusion.16.y_ref
  252.0 2.6 convolution_convert_fusion
  256.3 3.3 collective-permute-start.27
  259.7 2.6 copy.60.xt_ref
  262.3 2.6 fusion.23
  264.9 2.6 copy.61.xt_ref
  268.9 6.0 %shard_map.277 = (f32[128,1536]{1,0:T(8,128)S(1)}, bf16[128,1536]{1,0:T(8,128)(2,1)}, bf16[128,1536]{1,0:T(8,128)(2,1)}, bf16[128,1536]{1,0:T(8,128)(2,1)}) custom-call(bf16[512,1536]{1,0:T(8,128)(2,1)S(1)} %copy-done.26, bf16[1536,1536]{1,0:T(8,128)(2,1)} %b_ref.1), custom_call_target="tpu_custom_call" | custom-call | tf_op jit(solution)/shard_map/pallas_call | solution.py:704
  275.8 5.2 shard_map.278
  281.2 5.2 shard_map.279
  290.2 4.3 shard_map.281
  296.9 6.9 %collective-permute-start.32 = (bf16[1632,128]{1,0:T(8,128)(2,1)S(1)}, bf16[1632,128]{1,0:T(8,128)(2,1)S(1)}, u32[]{:S(2)}, u32[]{:S(2)}) collective-permute-start(bf16[1632,128]{1,0:T(8,128)(2,1)S(1)} %shard_map.280.rest_0_.rest_4_), channel_id=1, source_target_pairs={{0,3},{1,0},{2,1},{3,2},{4,7},{5,4},{6,5},{7,6},{8,11},{9,8},{10,9... | collective-permute-start | bytes 1253384 | tf_op jit(solution)/shard_map/ppermute | solution.py:21
  306.0 2.4 shard_map.282
  310.4 2.4 shard_map.283
  313.8 27.9 %collective-permute-done.31.rest_2_.rest_6_ = bf16[1632,128]{1,0:T(8,128)(2,1)S(1)} collective-permute-done((bf16[1632,128]{1,0:T(8,128)(2,1)S(1)}, bf16[1632,128]{1,0:T(8,128)(2,1)S(1)}, u32[]{:S(2)}, u32[]{:S(2)}) %collective-permute-start.31) | collective-permute-done | bytes 417824 | tf_op jit(solution)/shard_map/ppermute | solution.py:21
  342.8 2.0 collective-permute-start.38
  344.8 10.8 %shard_map.284 = (bf16[1536,512]{1,0:T(8,128)(2,1)S(1)}, bf16[1536,640]{1,0:T(8,128)(2,1)S(1)}, bf16[1536,640]{1,0:T(8,128)(2,1)S(1)}) custom-call(s32[2,4]{1,0:T(2,128)S(1)} %pad_add_fusion.1.span_ref, bf16[1536,512]{1,0:T(8,128)(2,1)S(1)} %copy-done.53, bf16[1536,640]{1,0:T(8,128)(2,1)S(1)} %copy-done.46, bf16[1536,640]{1,0:T(8,128)(2,1)S(1)} %copy-done.49, ...), custom_call_target="tpu_custom_call" | custom-call | flops 30198988800 | bytes 62914560 | tf_op jit(solution)/shard_map/pallas_call | solution.py:555
  360.9 6.6 %shard_map.287 = (bf16[4,192,1536]{2,1,0:T(8,128)(2,1)}, bf16[4,192,1536]{2,1,0:T(8,128)(2,1)}) custom-call(s32[2]{0:T(128)S(1)} %pad_add_fusion.2.at_ref, bf16[1536,640]{1,0:T(8,128)(2,1)S(1)} %copy-done.21, bf16[1536,640]{1,0:T(8,128)(2,1)S(1)} %get-tuple-element.256.y_ref.dv_ref), custom_call_target="tpu_custom_call" | custom-call | tf_op jit(solution)/shard_map/pallas_call | solution.py:71
  367.4 6.5 %shard_map.288 = (bf16[4,192,1536]{2,1,0:T(8,128)(2,1)}, bf16[4,192,1536]{2,1,0:T(8,128)(2,1)}) custom-call(s32[2]{0:T(128)S(1)} %pad_add_fusion.2.at_ref, bf16[1536,640]{1,0:T(8,128)(2,1)S(1)} %copy-done.21, bf16[1536,640]{1,0:T(8,128)(2,1)S(1)} %get-tuple-element.289.y_ref.dk_ref), custom_call_target="tpu_custom_call" | custom-call | tf_op jit(solution)/shard_map/pallas_call | solution.py:71
  374.0 3.3 collective-permute-done.37.refs_2_
  377.3 5.3 shard_map.289
  384.9 12.1 %shard_map.290 = (f32[128,1536]{1,0:T(8,128)S(1)}, bf16[128,1536]{1,0:T(8,128)(2,1)}, bf16[128,1536]{1,0:T(8,128)(2,1)}, bf16[128,1536]{1,0:T(8,128)(2,1)}, f32[8,1536]{1,0:T(8,128)S(1)}) custom-call(bf16[1536,512]{1,0:T(8,128)(2,1)} %copy-done.27, bf16[1536,640]{1,0:T(8,128)(2,1)} %copy-done.8, bf16[1536,640]{1,0:T(8,128)(2,1)} %copy-done.10, ...), custom_call_target="tpu_custom_call" | custom-call | tf_op jit(solution)/shard_map/pallas_call | solution.py:681
  399.3 6.1 %collective-permute-done.44.refs_1_.refs_9_ = bf16[1,192,2304]{2,1,0:T(8,128)(2,1)S(1)} collective-permute-done((bf16[1,192,2304]{2,1,0:T(8,128)(2,1)}, bf16[1,192,2304]{2,1,0:T(8,128)(2,1)S(1)}, u32[]{:S(2)}, u32[]{:S(2)}) %collective-permute-start.44) | collective-permute-done | bytes 884768 | tf_op jit(solution)/shard_map/ppermute | solution.py:43
  405.7 3.0 shard_map.292
  415.8 2.0 collective-permute-start.50
  425.4 12.1 %shard_map.296 = (f32[512,1536]{1,0:T(8,128)}, f32[8,1536]{1,0:T(8,128)S(1)}) custom-call(bf16[1536,640]{1,0:T(8,128)(2,1)S(1)} %copy-done.9, bf16[1536,640]{1,0:T(8,128)(2,1)S(1)} %copy-done.11, bf16[1536,1536]{1,0:T(8,128)(2,1)} %copy-done.4, bf16[1536,1536]{1,0:T(8,128)(2,1)} %copy-done.5, bf16[512,1536]{1,0:T(8,128)(2,1)S(1)} %bitcast.140, ...), custom_call_target="tpu_custom_call" | custom-call | tf_op jit(solution)/shard_map/pallas_call | solution.py:636
  445.2 4.2 collective-permute-done.49.refs_6_
  451.8 5.0 collective-permute-done.54.refs_3_
  456.8 3.0 collective-permute-done.53.refs_1_
  463.7 2.9 collective-permute-done.51.refs_1_.refs_3_
  466.7 2.7 collective-permute-done.52.refs_1_.refs_3_
  469.4 3.8 collective-permute-done.56
  480.9 2.9 collective-permute-done.60
  484.5 3.6 collective-permute-done.61
  495.9 2.9 collective-permute-start.65
  500.8 13.5 %collective-permute-done.67 = bf16[2,192,384]{2,1,0:T(8,128)(2,1)S(1)} collective-permute-done((bf16[2,192,384]{2,1,0:T(8,128)(2,1)S(1)}, bf16[2,192,384]{2,1,0:T(8,128)(2,1)S(1)}, u32[]{:S(2)}, u32[]{:S(2)}) %collective-permute-start.67) | collective-permute-done | bytes 294944 | tf_op jit(solution)/shard_map/ppermute | solution.py:21
  517.9 4.3 shard_map.303
  522.1 6.3 %collective-permute-done.63 = f32[8,1536]{1,0:T(8,128)S(1)} collective-permute-done((f32[8,1536]{1,0:T(8,128)S(1)}, f32[8,1536]{1,0:T(8,128)S(1)}, u32[]{:S(2)}, u32[]{:S(2)}) %collective-permute-start.63) | collective-permute-done | bytes 49184 | tf_op jit(solution)/shard_map/ppermute | solution.py:43
  (506 shorter events, 130.1 us)
Async XLA Ops:
  7.2 124.5 %all-gather.3.cloned.1.call-start = ((), (), s32[]{:S(2)}) async-start(), calls=%async_computation | async-start | bytes 3932160 | tf_op jit(solution)/shard_map/all_gather | solution.py:826
  8.5 24.3 %collective-permute-start.2 = (bf16[2,192,384]{2,1,0:T(8,128)(2,1)S(1)}, bf16[2,192,384]{2,1,0:T(8,128)(2,1)S(1)}, u32[]{:S(2)}, u32[]{:S(2)}) collective-permute-start(bf16[2,192,384]{2,1,0:T(8,128)(2,1)S(1)} %bitcast.151), channel_id=1, source_target_pairs={{0,3},{1,0},{2,1},{3,2},{4,7},{5,4},{6,5},{7,6},{8,11},{9,8},{10,9... | collective-permute-start | bytes 884744 | tf_op jit(solution)/shard_map/ppermute | solution.py:21
  13.6 25.1 %collective-permute-start.1 = (bf16[2,192,384]{2,1,0:T(8,128)(2,1)S(1)}, bf16[2,192,384]{2,1,0:T(8,128)(2,1)S(1)}, u32[]{:S(2)}, u32[]{:S(2)}) collective-permute-start(bf16[2,192,384]{2,1,0:T(8,128)(2,1)S(1)} %bitcast.152), channel_id=1, source_target_pairs={{0,2},{1,3},{2,0},{3,1},{4,6},{5,7},{6,4},{7,5},{8,10},{9,11},{10,... | collective-permute-start | bytes 884744 | tf_op jit(solution)/shard_map/ppermute | solution.py:21
  13.6 25.1 %collective-permute-start = (bf16[2,192,384]{2,1,0:T(8,128)(2,1)S(1)}, bf16[2,192,384]{2,1,0:T(8,128)(2,1)S(1)}, u32[]{:S(2)}, u32[]{:S(2)}) collective-permute-start(bf16[2,192,384]{2,1,0:T(8,128)(2,1)S(1)} %bitcast.153), channel_id=1, source_target_pairs={{0,1},{1,2},{2,3},{3,0},{4,5},{5,6},{6,7},{7,4},{8,9},{9,10},{10,1... | collective-permute-start | bytes 884744 | tf_op jit(solution)/shard_map/ppermute | solution.py:21
  38.8 8.7 %collective-permute-start.5 = (bf16[2,192,384]{2,1,0:T(8,128)(2,1)S(1)}, bf16[2,192,384]{2,1,0:T(8,128)(2,1)S(1)}, u32[]{:S(2)}, u32[]{:S(2)}) collective-permute-start(bf16[2,192,384]{2,1,0:T(8,128)(2,1)S(1)} %pad_maximum_fusion.9), channel_id=1, source_target_pairs={{0,3},{1,0},{2,1},{3,2},{4,7},{5,4},{6,5},{7,6},{8,11},{9,8},{10,9... | collective-permute-start | bytes 884744 | tf_op jit(solution)/shard_map/ppermute | solution.py:21
  38.8 28.1 %collective-permute-start.4 = (bf16[2,192,384]{2,1,0:T(8,128)(2,1)S(1)}, bf16[2,192,384]{2,1,0:T(8,128)(2,1)S(1)}, u32[]{:S(2)}, u32[]{:S(2)}) collective-permute-start(bf16[2,192,384]{2,1,0:T(8,128)(2,1)S(1)} %pad_maximum_fusion.9), channel_id=1, source_target_pairs={{0,2},{1,3},{2,0},{3,1},{4,6},{5,7},{6,4},{7,5},{8,10},{9,11},{10,... | collective-permute-start | bytes 884744 | tf_op jit(solution)/shard_map/ppermute | solution.py:21
  41.7 25.3 %collective-permute-start.3 = (bf16[2,192,384]{2,1,0:T(8,128)(2,1)S(1)}, bf16[2,192,384]{2,1,0:T(8,128)(2,1)S(1)}, u32[]{:S(2)}, u32[]{:S(2)}) collective-permute-start(bf16[2,192,384]{2,1,0:T(8,128)(2,1)S(1)} %pad_maximum_fusion.9), channel_id=1, source_target_pairs={{0,1},{1,2},{2,3},{3,0},{4,5},{5,6},{6,7},{7,4},{8,9},{9,10},{10,1... | collective-permute-start | bytes 884744 | tf_op jit(solution)/shard_map/ppermute | solution.py:21
  44.3 24.7 %collective-permute-start.6 = (bf16[1,3,192,384]{3,2,1,0:T(8,128)(2,1)S(1)}, bf16[1,3,192,384]{3,2,1,0:T(8,128)(2,1)}, u32[]{:S(2)}, u32[]{:S(2)}) collective-permute-start(bf16[1,3,192,384]{3,2,1,0:T(8,128)(2,1)S(1)} %maximum_bitcast_fusion.2), channel_id=1, source_target_pairs={{0,8},{4,12},{8,0},{12,4},{16,24},{20,28},{24,16},{28,20},{1,9},{5... | collective-permute-start | bytes 1327112 | tf_op jit(solution)/shard_map/ppermute | solution.py:43
  45.9 24.3 %collective-permute-start.7 = (bf16[1,3,192,384]{3,2,1,0:T(8,128)(2,1)S(1)}, bf16[1,3,192,384]{3,2,1,0:T(8,128)(2,1)}, u32[]{:S(2)}, u32[]{:S(2)}) collective-permute-start(bf16[1,3,192,384]{3,2,1,0:T(8,128)(2,1)S(1)} %maximum_bitcast_fusion.3), channel_id=1, source_target_pairs={{0,16},{4,20},{8,24},{12,28},{16,0},{20,4},{24,8},{28,12},{1,17},{... | collective-permute-start | bytes 1327112 | tf_op jit(solution)/shard_map/ppermute | solution.py:43
  71.3 20.2 %collective-permute-start.8 = (bf16[2,3,192,384]{3,2,1,0:T(8,128)(2,1)S(1)}, bf16[2,3,192,384]{3,2,1,0:T(8,128)(2,1)S(1)}, u32[]{:S(2)}, u32[]{:S(2)}) collective-permute-start(bf16[2,3,192,384]{3,2,1,0:T(8,128)(2,1)S(1)} %pad_maximum_fusion.3), channel_id=1, source_target_pairs={{0,16},{4,20},{8,24},{12,28},{16,0},{20,4},{24,8},{28,12},{1,17},{... | collective-permute-start | bytes 2654216 | tf_op jit(solution)/shard_map/ppermute | solution.py:43
  73.2 19.9 %collective-permute-start.9 = (bf16[2,3,192,384]{3,2,1,0:T(8,128)(2,1)S(1)}, bf16[2,3,192,384]{3,2,1,0:T(8,128)(2,1)S(1)}, u32[]{:S(2)}, u32[]{:S(2)}) collective-permute-start(bf16[2,3,192,384]{3,2,1,0:T(8,128)(2,1)S(1)} %pad_maximum_fusion.4), channel_id=1, source_target_pairs={{0,8},{4,12},{8,0},{12,4},{16,24},{20,28},{24,16},{28,20},{1,9},{5... | collective-permute-start | bytes 2654216 | tf_op jit(solution)/shard_map/ppermute | solution.py:43
  91.7 4.5 collective-permute-start.12
  93.3 17.1 %collective-permute-start.15 = (bf16[4,3,192,384]{3,2,1,0:T(8,128)(2,1)S(1)}, bf16[4,3,192,384]{3,2,1,0:T(8,128)(2,1)S(1)}, u32[]{:S(2)}, u32[]{:S(2)}) collective-permute-start(bf16[4,3,192,384]{3,2,1,0:T(8,128)(2,1)S(1)} %constant_dynamic-update-slice_fusion.2.refs_1_), channel_id=1, source_target_pairs={{0,4},{4,0},{8,12},{12,8},{16,20},{20,16},{24,28},{28,24},{1,5},{5... | collective-permute-start | bytes 5308424 | tf_op jit(solution)/shard_map/ppermute | solution.py:43
  93.6 12.6 %collective-permute-start.10 = (bf16[1,3,192,384]{3,2,1,0:T(8,128)(2,1)S(1)}, bf16[1,3,192,384]{3,2,1,0:T(8,128)(2,1)S(1)}, u32[]{:S(2)}, u32[]{:S(2)}) collective-permute-start(bf16[1,3,192,384]{3,2,1,0:T(8,128)(2,1)S(1)} %maximum_bitcast_fusion), channel_id=1, source_target_pairs={{0,8},{4,12},{8,0},{12,4},{16,24},{20,28},{24,16},{28,20},{1,9},{5... | collective-permute-start | bytes 1327112 | tf_op jit(solution)/shard_map/ppermute | solution.py:43
  95.1 12.3 %collective-permute-start.11 = (bf16[1,3,192,384]{3,2,1,0:T(8,128)(2,1)S(1)}, bf16[1,3,192,384]{3,2,1,0:T(8,128)(2,1)S(1)}, u32[]{:S(2)}, u32[]{:S(2)}) collective-permute-start(bf16[1,3,192,384]{3,2,1,0:T(8,128)(2,1)S(1)} %maximum_bitcast_fusion.1), channel_id=1, source_target_pairs={{0,16},{4,20},{8,24},{12,28},{16,0},{20,4},{24,8},{28,12},{1,17},{... | collective-permute-start | bytes 1327112 | tf_op jit(solution)/shard_map/ppermute | solution.py:43
  107.5 21.1 %collective-permute-start.14 = (bf16[2,3,192,384]{3,2,1,0:T(8,128)(2,1)S(1)}, bf16[2,3,192,384]{3,2,1,0:T(8,128)(2,1)S(1)}, u32[]{:S(2)}, u32[]{:S(2)}) collective-permute-start(bf16[2,3,192,384]{3,2,1,0:T(8,128)(2,1)S(1)} %pad_maximum_fusion.6), channel_id=1, source_target_pairs={{0,8},{4,12},{8,0},{12,4},{16,24},{20,28},{24,16},{28,20},{1,9},{5... | collective-permute-start | bytes 2654216 | tf_op jit(solution)/shard_map/ppermute | solution.py:43
  108.2 20.9 %collective-permute-start.13 = (bf16[2,3,192,384]{3,2,1,0:T(8,128)(2,1)S(1)}, bf16[2,3,192,384]{3,2,1,0:T(8,128)(2,1)S(1)}, u32[]{:S(2)}, u32[]{:S(2)}) collective-permute-start(bf16[2,3,192,384]{3,2,1,0:T(8,128)(2,1)S(1)} %pad_maximum_fusion.5), channel_id=1, source_target_pairs={{0,16},{4,20},{8,24},{12,28},{16,0},{20,4},{24,8},{28,12},{1,17},{... | collective-permute-start | bytes 2654216 | tf_op jit(solution)/shard_map/ppermute | solution.py:43
  130.2 5.8 %collective-permute-start.17 = (bf16[4,3,192,384]{3,2,1,0:T(8,128)(2,1)}, bf16[4,3,192,384]{3,2,1,0:T(8,128)(2,1)}, u32[]{:S(2)}, u32[]{:S(2)}) collective-permute-start(bf16[4,3,192,384]{3,2,1,0:T(8,128)(2,1)} %constant_dynamic-update-slice_fusion.7.refs_3_.refs_2_), channel_id=1, source_target_pairs={{0,4},{4,0},{8,12},{12,8},{16,20},{20,16},{24,28},{28,24},{1,5},{5... | collective-permute-start | bytes 5308424 | tf_op jit(solution)/shard_map/ppermute | solution.py:43
  131.2 5.6 %collective-permute-start.16 = (bf16[4,3,192,384]{3,2,1,0:T(8,128)(2,1)}, bf16[4,3,192,384]{3,2,1,0:T(8,128)(2,1)}, u32[]{:S(2)}, u32[]{:S(2)}) collective-permute-start(bf16[4,3,192,384]{3,2,1,0:T(8,128)(2,1)} %constant_dynamic-update-slice_fusion.4.refs_1_.refs_0_), channel_id=1, source_target_pairs={{0,4},{4,0},{8,12},{12,8},{16,20},{20,16},{24,28},{28,24},{1,5},{5... | collective-permute-start | bytes 5308424 | tf_op jit(solution)/shard_map/ppermute | solution.py:43
  160.1 14.1 %collective-permute-start.18 = (bf16[1632,128]{1,0:T(8,128)(2,1)}, bf16[1632,128]{1,0:T(8,128)(2,1)}, u32[]{:S(2)}, u32[]{:S(2)}) collective-permute-start(bf16[1632,128]{1,0:T(8,128)(2,1)} %get-tuple-element.203), channel_id=1, source_target_pairs={{0,3},{1,0},{2,1},{3,2},{4,7},{5,4},{6,5},{7,6},{8,11},{9,8},{10,9... | collective-permute-start | bytes 1253384 | tf_op jit(solution)/shard_map/ppermute | solution.py:21
  160.1 38.8 %collective-permute-start.19 = (bf16[1632,128]{1,0:T(8,128)(2,1)}, bf16[1632,128]{1,0:T(8,128)(2,1)}, u32[]{:S(2)}, u32[]{:S(2)}) collective-permute-start(bf16[1632,128]{1,0:T(8,128)(2,1)} %get-tuple-element.204), channel_id=1, source_target_pairs={{0,2},{1,3},{2,0},{3,1},{4,6},{5,7},{6,4},{7,5},{8,10},{9,11},{10,... | collective-permute-start | bytes 1253384 | tf_op jit(solution)/shard_map/ppermute | solution.py:21
  161.9 37.0 %collective-permute-start.20 = (bf16[1632,128]{1,0:T(8,128)(2,1)}, bf16[1632,128]{1,0:T(8,128)(2,1)}, u32[]{:S(2)}, u32[]{:S(2)}) collective-permute-start(bf16[1632,128]{1,0:T(8,128)(2,1)} %get-tuple-element.205), channel_id=1, source_target_pairs={{0,1},{1,2},{2,3},{3,0},{4,5},{5,6},{6,7},{7,4},{8,9},{9,10},{10,1... | collective-permute-start | bytes 1253384 | tf_op jit(solution)/shard_map/ppermute | solution.py:21
  205.1 10.6 %collective-permute-start.26 = (bf16[128,1536]{1,0:T(8,128)(2,1)S(1)}, bf16[128,1536]{1,0:T(8,128)(2,1)S(1)}, u32[]{:S(2)}, u32[]{:S(2)}) collective-permute-start(bf16[128,1536]{1,0:T(8,128)(2,1)S(1)} %add_convert_fusion), channel_id=1, source_target_pairs={{0,3},{1,0},{2,1},{3,2},{4,7},{5,4},{6,5},{7,6},{8,11},{9,8},{10,9... | collective-permute-start | bytes 1179656 | tf_op jit(solution)/shard_map/ppermute | solution.py:21
  205.2 36.4 %collective-permute-start.25 = (bf16[128,1536]{1,0:T(8,128)(2,1)S(1)}, bf16[128,1536]{1,0:T(8,128)(2,1)S(1)}, u32[]{:S(2)}, u32[]{:S(2)}) collective-permute-start(bf16[128,1536]{1,0:T(8,128)(2,1)S(1)} %add_convert_fusion), channel_id=1, source_target_pairs={{0,2},{1,3},{2,0},{3,1},{4,6},{5,7},{6,4},{7,5},{8,10},{9,11},{10,... | collective-permute-start | bytes 1179656 | tf_op jit(solution)/shard_map/ppermute | solution.py:21
  207.0 34.5 %collective-permute-start.24 = (bf16[128,1536]{1,0:T(8,128)(2,1)S(1)}, bf16[128,1536]{1,0:T(8,128)(2,1)S(1)}, u32[]{:S(2)}, u32[]{:S(2)}) collective-permute-start(bf16[128,1536]{1,0:T(8,128)(2,1)S(1)} %add_convert_fusion), channel_id=1, source_target_pairs={{0,1},{1,2},{2,3},{3,0},{4,5},{5,6},{6,7},{7,4},{8,9},{9,10},{10,1... | collective-permute-start | bytes 1179656 | tf_op jit(solution)/shard_map/ppermute | solution.py:21
  255.8 31.1 %collective-permute-start.29 = (bf16[128,1536]{1,0:T(8,128)(2,1)}, bf16[128,1536]{1,0:T(8,128)(2,1)}, u32[]{:S(2)}, u32[]{:S(2)}) collective-permute-start(bf16[128,1536]{1,0:T(8,128)(2,1)} %get-tuple-element.418), channel_id=1, source_target_pairs={{0,1},{1,2},{2,3},{3,0},{4,5},{5,6},{6,7},{7,4},{8,9},{9,10},{10,1... | collective-permute-start | bytes 1179656 | tf_op jit(solution)/shard_map/ppermute | solution.py:21
  255.8 31.1 %collective-permute-start.28 = (bf16[128,1536]{1,0:T(8,128)(2,1)}, bf16[128,1536]{1,0:T(8,128)(2,1)}, u32[]{:S(2)}, u32[]{:S(2)}) collective-permute-start(bf16[128,1536]{1,0:T(8,128)(2,1)} %get-tuple-element.419), channel_id=1, source_target_pairs={{0,2},{1,3},{2,0},{3,1},{4,6},{5,7},{6,4},{7,5},{8,10},{9,11},{10,... | collective-permute-start | bytes 1179656 | tf_op jit(solution)/shard_map/ppermute | solution.py:21
  256.3 30.6 %collective-permute-start.27 = (bf16[128,1536]{1,0:T(8,128)(2,1)}, bf16[128,1536]{1,0:T(8,128)(2,1)}, u32[]{:S(2)}, u32[]{:S(2)}) collective-permute-start(bf16[128,1536]{1,0:T(8,128)(2,1)} %get-tuple-element.420), channel_id=1, source_target_pairs={{0,3},{1,0},{2,1},{3,2},{4,7},{5,4},{6,5},{7,6},{8,11},{9,8},{10,9... | collective-permute-start | bytes 1179656 | tf_op jit(solution)/shard_map/ppermute | solution.py:21
  281.1 23.7 %collective-permute-start.33 = (bf16[4,192,1536]{2,1,0:T(8,128)(2,1)}, bf16[4,192,1536]{2,1,0:T(8,128)(2,1)S(1)}, u32[]{:S(2)}, u32[]{:S(2)}) collective-permute-start(bf16[4,192,1536]{2,1,0:T(8,128)(2,1)} %get-tuple-element.221), channel_id=1, source_target_pairs={{0,4},{4,0},{8,12},{12,8},{16,20},{20,16},{24,28},{28,24},{1,5},{5... | collective-permute-start | bytes 7077896 | tf_op jit(solution)/shard_map/ppermute | solution.py:43
  286.4 19.5 %collective-permute-start.34 = (bf16[4,192,1536]{2,1,0:T(8,128)(2,1)}, bf16[4,192,1536]{2,1,0:T(8,128)(2,1)S(1)}, u32[]{:S(2)}, u32[]{:S(2)}) collective-permute-start(bf16[4,192,1536]{2,1,0:T(8,128)(2,1)} %get-tuple-element.223), channel_id=1, source_target_pairs={{0,4},{4,0},{8,12},{12,8},{16,20},{20,16},{24,28},{28,24},{1,5},{5... | collective-permute-start | bytes 7077896 | tf_op jit(solution)/shard_map/ppermute | solution.py:43
  294.5 11.5 %collective-permute-start.35 = (bf16[4,192,1536]{2,1,0:T(8,128)(2,1)}, bf16[4,192,1536]{2,1,0:T(8,128)(2,1)S(1)}, u32[]{:S(2)}, u32[]{:S(2)}) collective-permute-start(bf16[4,192,1536]{2,1,0:T(8,128)(2,1)} %get-tuple-element.230), channel_id=1, source_target_pairs={{0,4},{4,0},{8,12},{12,8},{16,20},{20,16},{24,28},{28,24},{1,5},{5... | collective-permute-start | bytes 7077896 | tf_op jit(solution)/shard_map/ppermute | solution.py:43
  296.9 16.9 %collective-permute-start.32 = (bf16[1632,128]{1,0:T(8,128)(2,1)S(1)}, bf16[1632,128]{1,0:T(8,128)(2,1)S(1)}, u32[]{:S(2)}, u32[]{:S(2)}) collective-permute-start(bf16[1632,128]{1,0:T(8,128)(2,1)S(1)} %shard_map.280.rest_0_.rest_4_), channel_id=1, source_target_pairs={{0,3},{1,0},{2,1},{3,2},{4,7},{5,4},{6,5},{7,6},{8,11},{9,8},{10,9... | collective-permute-start | bytes 1253384 | tf_op jit(solution)/shard_map/ppermute | solution.py:21
  303.8 37.9 %collective-permute-start.31 = (bf16[1632,128]{1,0:T(8,128)(2,1)S(1)}, bf16[1632,128]{1,0:T(8,128)(2,1)S(1)}, u32[]{:S(2)}, u32[]{:S(2)}) collective-permute-start(bf16[1632,128]{1,0:T(8,128)(2,1)S(1)} %shard_map.280.rest_0_.rest_4_), channel_id=1, source_target_pairs={{0,2},{1,3},{2,0},{3,1},{4,6},{5,7},{6,4},{7,5},{8,10},{9,11},{10,... | collective-permute-start | bytes 1253384 | tf_op jit(solution)/shard_map/ppermute | solution.py:21
  304.8 36.9 %collective-permute-start.30 = (bf16[1632,128]{1,0:T(8,128)(2,1)S(1)}, bf16[1632,128]{1,0:T(8,128)(2,1)S(1)}, u32[]{:S(2)}, u32[]{:S(2)}) collective-permute-start(bf16[1632,128]{1,0:T(8,128)(2,1)S(1)} %shard_map.280.rest_0_.rest_4_), channel_id=1, source_target_pairs={{0,1},{1,2},{2,3},{3,0},{4,5},{5,6},{6,7},{7,4},{8,9},{9,10},{10,1... | collective-permute-start | bytes 1253384 | tf_op jit(solution)/shard_map/ppermute | solution.py:21
  308.4 47.3 %collective-permute-start.39 = (bf16[2,192,2304]{2,1,0:T(8,128)(2,1)}, bf16[2,192,2304]{2,1,0:T(8,128)(2,1)S(1)}, u32[]{:S(2)}, u32[]{:S(2)}) collective-permute-start(bf16[2,192,2304]{2,1,0:T(8,128)(2,1)} %get-tuple-element.234), channel_id=1, source_target_pairs={{0,8},{4,12},{8,0},{12,4},{16,24},{20,28},{24,16},{28,20},{1,9},{5... | collective-permute-start | bytes 5308424 | tf_op jit(solution)/shard_map/ppermute | solution.py:43
  312.8 44.5 %collective-permute-start.40 = (bf16[2,192,2304]{2,1,0:T(8,128)(2,1)}, bf16[2,192,2304]{2,1,0:T(8,128)(2,1)S(1)}, u32[]{:S(2)}, u32[]{:S(2)}) collective-permute-start(bf16[2,192,2304]{2,1,0:T(8,128)(2,1)} %get-tuple-element.237), channel_id=1, source_target_pairs={{0,16},{4,20},{8,24},{12,28},{16,0},{20,4},{24,8},{28,12},{1,17},{... | collective-permute-start | bytes 5308424 | tf_op jit(solution)/shard_map/ppermute | solution.py:43
  341.7 32.3 %collective-permute-start.36 = (bf16[128,1536]{1,0:T(8,128)(2,1)}, bf16[128,1536]{1,0:T(8,128)(2,1)S(1)}, u32[]{:S(2)}, u32[]{:S(2)}) collective-permute-start(bf16[128,1536]{1,0:T(8,128)(2,1)} %get-tuple-element.242), channel_id=1, source_target_pairs={{0,3},{1,0},{2,1},{3,2},{4,7},{5,4},{6,5},{7,6},{8,11},{9,8},{10,9... | collective-permute-start | bytes 1179656 | tf_op jit(solution)/shard_map/ppermute | solution.py:21
  341.7 35.6 %collective-permute-start.37 = (bf16[128,1536]{1,0:T(8,128)(2,1)}, bf16[128,1536]{1,0:T(8,128)(2,1)S(1)}, u32[]{:S(2)}, u32[]{:S(2)}) collective-permute-start(bf16[128,1536]{1,0:T(8,128)(2,1)} %get-tuple-element.243), channel_id=1, source_target_pairs={{0,2},{1,3},{2,0},{3,1},{4,6},{5,7},{6,4},{7,5},{8,10},{9,11},{10,... | collective-permute-start | bytes 1179656 | tf_op jit(solution)/shard_map/ppermute | solution.py:21
  342.8 34.5 %collective-permute-start.38 = (bf16[128,1536]{1,0:T(8,128)(2,1)}, bf16[128,1536]{1,0:T(8,128)(2,1)S(1)}, u32[]{:S(2)}, u32[]{:S(2)}) collective-permute-start(bf16[128,1536]{1,0:T(8,128)(2,1)} %get-tuple-element.244), channel_id=1, source_target_pairs={{0,1},{1,2},{2,3},{3,0},{4,5},{5,6},{6,7},{7,4},{8,9},{9,10},{10,1... | collective-permute-start | bytes 1179656 | tf_op jit(solution)/shard_map/ppermute | solution.py:21
  382.6 15.3 %collective-permute-start.41 = (bf16[4,192,1536]{2,1,0:T(8,128)(2,1)}, bf16[4,192,1536]{2,1,0:T(8,128)(2,1)S(1)}, u32[]{:S(2)}, u32[]{:S(2)}) collective-permute-start(bf16[4,192,1536]{2,1,0:T(8,128)(2,1)} %get-tuple-element.263), channel_id=1, source_target_pairs={{0,4},{4,0},{8,12},{12,8},{16,20},{20,16},{24,28},{28,24},{1,5},{5... | collective-permute-start | bytes 7077896 | tf_op jit(solution)/shard_map/ppermute | solution.py:43
  382.6 16.7 %collective-permute-start.42 = (bf16[4,192,1536]{2,1,0:T(8,128)(2,1)}, bf16[4,192,1536]{2,1,0:T(8,128)(2,1)}, u32[]{:S(2)}, u32[]{:S(2)}) collective-permute-start(bf16[4,192,1536]{2,1,0:T(8,128)(2,1)} %get-tuple-element.264), channel_id=1, source_target_pairs={{0,4},{4,0},{8,12},{12,8},{16,20},{20,16},{24,28},{28,24},{1,5},{5... | collective-permute-start | bytes 7077896 | tf_op jit(solution)/shard_map/ppermute | solution.py:43
  383.1 16.2 %collective-permute-start.43 = (bf16[4,192,1536]{2,1,0:T(8,128)(2,1)}, bf16[4,192,1536]{2,1,0:T(8,128)(2,1)S(1)}, u32[]{:S(2)}, u32[]{:S(2)}) collective-permute-start(bf16[4,192,1536]{2,1,0:T(8,128)(2,1)} %get-tuple-element.262), channel_id=1, source_target_pairs={{0,4},{4,0},{8,12},{12,8},{16,20},{20,16},{24,28},{28,24},{1,5},{5... | collective-permute-start | bytes 7077896 | tf_op jit(solution)/shard_map/ppermute | solution.py:43
  383.1 22.2 %collective-permute-start.44 = (bf16[1,192,2304]{2,1,0:T(8,128)(2,1)}, bf16[1,192,2304]{2,1,0:T(8,128)(2,1)S(1)}, u32[]{:S(2)}, u32[]{:S(2)}) collective-permute-start(bf16[1,192,2304]{2,1,0:T(8,128)(2,1)} %get-tuple-element.250), channel_id=1, source_target_pairs={{0,16},{4,20},{8,24},{12,28},{16,0},{20,4},{24,8},{28,12},{1,17},{... | collective-permute-start | bytes 2654216 | tf_op jit(solution)/shard_map/ppermute | solution.py:43
  383.7 22.0 %collective-permute-start.45 = (bf16[1,192,2304]{2,1,0:T(8,128)(2,1)}, bf16[1,192,2304]{2,1,0:T(8,128)(2,1)}, u32[]{:S(2)}, u32[]{:S(2)}) collective-permute-start(bf16[1,192,2304]{2,1,0:T(8,128)(2,1)} %get-tuple-element.252), channel_id=1, source_target_pairs={{0,8},{4,12},{8,0},{12,4},{16,24},{20,28},{24,16},{28,20},{1,9},{5... | collective-permute-start | bytes 2654216 | tf_op jit(solution)/shard_map/ppermute | solution.py:43
  408.8 28.8 %collective-permute-start.47 = (bf16[2,192,1536]{2,1,0:T(8,128)(2,1)}, bf16[2,192,1536]{2,1,0:T(8,128)(2,1)S(1)}, u32[]{:S(2)}, u32[]{:S(2)}) collective-permute-start(bf16[2,192,1536]{2,1,0:T(8,128)(2,1)} %get-tuple-element.277), channel_id=1, source_target_pairs={{0,16},{4,20},{8,24},{12,28},{16,0},{20,4},{24,8},{28,12},{1,17},{... | collective-permute-start | bytes 3538952 | tf_op jit(solution)/shard_map/ppermute | solution.py:43
  411.9 27.2 %collective-permute-start.46 = (bf16[2,192,1536]{2,1,0:T(8,128)(2,1)}, bf16[2,192,1536]{2,1,0:T(8,128)(2,1)S(1)}, u32[]{:S(2)}, u32[]{:S(2)}) collective-permute-start(bf16[2,192,1536]{2,1,0:T(8,128)(2,1)} %get-tuple-element.273), channel_id=1, source_target_pairs={{0,8},{4,12},{8,0},{12,4},{16,24},{20,28},{24,16},{28,20},{1,9},{5... | collective-permute-start | bytes 3538952 | tf_op jit(solution)/shard_map/ppermute | solution.py:43
  413.7 30.7 %collective-permute-start.48 = (bf16[128,1536]{1,0:T(8,128)(2,1)}, bf16[128,1536]{1,0:T(8,128)(2,1)S(1)}, u32[]{:S(2)}, u32[]{:S(2)}) collective-permute-start(bf16[128,1536]{1,0:T(8,128)(2,1)} %get-tuple-element.299), channel_id=1, source_target_pairs={{0,3},{1,0},{2,1},{3,2},{4,7},{5,4},{6,5},{7,6},{8,11},{9,8},{10,9... | collective-permute-start | bytes 1179656 | tf_op jit(solution)/shard_map/ppermute | solution.py:21
  413.9 35.4 %collective-permute-start.49 = (bf16[128,1536]{1,0:T(8,128)(2,1)}, bf16[128,1536]{1,0:T(8,128)(2,1)S(1)}, u32[]{:S(2)}, u32[]{:S(2)}) collective-permute-start(bf16[128,1536]{1,0:T(8,128)(2,1)} %get-tuple-element.300), channel_id=1, source_target_pairs={{0,2},{1,3},{2,0},{3,1},{4,6},{5,7},{6,4},{7,5},{8,10},{9,11},{10,... | collective-permute-start | bytes 1179656 | tf_op jit(solution)/shard_map/ppermute | solution.py:21
  415.8 34.3 %collective-permute-start.50 = (bf16[128,1536]{1,0:T(8,128)(2,1)}, bf16[128,1536]{1,0:T(8,128)(2,1)}, u32[]{:S(2)}, u32[]{:S(2)}) collective-permute-start(bf16[128,1536]{1,0:T(8,128)(2,1)} %get-tuple-element.301), channel_id=1, source_target_pairs={{0,1},{1,2},{2,3},{3,0},{4,5},{5,6},{6,7},{7,4},{8,9},{9,10},{10,1... | collective-permute-start | bytes 1179656 | tf_op jit(solution)/shard_map/ppermute | solution.py:21
  440.3 16.5 %collective-permute-start.54 = (bf16[1,192,1536]{2,1,0:T(8,128)(2,1)}, bf16[1,192,1536]{2,1,0:T(8,128)(2,1)S(1)}, u32[]{:S(2)}, u32[]{:S(2)}) collective-permute-start(bf16[1,192,1536]{2,1,0:T(8,128)(2,1)} %get-tuple-element.295), channel_id=1, source_target_pairs={{0,8},{4,12},{8,0},{12,4},{16,24},{20,28},{24,16},{28,20},{1,9},{5... | collective-permute-start | bytes 1769480 | tf_op jit(solution)/shard_map/ppermute | solution.py:43
  443.3 16.5 %collective-permute-start.53 = (bf16[1,192,1536]{2,1,0:T(8,128)(2,1)}, bf16[1,192,1536]{2,1,0:T(8,128)(2,1)S(1)}, u32[]{:S(2)}, u32[]{:S(2)}) collective-permute-start(bf16[1,192,1536]{2,1,0:T(8,128)(2,1)} %get-tuple-element.292), channel_id=1, source_target_pairs={{0,16},{4,20},{8,24},{12,28},{16,0},{20,4},{24,8},{28,12},{1,17},{... | collective-permute-start | bytes 1769480 | tf_op jit(solution)/shard_map/ppermute | solution.py:43
  450.1 16.6 %collective-permute-start.51 = (bf16[2,192,768]{2,1,0:T(8,128)(2,1)S(1)}, bf16[2,192,768]{2,1,0:T(8,128)(2,1)S(1)}, u32[]{:S(2)}, u32[]{:S(2)}) collective-permute-start(bf16[2,192,768]{2,1,0:T(8,128)(2,1)S(1)} %copy-done.127), channel_id=1, source_target_pairs={{0,8},{4,12},{8,0},{12,4},{16,24},{20,28},{24,16},{28,20},{1,9},{5... | collective-permute-start | bytes 1769480 | tf_op jit(solution)/shard_map/ppermute | solution.py:43
  450.6 18.7 %collective-permute-start.52 = (bf16[2,192,768]{2,1,0:T(8,128)(2,1)S(1)}, bf16[2,192,768]{2,1,0:T(8,128)(2,1)S(1)}, u32[]{:S(2)}, u32[]{:S(2)}) collective-permute-start(bf16[2,192,768]{2,1,0:T(8,128)(2,1)S(1)} %copy-done.126), channel_id=1, source_target_pairs={{0,16},{4,20},{8,24},{12,28},{16,0},{20,4},{24,8},{28,12},{1,17},{... | collective-permute-start | bytes 1769480 | tf_op jit(solution)/shard_map/ppermute | solution.py:43
  461.7 7.7 %collective-permute-start.55 = (bf16[2,192,384]{2,1,0:T(8,128)(2,1)S(1)}, bf16[2,192,384]{2,1,0:T(8,128)(2,1)S(1)}, u32[]{:S(2)}, u32[]{:S(2)}) collective-permute-start(bf16[2,192,384]{2,1,0:T(8,128)(2,1)S(1)} %get-tuple-element.306), channel_id=1, source_target_pairs={{0,3},{1,0},{2,1},{3,2},{4,7},{5,4},{6,5},{7,6},{8,11},{9,8},{10,9... | collective-permute-start | bytes 884744 | tf_op jit(solution)/shard_map/ppermute | solution.py:21
  462.0 11.2 %collective-permute-start.56 = (bf16[2,192,384]{2,1,0:T(8,128)(2,1)S(1)}, bf16[2,192,384]{2,1,0:T(8,128)(2,1)S(1)}, u32[]{:S(2)}, u32[]{:S(2)}) collective-permute-start(bf16[2,192,384]{2,1,0:T(8,128)(2,1)S(1)} %get-tuple-element.307), channel_id=1, source_target_pairs={{0,1},{1,2},{2,3},{3,0},{4,5},{5,6},{6,7},{7,4},{8,9},{9,10},{10,1... | collective-permute-start | bytes 884744 | tf_op jit(solution)/shard_map/ppermute | solution.py:21
  474.1 14.8 %collective-permute-start.58 = (bf16[1,192,768]{2,1,0:T(8,128)(2,1)}, bf16[1,192,768]{2,1,0:T(8,128)(2,1)S(1)}, u32[]{:S(2)}, u32[]{:S(2)}) collective-permute-start(bf16[1,192,768]{2,1,0:T(8,128)(2,1)} %get-tuple-element.314), channel_id=1, source_target_pairs={{0,8},{4,12},{8,0},{12,4},{16,24},{20,28},{24,16},{28,20},{1,9},{5... | collective-permute-start | bytes 884744 | tf_op jit(solution)/shard_map/ppermute | solution.py:43
  475.5 14.1 %collective-permute-start.57 = (bf16[1,192,768]{2,1,0:T(8,128)(2,1)}, bf16[1,192,768]{2,1,0:T(8,128)(2,1)S(1)}, u32[]{:S(2)}, u32[]{:S(2)}) collective-permute-start(bf16[1,192,768]{2,1,0:T(8,128)(2,1)} %get-tuple-element.310), channel_id=1, source_target_pairs={{0,16},{4,20},{8,24},{12,28},{16,0},{20,4},{24,8},{28,12},{1,17},{... | collective-permute-start | bytes 884744 | tf_op jit(solution)/shard_map/ppermute | solution.py:43
  483.8 4.3 collective-permute-start.61
  488.9 25.4 %collective-permute-start.67 = (bf16[2,192,384]{2,1,0:T(8,128)(2,1)S(1)}, bf16[2,192,384]{2,1,0:T(8,128)(2,1)S(1)}, u32[]{:S(2)}, u32[]{:S(2)}) collective-permute-start(bf16[2,192,384]{2,1,0:T(8,128)(2,1)S(1)} %get-tuple-element.334), channel_id=1, source_target_pairs={{0,2},{1,3},{2,0},{3,1},{4,6},{5,7},{6,4},{7,5},{8,10},{9,11},{10,... | collective-permute-start | bytes 884744 | tf_op jit(solution)/shard_map/ppermute | solution.py:21
  493.2 22.4 %collective-permute-start.62 = (f32[8,1536]{1,0:T(8,128)S(1)}, f32[8,1536]{1,0:T(8,128)S(1)}, u32[]{:S(2)}, u32[]{:S(2)}) collective-permute-start(f32[8,1536]{1,0:T(8,128)S(1)} %add.357), channel_id=1, source_target_pairs={{0,1},{1,0},{2,3},{3,2},{4,5},{5,4},{6,7},{7,6},{8,9},{9,8},{10,11... | collective-permute-start | bytes 147464 | tf_op jit(solution)/shard_map/ppermute | solution.py:43
  494.3 36.7 %collective-permute-start.66 = (bf16[2,192,384]{2,1,0:T(8,128)(2,1)}, bf16[2,192,384]{2,1,0:T(8,128)(2,1)}, u32[]{:S(2)}, u32[]{:S(2)}) collective-permute-start(bf16[2,192,384]{2,1,0:T(8,128)(2,1)} %pad_maximum_fusion.12), channel_id=1, source_target_pairs={{0,1},{1,2},{2,3},{3,0},{4,5},{5,6},{6,7},{7,4},{8,9},{9,10},{10,1... | collective-permute-start | bytes 884744 | tf_op jit(solution)/shard_map/ppermute | solution.py:21
  495.9 35.0 %collective-permute-start.65 = (bf16[2,192,384]{2,1,0:T(8,128)(2,1)}, bf16[2,192,384]{2,1,0:T(8,128)(2,1)}, u32[]{:S(2)}, u32[]{:S(2)}) collective-permute-start(bf16[2,192,384]{2,1,0:T(8,128)(2,1)} %pad_maximum_fusion.11), channel_id=1, source_target_pairs={{0,2},{1,3},{2,0},{3,1},{4,6},{5,7},{6,4},{7,5},{8,10},{9,11},{10,... | collective-permute-start | bytes 884744 | tf_op jit(solution)/shard_map/ppermute | solution.py:21
  499.6 31.3 %collective-permute-start.64 = (bf16[2,192,384]{2,1,0:T(8,128)(2,1)}, bf16[2,192,384]{2,1,0:T(8,128)(2,1)}, u32[]{:S(2)}, u32[]{:S(2)}) collective-permute-start(bf16[2,192,384]{2,1,0:T(8,128)(2,1)} %pad_maximum_fusion.10), channel_id=1, source_target_pairs={{0,3},{1,0},{2,1},{3,2},{4,7},{5,4},{6,5},{7,6},{8,11},{9,8},{10,9... | collective-permute-start | bytes 884744 | tf_op jit(solution)/shard_map/ppermute | solution.py:21
  515.5 12.9 %collective-permute-start.63 = (f32[8,1536]{1,0:T(8,128)S(1)}, f32[8,1536]{1,0:T(8,128)S(1)}, u32[]{:S(2)}, u32[]{:S(2)}) collective-permute-start(f32[8,1536]{1,0:T(8,128)S(1)} %add.358), channel_id=1, source_target_pairs={{0,2},{1,3},{2,0},{3,1},{4,6},{5,7},{6,4},{7,5},{8,10},{9,11},{10,... | collective-permute-start | bytes 147464 | tf_op jit(solution)/shard_map/ppermute | solution.py:43
  (139 other events, 1569.0 us)
Sparse Core Ops, SparseCore 0:
  68.8 61.7 all-gather.2

commit v6 on v5

--- a/solution.py
+++ b/solution.py
@@ -855,11 +855,10 @@
     ]
     wo = place(output_weight, qo_pieces, offsets, cuts, o_unit, True, at, n_dp, n_t)
     sent = attend_forward(queries, keys, values, key_image, row_image, span, n_t)
-    sent = after(sent, wo)
     got = [sent[0]] + [rotate(sent[k], n_t, -k) for k in range(1, n_t)]
     count_part = after(jnp.full((8, 128), jnp.sum(valid).astype(F32)), *sent[1:])
     count_total = all_sum(count_part, [("dp", n_dp)])[0, 0]
-    got = after(got, count_total)
+    got = after(got, count_total, wo)
     attended, stat = combine(got, heads)
     entropy = stat[:heads] - stat[heads:]
     own_valid = row_valid[:, :own_rows]

time: 546 us -> 537 us (0.984)
  waiting for transfers between devices: 210 us -> 204 us
  transfers between devices with their start and end apart: 69 -> 69, of which waited for: 32 -> 32; matrix products, arithmetic and copies ran while one was open for 11% -> 11% of each run, Pallas kernels for 19% -> 20%
where the time goes in v6:
time: 537 us; the launch traced here: 532 us
  waiting for transfers between devices  204 us (38%)
  Pallas kernels  136 us (25%)
  starting transfers between devices  74.3 us (14%)
  local copies, waits for them, and re-layouts  60.2 us (11%)
  other arithmetic  25 us (5%)
  between operations  19.1 us (4%)
  matrix products  13.5 us (3%)
    ppermute x30, waiting for transfers between devices, rotate(): lax.ppermute(x, 'tensor', [(i, (i + shift) % count) for i in range(count)])  132 us
    ppermute x38, waiting for transfers between devices, partner(): return lax.ppermute(x, axis, [(i, i ^ offset) for i in range(count)])  72.4 us
    ppermute x30, starting transfers between devices, rotate(): lax.ppermute(x, 'tensor', [(i, (i + shift) % count) for i in range(count)])  44.5 us
    pallas_call x6, Pallas kernels, gradient(): pl.pallas_call(partial(gradient_kernel, natural, turned, n_dp), grid=(3,)...  33.1 us
    unnamed x279, local copies, waits for them, and re-layouts  29.8 us
    ppermute x38, starting transfers between devices, partner(): return lax.ppermute(x, axis, [(i, i ^ offset) for i in range(count)])  29.8 us
    pallas_call x4, Pallas kernels, place(): pl.pallas_call(kernel, out_shape=outs, in_specs=[pl.BlockSpec(memory_spac...  21.7 us
    pallas_call x12, Pallas kernels, reduce_cut(): pl.pallas_call(partial(cut_kernel, widths), grid=(count // 2,), in_specs=...  19.7 us
  transfers between devices with their start and end apart: 69, of which 32 were waited for; matrix products, arithmetic and copies ran while one was open for 11% of the time, Pallas kernels for 20%

profile of v6, /device:TPU:0, one launch (start us, length us, event | category | flops | bytes accessed | tf_op | source)
XLA Modules:
  0.0 531.9 jit_solution(6432623892745411364)
XLA Ops:
  8.5 5.1 collective-permute-start.2
  14.6 7.9 %fusion.40 = (bf16[1536,1,384]{2,1,0:T(2,128)(2,1)}, bf16[1536,1,384]{2,1,0:T(2,128)(2,1)}) fusion(bf16[1536,2,384]{2,1,0:T(2,128)(2,1)} %param.27), kind=kLoop, calls=%fused_computation.177 | loop fusion | bytes 4718592 | tf_op jit(solution)/shard_map/slice | solution.py:814
  26.2 4.2 copy_bitcast_fusion
  32.8 5.9 %collective-permute-done.1 = bf16[2,192,384]{2,1,0:T(8,128)(2,1)S(1)} collective-permute-done((bf16[2,192,384]{2,1,0:T(8,128)(2,1)S(1)}, bf16[2,192,384]{2,1,0:T(8,128)(2,1)S(1)}, u32[]{:S(2)}, u32[]{:S(2)}) %collective-permute-start.1) | collective-permute-done | bytes 294944 | tf_op jit(solution)/shard_map/ppermute | solution.py:21
  38.8 2.9 collective-permute-start.4
  41.7 2.5 collective-permute-start.3
  47.5 19.5 %collective-permute-done.4 = bf16[2,192,384]{2,1,0:T(8,128)(2,1)S(1)} collective-permute-done((bf16[2,192,384]{2,1,0:T(8,128)(2,1)S(1)}, bf16[2,192,384]{2,1,0:T(8,128)(2,1)S(1)}, u32[]{:S(2)}, u32[]{:S(2)}) %collective-permute-start.4) | collective-permute-done | bytes 294944 | tf_op jit(solution)/shard_map/ppermute | solution.py:21
  74.9 16.7 %collective-permute-done.8 = bf16[2,3,192,384]{3,2,1,0:T(8,128)(2,1)S(1)} collective-permute-done((bf16[2,3,192,384]{3,2,1,0:T(8,128)(2,1)S(1)}, bf16[2,3,192,384]{3,2,1,0:T(8,128)(2,1)S(1)}, u32[]{:S(2)}, u32[]{:S(2)}) %collective-permute-start.8) | collective-permute-done | bytes 884768 | tf_op jit(solution)/shard_map/ppermute | solution.py:43
  96.2 5.3 shard_map.271
  104.1 2.1 collective-permute-done.10
  110.4 5.3 shard_map.272
  119.3 9.3 %collective-permute-done.14 = bf16[2,3,192,384]{3,2,1,0:T(8,128)(2,1)S(1)} collective-permute-done((bf16[2,3,192,384]{3,2,1,0:T(8,128)(2,1)S(1)}, bf16[2,3,192,384]{3,2,1,0:T(8,128)(2,1)S(1)}, u32[]{:S(2)}, u32[]{:S(2)}) %collective-permute-start.14) | collective-permute-done | bytes 884768 | tf_op jit(solution)/shard_map/ppermute | solution.py:43
  131.7 2.7 dynamic-slice_bitcast_fusion
  136.7 7.5 %shard_map.273 = (bf16[1536,1536]{1,0:T(8,128)(2,1)S(1)}, bf16[1536,512]{1,0:T(8,128)(2,1)S(1)}, bf16[1536,512]{1,0:T(8,128)(2,1)S(1)}) custom-call(s32[2]{0:T(128)S(1)} %pad_add_fusion.2.at_ref, bf16[512,1536]{1,0:T(8,128)(2,1)S(1)} %fusion.7.x_ref, bf16[1536,384]{1,0:T(8,128)(2,1)S(1)} %copy-done.56, ...), custom_call_target="tpu_custom_call" | custom-call | tf_op jit(solution)/shard_map/pallas_call | solution.py:269
  145.4 9.3 %shard_map.274 = (bf16[1632,128]{1,0:T(8,128)(2,1)S(1)}, bf16[1632,128]{1,0:T(8,128)(2,1)}, bf16[1632,128]{1,0:T(8,128)(2,1)}, bf16[1632,128]{1,0:T(8,128)(2,1)}) custom-call(s32[2,4]{1,0:T(2,128)S(1)} %pad_add_fusion.1.span_ref, bf16[1536,512]{1,0:T(8,128)(2,1)S(1)} %get-tuple-element.193.q_ref, bf16[1536,640]{1,0:T(8,128)(2,1)S(1)} %copy-done.45, ...), custom_call_target="tpu_custom_call" | custom-call | tf_op jit(solution)/shard_map/pallas_call | solution.py:401
  155.9 2.0 collective-permute-start.20
  161.9 2.2 collective-permute-done.22
  166.0 3.6 shard_map.275
  170.2 23.2 %collective-permute-done.19.refs_2_ = bf16[1632,128]{1,0:T(8,128)(2,1)} collective-permute-done((bf16[1632,128]{1,0:T(8,128)(2,1)}, bf16[1632,128]{1,0:T(8,128)(2,1)}, u32[]{:S(2)}, u32[]{:S(2)}) %collective-permute-start.19) | collective-permute-done | bytes 417824 | tf_op jit(solution)/shard_map/ppermute | solution.py:21
  198.5 2.1 collective-permute-start.24
  200.9 8.2 %collective-permute-done.26 = bf16[128,1536]{1,0:T(8,128)(2,1)S(1)} collective-permute-done((bf16[128,1536]{1,0:T(8,128)(2,1)S(1)}, bf16[128,1536]{1,0:T(8,128)(2,1)S(1)}, u32[]{:S(2)}, u32[]{:S(2)}) %collective-permute-start.26) | collective-permute-done | bytes 393248 | tf_op jit(solution)/shard_map/ppermute | solution.py:21
  209.0 24.0 %collective-permute-done.25 = bf16[128,1536]{1,0:T(8,128)(2,1)S(1)} collective-permute-done((bf16[128,1536]{1,0:T(8,128)(2,1)S(1)}, bf16[128,1536]{1,0:T(8,128)(2,1)S(1)}, u32[]{:S(2)}, u32[]{:S(2)}) %collective-permute-start.25) | collective-permute-done | bytes 393248 | tf_op jit(solution)/shard_map/ppermute | solution.py:21
  233.1 4.9 multiply_convert_fusion
  238.0 3.7 fusion.16.y_ref
  241.7 2.6 convolution_convert_fusion
  245.6 1.7 collective-permute-start.28
  247.3 2.9 collective-permute-start.27
  250.2 2.6 copy.60.xt_ref
  252.8 2.6 fusion.23
  255.4 2.6 copy.61.xt_ref
  259.5 6.0 %shard_map.277 = (f32[128,1536]{1,0:T(8,128)S(1)}, bf16[128,1536]{1,0:T(8,128)(2,1)}, bf16[128,1536]{1,0:T(8,128)(2,1)}, bf16[128,1536]{1,0:T(8,128)(2,1)}) custom-call(bf16[512,1536]{1,0:T(8,128)(2,1)S(1)} %copy-done.26, bf16[1536,1536]{1,0:T(8,128)(2,1)} %b_ref.1), custom_call_target="tpu_custom_call" | custom-call | tf_op jit(solution)/shard_map/pallas_call | solution.py:704
  266.4 5.2 shard_map.278
  271.7 5.2 shard_map.279
  277.5 1.8 multiply_reduce_fusion
  280.7 4.3 shard_map.281
  287.4 7.3 %collective-permute-start.32 = (bf16[1632,128]{1,0:T(8,128)(2,1)S(1)}, bf16[1632,128]{1,0:T(8,128)(2,1)S(1)}, u32[]{:S(2)}, u32[]{:S(2)}) collective-permute-start(bf16[1632,128]{1,0:T(8,128)(2,1)S(1)} %shard_map.280.rest_0_.rest_4_), channel_id=1, source_target_pairs={{0,3},{1,0},{2,1},{3,2},{4,7},{5,4},{6,5},{7,6},{8,11},{9,8},{10,9... | collective-permute-start | bytes 1253384 | tf_op jit(solution)/shard_map/ppermute | solution.py:21
  296.5 2.4 shard_map.282
  300.1 2.4 shard_map.283
  304.8 26.7 %collective-permute-done.31.rest_2_.rest_6_ = bf16[1632,128]{1,0:T(8,128)(2,1)S(1)} collective-permute-done((bf16[1632,128]{1,0:T(8,128)(2,1)S(1)}, bf16[1632,128]{1,0:T(8,128)(2,1)S(1)}, u32[]{:S(2)}, u32[]{:S(2)}) %collective-permute-start.31) | collective-permute-done | bytes 417824 | tf_op jit(solution)/shard_map/ppermute | solution.py:21
  331.5 2.3 collective-permute-start.37
  333.8 2.0 collective-permute-start.38
  335.8 12.5 %shard_map.284 = (bf16[1536,512]{1,0:T(8,128)(2,1)S(1)}, bf16[1536,640]{1,0:T(8,128)(2,1)S(1)}, bf16[1536,640]{1,0:T(8,128)(2,1)S(1)}) custom-call(s32[2,4]{1,0:T(2,128)S(1)} %pad_add_fusion.1.span_ref, bf16[1536,512]{1,0:T(8,128)(2,1)S(1)} %copy-done.53, bf16[1536,640]{1,0:T(8,128)(2,1)S(1)} %copy-done.46, bf16[1536,640]{1,0:T(8,128)(2,1)S(1)} %copy-done.49, ...), custom_call_target="tpu_custom_call" | custom-call | flops 30198988800 | bytes 62914560 | tf_op jit(solution)/shard_map/pallas_call | solution.py:555
  353.6 6.6 %shard_map.287 = (bf16[4,192,1536]{2,1,0:T(8,128)(2,1)}, bf16[4,192,1536]{2,1,0:T(8,128)(2,1)}) custom-call(s32[2]{0:T(128)S(1)} %pad_add_fusion.2.at_ref, bf16[1536,640]{1,0:T(8,128)(2,1)S(1)} %copy-done.21, bf16[1536,640]{1,0:T(8,128)(2,1)S(1)} %get-tuple-element.248.y_ref.dv_ref), custom_call_target="tpu_custom_call" | custom-call | tf_op jit(solution)/shard_map/pallas_call | solution.py:71
  360.2 6.5 %shard_map.288 = (bf16[4,192,1536]{2,1,0:T(8,128)(2,1)}, bf16[4,192,1536]{2,1,0:T(8,128)(2,1)}) custom-call(s32[2]{0:T(128)S(1)} %pad_add_fusion.2.at_ref, bf16[1536,640]{1,0:T(8,128)(2,1)S(1)} %copy-done.21, bf16[1536,640]{1,0:T(8,128)(2,1)S(1)} %get-tuple-element.281.y_ref.dk_ref), custom_call_target="tpu_custom_call" | custom-call | tf_op jit(solution)/shard_map/pallas_call | solution.py:71
  368.3 5.3 shard_map.289
  375.4 12.1 %shard_map.290 = (f32[128,1536]{1,0:T(8,128)S(1)}, bf16[128,1536]{1,0:T(8,128)(2,1)}, bf16[128,1536]{1,0:T(8,128)(2,1)}, bf16[128,1536]{1,0:T(8,128)(2,1)}, f32[8,1536]{1,0:T(8,128)S(1)}) custom-call(bf16[1536,512]{1,0:T(8,128)(2,1)} %copy-done.27, bf16[1536,640]{1,0:T(8,128)(2,1)} %copy-done.8, bf16[1536,640]{1,0:T(8,128)(2,1)} %copy-done.10, ...), custom_call_target="tpu_custom_call" | custom-call | tf_op jit(solution)/shard_map/pallas_call | solution.py:681
  389.7 6.6 %collective-permute-done.44.refs_1_.refs_9_ = bf16[1,192,2304]{2,1,0:T(8,128)(2,1)S(1)} collective-permute-done((bf16[1,192,2304]{2,1,0:T(8,128)(2,1)}, bf16[1,192,2304]{2,1,0:T(8,128)(2,1)S(1)}, u32[]{:S(2)}, u32[]{:S(2)}) %collective-permute-start.44) | collective-permute-done | bytes 884768 | tf_op jit(solution)/shard_map/ppermute | solution.py:43
  396.4 3.1 shard_map.292
  405.3 2.0 collective-permute-start.50
  414.9 12.1 %shard_map.296 = (f32[512,1536]{1,0:T(8,128)}, f32[8,1536]{1,0:T(8,128)S(1)}) custom-call(bf16[1536,640]{1,0:T(8,128)(2,1)S(1)} %copy-done.9, bf16[1536,640]{1,0:T(8,128)(2,1)S(1)} %copy-done.11, bf16[1536,1536]{1,0:T(8,128)(2,1)} %copy-done.4, bf16[1536,1536]{1,0:T(8,128)(2,1)} %copy-done.5, bf16[512,1536]{1,0:T(8,128)(2,1)S(1)} %bitcast.140, ...), custom_call_target="tpu_custom_call" | custom-call | tf_op jit(solution)/shard_map/pallas_call | solution.py:636
  427.5 2.6 collective-permute-done.46.refs_1_.refs_3_
  435.6 3.5 collective-permute-done.49.refs_6_
  441.2 6.5 %collective-permute-done.54.refs_3_ = bf16[1,192,1536]{2,1,0:T(8,128)(2,1)S(1)} collective-permute-done((bf16[1,192,1536]{2,1,0:T(8,128)(2,1)}, bf16[1,192,1536]{2,1,0:T(8,128)(2,1)S(1)}, u32[]{:S(2)}, u32[]{:S(2)}) %collective-permute-start.54) | collective-permute-done | bytes 589856 | tf_op jit(solution)/shard_map/ppermute | solution.py:43
  447.8 2.4 collective-permute-done.53.refs_1_
  452.5 1.7 collective-permute-start.56
  454.2 3.5 collective-permute-done.51.refs_1_.refs_3_
  457.7 2.2 collective-permute-done.52.refs_1_.refs_3_
  459.8 3.1 collective-permute-done.56
  470.4 2.5 collective-permute-done.60
  474.3 3.0 collective-permute-done.61
  486.0 2.0 collective-permute-start.65
  490.3 14.6 %collective-permute-done.67 = bf16[2,192,384]{2,1,0:T(8,128)(2,1)S(1)} collective-permute-done((bf16[2,192,384]{2,1,0:T(8,128)(2,1)S(1)}, bf16[2,192,384]{2,1,0:T(8,128)(2,1)S(1)}, u32[]{:S(2)}, u32[]{:S(2)}) %collective-permute-start.67) | collective-permute-done | bytes 294944 | tf_op jit(solution)/shard_map/ppermute | solution.py:21
  508.5 4.3 shard_map.303
  512.8 6.3 %collective-permute-done.63 = f32[8,1536]{1,0:T(8,128)S(1)} collective-permute-done((f32[8,1536]{1,0:T(8,128)S(1)}, f32[8,1536]{1,0:T(8,128)S(1)}, u32[]{:S(2)}, u32[]{:S(2)}) %collective-permute-start.63) | collective-permute-done | bytes 49184 | tf_op jit(solution)/shard_map/ppermute | solution.py:43
  (506 shorter events, 127.1 us)
Async XLA Ops:
  7.2 124.5 %all-gather.3.cloned.1.call-start = ((), (), s32[]{:S(2)}) async-start(), calls=%async_computation | async-start | bytes 3932160 | tf_op jit(solution)/shard_map/all_gather | solution.py:826
  8.5 24.3 %collective-permute-start.2 = (bf16[2,192,384]{2,1,0:T(8,128)(2,1)S(1)}, bf16[2,192,384]{2,1,0:T(8,128)(2,1)S(1)}, u32[]{:S(2)}, u32[]{:S(2)}) collective-permute-start(bf16[2,192,384]{2,1,0:T(8,128)(2,1)S(1)} %bitcast.151), channel_id=1, source_target_pairs={{0,3},{1,0},{2,1},{3,2},{4,7},{5,4},{6,5},{7,6},{8,11},{9,8},{10,9... | collective-permute-start | bytes 884744 | tf_op jit(solution)/shard_map/ppermute | solution.py:21
  13.6 25.1 %collective-permute-start.1 = (bf16[2,192,384]{2,1,0:T(8,128)(2,1)S(1)}, bf16[2,192,384]{2,1,0:T(8,128)(2,1)S(1)}, u32[]{:S(2)}, u32[]{:S(2)}) collective-permute-start(bf16[2,192,384]{2,1,0:T(8,128)(2,1)S(1)} %bitcast.152), channel_id=1, source_target_pairs={{0,2},{1,3},{2,0},{3,1},{4,6},{5,7},{6,4},{7,5},{8,10},{9,11},{10,... | collective-permute-start | bytes 884744 | tf_op jit(solution)/shard_map/ppermute | solution.py:21
  13.6 25.1 %collective-permute-start = (bf16[2,192,384]{2,1,0:T(8,128)(2,1)S(1)}, bf16[2,192,384]{2,1,0:T(8,128)(2,1)S(1)}, u32[]{:S(2)}, u32[]{:S(2)}) collective-permute-start(bf16[2,192,384]{2,1,0:T(8,128)(2,1)S(1)} %bitcast.153), channel_id=1, source_target_pairs={{0,1},{1,2},{2,3},{3,0},{4,5},{5,6},{6,7},{7,4},{8,9},{9,10},{10,1... | collective-permute-start | bytes 884744 | tf_op jit(solution)/shard_map/ppermute | solution.py:21
  38.8 8.7 %collective-permute-start.5 = (bf16[2,192,384]{2,1,0:T(8,128)(2,1)S(1)}, bf16[2,192,384]{2,1,0:T(8,128)(2,1)S(1)}, u32[]{:S(2)}, u32[]{:S(2)}) collective-permute-start(bf16[2,192,384]{2,1,0:T(8,128)(2,1)S(1)} %pad_maximum_fusion.9), channel_id=1, source_target_pairs={{0,3},{1,0},{2,1},{3,2},{4,7},{5,4},{6,5},{7,6},{8,11},{9,8},{10,9... | collective-permute-start | bytes 884744 | tf_op jit(solution)/shard_map/ppermute | solution.py:21
  38.8 28.1 %collective-permute-start.4 = (bf16[2,192,384]{2,1,0:T(8,128)(2,1)S(1)}, bf16[2,192,384]{2,1,0:T(8,128)(2,1)S(1)}, u32[]{:S(2)}, u32[]{:S(2)}) collective-permute-start(bf16[2,192,384]{2,1,0:T(8,128)(2,1)S(1)} %pad_maximum_fusion.9), channel_id=1, source_target_pairs={{0,2},{1,3},{2,0},{3,1},{4,6},{5,7},{6,4},{7,5},{8,10},{9,11},{10,... | collective-permute-start | bytes 884744 | tf_op jit(solution)/shard_map/ppermute | solution.py:21
  41.7 25.3 %collective-permute-start.3 = (bf16[2,192,384]{2,1,0:T(8,128)(2,1)S(1)}, bf16[2,192,384]{2,1,0:T(8,128)(2,1)S(1)}, u32[]{:S(2)}, u32[]{:S(2)}) collective-permute-start(bf16[2,192,384]{2,1,0:T(8,128)(2,1)S(1)} %pad_maximum_fusion.9), channel_id=1, source_target_pairs={{0,1},{1,2},{2,3},{3,0},{4,5},{5,6},{6,7},{7,4},{8,9},{9,10},{10,1... | collective-permute-start | bytes 884744 | tf_op jit(solution)/shard_map/ppermute | solution.py:21
  44.3 24.7 %collective-permute-start.6 = (bf16[1,3,192,384]{3,2,1,0:T(8,128)(2,1)S(1)}, bf16[1,3,192,384]{3,2,1,0:T(8,128)(2,1)}, u32[]{:S(2)}, u32[]{:S(2)}) collective-permute-start(bf16[1,3,192,384]{3,2,1,0:T(8,128)(2,1)S(1)} %maximum_bitcast_fusion.2), channel_id=1, source_target_pairs={{0,8},{4,12},{8,0},{12,4},{16,24},{20,28},{24,16},{28,20},{1,9},{5... | collective-permute-start | bytes 1327112 | tf_op jit(solution)/shard_map/ppermute | solution.py:43
  45.9 24.3 %collective-permute-start.7 = (bf16[1,3,192,384]{3,2,1,0:T(8,128)(2,1)S(1)}, bf16[1,3,192,384]{3,2,1,0:T(8,128)(2,1)}, u32[]{:S(2)}, u32[]{:S(2)}) collective-permute-start(bf16[1,3,192,384]{3,2,1,0:T(8,128)(2,1)S(1)} %maximum_bitcast_fusion.3), channel_id=1, source_target_pairs={{0,16},{4,20},{8,24},{12,28},{16,0},{20,4},{24,8},{28,12},{1,17},{... | collective-permute-start | bytes 1327112 | tf_op jit(solution)/shard_map/ppermute | solution.py:43
  71.3 20.2 %collective-permute-start.8 = (bf16[2,3,192,384]{3,2,1,0:T(8,128)(2,1)S(1)}, bf16[2,3,192,384]{3,2,1,0:T(8,128)(2,1)S(1)}, u32[]{:S(2)}, u32[]{:S(2)}) collective-permute-start(bf16[2,3,192,384]{3,2,1,0:T(8,128)(2,1)S(1)} %pad_maximum_fusion.3), channel_id=1, source_target_pairs={{0,16},{4,20},{8,24},{12,28},{16,0},{20,4},{24,8},{28,12},{1,17},{... | collective-permute-start | bytes 2654216 | tf_op jit(solution)/shard_map/ppermute | solution.py:43
  73.2 19.9 %collective-permute-start.9 = (bf16[2,3,192,384]{3,2,1,0:T(8,128)(2,1)S(1)}, bf16[2,3,192,384]{3,2,1,0:T(8,128)(2,1)S(1)}, u32[]{:S(2)}, u32[]{:S(2)}) collective-permute-start(bf16[2,3,192,384]{3,2,1,0:T(8,128)(2,1)S(1)} %pad_maximum_fusion.4), channel_id=1, source_target_pairs={{0,8},{4,12},{8,0},{12,4},{16,24},{20,28},{24,16},{28,20},{1,9},{5... | collective-permute-start | bytes 2654216 | tf_op jit(solution)/shard_map/ppermute | solution.py:43
  91.7 4.5 collective-permute-start.12
  93.3 17.1 %collective-permute-start.15 = (bf16[4,3,192,384]{3,2,1,0:T(8,128)(2,1)S(1)}, bf16[4,3,192,384]{3,2,1,0:T(8,128)(2,1)S(1)}, u32[]{:S(2)}, u32[]{:S(2)}) collective-permute-start(bf16[4,3,192,384]{3,2,1,0:T(8,128)(2,1)S(1)} %constant_dynamic-update-slice_fusion.2.refs_1_), channel_id=1, source_target_pairs={{0,4},{4,0},{8,12},{12,8},{16,20},{20,16},{24,28},{28,24},{1,5},{5... | collective-permute-start | bytes 5308424 | tf_op jit(solution)/shard_map/ppermute | solution.py:43
  93.6 12.6 %collective-permute-start.10 = (bf16[1,3,192,384]{3,2,1,0:T(8,128)(2,1)S(1)}, bf16[1,3,192,384]{3,2,1,0:T(8,128)(2,1)S(1)}, u32[]{:S(2)}, u32[]{:S(2)}) collective-permute-start(bf16[1,3,192,384]{3,2,1,0:T(8,128)(2,1)S(1)} %maximum_bitcast_fusion), channel_id=1, source_target_pairs={{0,8},{4,12},{8,0},{12,4},{16,24},{20,28},{24,16},{28,20},{1,9},{5... | collective-permute-start | bytes 1327112 | tf_op jit(solution)/shard_map/ppermute | solution.py:43
  95.1 12.3 %collective-permute-start.11 = (bf16[1,3,192,384]{3,2,1,0:T(8,128)(2,1)S(1)}, bf16[1,3,192,384]{3,2,1,0:T(8,128)(2,1)S(1)}, u32[]{:S(2)}, u32[]{:S(2)}) collective-permute-start(bf16[1,3,192,384]{3,2,1,0:T(8,128)(2,1)S(1)} %maximum_bitcast_fusion.1), channel_id=1, source_target_pairs={{0,16},{4,20},{8,24},{12,28},{16,0},{20,4},{24,8},{28,12},{1,17},{... | collective-permute-start | bytes 1327112 | tf_op jit(solution)/shard_map/ppermute | solution.py:43
  107.5 21.1 %collective-permute-start.14 = (bf16[2,3,192,384]{3,2,1,0:T(8,128)(2,1)S(1)}, bf16[2,3,192,384]{3,2,1,0:T(8,128)(2,1)S(1)}, u32[]{:S(2)}, u32[]{:S(2)}) collective-permute-start(bf16[2,3,192,384]{3,2,1,0:T(8,128)(2,1)S(1)} %pad_maximum_fusion.6), channel_id=1, source_target_pairs={{0,8},{4,12},{8,0},{12,4},{16,24},{20,28},{24,16},{28,20},{1,9},{5... | collective-permute-start | bytes 2654216 | tf_op jit(solution)/shard_map/ppermute | solution.py:43
  108.2 20.9 %collective-permute-start.13 = (bf16[2,3,192,384]{3,2,1,0:T(8,128)(2,1)S(1)}, bf16[2,3,192,384]{3,2,1,0:T(8,128)(2,1)S(1)}, u32[]{:S(2)}, u32[]{:S(2)}) collective-permute-start(bf16[2,3,192,384]{3,2,1,0:T(8,128)(2,1)S(1)} %pad_maximum_fusion.5), channel_id=1, source_target_pairs={{0,16},{4,20},{8,24},{12,28},{16,0},{20,4},{24,8},{28,12},{1,17},{... | collective-permute-start | bytes 2654216 | tf_op jit(solution)/shard_map/ppermute | solution.py:43
  130.2 5.8 %collective-permute-start.17 = (bf16[4,3,192,384]{3,2,1,0:T(8,128)(2,1)}, bf16[4,3,192,384]{3,2,1,0:T(8,128)(2,1)}, u32[]{:S(2)}, u32[]{:S(2)}) collective-permute-start(bf16[4,3,192,384]{3,2,1,0:T(8,128)(2,1)} %constant_dynamic-update-slice_fusion.7.refs_3_.refs_2_), channel_id=1, source_target_pairs={{0,4},{4,0},{8,12},{12,8},{16,20},{20,16},{24,28},{28,24},{1,5},{5... | collective-permute-start | bytes 5308424 | tf_op jit(solution)/shard_map/ppermute | solution.py:43
  131.2 5.6 %collective-permute-start.16 = (bf16[4,3,192,384]{3,2,1,0:T(8,128)(2,1)}, bf16[4,3,192,384]{3,2,1,0:T(8,128)(2,1)}, u32[]{:S(2)}, u32[]{:S(2)}) collective-permute-start(bf16[4,3,192,384]{3,2,1,0:T(8,128)(2,1)} %constant_dynamic-update-slice_fusion.4.refs_1_.refs_0_), channel_id=1, source_target_pairs={{0,4},{4,0},{8,12},{12,8},{16,20},{20,16},{24,28},{28,24},{1,5},{5... | collective-permute-start | bytes 5308424 | tf_op jit(solution)/shard_map/ppermute | solution.py:43
  155.9 14.4 %collective-permute-start.18 = (bf16[1632,128]{1,0:T(8,128)(2,1)}, bf16[1632,128]{1,0:T(8,128)(2,1)}, u32[]{:S(2)}, u32[]{:S(2)}) collective-permute-start(bf16[1632,128]{1,0:T(8,128)(2,1)} %get-tuple-element.195), channel_id=1, source_target_pairs={{0,3},{1,0},{2,1},{3,2},{4,7},{5,4},{6,5},{7,6},{8,11},{9,8},{10,9... | collective-permute-start | bytes 1253384 | tf_op jit(solution)/shard_map/ppermute | solution.py:21
  155.9 37.6 %collective-permute-start.19 = (bf16[1632,128]{1,0:T(8,128)(2,1)}, bf16[1632,128]{1,0:T(8,128)(2,1)}, u32[]{:S(2)}, u32[]{:S(2)}) collective-permute-start(bf16[1632,128]{1,0:T(8,128)(2,1)} %get-tuple-element.196), channel_id=1, source_target_pairs={{0,2},{1,3},{2,0},{3,1},{4,6},{5,7},{6,4},{7,5},{8,10},{9,11},{10,... | collective-permute-start | bytes 1253384 | tf_op jit(solution)/shard_map/ppermute | solution.py:21
  155.9 37.5 %collective-permute-start.20 = (bf16[1632,128]{1,0:T(8,128)(2,1)}, bf16[1632,128]{1,0:T(8,128)(2,1)}, u32[]{:S(2)}, u32[]{:S(2)}) collective-permute-start(bf16[1632,128]{1,0:T(8,128)(2,1)} %get-tuple-element.197), channel_id=1, source_target_pairs={{0,1},{1,2},{2,3},{3,0},{4,5},{5,6},{6,7},{7,4},{8,9},{9,10},{10,1... | collective-permute-start | bytes 1253384 | tf_op jit(solution)/shard_map/ppermute | solution.py:21
  164.0 5.6 %collective-permute-start.23 = (f32[8,128]{1,0:T(8,128)S(1)}, f32[8,128]{1,0:T(8,128)S(1)}, u32[]{:S(2)}, u32[]{:S(2)}) collective-permute-start(f32[8,128]{1,0:T(8,128)S(1)} %add.341), channel_id=1, source_target_pairs={{0,16},{4,20},{8,24},{12,28},{16,0},{20,4},{24,8},{28,12},{1,17},{... | collective-permute-start | bytes 12296 | tf_op jit(solution)/shard_map/ppermute | solution.py:43
  197.2 11.8 %collective-permute-start.26 = (bf16[128,1536]{1,0:T(8,128)(2,1)S(1)}, bf16[128,1536]{1,0:T(8,128)(2,1)S(1)}, u32[]{:S(2)}, u32[]{:S(2)}) collective-permute-start(bf16[128,1536]{1,0:T(8,128)(2,1)S(1)} %add_convert_fusion), channel_id=1, source_target_pairs={{0,3},{1,0},{2,1},{3,2},{4,7},{5,4},{6,5},{7,6},{8,11},{9,8},{10,9... | collective-permute-start | bytes 1179656 | tf_op jit(solution)/shard_map/ppermute | solution.py:21
  197.3 35.8 %collective-permute-start.25 = (bf16[128,1536]{1,0:T(8,128)(2,1)S(1)}, bf16[128,1536]{1,0:T(8,128)(2,1)S(1)}, u32[]{:S(2)}, u32[]{:S(2)}) collective-permute-start(bf16[128,1536]{1,0:T(8,128)(2,1)S(1)} %add_convert_fusion), channel_id=1, source_target_pairs={{0,2},{1,3},{2,0},{3,1},{4,6},{5,7},{6,4},{7,5},{8,10},{9,11},{10,... | collective-permute-start | bytes 1179656 | tf_op jit(solution)/shard_map/ppermute | solution.py:21
  198.5 34.5 %collective-permute-start.24 = (bf16[128,1536]{1,0:T(8,128)(2,1)S(1)}, bf16[128,1536]{1,0:T(8,128)(2,1)S(1)}, u32[]{:S(2)}, u32[]{:S(2)}) collective-permute-start(bf16[128,1536]{1,0:T(8,128)(2,1)S(1)} %add_convert_fusion), channel_id=1, source_target_pairs={{0,1},{1,2},{2,3},{3,0},{4,5},{5,6},{6,7},{7,4},{8,9},{9,10},{10,1... | collective-permute-start | bytes 1179656 | tf_op jit(solution)/shard_map/ppermute | solution.py:21
  245.6 31.9 %collective-permute-start.29 = (bf16[128,1536]{1,0:T(8,128)(2,1)}, bf16[128,1536]{1,0:T(8,128)(2,1)}, u32[]{:S(2)}, u32[]{:S(2)}) collective-permute-start(bf16[128,1536]{1,0:T(8,128)(2,1)} %get-tuple-element.410), channel_id=1, source_target_pairs={{0,1},{1,2},{2,3},{3,0},{4,5},{5,6},{6,7},{7,4},{8,9},{9,10},{10,1... | collective-permute-start | bytes 1179656 | tf_op jit(solution)/shard_map/ppermute | solution.py:21
  245.6 31.9 %collective-permute-start.28 = (bf16[128,1536]{1,0:T(8,128)(2,1)}, bf16[128,1536]{1,0:T(8,128)(2,1)}, u32[]{:S(2)}, u32[]{:S(2)}) collective-permute-start(bf16[128,1536]{1,0:T(8,128)(2,1)} %get-tuple-element.411), channel_id=1, source_target_pairs={{0,2},{1,3},{2,0},{3,1},{4,6},{5,7},{6,4},{7,5},{8,10},{9,11},{10,... | collective-permute-start | bytes 1179656 | tf_op jit(solution)/shard_map/ppermute | solution.py:21
  247.3 30.2 %collective-permute-start.27 = (bf16[128,1536]{1,0:T(8,128)(2,1)}, bf16[128,1536]{1,0:T(8,128)(2,1)}, u32[]{:S(2)}, u32[]{:S(2)}) collective-permute-start(bf16[128,1536]{1,0:T(8,128)(2,1)} %get-tuple-element.412), channel_id=1, source_target_pairs={{0,3},{1,0},{2,1},{3,2},{4,7},{5,4},{6,5},{7,6},{8,11},{9,8},{10,9... | collective-permute-start | bytes 1179656 | tf_op jit(solution)/shard_map/ppermute | solution.py:21
  271.6 23.1 %collective-permute-start.33 = (bf16[4,192,1536]{2,1,0:T(8,128)(2,1)}, bf16[4,192,1536]{2,1,0:T(8,128)(2,1)S(1)}, u32[]{:S(2)}, u32[]{:S(2)}) collective-permute-start(bf16[4,192,1536]{2,1,0:T(8,128)(2,1)} %get-tuple-element.213), channel_id=1, source_target_pairs={{0,4},{4,0},{8,12},{12,8},{16,20},{20,16},{24,28},{28,24},{1,5},{5... | collective-permute-start | bytes 7077896 | tf_op jit(solution)/shard_map/ppermute | solution.py:43
  277.0 19.5 %collective-permute-start.34 = (bf16[4,192,1536]{2,1,0:T(8,128)(2,1)}, bf16[4,192,1536]{2,1,0:T(8,128)(2,1)S(1)}, u32[]{:S(2)}, u32[]{:S(2)}) collective-permute-start(bf16[4,192,1536]{2,1,0:T(8,128)(2,1)} %get-tuple-element.215), channel_id=1, source_target_pairs={{0,4},{4,0},{8,12},{12,8},{16,20},{20,16},{24,28},{28,24},{1,5},{5... | collective-permute-start | bytes 7077896 | tf_op jit(solution)/shard_map/ppermute | solution.py:43
  285.0 11.5 %collective-permute-start.35 = (bf16[4,192,1536]{2,1,0:T(8,128)(2,1)}, bf16[4,192,1536]{2,1,0:T(8,128)(2,1)S(1)}, u32[]{:S(2)}, u32[]{:S(2)}) collective-permute-start(bf16[4,192,1536]{2,1,0:T(8,128)(2,1)} %get-tuple-element.222), channel_id=1, source_target_pairs={{0,4},{4,0},{8,12},{12,8},{16,20},{20,16},{24,28},{28,24},{1,5},{5... | collective-permute-start | bytes 7077896 | tf_op jit(solution)/shard_map/ppermute | solution.py:43
  287.4 17.4 %collective-permute-start.32 = (bf16[1632,128]{1,0:T(8,128)(2,1)S(1)}, bf16[1632,128]{1,0:T(8,128)(2,1)S(1)}, u32[]{:S(2)}, u32[]{:S(2)}) collective-permute-start(bf16[1632,128]{1,0:T(8,128)(2,1)S(1)} %shard_map.280.rest_0_.rest_4_), channel_id=1, source_target_pairs={{0,3},{1,0},{2,1},{3,2},{4,7},{5,4},{6,5},{7,6},{8,11},{9,8},{10,9... | collective-permute-start | bytes 1253384 | tf_op jit(solution)/shard_map/ppermute | solution.py:21
  294.7 36.8 %collective-permute-start.31 = (bf16[1632,128]{1,0:T(8,128)(2,1)S(1)}, bf16[1632,128]{1,0:T(8,128)(2,1)S(1)}, u32[]{:S(2)}, u32[]{:S(2)}) collective-permute-start(bf16[1632,128]{1,0:T(8,128)(2,1)S(1)} %shard_map.280.rest_0_.rest_4_), channel_id=1, source_target_pairs={{0,2},{1,3},{2,0},{3,1},{4,6},{5,7},{6,4},{7,5},{8,10},{9,11},{10,... | collective-permute-start | bytes 1253384 | tf_op jit(solution)/shard_map/ppermute | solution.py:21
  294.8 36.8 %collective-permute-start.30 = (bf16[1632,128]{1,0:T(8,128)(2,1)S(1)}, bf16[1632,128]{1,0:T(8,128)(2,1)S(1)}, u32[]{:S(2)}, u32[]{:S(2)}) collective-permute-start(bf16[1632,128]{1,0:T(8,128)(2,1)S(1)} %shard_map.280.rest_0_.rest_4_), channel_id=1, source_target_pairs={{0,1},{1,2},{2,3},{3,0},{4,5},{5,6},{6,7},{7,4},{8,9},{9,10},{10,1... | collective-permute-start | bytes 1253384 | tf_op jit(solution)/shard_map/ppermute | solution.py:21
  298.9 49.5 %collective-permute-start.39 = (bf16[2,192,2304]{2,1,0:T(8,128)(2,1)}, bf16[2,192,2304]{2,1,0:T(8,128)(2,1)S(1)}, u32[]{:S(2)}, u32[]{:S(2)}) collective-permute-start(bf16[2,192,2304]{2,1,0:T(8,128)(2,1)} %get-tuple-element.226), channel_id=1, source_target_pairs={{0,8},{4,12},{8,0},{12,4},{16,24},{20,28},{24,16},{28,20},{1,9},{5... | collective-permute-start | bytes 5308424 | tf_op jit(solution)/shard_map/ppermute | solution.py:43
  302.5 47.4 %collective-permute-start.40 = (bf16[2,192,2304]{2,1,0:T(8,128)(2,1)}, bf16[2,192,2304]{2,1,0:T(8,128)(2,1)S(1)}, u32[]{:S(2)}, u32[]{:S(2)}) collective-permute-start(bf16[2,192,2304]{2,1,0:T(8,128)(2,1)} %get-tuple-element.229), channel_id=1, source_target_pairs={{0,16},{4,20},{8,24},{12,28},{16,0},{20,4},{24,8},{28,12},{1,17},{... | collective-permute-start | bytes 5308424 | tf_op jit(solution)/shard_map/ppermute | solution.py:43
  331.5 35.2 %collective-permute-start.36 = (bf16[128,1536]{1,0:T(8,128)(2,1)}, bf16[128,1536]{1,0:T(8,128)(2,1)S(1)}, u32[]{:S(2)}, u32[]{:S(2)}) collective-permute-start(bf16[128,1536]{1,0:T(8,128)(2,1)} %get-tuple-element.234), channel_id=1, source_target_pairs={{0,3},{1,0},{2,1},{3,2},{4,7},{5,4},{6,5},{7,6},{8,11},{9,8},{10,9... | collective-permute-start | bytes 1179656 | tf_op jit(solution)/shard_map/ppermute | solution.py:21
  331.5 36.7 %collective-permute-start.37 = (bf16[128,1536]{1,0:T(8,128)(2,1)}, bf16[128,1536]{1,0:T(8,128)(2,1)S(1)}, u32[]{:S(2)}, u32[]{:S(2)}) collective-permute-start(bf16[128,1536]{1,0:T(8,128)(2,1)} %get-tuple-element.235), channel_id=1, source_target_pairs={{0,2},{1,3},{2,0},{3,1},{4,6},{5,7},{6,4},{7,5},{8,10},{9,11},{10,... | collective-permute-start | bytes 1179656 | tf_op jit(solution)/shard_map/ppermute | solution.py:21
  333.8 34.5 %collective-permute-start.38 = (bf16[128,1536]{1,0:T(8,128)(2,1)}, bf16[128,1536]{1,0:T(8,128)(2,1)S(1)}, u32[]{:S(2)}, u32[]{:S(2)}) collective-permute-start(bf16[128,1536]{1,0:T(8,128)(2,1)} %get-tuple-element.236), channel_id=1, source_target_pairs={{0,1},{1,2},{2,3},{3,0},{4,5},{5,6},{6,7},{7,4},{8,9},{9,10},{10,1... | collective-permute-start | bytes 1179656 | tf_op jit(solution)/shard_map/ppermute | solution.py:21
  373.5 14.7 %collective-permute-start.41 = (bf16[4,192,1536]{2,1,0:T(8,128)(2,1)}, bf16[4,192,1536]{2,1,0:T(8,128)(2,1)S(1)}, u32[]{:S(2)}, u32[]{:S(2)}) collective-permute-start(bf16[4,192,1536]{2,1,0:T(8,128)(2,1)} %get-tuple-element.255), channel_id=1, source_target_pairs={{0,4},{4,0},{8,12},{12,8},{16,20},{20,16},{24,28},{28,24},{1,5},{5... | collective-permute-start | bytes 7077896 | tf_op jit(solution)/shard_map/ppermute | solution.py:43
  373.6 16.2 %collective-permute-start.42 = (bf16[4,192,1536]{2,1,0:T(8,128)(2,1)}, bf16[4,192,1536]{2,1,0:T(8,128)(2,1)}, u32[]{:S(2)}, u32[]{:S(2)}) collective-permute-start(bf16[4,192,1536]{2,1,0:T(8,128)(2,1)} %get-tuple-element.256), channel_id=1, source_target_pairs={{0,4},{4,0},{8,12},{12,8},{16,20},{20,16},{24,28},{28,24},{1,5},{5... | collective-permute-start | bytes 7077896 | tf_op jit(solution)/shard_map/ppermute | solution.py:43
  374.1 15.7 %collective-permute-start.43 = (bf16[4,192,1536]{2,1,0:T(8,128)(2,1)}, bf16[4,192,1536]{2,1,0:T(8,128)(2,1)S(1)}, u32[]{:S(2)}, u32[]{:S(2)}) collective-permute-start(bf16[4,192,1536]{2,1,0:T(8,128)(2,1)} %get-tuple-element.254), channel_id=1, source_target_pairs={{0,4},{4,0},{8,12},{12,8},{16,20},{20,16},{24,28},{28,24},{1,5},{5... | collective-permute-start | bytes 7077896 | tf_op jit(solution)/shard_map/ppermute | solution.py:43
  374.1 22.2 %collective-permute-start.44 = (bf16[1,192,2304]{2,1,0:T(8,128)(2,1)}, bf16[1,192,2304]{2,1,0:T(8,128)(2,1)S(1)}, u32[]{:S(2)}, u32[]{:S(2)}) collective-permute-start(bf16[1,192,2304]{2,1,0:T(8,128)(2,1)} %get-tuple-element.242), channel_id=1, source_target_pairs={{0,16},{4,20},{8,24},{12,28},{16,0},{20,4},{24,8},{28,12},{1,17},{... | collective-permute-start | bytes 2654216 | tf_op jit(solution)/shard_map/ppermute | solution.py:43
  374.1 22.3 %collective-permute-start.45 = (bf16[1,192,2304]{2,1,0:T(8,128)(2,1)}, bf16[1,192,2304]{2,1,0:T(8,128)(2,1)}, u32[]{:S(2)}, u32[]{:S(2)}) collective-permute-start(bf16[1,192,2304]{2,1,0:T(8,128)(2,1)} %get-tuple-element.244), channel_id=1, source_target_pairs={{0,8},{4,12},{8,0},{12,4},{16,24},{20,28},{24,16},{28,20},{1,9},{5... | collective-permute-start | bytes 2654216 | tf_op jit(solution)/shard_map/ppermute | solution.py:43
  399.6 27.9 %collective-permute-start.47 = (bf16[2,192,1536]{2,1,0:T(8,128)(2,1)}, bf16[2,192,1536]{2,1,0:T(8,128)(2,1)S(1)}, u32[]{:S(2)}, u32[]{:S(2)}) collective-permute-start(bf16[2,192,1536]{2,1,0:T(8,128)(2,1)} %get-tuple-element.269), channel_id=1, source_target_pairs={{0,16},{4,20},{8,24},{12,28},{16,0},{20,4},{24,8},{28,12},{1,17},{... | collective-permute-start | bytes 3538952 | tf_op jit(solution)/shard_map/ppermute | solution.py:43
  402.9 27.2 %collective-permute-start.46 = (bf16[2,192,1536]{2,1,0:T(8,128)(2,1)}, bf16[2,192,1536]{2,1,0:T(8,128)(2,1)S(1)}, u32[]{:S(2)}, u32[]{:S(2)}) collective-permute-start(bf16[2,192,1536]{2,1,0:T(8,128)(2,1)} %get-tuple-element.265), channel_id=1, source_target_pairs={{0,8},{4,12},{8,0},{12,4},{16,24},{20,28},{24,16},{28,20},{1,9},{5... | collective-permute-start | bytes 3538952 | tf_op jit(solution)/shard_map/ppermute | solution.py:43
  404.1 30.7 %collective-permute-start.48 = (bf16[128,1536]{1,0:T(8,128)(2,1)}, bf16[128,1536]{1,0:T(8,128)(2,1)S(1)}, u32[]{:S(2)}, u32[]{:S(2)}) collective-permute-start(bf16[128,1536]{1,0:T(8,128)(2,1)} %get-tuple-element.291), channel_id=1, source_target_pairs={{0,3},{1,0},{2,1},{3,2},{4,7},{5,4},{6,5},{7,6},{8,11},{9,8},{10,9... | collective-permute-start | bytes 1179656 | tf_op jit(solution)/shard_map/ppermute | solution.py:21
  404.4 34.6 %collective-permute-start.49 = (bf16[128,1536]{1,0:T(8,128)(2,1)}, bf16[128,1536]{1,0:T(8,128)(2,1)S(1)}, u32[]{:S(2)}, u32[]{:S(2)}) collective-permute-start(bf16[128,1536]{1,0:T(8,128)(2,1)} %get-tuple-element.292), channel_id=1, source_target_pairs={{0,2},{1,3},{2,0},{3,1},{4,6},{5,7},{6,4},{7,5},{8,10},{9,11},{10,... | collective-permute-start | bytes 1179656 | tf_op jit(solution)/shard_map/ppermute | solution.py:21
  405.3 34.6 %collective-permute-start.50 = (bf16[128,1536]{1,0:T(8,128)(2,1)}, bf16[128,1536]{1,0:T(8,128)(2,1)}, u32[]{:S(2)}, u32[]{:S(2)}) collective-permute-start(bf16[128,1536]{1,0:T(8,128)(2,1)} %get-tuple-element.293), channel_id=1, source_target_pairs={{0,1},{1,2},{2,3},{3,0},{4,5},{5,6},{6,7},{7,4},{8,9},{9,10},{10,1... | collective-permute-start | bytes 1179656 | tf_op jit(solution)/shard_map/ppermute | solution.py:21
  431.3 16.5 %collective-permute-start.54 = (bf16[1,192,1536]{2,1,0:T(8,128)(2,1)}, bf16[1,192,1536]{2,1,0:T(8,128)(2,1)S(1)}, u32[]{:S(2)}, u32[]{:S(2)}) collective-permute-start(bf16[1,192,1536]{2,1,0:T(8,128)(2,1)} %get-tuple-element.287), channel_id=1, source_target_pairs={{0,8},{4,12},{8,0},{12,4},{16,24},{20,28},{24,16},{28,20},{1,9},{5... | collective-permute-start | bytes 1769480 | tf_op jit(solution)/shard_map/ppermute | solution.py:43
  433.7 16.5 %collective-permute-start.53 = (bf16[1,192,1536]{2,1,0:T(8,128)(2,1)}, bf16[1,192,1536]{2,1,0:T(8,128)(2,1)S(1)}, u32[]{:S(2)}, u32[]{:S(2)}) collective-permute-start(bf16[1,192,1536]{2,1,0:T(8,128)(2,1)} %get-tuple-element.284), channel_id=1, source_target_pairs={{0,16},{4,20},{8,24},{12,28},{16,0},{20,4},{24,8},{28,12},{1,17},{... | collective-permute-start | bytes 1769480 | tf_op jit(solution)/shard_map/ppermute | solution.py:43
  439.8 17.8 %collective-permute-start.51 = (bf16[2,192,768]{2,1,0:T(8,128)(2,1)S(1)}, bf16[2,192,768]{2,1,0:T(8,128)(2,1)S(1)}, u32[]{:S(2)}, u32[]{:S(2)}) collective-permute-start(bf16[2,192,768]{2,1,0:T(8,128)(2,1)S(1)} %copy-done.127), channel_id=1, source_target_pairs={{0,8},{4,12},{8,0},{12,4},{16,24},{20,28},{24,16},{28,20},{1,9},{5... | collective-permute-start | bytes 1769480 | tf_op jit(solution)/shard_map/ppermute | solution.py:43
  440.3 19.5 %collective-permute-start.52 = (bf16[2,192,768]{2,1,0:T(8,128)(2,1)S(1)}, bf16[2,192,768]{2,1,0:T(8,128)(2,1)S(1)}, u32[]{:S(2)}, u32[]{:S(2)}) collective-permute-start(bf16[2,192,768]{2,1,0:T(8,128)(2,1)S(1)} %copy-done.126), channel_id=1, source_target_pairs={{0,16},{4,20},{8,24},{12,28},{16,0},{20,4},{24,8},{28,12},{1,17},{... | collective-permute-start | bytes 1769480 | tf_op jit(solution)/shard_map/ppermute | solution.py:43
  452.1 7.7 %collective-permute-start.55 = (bf16[2,192,384]{2,1,0:T(8,128)(2,1)S(1)}, bf16[2,192,384]{2,1,0:T(8,128)(2,1)S(1)}, u32[]{:S(2)}, u32[]{:S(2)}) collective-permute-start(bf16[2,192,384]{2,1,0:T(8,128)(2,1)S(1)} %get-tuple-element.298), channel_id=1, source_target_pairs={{0,3},{1,0},{2,1},{3,2},{4,7},{5,4},{6,5},{7,6},{8,11},{9,8},{10,9... | collective-permute-start | bytes 884744 | tf_op jit(solution)/shard_map/ppermute | solution.py:21
  452.5 10.4 %collective-permute-start.56 = (bf16[2,192,384]{2,1,0:T(8,128)(2,1)S(1)}, bf16[2,192,384]{2,1,0:T(8,128)(2,1)S(1)}, u32[]{:S(2)}, u32[]{:S(2)}) collective-permute-start(bf16[2,192,384]{2,1,0:T(8,128)(2,1)S(1)} %get-tuple-element.299), channel_id=1, source_target_pairs={{0,1},{1,2},{2,3},{3,0},{4,5},{5,6},{6,7},{7,4},{8,9},{9,10},{10,1... | collective-permute-start | bytes 884744 | tf_op jit(solution)/shard_map/ppermute | solution.py:21
  463.8 15.1 %collective-permute-start.58 = (bf16[1,192,768]{2,1,0:T(8,128)(2,1)}, bf16[1,192,768]{2,1,0:T(8,128)(2,1)S(1)}, u32[]{:S(2)}, u32[]{:S(2)}) collective-permute-start(bf16[1,192,768]{2,1,0:T(8,128)(2,1)} %get-tuple-element.306), channel_id=1, source_target_pairs={{0,8},{4,12},{8,0},{12,4},{16,24},{20,28},{24,16},{28,20},{1,9},{5... | collective-permute-start | bytes 884744 | tf_op jit(solution)/shard_map/ppermute | solution.py:43
  465.3 14.3 %collective-permute-start.57 = (bf16[1,192,768]{2,1,0:T(8,128)(2,1)}, bf16[1,192,768]{2,1,0:T(8,128)(2,1)S(1)}, u32[]{:S(2)}, u32[]{:S(2)}) collective-permute-start(bf16[1,192,768]{2,1,0:T(8,128)(2,1)} %get-tuple-element.302), channel_id=1, source_target_pairs={{0,16},{4,20},{8,24},{12,28},{16,0},{20,4},{24,8},{28,12},{1,17},{... | collective-permute-start | bytes 884744 | tf_op jit(solution)/shard_map/ppermute | solution.py:43
  478.0 26.9 %collective-permute-start.67 = (bf16[2,192,384]{2,1,0:T(8,128)(2,1)S(1)}, bf16[2,192,384]{2,1,0:T(8,128)(2,1)S(1)}, u32[]{:S(2)}, u32[]{:S(2)}) collective-permute-start(bf16[2,192,384]{2,1,0:T(8,128)(2,1)S(1)} %get-tuple-element.326), channel_id=1, source_target_pairs={{0,2},{1,3},{2,0},{3,1},{4,6},{5,7},{6,4},{7,5},{8,10},{9,11},{10,... | collective-permute-start | bytes 884744 | tf_op jit(solution)/shard_map/ppermute | solution.py:21
  483.2 22.9 %collective-permute-start.62 = (f32[8,1536]{1,0:T(8,128)S(1)}, f32[8,1536]{1,0:T(8,128)S(1)}, u32[]{:S(2)}, u32[]{:S(2)}) collective-permute-start(f32[8,1536]{1,0:T(8,128)S(1)} %add.357), channel_id=1, source_target_pairs={{0,1},{1,0},{2,3},{3,2},{4,5},{5,4},{6,7},{7,6},{8,9},{9,8},{10,11... | collective-permute-start | bytes 147464 | tf_op jit(solution)/shard_map/ppermute | solution.py:43
  484.7 36.9 %collective-permute-start.66 = (bf16[2,192,384]{2,1,0:T(8,128)(2,1)}, bf16[2,192,384]{2,1,0:T(8,128)(2,1)}, u32[]{:S(2)}, u32[]{:S(2)}) collective-permute-start(bf16[2,192,384]{2,1,0:T(8,128)(2,1)} %pad_maximum_fusion.12), channel_id=1, source_target_pairs={{0,1},{1,2},{2,3},{3,0},{4,5},{5,6},{6,7},{7,4},{8,9},{9,10},{10,1... | collective-permute-start | bytes 884744 | tf_op jit(solution)/shard_map/ppermute | solution.py:21
  486.0 35.6 %collective-permute-start.65 = (bf16[2,192,384]{2,1,0:T(8,128)(2,1)}, bf16[2,192,384]{2,1,0:T(8,128)(2,1)}, u32[]{:S(2)}, u32[]{:S(2)}) collective-permute-start(bf16[2,192,384]{2,1,0:T(8,128)(2,1)} %pad_maximum_fusion.11), channel_id=1, source_target_pairs={{0,2},{1,3},{2,0},{3,1},{4,6},{5,7},{6,4},{7,5},{8,10},{9,11},{10,... | collective-permute-start | bytes 884744 | tf_op jit(solution)/shard_map/ppermute | solution.py:21
  488.8 32.8 %collective-permute-start.64 = (bf16[2,192,384]{2,1,0:T(8,128)(2,1)}, bf16[2,192,384]{2,1,0:T(8,128)(2,1)}, u32[]{:S(2)}, u32[]{:S(2)}) collective-permute-start(bf16[2,192,384]{2,1,0:T(8,128)(2,1)} %pad_maximum_fusion.10), channel_id=1, source_target_pairs={{0,3},{1,0},{2,1},{3,2},{4,7},{5,4},{6,5},{7,6},{8,11},{9,8},{10,9... | collective-permute-start | bytes 884744 | tf_op jit(solution)/shard_map/ppermute | solution.py:21
  506.1 12.9 %collective-permute-start.63 = (f32[8,1536]{1,0:T(8,128)S(1)}, f32[8,1536]{1,0:T(8,128)S(1)}, u32[]{:S(2)}, u32[]{:S(2)}) collective-permute-start(f32[8,1536]{1,0:T(8,128)S(1)} %add.358), channel_id=1, source_target_pairs={{0,2},{1,3},{2,0},{3,1},{4,6},{5,7},{6,4},{7,5},{8,10},{9,11},{10,... | collective-permute-start | bytes 147464 | tf_op jit(solution)/shard_map/ppermute | solution.py:43
  (139 other events, 1646.6 us)
Sparse Core Ops, SparseCore 0:
  68.8 61.7 all-gather.2

commit v7 on v6

--- a/solution.py
+++ b/solution.py
@@ -880,8 +880,8 @@
     back_blocks = [back_terms[k * own_rows : (k + 1) * own_rows] for k in range(n_t)]
     back_arrived = send_blocks(back_blocks, n_t)
     late_activation, late_hidden = after([activation, back_hidden], back_terms)
-    down_keep, down_send = gradient(cot_all.T, late_activation, True, at, n_dp)
-    up_keep, up_send = gradient(feed_all.T, late_hidden, True, at, n_dp)
+    down_keep, down_send = gradient(cot_all, late_activation, True, at, n_dp, True)
+    up_keep, up_send = gradient(feed_all, late_hidden, True, at, n_dp, True)
     result_terms = blocks_of_product(late_activation, down_weight, n_t)
     back_feed = add_up(after(back_arrived, down_send, up_send, *result_terms))
     down_got, up_got = partner(down_send, "dp", n_dp, 1), partner(up_send, "dp", n_dp, 1)

time: 537 us -> 538 us (level)
  starting transfers between devices: 74.3 us -> 84.6 us
  local copies, waits for them, and re-layouts: 60.2 us -> 53.4 us
  waiting for transfers between devices: 204 us -> 210 us
    ppermute x38, starting transfers between devices: 29.8 us -> 37.3 us  [partner(): return lax.ppermute(x, axis, [(i, i ^ offset) for i in range(count)])]
    ppermute x30, waiting for transfers between devices: 132 us -> 138 us  [rotate(): lax.ppermute(x, 'tensor', [(i, (i + shift) % count) for i in range(count)])]
    unnamed x279 -> x251, local copies, waits for them, and re-layouts: 29.8 us -> 25.2 us
  transfers between devices with their start and end apart: 69 -> 69, of which waited for: 32 -> 31; matrix products, arithmetic and copies ran while one was open for 11% -> 10% of each run, Pallas kernels for 20% -> 20%
where the time goes in v7:
time: 538 us; the launch traced here: 533 us
  waiting for transfers between devices  210 us (39%)
  Pallas kernels  132 us (25%)
  starting transfers between devices  84.6 us (16%)
  local copies, waits for them, and re-layouts  53.4 us (10%)
  other arithmetic  23 us (4%)
  between operations  19.1 us (4%)
  matrix products  11.3 us (2%)
    ppermute x30, waiting for transfers between devices, rotate(): lax.ppermute(x, 'tensor', [(i, (i + shift) % count) for i in range(count)])  138 us
    ppermute x38, waiting for transfers between devices, partner(): return lax.ppermute(x, axis, [(i, i ^ offset) for i in range(count)])  71.5 us
    ppermute x30, starting transfers between devices, rotate(): lax.ppermute(x, 'tensor', [(i, (i + shift) % count) for i in range(count)])  47.3 us
    ppermute x38, starting transfers between devices, partner(): return lax.ppermute(x, axis, [(i, i ^ offset) for i in range(count)])  37.3 us
    pallas_call x6, Pallas kernels, gradient(): pl.pallas_call(partial(gradient_kernel, natural, turned, n_dp), grid=(3,)...  33.7 us
    unnamed x251, local copies, waits for them, and re-layouts  25.2 us
    pallas_call x4, Pallas kernels, place(): pl.pallas_call(kernel, out_shape=outs, in_specs=[pl.BlockSpec(memory_spac...  21.6 us
    pallas_call x12, Pallas kernels, reduce_cut(): pl.pallas_call(partial(cut_kernel, widths), grid=(count // 2,), in_specs=...  19.6 us
  transfers between devices with their start and end apart: 69, of which 31 were waited for; matrix products, arithmetic and copies ran while one was open for 10% of the time, Pallas kernels for 20%

profile of v7, /device:TPU:0, one launch (start us, length us, event | category | flops | bytes accessed | tf_op | source)
XLA Modules:
  0.0 532.9 jit_solution(5393275390337326954)
XLA Ops:
  8.5 5.1 collective-permute-start.2
  14.6 8.0 %fusion.38 = (bf16[1536,1,384]{2,1,0:T(2,128)(2,1)}, bf16[1536,1,384]{2,1,0:T(2,128)(2,1)}) fusion(bf16[1536,2,384]{2,1,0:T(2,128)(2,1)} %param.27), kind=kLoop, calls=%fused_computation.175 | loop fusion | bytes 4718592 | tf_op jit(solution)/shard_map/slice | solution.py:814
  26.3 4.2 copy_bitcast_fusion
  32.9 5.8 %collective-permute-done.1 = bf16[2,192,384]{2,1,0:T(8,128)(2,1)S(1)} collective-permute-done((bf16[2,192,384]{2,1,0:T(8,128)(2,1)S(1)}, bf16[2,192,384]{2,1,0:T(8,128)(2,1)S(1)}, u32[]{:S(2)}, u32[]{:S(2)}) %collective-permute-start.1) | collective-permute-done | bytes 294944 | tf_op jit(solution)/shard_map/ppermute | solution.py:21
  38.8 2.9 collective-permute-start.4
  41.7 2.4 collective-permute-start.3
  47.5 19.6 %collective-permute-done.4 = bf16[2,192,384]{2,1,0:T(8,128)(2,1)} collective-permute-done((bf16[2,192,384]{2,1,0:T(8,128)(2,1)S(1)}, bf16[2,192,384]{2,1,0:T(8,128)(2,1)}, u32[]{:S(2)}, u32[]{:S(2)}) %collective-permute-start.4) | collective-permute-done | bytes 294944 | tf_op jit(solution)/shard_map/ppermute | solution.py:21
  74.3 16.7 %collective-permute-done.8 = bf16[2,3,192,384]{3,2,1,0:T(8,128)(2,1)S(1)} collective-permute-done((bf16[2,3,192,384]{3,2,1,0:T(8,128)(2,1)S(1)}, bf16[2,3,192,384]{3,2,1,0:T(8,128)(2,1)S(1)}, u32[]{:S(2)}, u32[]{:S(2)}) %collective-permute-start.8) | collective-permute-done | bytes 884768 | tf_op jit(solution)/shard_map/ppermute | solution.py:43
  98.8 5.2 shard_map.271
  113.0 5.2 shard_map.272
  121.8 7.8 %collective-permute-done.14 = bf16[2,3,192,384]{3,2,1,0:T(8,128)(2,1)S(1)} collective-permute-done((bf16[2,3,192,384]{3,2,1,0:T(8,128)(2,1)S(1)}, bf16[2,3,192,384]{3,2,1,0:T(8,128)(2,1)S(1)}, u32[]{:S(2)}, u32[]{:S(2)}) %collective-permute-start.14) | collective-permute-done | bytes 884768 | tf_op jit(solution)/shard_map/ppermute | solution.py:43
  132.7 2.7 dynamic-slice_bitcast_fusion
  137.7 7.5 %shard_map.273 = (bf16[1536,1536]{1,0:T(8,128)(2,1)S(1)}, bf16[1536,512]{1,0:T(8,128)(2,1)S(1)}, bf16[1536,512]{1,0:T(8,128)(2,1)S(1)}) custom-call(s32[2]{0:T(128)S(1)} %pad_add_fusion.2.at_ref, bf16[512,1536]{1,0:T(8,128)(2,1)S(1)} %fusion.7.x_ref, bf16[1536,384]{1,0:T(8,128)(2,1)S(1)} %copy-done.50, ...), custom_call_target="tpu_custom_call" | custom-call | tf_op jit(solution)/shard_map/pallas_call | solution.py:269
  146.4 8.0 %shard_map.274 = (bf16[1632,128]{1,0:T(8,128)(2,1)S(1)}, bf16[1632,128]{1,0:T(8,128)(2,1)}, bf16[1632,128]{1,0:T(8,128)(2,1)}, bf16[1632,128]{1,0:T(8,128)(2,1)}) custom-call(s32[2,4]{1,0:T(2,128)S(1)} %pad_add_fusion.1.span_ref, bf16[1536,512]{1,0:T(8,128)(2,1)S(1)} %get-tuple-element.193.q_ref, bf16[1536,640]{1,0:T(8,128)(2,1)S(1)} %copy-done.41, ...), custom_call_target="tpu_custom_call" | custom-call | tf_op jit(solution)/shard_map/pallas_call | solution.py:401
  155.6 3.2 collective-permute-start.19
  162.7 2.6 collective-permute-start.22
  169.2 3.6 shard_map.275
  173.3 21.8 %collective-permute-done.19.refs_2_ = bf16[1632,128]{1,0:T(8,128)(2,1)} collective-permute-done((bf16[1632,128]{1,0:T(8,128)(2,1)}, bf16[1632,128]{1,0:T(8,128)(2,1)}, u32[]{:S(2)}, u32[]{:S(2)}) %collective-permute-start.19) | collective-permute-done | bytes 417824 | tf_op jit(solution)/shard_map/ppermute | solution.py:21
  198.9 2.1 collective-permute-start.24
  201.2 7.4 %collective-permute-done.26 = bf16[128,1536]{1,0:T(8,128)(2,1)S(1)} collective-permute-done((bf16[128,1536]{1,0:T(8,128)(2,1)S(1)}, bf16[128,1536]{1,0:T(8,128)(2,1)S(1)}, u32[]{:S(2)}, u32[]{:S(2)}) %collective-permute-start.26) | collective-permute-done | bytes 393248 | tf_op jit(solution)/shard_map/ppermute | solution.py:21
  208.7 24.7 %collective-permute-done.25 = bf16[128,1536]{1,0:T(8,128)(2,1)S(1)} collective-permute-done((bf16[128,1536]{1,0:T(8,128)(2,1)S(1)}, bf16[128,1536]{1,0:T(8,128)(2,1)S(1)}, u32[]{:S(2)}, u32[]{:S(2)}) %collective-permute-start.25) | collective-permute-done | bytes 393248 | tf_op jit(solution)/shard_map/ppermute | solution.py:21
  233.4 2.7 multiply_convert_fusion
  236.2 3.7 fusion.16.y_ref
  239.9 2.6 convolution_convert_fusion
  244.9 2.9 collective-permute-start.27
  247.8 4.9 shard_map.277
  253.7 5.3 shard_map.278
  259.1 5.3 shard_map.279
  265.0 8.3 %collective-permute-done.28 = bf16[128,1536]{1,0:T(8,128)(2,1)} collective-permute-done((bf16[128,1536]{1,0:T(8,128)(2,1)}, bf16[128,1536]{1,0:T(8,128)(2,1)}, u32[]{:S(2)}, u32[]{:S(2)}) %collective-permute-start.28) | collective-permute-done | bytes 393248 | tf_op jit(solution)/shard_map/ppermute | solution.py:21
  273.3 2.4 multiply_reduce_fusion
  277.0 4.3 shard_map.281
  283.5 9.1 %collective-permute-start.32 = (bf16[1632,128]{1,0:T(8,128)(2,1)S(1)}, bf16[1632,128]{1,0:T(8,128)(2,1)S(1)}, u32[]{:S(2)}, u32[]{:S(2)}) collective-permute-start(bf16[1632,128]{1,0:T(8,128)(2,1)S(1)} %shard_map.280.rest_0_.rest_4_), channel_id=1, source_target_pairs={{0,3},{1,0},{2,1},{3,2},{4,7},{5,4},{6,5},{7,6},{8,11},{9,8},{10,9... | collective-permute-start | bytes 1253384 | tf_op jit(solution)/shard_map/ppermute | solution.py:21
  294.3 2.4 shard_map.282
  296.7 2.3 collective-permute-start.39
  299.0 2.4 shard_map.283
  301.4 2.1 collective-permute-start.40
  303.5 26.3 %collective-permute-done.31.rest_2_.rest_6_ = bf16[1632,128]{1,0:T(8,128)(2,1)S(1)} collective-permute-done((bf16[1632,128]{1,0:T(8,128)(2,1)S(1)}, bf16[1632,128]{1,0:T(8,128)(2,1)S(1)}, u32[]{:S(2)}, u32[]{:S(2)}) %collective-permute-start.31) | collective-permute-done | bytes 417824 | tf_op jit(solution)/shard_map/ppermute | solution.py:21
  329.9 1.9 collective-permute-start.37
  331.8 2.0 collective-permute-start.38
  333.8 10.7 %shard_map.284 = (bf16[1536,512]{1,0:T(8,128)(2,1)S(1)}, bf16[1536,640]{1,0:T(8,128)(2,1)S(1)}, bf16[1536,640]{1,0:T(8,128)(2,1)S(1)}) custom-call(s32[2,4]{1,0:T(2,128)S(1)} %pad_add_fusion.1.span_ref, bf16[1536,512]{1,0:T(8,128)(2,1)S(1)} %copy-done.49, bf16[1536,640]{1,0:T(8,128)(2,1)S(1)} %copy-done.42, bf16[1536,640]{1,0:T(8,128)(2,1)S(1)} %copy-done.45, ...), custom_call_target="tpu_custom_call" | custom-call | flops 30198988800 | bytes 62914560 | tf_op jit(solution)/shard_map/pallas_call | solution.py:555
  349.7 6.5 %shard_map.287 = (bf16[4,192,1536]{2,1,0:T(8,128)(2,1)}, bf16[4,192,1536]{2,1,0:T(8,128)(2,1)}) custom-call(s32[2]{0:T(128)S(1)} %pad_add_fusion.2.at_ref, bf16[1536,640]{1,0:T(8,128)(2,1)S(1)} %copy-done.20, bf16[1536,640]{1,0:T(8,128)(2,1)S(1)} %get-tuple-element.248.y_ref.dv_ref), custom_call_target="tpu_custom_call" | custom-call | tf_op jit(solution)/shard_map/pallas_call | solution.py:71
  356.2 6.6 %shard_map.288 = (bf16[4,192,1536]{2,1,0:T(8,128)(2,1)}, bf16[4,192,1536]{2,1,0:T(8,128)(2,1)}) custom-call(s32[2]{0:T(128)S(1)} %pad_add_fusion.2.at_ref, bf16[1536,640]{1,0:T(8,128)(2,1)S(1)} %copy-done.20, bf16[1536,640]{1,0:T(8,128)(2,1)S(1)} %get-tuple-element.281.y_ref.dk_ref), custom_call_target="tpu_custom_call" | custom-call | tf_op jit(solution)/shard_map/pallas_call | solution.py:71
  362.8 3.2 collective-permute-done.37.refs_2_
  366.0 5.7 %shard_map.289 = (bf16[4,192,1536]{2,1,0:T(8,128)(2,1)}, bf16[4,192,1536]{2,1,0:T(8,128)(2,1)}) custom-call(s32[2]{0:T(128)S(1)} %pad_add_fusion.2.at_ref, bf16[1536,512]{1,0:T(8,128)(2,1)S(1)} %copy-done.47, bf16[1536,512]{1,0:T(8,128)(2,1)S(1)} %get-tuple-element.257.y_ref.dq_ref), custom_call_target="tpu_custom_call" | custom-call | tf_op jit(solution)/shard_map/pallas_call | solution.py:71
  372.4 3.2 collective-permute-start.44
  376.8 12.0 %shard_map.290 = (f32[128,1536]{1,0:T(8,128)S(1)}, bf16[128,1536]{1,0:T(8,128)(2,1)}, bf16[128,1536]{1,0:T(8,128)(2,1)}, bf16[128,1536]{1,0:T(8,128)(2,1)S(1)}, f32[8,1536]{1,0:T(8,128)S(1)}) custom-call(bf16[1536,512]{1,0:T(8,128)(2,1)} %copy-done.23, bf16[1536,640]{1,0:T(8,128)(2,1)} %copy-done.7, bf16[1536,640]{1,0:T(8,128)(2,1)} %copy-done.9, ...), custom_call_target="tpu_custom_call" | custom-call | tf_op jit(solution)/shard_map/pallas_call | solution.py:681
  391.2 4.9 collective-permute-done.44.refs_1_.refs_9_
  397.7 3.1 shard_map.292
  405.3 2.0 collective-permute-start.50
  415.6 12.1 %shard_map.296 = (f32[512,1536]{1,0:T(8,128)}, f32[8,1536]{1,0:T(8,128)S(1)}) custom-call(bf16[1536,640]{1,0:T(8,128)(2,1)S(1)} %copy-done.8, bf16[1536,640]{1,0:T(8,128)(2,1)S(1)} %copy-done.10, bf16[1536,1536]{1,0:T(8,128)(2,1)} %copy-done.4, bf16[1536,1536]{1,0:T(8,128)(2,1)} %copy-done.5, bf16[512,1536]{1,0:T(8,128)(2,1)S(1)} %bitcast.137, ...), custom_call_target="tpu_custom_call" | custom-call | tf_op jit(solution)/shard_map/pallas_call | solution.py:636
  428.2 2.5 collective-permute-done.46.refs_1_.refs_3_
  435.2 3.7 collective-permute-done.49.refs_6_
  440.7 7.7 %collective-permute-done.54.refs_3_ = bf16[1,192,1536]{2,1,0:T(8,128)(2,1)S(1)} collective-permute-done((bf16[1,192,1536]{2,1,0:T(8,128)(2,1)}, bf16[1,192,1536]{2,1,0:T(8,128)(2,1)S(1)}, u32[]{:S(2)}, u32[]{:S(2)}) %collective-permute-start.54) | collective-permute-done | bytes 589856 | tf_op jit(solution)/shard_map/ppermute | solution.py:43
  448.4 2.3 collective-permute-done.53.refs_1_
  454.7 3.8 collective-permute-done.51.refs_1_.refs_3_
  458.5 2.1 collective-permute-done.52.refs_1_.refs_3_
  460.6 2.1 collective-permute-done.56
  470.4 2.7 collective-permute-done.60
  474.4 3.0 collective-permute-done.61
  485.1 1.7 pad_maximum_fusion.11
  489.2 1.7 collective-permute-start.64
  490.9 15.0 %collective-permute-done.67 = bf16[2,192,384]{2,1,0:T(8,128)(2,1)S(1)} collective-permute-done((bf16[2,192,384]{2,1,0:T(8,128)(2,1)}, bf16[2,192,384]{2,1,0:T(8,128)(2,1)S(1)}, u32[]{:S(2)}, u32[]{:S(2)}) %collective-permute-start.67) | collective-permute-done | bytes 294944 | tf_op jit(solution)/shard_map/ppermute | solution.py:21
  507.5 4.2 shard_map.303
  511.7 8.3 %collective-permute-done.63 = f32[8,1536]{1,0:T(8,128)S(1)} collective-permute-done((f32[8,1536]{1,0:T(8,128)S(1)}, f32[8,1536]{1,0:T(8,128)S(1)}, u32[]{:S(2)}, u32[]{:S(2)}) %collective-permute-start.63) | collective-permute-done | bytes 49184 | tf_op jit(solution)/shard_map/ppermute | solution.py:43
  (475 shorter events, 125.0 us)
Async XLA Ops:
  7.2 125.5 %all-gather.3.cloned.1.call-start = ((), (), s32[]{:S(2)}) async-start(), calls=%async_computation | async-start | bytes 3932160 | tf_op jit(solution)/shard_map/all_gather | solution.py:826
  8.5 24.4 %collective-permute-start.2 = (bf16[2,192,384]{2,1,0:T(8,128)(2,1)S(1)}, bf16[2,192,384]{2,1,0:T(8,128)(2,1)S(1)}, u32[]{:S(2)}, u32[]{:S(2)}) collective-permute-start(bf16[2,192,384]{2,1,0:T(8,128)(2,1)S(1)} %bitcast.145), channel_id=1, source_target_pairs={{0,3},{1,0},{2,1},{3,2},{4,7},{5,4},{6,5},{7,6},{8,11},{9,8},{10,9... | collective-permute-start | bytes 884744 | tf_op jit(solution)/shard_map/ppermute | solution.py:21
  13.6 25.1 %collective-permute-start.1 = (bf16[2,192,384]{2,1,0:T(8,128)(2,1)S(1)}, bf16[2,192,384]{2,1,0:T(8,128)(2,1)S(1)}, u32[]{:S(2)}, u32[]{:S(2)}) collective-permute-start(bf16[2,192,384]{2,1,0:T(8,128)(2,1)S(1)} %bitcast.146), channel_id=1, source_target_pairs={{0,2},{1,3},{2,0},{3,1},{4,6},{5,7},{6,4},{7,5},{8,10},{9,11},{10,... | collective-permute-start | bytes 884744 | tf_op jit(solution)/shard_map/ppermute | solution.py:21
  13.6 25.1 %collective-permute-start = (bf16[2,192,384]{2,1,0:T(8,128)(2,1)S(1)}, bf16[2,192,384]{2,1,0:T(8,128)(2,1)S(1)}, u32[]{:S(2)}, u32[]{:S(2)}) collective-permute-start(bf16[2,192,384]{2,1,0:T(8,128)(2,1)S(1)} %bitcast.147), channel_id=1, source_target_pairs={{0,1},{1,2},{2,3},{3,0},{4,5},{5,6},{6,7},{7,4},{8,9},{9,10},{10,1... | collective-permute-start | bytes 884744 | tf_op jit(solution)/shard_map/ppermute | solution.py:21
  38.8 8.7 %collective-permute-start.5 = (bf16[2,192,384]{2,1,0:T(8,128)(2,1)S(1)}, bf16[2,192,384]{2,1,0:T(8,128)(2,1)}, u32[]{:S(2)}, u32[]{:S(2)}) collective-permute-start(bf16[2,192,384]{2,1,0:T(8,128)(2,1)S(1)} %pad_maximum_fusion.9), channel_id=1, source_target_pairs={{0,3},{1,0},{2,1},{3,2},{4,7},{5,4},{6,5},{7,6},{8,11},{9,8},{10,9... | collective-permute-start | bytes 884744 | tf_op jit(solution)/shard_map/ppermute | solution.py:21
  38.8 28.3 %collective-permute-start.4 = (bf16[2,192,384]{2,1,0:T(8,128)(2,1)S(1)}, bf16[2,192,384]{2,1,0:T(8,128)(2,1)}, u32[]{:S(2)}, u32[]{:S(2)}) collective-permute-start(bf16[2,192,384]{2,1,0:T(8,128)(2,1)S(1)} %pad_maximum_fusion.9), channel_id=1, source_target_pairs={{0,2},{1,3},{2,0},{3,1},{4,6},{5,7},{6,4},{7,5},{8,10},{9,11},{10,... | collective-permute-start | bytes 884744 | tf_op jit(solution)/shard_map/ppermute | solution.py:21
  41.7 25.4 %collective-permute-start.3 = (bf16[2,192,384]{2,1,0:T(8,128)(2,1)S(1)}, bf16[2,192,384]{2,1,0:T(8,128)(2,1)}, u32[]{:S(2)}, u32[]{:S(2)}) collective-permute-start(bf16[2,192,384]{2,1,0:T(8,128)(2,1)S(1)} %pad_maximum_fusion.9), channel_id=1, source_target_pairs={{0,1},{1,2},{2,3},{3,0},{4,5},{5,6},{6,7},{7,4},{8,9},{9,10},{10,1... | collective-permute-start | bytes 884744 | tf_op jit(solution)/shard_map/ppermute | solution.py:21
  44.3 24.1 %collective-permute-start.6 = (bf16[1,3,192,384]{3,2,1,0:T(8,128)(2,1)S(1)}, bf16[1,3,192,384]{3,2,1,0:T(8,128)(2,1)}, u32[]{:S(2)}, u32[]{:S(2)}) collective-permute-start(bf16[1,3,192,384]{3,2,1,0:T(8,128)(2,1)S(1)} %maximum_bitcast_fusion.2), channel_id=1, source_target_pairs={{0,8},{4,12},{8,0},{12,4},{16,24},{20,28},{24,16},{28,20},{1,9},{5... | collective-permute-start | bytes 1327112 | tf_op jit(solution)/shard_map/ppermute | solution.py:43
  45.9 23.7 %collective-permute-start.7 = (bf16[1,3,192,384]{3,2,1,0:T(8,128)(2,1)S(1)}, bf16[1,3,192,384]{3,2,1,0:T(8,128)(2,1)}, u32[]{:S(2)}, u32[]{:S(2)}) collective-permute-start(bf16[1,3,192,384]{3,2,1,0:T(8,128)(2,1)S(1)} %maximum_bitcast_fusion.3), channel_id=1, source_target_pairs={{0,16},{4,20},{8,24},{12,28},{16,0},{20,4},{24,8},{28,12},{1,17},{... | collective-permute-start | bytes 1327112 | tf_op jit(solution)/shard_map/ppermute | solution.py:43
  70.8 20.2 %collective-permute-start.8 = (bf16[2,3,192,384]{3,2,1,0:T(8,128)(2,1)S(1)}, bf16[2,3,192,384]{3,2,1,0:T(8,128)(2,1)S(1)}, u32[]{:S(2)}, u32[]{:S(2)}) collective-permute-start(bf16[2,3,192,384]{3,2,1,0:T(8,128)(2,1)S(1)} %pad_maximum_fusion.3), channel_id=1, source_target_pairs={{0,16},{4,20},{8,24},{12,28},{16,0},{20,4},{24,8},{28,12},{1,17},{... | collective-permute-start | bytes 2654216 | tf_op jit(solution)/shard_map/ppermute | solution.py:43
  72.7 20.9 %collective-permute-start.9 = (bf16[2,3,192,384]{3,2,1,0:T(8,128)(2,1)S(1)}, bf16[2,3,192,384]{3,2,1,0:T(8,128)(2,1)S(1)}, u32[]{:S(2)}, u32[]{:S(2)}) collective-permute-start(bf16[2,3,192,384]{3,2,1,0:T(8,128)(2,1)S(1)} %pad_maximum_fusion.4), channel_id=1, source_target_pairs={{0,8},{4,12},{8,0},{12,4},{16,24},{20,28},{24,16},{28,20},{1,9},{5... | collective-permute-start | bytes 2654216 | tf_op jit(solution)/shard_map/ppermute | solution.py:43
  91.2 7.6 %collective-permute-start.12 = (bf16[4,3,192,384]{3,2,1,0:T(8,128)(2,1)S(1)}, bf16[4,3,192,384]{3,2,1,0:T(8,128)(2,1)S(1)}, u32[]{:S(2)}, u32[]{:S(2)}) collective-permute-start(bf16[4,3,192,384]{3,2,1,0:T(8,128)(2,1)S(1)} %constant_dynamic-update-slice_fusion.refs_1_), channel_id=1, source_target_pairs={{0,4},{4,0},{8,12},{12,8},{16,20},{20,16},{24,28},{28,24},{1,5},{5... | collective-permute-start | bytes 5308424 | tf_op jit(solution)/shard_map/ppermute | solution.py:43
  93.7 19.3 %collective-permute-start.15 = (bf16[4,3,192,384]{3,2,1,0:T(8,128)(2,1)S(1)}, bf16[4,3,192,384]{3,2,1,0:T(8,128)(2,1)S(1)}, u32[]{:S(2)}, u32[]{:S(2)}) collective-permute-start(bf16[4,3,192,384]{3,2,1,0:T(8,128)(2,1)S(1)} %constant_dynamic-update-slice_fusion.2.refs_1_), channel_id=1, source_target_pairs={{0,4},{4,0},{8,12},{12,8},{16,20},{20,16},{24,28},{28,24},{1,5},{5... | collective-permute-start | bytes 5308424 | tf_op jit(solution)/shard_map/ppermute | solution.py:43
  95.6 12.1 %collective-permute-start.10 = (bf16[1,3,192,384]{3,2,1,0:T(8,128)(2,1)S(1)}, bf16[1,3,192,384]{3,2,1,0:T(8,128)(2,1)S(1)}, u32[]{:S(2)}, u32[]{:S(2)}) collective-permute-start(bf16[1,3,192,384]{3,2,1,0:T(8,128)(2,1)S(1)} %maximum_bitcast_fusion), channel_id=1, source_target_pairs={{0,8},{4,12},{8,0},{12,4},{16,24},{20,28},{24,16},{28,20},{1,9},{5... | collective-permute-start | bytes 1327112 | tf_op jit(solution)/shard_map/ppermute | solution.py:43
  97.2 11.8 %collective-permute-start.11 = (bf16[1,3,192,384]{3,2,1,0:T(8,128)(2,1)S(1)}, bf16[1,3,192,384]{3,2,1,0:T(8,128)(2,1)S(1)}, u32[]{:S(2)}, u32[]{:S(2)}) collective-permute-start(bf16[1,3,192,384]{3,2,1,0:T(8,128)(2,1)S(1)} %maximum_bitcast_fusion.1), channel_id=1, source_target_pairs={{0,16},{4,20},{8,24},{12,28},{16,0},{20,4},{24,8},{28,12},{1,17},{... | collective-permute-start | bytes 1327112 | tf_op jit(solution)/shard_map/ppermute | solution.py:43
  109.1 20.5 %collective-permute-start.14 = (bf16[2,3,192,384]{3,2,1,0:T(8,128)(2,1)S(1)}, bf16[2,3,192,384]{3,2,1,0:T(8,128)(2,1)S(1)}, u32[]{:S(2)}, u32[]{:S(2)}) collective-permute-start(bf16[2,3,192,384]{3,2,1,0:T(8,128)(2,1)S(1)} %pad_maximum_fusion.6), channel_id=1, source_target_pairs={{0,8},{4,12},{8,0},{12,4},{16,24},{20,28},{24,16},{28,20},{1,9},{5... | collective-permute-start | bytes 2654216 | tf_op jit(solution)/shard_map/ppermute | solution.py:43
  109.8 20.3 %collective-permute-start.13 = (bf16[2,3,192,384]{3,2,1,0:T(8,128)(2,1)S(1)}, bf16[2,3,192,384]{3,2,1,0:T(8,128)(2,1)S(1)}, u32[]{:S(2)}, u32[]{:S(2)}) collective-permute-start(bf16[2,3,192,384]{3,2,1,0:T(8,128)(2,1)S(1)} %pad_maximum_fusion.5), channel_id=1, source_target_pairs={{0,16},{4,20},{8,24},{12,28},{16,0},{20,4},{24,8},{28,12},{1,17},{... | collective-permute-start | bytes 2654216 | tf_op jit(solution)/shard_map/ppermute | solution.py:43
  131.2 5.8 %collective-permute-start.17 = (bf16[4,3,192,384]{3,2,1,0:T(8,128)(2,1)}, bf16[4,3,192,384]{3,2,1,0:T(8,128)(2,1)}, u32[]{:S(2)}, u32[]{:S(2)}) collective-permute-start(bf16[4,3,192,384]{3,2,1,0:T(8,128)(2,1)} %constant_dynamic-update-slice_fusion.7.refs_3_.refs_2_), channel_id=1, source_target_pairs={{0,4},{4,0},{8,12},{12,8},{16,20},{20,16},{24,28},{28,24},{1,5},{5... | collective-permute-start | bytes 5308424 | tf_op jit(solution)/shard_map/ppermute | solution.py:43
  132.2 5.5 %collective-permute-start.16 = (bf16[4,3,192,384]{3,2,1,0:T(8,128)(2,1)}, bf16[4,3,192,384]{3,2,1,0:T(8,128)(2,1)}, u32[]{:S(2)}, u32[]{:S(2)}) collective-permute-start(bf16[4,3,192,384]{3,2,1,0:T(8,128)(2,1)} %constant_dynamic-update-slice_fusion.4.refs_1_.refs_0_), channel_id=1, source_target_pairs={{0,4},{4,0},{8,12},{12,8},{16,20},{20,16},{24,28},{28,24},{1,5},{5... | collective-permute-start | bytes 5308424 | tf_op jit(solution)/shard_map/ppermute | solution.py:43
  155.6 17.7 %collective-permute-start.18 = (bf16[1632,128]{1,0:T(8,128)(2,1)}, bf16[1632,128]{1,0:T(8,128)(2,1)}, u32[]{:S(2)}, u32[]{:S(2)}) collective-permute-start(bf16[1632,128]{1,0:T(8,128)(2,1)} %get-tuple-element.195), channel_id=1, source_target_pairs={{0,3},{1,0},{2,1},{3,2},{4,7},{5,4},{6,5},{7,6},{8,11},{9,8},{10,9... | collective-permute-start | bytes 1253384 | tf_op jit(solution)/shard_map/ppermute | solution.py:21
  155.6 39.5 %collective-permute-start.19 = (bf16[1632,128]{1,0:T(8,128)(2,1)}, bf16[1632,128]{1,0:T(8,128)(2,1)}, u32[]{:S(2)}, u32[]{:S(2)}) collective-permute-start(bf16[1632,128]{1,0:T(8,128)(2,1)} %get-tuple-element.196), channel_id=1, source_target_pairs={{0,2},{1,3},{2,0},{3,1},{4,6},{5,7},{6,4},{7,5},{8,10},{9,11},{10,... | collective-permute-start | bytes 1253384 | tf_op jit(solution)/shard_map/ppermute | solution.py:21
  158.8 36.4 %collective-permute-start.20 = (bf16[1632,128]{1,0:T(8,128)(2,1)}, bf16[1632,128]{1,0:T(8,128)(2,1)}, u32[]{:S(2)}, u32[]{:S(2)}) collective-permute-start(bf16[1632,128]{1,0:T(8,128)(2,1)} %get-tuple-element.197), channel_id=1, source_target_pairs={{0,1},{1,2},{2,3},{3,0},{4,5},{5,6},{6,7},{7,4},{8,9},{9,10},{10,1... | collective-permute-start | bytes 1253384 | tf_op jit(solution)/shard_map/ppermute | solution.py:21
  167.0 5.8 %collective-permute-start.23 = (f32[8,128]{1,0:T(8,128)S(1)}, f32[8,128]{1,0:T(8,128)S(1)}, u32[]{:S(2)}, u32[]{:S(2)}) collective-permute-start(f32[8,128]{1,0:T(8,128)S(1)} %add.341), channel_id=1, source_target_pairs={{0,16},{4,20},{8,24},{12,28},{16,0},{20,4},{24,8},{28,12},{1,17},{... | collective-permute-start | bytes 12296 | tf_op jit(solution)/shard_map/ppermute | solution.py:43
  198.3 10.4 %collective-permute-start.26 = (bf16[128,1536]{1,0:T(8,128)(2,1)S(1)}, bf16[128,1536]{1,0:T(8,128)(2,1)S(1)}, u32[]{:S(2)}, u32[]{:S(2)}) collective-permute-start(bf16[128,1536]{1,0:T(8,128)(2,1)S(1)} %add_convert_fusion), channel_id=1, source_target_pairs={{0,3},{1,0},{2,1},{3,2},{4,7},{5,4},{6,5},{7,6},{8,11},{9,8},{10,9... | collective-permute-start | bytes 1179656 | tf_op jit(solution)/shard_map/ppermute | solution.py:21
  198.4 35.0 %collective-permute-start.25 = (bf16[128,1536]{1,0:T(8,128)(2,1)S(1)}, bf16[128,1536]{1,0:T(8,128)(2,1)S(1)}, u32[]{:S(2)}, u32[]{:S(2)}) collective-permute-start(bf16[128,1536]{1,0:T(8,128)(2,1)S(1)} %add_convert_fusion), channel_id=1, source_target_pairs={{0,2},{1,3},{2,0},{3,1},{4,6},{5,7},{6,4},{7,5},{8,10},{9,11},{10,... | collective-permute-start | bytes 1179656 | tf_op jit(solution)/shard_map/ppermute | solution.py:21
  198.9 34.5 %collective-permute-start.24 = (bf16[128,1536]{1,0:T(8,128)(2,1)S(1)}, bf16[128,1536]{1,0:T(8,128)(2,1)S(1)}, u32[]{:S(2)}, u32[]{:S(2)}) collective-permute-start(bf16[128,1536]{1,0:T(8,128)(2,1)S(1)} %add_convert_fusion), channel_id=1, source_target_pairs={{0,1},{1,2},{2,3},{3,0},{4,5},{5,6},{6,7},{7,4},{8,9},{9,10},{10,1... | collective-permute-start | bytes 1179656 | tf_op jit(solution)/shard_map/ppermute | solution.py:21
  243.6 21.3 %collective-permute-start.29 = (bf16[128,1536]{1,0:T(8,128)(2,1)}, bf16[128,1536]{1,0:T(8,128)(2,1)}, u32[]{:S(2)}, u32[]{:S(2)}) collective-permute-start(bf16[128,1536]{1,0:T(8,128)(2,1)} %get-tuple-element.410), channel_id=1, source_target_pairs={{0,1},{1,2},{2,3},{3,0},{4,5},{5,6},{6,7},{7,4},{8,9},{9,10},{10,1... | collective-permute-start | bytes 1179656 | tf_op jit(solution)/shard_map/ppermute | solution.py:21
  243.6 29.7 %collective-permute-start.28 = (bf16[128,1536]{1,0:T(8,128)(2,1)}, bf16[128,1536]{1,0:T(8,128)(2,1)}, u32[]{:S(2)}, u32[]{:S(2)}) collective-permute-start(bf16[128,1536]{1,0:T(8,128)(2,1)} %get-tuple-element.411), channel_id=1, source_target_pairs={{0,2},{1,3},{2,0},{3,1},{4,6},{5,7},{6,4},{7,5},{8,10},{9,11},{10,... | collective-permute-start | bytes 1179656 | tf_op jit(solution)/shard_map/ppermute | solution.py:21
  244.9 28.4 %collective-permute-start.27 = (bf16[128,1536]{1,0:T(8,128)(2,1)}, bf16[128,1536]{1,0:T(8,128)(2,1)}, u32[]{:S(2)}, u32[]{:S(2)}) collective-permute-start(bf16[128,1536]{1,0:T(8,128)(2,1)} %get-tuple-element.412), channel_id=1, source_target_pairs={{0,3},{1,0},{2,1},{3,2},{4,7},{5,4},{6,5},{7,6},{8,11},{9,8},{10,9... | collective-permute-start | bytes 1179656 | tf_op jit(solution)/shard_map/ppermute | solution.py:21
  259.0 34.0 %collective-permute-start.33 = (bf16[4,192,1536]{2,1,0:T(8,128)(2,1)}, bf16[4,192,1536]{2,1,0:T(8,128)(2,1)S(1)}, u32[]{:S(2)}, u32[]{:S(2)}) collective-permute-start(bf16[4,192,1536]{2,1,0:T(8,128)(2,1)} %get-tuple-element.213), channel_id=1, source_target_pairs={{0,4},{4,0},{8,12},{12,8},{16,20},{20,16},{24,28},{28,24},{1,5},{5... | collective-permute-start | bytes 7077896 | tf_op jit(solution)/shard_map/ppermute | solution.py:43
  264.5 29.8 %collective-permute-start.34 = (bf16[4,192,1536]{2,1,0:T(8,128)(2,1)}, bf16[4,192,1536]{2,1,0:T(8,128)(2,1)S(1)}, u32[]{:S(2)}, u32[]{:S(2)}) collective-permute-start(bf16[4,192,1536]{2,1,0:T(8,128)(2,1)} %get-tuple-element.215), channel_id=1, source_target_pairs={{0,4},{4,0},{8,12},{12,8},{16,20},{20,16},{24,28},{28,24},{1,5},{5... | collective-permute-start | bytes 7077896 | tf_op jit(solution)/shard_map/ppermute | solution.py:43
  281.3 12.9 %collective-permute-start.35 = (bf16[4,192,1536]{2,1,0:T(8,128)(2,1)}, bf16[4,192,1536]{2,1,0:T(8,128)(2,1)S(1)}, u32[]{:S(2)}, u32[]{:S(2)}) collective-permute-start(bf16[4,192,1536]{2,1,0:T(8,128)(2,1)} %get-tuple-element.222), channel_id=1, source_target_pairs={{0,4},{4,0},{8,12},{12,8},{16,20},{20,16},{24,28},{28,24},{1,5},{5... | collective-permute-start | bytes 7077896 | tf_op jit(solution)/shard_map/ppermute | solution.py:43
  283.5 20.0 %collective-permute-start.32 = (bf16[1632,128]{1,0:T(8,128)(2,1)S(1)}, bf16[1632,128]{1,0:T(8,128)(2,1)S(1)}, u32[]{:S(2)}, u32[]{:S(2)}) collective-permute-start(bf16[1632,128]{1,0:T(8,128)(2,1)S(1)} %shard_map.280.rest_0_.rest_4_), channel_id=1, source_target_pairs={{0,3},{1,0},{2,1},{3,2},{4,7},{5,4},{6,5},{7,6},{8,11},{9,8},{10,9... | collective-permute-start | bytes 1253384 | tf_op jit(solution)/shard_map/ppermute | solution.py:21
  292.7 37.2 %collective-permute-start.31 = (bf16[1632,128]{1,0:T(8,128)(2,1)S(1)}, bf16[1632,128]{1,0:T(8,128)(2,1)S(1)}, u32[]{:S(2)}, u32[]{:S(2)}) collective-permute-start(bf16[1632,128]{1,0:T(8,128)(2,1)S(1)} %shard_map.280.rest_0_.rest_4_), channel_id=1, source_target_pairs={{0,2},{1,3},{2,0},{3,1},{4,6},{5,7},{6,4},{7,5},{8,10},{9,11},{10,... | collective-permute-start | bytes 1253384 | tf_op jit(solution)/shard_map/ppermute | solution.py:21
  293.0 36.9 %collective-permute-start.30 = (bf16[1632,128]{1,0:T(8,128)(2,1)S(1)}, bf16[1632,128]{1,0:T(8,128)(2,1)S(1)}, u32[]{:S(2)}, u32[]{:S(2)}) collective-permute-start(bf16[1632,128]{1,0:T(8,128)(2,1)S(1)} %shard_map.280.rest_0_.rest_4_), channel_id=1, source_target_pairs={{0,1},{1,2},{2,3},{3,0},{4,5},{5,6},{6,7},{7,4},{8,9},{9,10},{10,1... | collective-permute-start | bytes 1253384 | tf_op jit(solution)/shard_map/ppermute | solution.py:21
  296.7 47.9 %collective-permute-start.39 = (bf16[2,192,2304]{2,1,0:T(8,128)(2,1)}, bf16[2,192,2304]{2,1,0:T(8,128)(2,1)S(1)}, u32[]{:S(2)}, u32[]{:S(2)}) collective-permute-start(bf16[2,192,2304]{2,1,0:T(8,128)(2,1)} %get-tuple-element.226), channel_id=1, source_target_pairs={{0,8},{4,12},{8,0},{12,4},{16,24},{20,28},{24,16},{28,20},{1,9},{5... | collective-permute-start | bytes 5308424 | tf_op jit(solution)/shard_map/ppermute | solution.py:43
  301.4 44.7 %collective-permute-start.40 = (bf16[2,192,2304]{2,1,0:T(8,128)(2,1)}, bf16[2,192,2304]{2,1,0:T(8,128)(2,1)S(1)}, u32[]{:S(2)}, u32[]{:S(2)}) collective-permute-start(bf16[2,192,2304]{2,1,0:T(8,128)(2,1)} %get-tuple-element.229), channel_id=1, source_target_pairs={{0,16},{4,20},{8,24},{12,28},{16,0},{20,4},{24,8},{28,12},{1,17},{... | collective-permute-start | bytes 5308424 | tf_op jit(solution)/shard_map/ppermute | solution.py:43
  329.9 33.0 %collective-permute-start.36 = (bf16[128,1536]{1,0:T(8,128)(2,1)S(1)}, bf16[128,1536]{1,0:T(8,128)(2,1)S(1)}, u32[]{:S(2)}, u32[]{:S(2)}) collective-permute-start(bf16[128,1536]{1,0:T(8,128)(2,1)S(1)} %copy-done.79), channel_id=1, source_target_pairs={{0,3},{1,0},{2,1},{3,2},{4,7},{5,4},{6,5},{7,6},{8,11},{9,8},{10,9... | collective-permute-start | bytes 1179656 | tf_op jit(solution)/shard_map/ppermute | solution.py:21
  329.9 36.1 %collective-permute-start.37 = (bf16[128,1536]{1,0:T(8,128)(2,1)S(1)}, bf16[128,1536]{1,0:T(8,128)(2,1)S(1)}, u32[]{:S(2)}, u32[]{:S(2)}) collective-permute-start(bf16[128,1536]{1,0:T(8,128)(2,1)S(1)} %copy-done.77), channel_id=1, source_target_pairs={{0,2},{1,3},{2,0},{3,1},{4,6},{5,7},{6,4},{7,5},{8,10},{9,11},{10,... | collective-permute-start | bytes 1179656 | tf_op jit(solution)/shard_map/ppermute | solution.py:21
  331.8 34.2 %collective-permute-start.38 = (bf16[128,1536]{1,0:T(8,128)(2,1)S(1)}, bf16[128,1536]{1,0:T(8,128)(2,1)S(1)}, u32[]{:S(2)}, u32[]{:S(2)}) collective-permute-start(bf16[128,1536]{1,0:T(8,128)(2,1)S(1)} %copy-done.75), channel_id=1, source_target_pairs={{0,1},{1,2},{2,3},{3,0},{4,5},{5,6},{6,7},{7,4},{8,9},{9,10},{10,1... | collective-permute-start | bytes 1179656 | tf_op jit(solution)/shard_map/ppermute | solution.py:21
  371.8 18.0 %collective-permute-start.41 = (bf16[4,192,1536]{2,1,0:T(8,128)(2,1)}, bf16[4,192,1536]{2,1,0:T(8,128)(2,1)S(1)}, u32[]{:S(2)}, u32[]{:S(2)}) collective-permute-start(bf16[4,192,1536]{2,1,0:T(8,128)(2,1)} %get-tuple-element.255), channel_id=1, source_target_pairs={{0,4},{4,0},{8,12},{12,8},{16,20},{20,16},{24,28},{28,24},{1,5},{5... | collective-permute-start | bytes 7077896 | tf_op jit(solution)/shard_map/ppermute | solution.py:43
  371.8 19.3 %collective-permute-start.42 = (bf16[4,192,1536]{2,1,0:T(8,128)(2,1)}, bf16[4,192,1536]{2,1,0:T(8,128)(2,1)}, u32[]{:S(2)}, u32[]{:S(2)}) collective-permute-start(bf16[4,192,1536]{2,1,0:T(8,128)(2,1)} %get-tuple-element.256), channel_id=1, source_target_pairs={{0,4},{4,0},{8,12},{12,8},{16,20},{20,16},{24,28},{28,24},{1,5},{5... | collective-permute-start | bytes 7077896 | tf_op jit(solution)/shard_map/ppermute | solution.py:43
  372.3 18.8 %collective-permute-start.43 = (bf16[4,192,1536]{2,1,0:T(8,128)(2,1)}, bf16[4,192,1536]{2,1,0:T(8,128)(2,1)S(1)}, u32[]{:S(2)}, u32[]{:S(2)}) collective-permute-start(bf16[4,192,1536]{2,1,0:T(8,128)(2,1)} %get-tuple-element.254), channel_id=1, source_target_pairs={{0,4},{4,0},{8,12},{12,8},{16,20},{20,16},{24,28},{28,24},{1,5},{5... | collective-permute-start | bytes 7077896 | tf_op jit(solution)/shard_map/ppermute | solution.py:43
  372.4 23.7 %collective-permute-start.44 = (bf16[1,192,2304]{2,1,0:T(8,128)(2,1)}, bf16[1,192,2304]{2,1,0:T(8,128)(2,1)S(1)}, u32[]{:S(2)}, u32[]{:S(2)}) collective-permute-start(bf16[1,192,2304]{2,1,0:T(8,128)(2,1)} %get-tuple-element.242), channel_id=1, source_target_pairs={{0,16},{4,20},{8,24},{12,28},{16,0},{20,4},{24,8},{28,12},{1,17},{... | collective-permute-start | bytes 2654216 | tf_op jit(solution)/shard_map/ppermute | solution.py:43
  375.6 22.0 %collective-permute-start.45 = (bf16[1,192,2304]{2,1,0:T(8,128)(2,1)}, bf16[1,192,2304]{2,1,0:T(8,128)(2,1)}, u32[]{:S(2)}, u32[]{:S(2)}) collective-permute-start(bf16[1,192,2304]{2,1,0:T(8,128)(2,1)} %get-tuple-element.244), channel_id=1, source_target_pairs={{0,8},{4,12},{8,0},{12,4},{16,24},{20,28},{24,16},{28,20},{1,9},{5... | collective-permute-start | bytes 2654216 | tf_op jit(solution)/shard_map/ppermute | solution.py:43
  400.7 27.4 %collective-permute-start.47 = (bf16[2,192,1536]{2,1,0:T(8,128)(2,1)}, bf16[2,192,1536]{2,1,0:T(8,128)(2,1)S(1)}, u32[]{:S(2)}, u32[]{:S(2)}) collective-permute-start(bf16[2,192,1536]{2,1,0:T(8,128)(2,1)} %get-tuple-element.269), channel_id=1, source_target_pairs={{0,16},{4,20},{8,24},{12,28},{16,0},{20,4},{24,8},{28,12},{1,17},{... | collective-permute-start | bytes 3538952 | tf_op jit(solution)/shard_map/ppermute | solution.py:43
  403.2 27.4 %collective-permute-start.46 = (bf16[2,192,1536]{2,1,0:T(8,128)(2,1)}, bf16[2,192,1536]{2,1,0:T(8,128)(2,1)S(1)}, u32[]{:S(2)}, u32[]{:S(2)}) collective-permute-start(bf16[2,192,1536]{2,1,0:T(8,128)(2,1)} %get-tuple-element.265), channel_id=1, source_target_pairs={{0,8},{4,12},{8,0},{12,4},{16,24},{20,28},{24,16},{28,20},{1,9},{5... | collective-permute-start | bytes 3538952 | tf_op jit(solution)/shard_map/ppermute | solution.py:43
  404.4 30.8 %collective-permute-start.48 = (bf16[128,1536]{1,0:T(8,128)(2,1)}, bf16[128,1536]{1,0:T(8,128)(2,1)S(1)}, u32[]{:S(2)}, u32[]{:S(2)}) collective-permute-start(bf16[128,1536]{1,0:T(8,128)(2,1)} %get-tuple-element.291), channel_id=1, source_target_pairs={{0,3},{1,0},{2,1},{3,2},{4,7},{5,4},{6,5},{7,6},{8,11},{9,8},{10,9... | collective-permute-start | bytes 1179656 | tf_op jit(solution)/shard_map/ppermute | solution.py:21
  404.9 34.0 %collective-permute-start.49 = (bf16[128,1536]{1,0:T(8,128)(2,1)}, bf16[128,1536]{1,0:T(8,128)(2,1)S(1)}, u32[]{:S(2)}, u32[]{:S(2)}) collective-permute-start(bf16[128,1536]{1,0:T(8,128)(2,1)} %get-tuple-element.292), channel_id=1, source_target_pairs={{0,2},{1,3},{2,0},{3,1},{4,6},{5,7},{6,4},{7,5},{8,10},{9,11},{10,... | collective-permute-start | bytes 1179656 | tf_op jit(solution)/shard_map/ppermute | solution.py:21
  405.3 33.5 %collective-permute-start.50 = (bf16[128,1536]{1,0:T(8,128)(2,1)S(1)}, bf16[128,1536]{1,0:T(8,128)(2,1)}, u32[]{:S(2)}, u32[]{:S(2)}) collective-permute-start(bf16[128,1536]{1,0:T(8,128)(2,1)S(1)} %get-tuple-element.293), channel_id=1, source_target_pairs={{0,1},{1,2},{2,3},{3,0},{4,5},{5,6},{6,7},{7,4},{8,9},{9,10},{10,1... | collective-permute-start | bytes 1179656 | tf_op jit(solution)/shard_map/ppermute | solution.py:21
  431.9 16.5 %collective-permute-start.54 = (bf16[1,192,1536]{2,1,0:T(8,128)(2,1)}, bf16[1,192,1536]{2,1,0:T(8,128)(2,1)S(1)}, u32[]{:S(2)}, u32[]{:S(2)}) collective-permute-start(bf16[1,192,1536]{2,1,0:T(8,128)(2,1)} %get-tuple-element.287), channel_id=1, source_target_pairs={{0,8},{4,12},{8,0},{12,4},{16,24},{20,28},{24,16},{28,20},{1,9},{5... | collective-permute-start | bytes 1769480 | tf_op jit(solution)/shard_map/ppermute | solution.py:43
  434.2 16.5 %collective-permute-start.53 = (bf16[1,192,1536]{2,1,0:T(8,128)(2,1)}, bf16[1,192,1536]{2,1,0:T(8,128)(2,1)S(1)}, u32[]{:S(2)}, u32[]{:S(2)}) collective-permute-start(bf16[1,192,1536]{2,1,0:T(8,128)(2,1)} %get-tuple-element.284), channel_id=1, source_target_pairs={{0,16},{4,20},{8,24},{12,28},{16,0},{20,4},{24,8},{28,12},{1,17},{... | collective-permute-start | bytes 1769480 | tf_op jit(solution)/shard_map/ppermute | solution.py:43
  438.9 19.6 %collective-permute-start.51 = (bf16[2,192,768]{2,1,0:T(8,128)(2,1)S(1)}, bf16[2,192,768]{2,1,0:T(8,128)(2,1)S(1)}, u32[]{:S(2)}, u32[]{:S(2)}) collective-permute-start(bf16[2,192,768]{2,1,0:T(8,128)(2,1)S(1)} %copy-done.115), channel_id=1, source_target_pairs={{0,8},{4,12},{8,0},{12,4},{16,24},{20,28},{24,16},{28,20},{1,9},{5... | collective-permute-start | bytes 1769480 | tf_op jit(solution)/shard_map/ppermute | solution.py:43
  439.7 20.8 %collective-permute-start.52 = (bf16[2,192,768]{2,1,0:T(8,128)(2,1)S(1)}, bf16[2,192,768]{2,1,0:T(8,128)(2,1)S(1)}, u32[]{:S(2)}, u32[]{:S(2)}) collective-permute-start(bf16[2,192,768]{2,1,0:T(8,128)(2,1)S(1)} %copy-done.114), channel_id=1, source_target_pairs={{0,16},{4,20},{8,24},{12,28},{16,0},{20,4},{24,8},{28,12},{1,17},{... | collective-permute-start | bytes 1769480 | tf_op jit(solution)/shard_map/ppermute | solution.py:43
  452.6 7.9 %collective-permute-start.55 = (bf16[2,192,384]{2,1,0:T(8,128)(2,1)S(1)}, bf16[2,192,384]{2,1,0:T(8,128)(2,1)S(1)}, u32[]{:S(2)}, u32[]{:S(2)}) collective-permute-start(bf16[2,192,384]{2,1,0:T(8,128)(2,1)S(1)} %get-tuple-element.298), channel_id=1, source_target_pairs={{0,3},{1,0},{2,1},{3,2},{4,7},{5,4},{6,5},{7,6},{8,11},{9,8},{10,9... | collective-permute-start | bytes 884744 | tf_op jit(solution)/shard_map/ppermute | solution.py:21
  453.2 9.5 %collective-permute-start.56 = (bf16[2,192,384]{2,1,0:T(8,128)(2,1)S(1)}, bf16[2,192,384]{2,1,0:T(8,128)(2,1)S(1)}, u32[]{:S(2)}, u32[]{:S(2)}) collective-permute-start(bf16[2,192,384]{2,1,0:T(8,128)(2,1)S(1)} %get-tuple-element.299), channel_id=1, source_target_pairs={{0,1},{1,2},{2,3},{3,0},{4,5},{5,6},{6,7},{7,4},{8,9},{9,10},{10,1... | collective-permute-start | bytes 884744 | tf_op jit(solution)/shard_map/ppermute | solution.py:21
  463.6 15.9 %collective-permute-start.58 = (bf16[1,192,768]{2,1,0:T(8,128)(2,1)}, bf16[1,192,768]{2,1,0:T(8,128)(2,1)S(1)}, u32[]{:S(2)}, u32[]{:S(2)}) collective-permute-start(bf16[1,192,768]{2,1,0:T(8,128)(2,1)} %get-tuple-element.306), channel_id=1, source_target_pairs={{0,8},{4,12},{8,0},{12,4},{16,24},{20,28},{24,16},{28,20},{1,9},{5... | collective-permute-start | bytes 884744 | tf_op jit(solution)/shard_map/ppermute | solution.py:43
  465.4 14.2 %collective-permute-start.57 = (bf16[1,192,768]{2,1,0:T(8,128)(2,1)}, bf16[1,192,768]{2,1,0:T(8,128)(2,1)S(1)}, u32[]{:S(2)}, u32[]{:S(2)}) collective-permute-start(bf16[1,192,768]{2,1,0:T(8,128)(2,1)} %get-tuple-element.302), channel_id=1, source_target_pairs={{0,16},{4,20},{8,24},{12,28},{16,0},{20,4},{24,8},{28,12},{1,17},{... | collective-permute-start | bytes 884744 | tf_op jit(solution)/shard_map/ppermute | solution.py:43
  478.2 27.7 %collective-permute-start.67 = (bf16[2,192,384]{2,1,0:T(8,128)(2,1)}, bf16[2,192,384]{2,1,0:T(8,128)(2,1)S(1)}, u32[]{:S(2)}, u32[]{:S(2)}) collective-permute-start(bf16[2,192,384]{2,1,0:T(8,128)(2,1)} %copy-done.80), channel_id=1, source_target_pairs={{0,2},{1,3},{2,0},{3,1},{4,6},{5,7},{6,4},{7,5},{8,10},{9,11},{10,... | collective-permute-start | bytes 884744 | tf_op jit(solution)/shard_map/ppermute | solution.py:21
  483.1 23.0 %collective-permute-start.62 = (f32[8,1536]{1,0:T(8,128)S(1)}, f32[8,1536]{1,0:T(8,128)S(1)}, u32[]{:S(2)}, u32[]{:S(2)}) collective-permute-start(f32[8,1536]{1,0:T(8,128)S(1)} %add.357), channel_id=1, source_target_pairs={{0,1},{1,0},{2,3},{3,2},{4,5},{5,4},{6,7},{7,6},{8,9},{9,8},{10,11... | collective-permute-start | bytes 147464 | tf_op jit(solution)/shard_map/ppermute | solution.py:43
  484.3 38.2 %collective-permute-start.66 = (bf16[2,192,384]{2,1,0:T(8,128)(2,1)}, bf16[2,192,384]{2,1,0:T(8,128)(2,1)}, u32[]{:S(2)}, u32[]{:S(2)}) collective-permute-start(bf16[2,192,384]{2,1,0:T(8,128)(2,1)} %pad_maximum_fusion.12), channel_id=1, source_target_pairs={{0,1},{1,2},{2,3},{3,0},{4,5},{5,6},{6,7},{7,4},{8,9},{9,10},{10,1... | collective-permute-start | bytes 884744 | tf_op jit(solution)/shard_map/ppermute | solution.py:21
  486.8 35.8 %collective-permute-start.65 = (bf16[2,192,384]{2,1,0:T(8,128)(2,1)}, bf16[2,192,384]{2,1,0:T(8,128)(2,1)}, u32[]{:S(2)}, u32[]{:S(2)}) collective-permute-start(bf16[2,192,384]{2,1,0:T(8,128)(2,1)} %pad_maximum_fusion.11), channel_id=1, source_target_pairs={{0,2},{1,3},{2,0},{3,1},{4,6},{5,7},{6,4},{7,5},{8,10},{9,11},{10,... | collective-permute-start | bytes 884744 | tf_op jit(solution)/shard_map/ppermute | solution.py:21
  489.2 33.4 %collective-permute-start.64 = (bf16[2,192,384]{2,1,0:T(8,128)(2,1)}, bf16[2,192,384]{2,1,0:T(8,128)(2,1)}, u32[]{:S(2)}, u32[]{:S(2)}) collective-permute-start(bf16[2,192,384]{2,1,0:T(8,128)(2,1)} %pad_maximum_fusion.10), channel_id=1, source_target_pairs={{0,3},{1,0},{2,1},{3,2},{4,7},{5,4},{6,5},{7,6},{8,11},{9,8},{10,9... | collective-permute-start | bytes 884744 | tf_op jit(solution)/shard_map/ppermute | solution.py:21
  506.1 14.0 %collective-permute-start.63 = (f32[8,1536]{1,0:T(8,128)S(1)}, f32[8,1536]{1,0:T(8,128)S(1)}, u32[]{:S(2)}, u32[]{:S(2)}) collective-permute-start(f32[8,1536]{1,0:T(8,128)S(1)} %add.358), channel_id=1, source_target_pairs={{0,2},{1,3},{2,0},{3,1},{4,6},{5,7},{6,4},{7,5},{8,10},{9,11},{10,... | collective-permute-start | bytes 147464 | tf_op jit(solution)/shard_map/ppermute | solution.py:43
  (125 other events, 1503.5 us)
Sparse Core Ops, SparseCore 0:
  68.2 61.7 all-gather.2
